TPU v7x, 256 devices: a whole 4x4x8 slice. The times are simulated.
256 devices in a mesh: task: 32 (over x, z_hi, core), tensor: 8 (over z_lo, y).
Axes of the slice: x: 4, y: 4, z: 8 (z_hi: 4, z_lo: 2; z = z_hi * 2 + z_lo), core: 2. Of those that a mesh axis runs over, the one named last changes fastest.
Arguments:
- tokens: bfloat16 [256, 8192], P('task', 'tensor'), may hold values from -6 to 6
- router: float32 [256, 16], P('task'), may hold values from 0 to 1
- gate_up_weight: bfloat16 [2, 8192, 29568], P(None, 'task', 'tensor'), may hold values from -0.0625 to 0.0625
- down_weight: bfloat16 [29568, 8192], P('tensor', 'task'), may hold values from -0.03125 to 0.03125
- lower_factor: bfloat16 [2, 8192, 4096], P(None, 'tensor', 'task'), may hold values from -0.0625 to 0.0625
- upper_factor: bfloat16 [2, 4096, 29568], P(None, 'task', 'tensor'), may hold values from -0.09375 to 0.09375
Outputs:
- mixed: float32 [256, 8192], P('tensor', 'task')
All inputs are finite; a program needn't handle non-finite values.
Results may differ from a plain program's by a relative error of at most 0.015.
Values may be sent and summed in bfloat16 or wider, within the bound.
No kernel may reach another device: no remote copies, remote signals or barrier semaphores. Data moves between devices by JAX's collectives and lax.ppermute only.
A program may use at most 64 MiB of HBM per device.

v0:
```python
import jax
import jax.numpy as jnp
from jax import lax
from jax.sharding import PartitionSpec as P

TASKS = 16
RANK = 256


def on_device(tokens, router, gate_up_weight, down_weight, lower_factor, upper_factor):
    task_count = lax.axis_size("task")
    tensor_count = lax.axis_size("tensor")
    row_part, weights = (
        lax.all_gather(tokens, "task", axis=0, tiled=True),
        lax.all_gather(router.astype(jnp.bfloat16), "task", axis=0, tiled=True).astype(
            router.dtype
        ),
    )
    features = lax.all_gather(row_part, "tensor", axis=1, tiled=True)
    model_width = features.shape[1]
    task_width = model_width // task_count
    tensor_width = model_width // tensor_count
    own_columns = lax.dynamic_slice_in_dim(
        features, lax.axis_index("task") * task_width, task_width, 1
    )
    tensor_columns = lax.dynamic_slice_in_dim(
        features, lax.axis_index("tensor") * tensor_width, tensor_width, 1
    )
    latent_part = jnp.einsum(
        "td,gdr->tgr", tensor_columns, lower_factor, preferred_element_type=jnp.float32
    )
    rank_sum = lax.psum(latent_part, "tensor")
    rank_cols = lower_factor.shape[2]
    global_rank = lax.axis_index("task") * rank_cols + jnp.arange(rank_cols, dtype=jnp.int32)
    task_ids = global_rank // RANK
    onehot = (task_ids[None, :] == jnp.arange(TASKS, dtype=jnp.int32)[:, None]).astype(jnp.float32)
    task_scale = jnp.dot(weights, onehot, precision=lax.Precision.HIGHEST)
    scaled = (rank_sum * task_scale[:, None, :]).astype(jnp.bfloat16)
    part = own_columns
    shared_part = lax.psum_scatter(
        jnp.einsum("td,gdf->tgf", part, gate_up_weight, preferred_element_type=jnp.float32),
        "task",
        scatter_dimension=0,
        tiled=True,
    )
    part = scaled
    task_part = lax.psum_scatter(
        jnp.einsum("tgr,grf->tgf", part, upper_factor, preferred_element_type=jnp.float32),
        "task",
        scatter_dimension=0,
        tiled=True,
    )
    summed = shared_part + task_part
    hidden = (jax.nn.silu(summed[:, 0]) * summed[:, 1]).astype(jnp.bfloat16)
    projected = jnp.dot(
        lax.all_gather(hidden, "task", axis=0, tiled=True),
        down_weight,
        preferred_element_type=jnp.float32,
    )
    return lax.psum_scatter(projected, "tensor", scatter_dimension=0, tiled=True)


def solution(mesh):
    in_specs = (
        P("task", "tensor"),
        P("task", None),
        P(None, "task", "tensor"),
        P("tensor", "task"),
        P(None, "tensor", "task"),
        P(None, "task", "tensor"),
    )
    out_specs = P("tensor", "task")
    return jax.shard_map(
        on_device, mesh=mesh, in_specs=in_specs, out_specs=out_specs, check_vma=False
    )
```

profile of v0, /device:TPU:1, one launch (start us, length us, event | category | flops | bytes accessed | tf_op | source)
XLA Modules:
  0.0 411.1 jit_solution(6725231558442215571)
XLA Ops:
  6.5 0.0 copy-start
  6.5 0.0 all-gather.3.cloned.1.call-start
  6.5 53.0 %all_gather.12 = bf16[256,1024]{1,0:T(8,128)(2,1)} all-gather(bf16[8,1024]{1,0:T(8,128)(2,1)} %param.6), channel_id=1, replica_groups=mesh['task'=32,'tensor'=8] {'task'}, dimensions={0}, use_global_device_ids=true | all-gather | bytes 540672 | tf_op jit(solution)/shard_map/all_gather | solution.py:14
  59.6 0.0 all-gather.3.cloned.1.call-update
  59.6 0.0 all-reduce.2.cloned.1.call-start
  59.7 49.2 %all-gather.3.cloned.1.call-done = bf16[256,8192]{1,0:T(8,128)(2,1)} async-done(((bf16[256,1024]{1,0:T(8,128)(2,1)}), bf16[256,8192]{1,0:T(8,128)(2,1)}) %all-gather.3.cloned.1.call-update) | async-done | bytes 4194320 | tf_op jit(solution)/shard_map/all_gather | solution.py:19
  108.9 2.2 fusion
  111.1 0.0 all-reduce.2.cloned.1.call-update
  111.1 0.0 reduce-scatter.5.cloned.1.call-start
  111.2 0.7 convert_element_type.11
  111.9 44.8 %all_gather.14 = bf16[256,16]{1,0:T(8,128)(2,1)S(1)} all-gather(bf16[8,16]{1,0:T(8,128)(2,1)S(1)} %convert_element_type.11), channel_id=1, replica_groups=mesh['task'=32,'tensor'=8] {'task'}, dimensions={0}, use_global_device_ids=true | all-gather | bytes 8448 | tf_op jit(solution)/shard_map/all_gather | solution.py:15
  156.6 0.1 convolution_bitcast_fusion
  156.8 27.7 %all-reduce.2.cloned.1.call-done = f32[256,2,128]{2,0,1:T(8,128)} async-done(((f32[256,2,128]{2,0,1:T(8,128)}), f32[256,2,128]{2,0,1:T(8,128)}) %all-reduce.2.cloned.1.call-update) | async-done | bytes 262160 | tf_op jit(solution)/shard_map/psum | solution.py:32
  184.5 0.0 copy-done
  184.5 0.0 copy-start.1
  184.5 2.3 fusion.3
  186.7 0.0 copy-done.1
  186.8 5.2 %bitcast_add_fusion = f32[256,2,3696]{2,0,1:T(8,128)} fusion(f32[2,256,3696]{2,1,0:T(8,128)S(1)} %fusion.3, bf16[2,256,3696]{1,2,0:T(8,128)(2,1)S(1)} %copy-done.1, bf16[256,8192]{1,0:T(8,128)(2,1)} %all-gather.3.cloned.1.call-done, s32[]{:T(128)S(6)} %select_n.15), kind=kOutput, calls=%fused_computation | convolution fusion | flops 970776576 | bytes 19054596 | tf_op jit(solution)/shard_map/td,gdf->tgf/dot_general | solution.py:41
  192.0 0.0 reduce-scatter.5.cloned.1.call-update
  192.0 0.0 all-gather.5.cloned.1.call-start
  192.0 122.3 %reduce-scatter.5.cloned.1.call-done = f32[8,2,3696]{2,0,1:T(8,128)} async-done(((f32[256,2,3696]{2,0,1:T(8,128)}), f32[8,2,3696]{2,0,1:T(8,128)}) %reduce-scatter.5.cloned.1.call-update) | async-done | bytes 236560 | tf_op jit(solution)/shard_map/reduce_scatter | solution.py:40
  314.4 1.6 fusion.8
  316.0 0.0 all-gather.5.cloned.1.call-update
  316.0 0.0 reduce-scatter.3.cloned.1.call-start
  316.1 53.3 %all-gather.5.cloned.1.call-done = bf16[256,3696]{1,0:T(8,128)(2,1)} async-done(((bf16[8,3696]{1,0:T(8,128)(2,1)}), bf16[256,3696]{1,0:T(8,128)(2,1)}) %all-gather.5.cloned.1.call-update) | async-done | bytes 1892368 | tf_op jit(solution)/shard_map/all_gather | solution.py:56
  369.4 3.5 fusion.12
  372.9 0.0 reduce-scatter.3.cloned.1.call-update
  372.9 31.6 %reduce-scatter.3.cloned.1.call-done = f32[32,256]{1,0:T(8,128)} async-done(((f32[256,256]{1,0:T(8,128)}), f32[32,256]{1,0:T(8,128)}) %reduce-scatter.3.cloned.1.call-update) | async-done | bytes 32784 | tf_op jit(solution)/shard_map/reduce_scatter | solution.py:60
  (1 shorter events, 0.0 us)
Async XLA Ops:
  6.5 177.9 %copy-start = (bf16[2,128,3696]{1,2,0:T(8,128)(2,1)S(1)}, bf16[2,128,3696]{1,2,0:T(8,128)(2,1)}, u32[]{:S(2)}) copy-start(bf16[2,128,3696]{1,2,0:T(8,128)(2,1)} %param.11) | copy-start | bytes 5677060
  6.5 102.3 %all-gather.3.cloned.1.call-start = ((), (), s32[]{:S(2)}) async-start(), calls=%async_computation.2 | async-start | bytes 4718592 | tf_op jit(solution)/shard_map/all_gather | solution.py:19
  59.6 124.9 %all-reduce.2.cloned.1.call-start = ((), (), s32[]{:S(2)}) async-start(), calls=%async_computation.3 | async-start | bytes 524288 | tf_op jit(solution)/shard_map/psum | solution.py:32
  111.1 203.3 %reduce-scatter.5.cloned.1.call-start = ((), (), s32[]{:S(2)}) async-start(), calls=%async_computation.6 | async-start | bytes 7839744 | tf_op jit(solution)/shard_map/reduce_scatter | solution.py:40
  184.5 2.3 copy-start.1
  192.0 177.4 %all-gather.5.cloned.1.call-start = ((), (), s32[]{:S(2)}) async-start(), calls=%async_computation.4 | async-start | bytes 1959936 | tf_op jit(solution)/shard_map/all_gather | solution.py:56
  316.0 88.5 %reduce-scatter.3.cloned.1.call-start = ((), (), s32[]{:S(2)}) async-start(), calls=%async_computation.5 | async-start | bytes 294912 | tf_op jit(solution)/shard_map/reduce_scatter | solution.py:60
Sparse Core Ops, SparseCore 0:
  59.7 49.0 all-gather.2
  111.5 72.9 all-reduce.1
  192.1 122.2 reduce-scatter.4
  316.9 52.4 all-gather.4
  373.0 31.4 reduce-scatter.2
where the time goes:
time: 416 us; the launch traced here: 411 us
  waiting for transfers between devices  284 us (68%)
  blocking collectives  97.8 us (24%)
  matrix products  13.3 us (3%)
  between operations  13.2 us (3%)
    reduce_scatter x1, waiting for transfers between devices, on_device(): lax.psum_scatter(jnp.einsum('td,gdf->tgf', part, gate_up_weight, preferre...  122 us
    all_gather x1, waiting for transfers between devices, on_device(): lax.all_gather(hidden, 'task', axis=0, tiled=True)  53.3 us
    all_gather x1, blocking collectives, on_device(): lax.all_gather(tokens, 'task', axis=0, tiled=True)  53 us
    all_gather x1, waiting for transfers between devices, on_device(): features = lax.all_gather(row_part, 'tensor', axis=1, tiled=True)  49.2 us
    all_gather x1, blocking collectives, on_device(): lax.all_gather(router.astype(jnp.bfloat16), 'task', axis=0, tiled=True)  44.8 us
    reduce_scatter x1, waiting for transfers between devices, on_device(): lax.psum_scatter(projected, 'tensor', scatter_dimension=0, tiled=True)  31.6 us
    psum x1, waiting for transfers between devices, on_device(): rank_sum = lax.psum(latent_part, 'tensor')  27.7 us
  transfers between devices with their start and end apart: 5, of which 5 were waited for; matrix products, arithmetic and copies ran while one was open for 0% of the time, Pallas kernels for 0%

commit v1 on v0

v1 whole, which is shorter than its diff:
```python
import functools

import jax
import jax.numpy as jnp
from jax import lax
from jax.experimental import pallas as pl
from jax.experimental.pallas import tpu as pltpu
from jax.sharding import PartitionSpec as P

F32 = jnp.float32
BF16 = jnp.bfloat16
TASKS = 16
NX, NZ, NC = 4, 4, 2
NQ = NX * NZ
VMEM_BYTES = 48 * 1024 * 1024


def task_of(x, z, c):
    return (x * NZ + z) * NC + c


def task_perm(move):
    pairs = []
    for x in range(NX):
        for z in range(NZ):
            for c in range(NC):
                pairs.append((task_of(x, z, c), task_of(*move(x, z, c))))
    return pairs


CORE = task_perm(lambda x, z, c: (x, z, 1 - c))
TO_X = {d: task_perm(lambda x, z, c, d=d: ((x + d) % NX, z, c)) for d in (1, 2, 3)}
TO_Z = {d: task_perm(lambda x, z, c, d=d: (x, (z + d) % NZ, c)) for d in (1, 2, 3)}
CHIPS = [[task_of(x, z, c) for x in range(NX) for z in range(NZ)] for c in range(NC)]


def call(kernel, out_shape, *args, scalars, **kw):
    return pl.pallas_call(
        kernel,
        out_shape=out_shape,
        grid_spec=pltpu.PrefetchScalarGridSpec(num_scalar_prefetch=1, **kw),
        compiler_params=pltpu.CompilerParams(vmem_limit_bytes=VMEM_BYTES),
    )(scalars, *args)


def whole(a):
    return pl.BlockSpec(a.shape, lambda *_: (0,) * len(a.shape))


def simple(kernel, out_shape, *args, scalars):
    outs = out_shape if isinstance(out_shape, (list, tuple)) else [out_shape]
    specs = [whole(o) for o in outs]
    return call(
        kernel,
        out_shape,
        *args,
        scalars=scalars,
        grid=(1,),
        in_specs=[whole(a) for a in args],
        out_specs=specs if isinstance(out_shape, (list, tuple)) else specs[0],
    )


def latent_kernel(width, s, own, other, low_own, low_other, out):
    q = s[3]

    def rows(ref):
        v = ref[...].astype(F32)
        return v.reshape(v.shape[0] * v.shape[1], v.shape[2])

    x = jnp.concatenate([rows(own), rows(other)], axis=0)
    low = jnp.concatenate([low_own[0], low_other[...]], axis=1)
    lat = jnp.dot(x[:, :width].astype(BF16), low, preferred_element_type=F32)
    tail = x[:, width:]
    lane = lax.broadcasted_iota(jnp.int32, tail.shape, 1)
    weight = jnp.sum(
        jnp.where((lane == q) | (lane == TASKS + q), tail, 0.0), axis=1, keepdims=True
    )
    lat = lat * weight
    ranks = lat.shape[1]
    lat = lat.reshape(2, own.shape[0], own.shape[1], ranks)
    out[:, :, :ranks] = jnp.concatenate([lat[0], lat[1]], axis=1).astype(BF16)
    feats = out.shape[2] - ranks
    start = pl.multiple_of(lax.rem(q, 2) * feats, feats)
    part = [r[:, :, pl.ds(start, feats)].astype(F32) for r in (own, other)]
    out[:, :, ranks:] = jnp.concatenate(part, axis=1).astype(BF16)


def mid_kernel(ranks, s, got, out):
    total = jnp.sum(got[:, :, :ranks].astype(F32), axis=0).astype(BF16)
    feats = got[s[3] // 2, :, ranks:]
    for j in range(out.shape[0]):
        out[j, :, :ranks] = total
        out[j, :, ranks:] = feats


def main_kernel(ranks, s, got, w_own, w_other, u_own, u_other, o0, o1, o2, o3, rows):
    x, z, c = s[0], s[1], s[2]
    half = (rows.shape[1] - ranks) // 2

    @pl.when(pl.program_id(0) == 0)
    def _():
        a = pl.multiple_of(ranks + c * half, half)
        b = pl.multiple_of(ranks + (1 - c) * half, half)
        for dx in range(NX):
            for dz in range(NZ):
                q = lax.rem(x + dx, NX) * NZ + lax.rem(z + dz, NZ)
                at = pl.ds(16 * (dx * NZ + dz), 16)
                rows[at, :half] = got[q, :, pl.ds(a, half)]
                rows[at, half : 2 * half] = got[q, :, pl.ds(b, half)]
                rows[at, 2 * half :] = got[q, :, :ranks]

    w = jnp.concatenate([w_own[0], w_other[...], u_own[0], u_other[...]], axis=0)
    p = jnp.dot(rows[...], w, preferred_element_type=F32)
    m = o0.shape[0]
    o0[...] = p[:m]
    o1[...] = p[m : 2 * m].astype(BF16)
    o2[...] = p[2 * m : 3 * m].astype(BF16)
    o3[...] = p[3 * m :].astype(BF16)


def x_sum_kernel(s, a0, a1, a2, a3, o0, o1, o2, o3):
    m = o0.shape[0]
    for i, o in enumerate((o0, o1, o2, o3)):
        at = pl.ds(i * m, m)
        t = a0[at] + a1[at].astype(F32) + a2[at].astype(F32) + a3[at].astype(F32)
        o[...] = t.astype(o.dtype)


def z_sum_kernel(s, a0, a1, a2, a3, keep, send):
    t = a0[...] + a1[...].astype(F32) + a2[...].astype(F32) + a3[...].astype(F32)
    m = keep.shape[0]
    keep[...] = t[:m]
    send[...] = t[m:]


def silu_kernel(s, keep, got, out):
    first = s[2] == 0
    gate = jnp.where(first, keep[...], got[...])
    up = jnp.where(first, got[...], keep[...])
    out[...] = (gate / (1.0 + jnp.exp(-gate)) * up).astype(BF16)


def down_kernel(s, h0, h1, h2, h3, w_own, w_other, out):
    x, z = s[0], s[1]
    h = jnp.concatenate([h0[...], h1[...], h2[...], h3[...]], axis=0)
    half = w_own.shape[1]
    for k, w in enumerate((w_own, w_other)):
        p = jnp.dot(h, w[...], preferred_element_type=F32)
        for dx in range(NX):
            for dz in range(NZ):
                q = lax.rem(x - dx + NX, NX) * NZ + lax.rem(z - dz + NZ, NZ)
                r = 8 * (dx * NZ + dz)
                out[q, :, half * k : half * (k + 1)] = p[r : r + 8].astype(out.dtype)


def out_sum_kernel(s, got, keep, send):
    t = jnp.sum(got[...].astype(F32), axis=0)
    half = keep.shape[-1]
    keep[...] = t[..., :half]
    send[...] = t[..., half:]


def on_device(tokens, router, gate_up_weight, down_weight, lower_factor, upper_factor):
    t = lax.axis_index("task").astype(jnp.int32)
    c = lax.rem(t, NC)
    q = t // NC
    x, z = q // NZ, lax.rem(q, NZ)
    s = jnp.stack([x, z, c, q])
    tensor = lax.axis_size("tensor")

    def permute(a, perm):
        return lax.ppermute(a, "task", perm)

    def sds(shape, dtype=BF16):
        return jax.ShapeDtypeStruct(shape, dtype)

    def other(a):
        return lax.dynamic_index_in_dim(a, 1 - c, 0, keepdims=False)

    def own_spec(a, block=None):
        return pl.BlockSpec((1, a.shape[1], block or a.shape[2]), lambda i, s: (s[2], 0, i))

    rows, width = tokens.shape
    ranks = 2 * lower_factor.shape[2]
    feats = 2 * gate_up_weight.shape[1]
    hid = gate_up_weight.shape[2]

    low_other = permute(other(lower_factor), CORE)
    w_other = permute(other(gate_up_weight), CORE)
    u_other = permute(other(upper_factor), CORE)
    down_other = permute(down_weight, CORE)

    high = lax.reduce_precision(router, 8, 7)
    low = router - high
    tail = jnp.concatenate([high, low], axis=1).astype(BF16)
    tail = jnp.pad(tail, ((0, 0), (0, 128 - tail.shape[1])))
    mine = jnp.concatenate([tokens, tail], axis=1)
    own_rows = lax.all_to_all(
        jnp.broadcast_to(mine[None], (NQ,) + mine.shape),
        "task",
        0,
        0,
        axis_index_groups=CHIPS,
    )
    other_rows = permute(own_rows, CORE)

    width_sum = ranks + feats
    payload = call(
        functools.partial(latent_kernel, width),
        sds((NQ, 2 * rows, width_sum)),
        own_rows,
        other_rows,
        lower_factor,
        low_other,
        scalars=s,
        grid=(1,),
        in_specs=[whole(own_rows), whole(other_rows), own_spec(lower_factor), whole(low_other)],
        out_specs=whole(sds((NQ, 2 * rows, width_sum))),
    )
    group = NQ * 2 * rows // tensor
    got = lax.all_to_all(payload.reshape(tensor, group, width_sum), "tensor", 0, 0)
    back = simple(
        functools.partial(mid_kernel, ranks), sds((tensor, group, width_sum)), got, scalars=s
    )
    got = lax.all_to_all(back, "tensor", 0, 0).reshape(NQ, 2 * rows, width_sum)

    block = 512
    m = NZ * 2 * rows
    tile = pl.BlockSpec((m, block), lambda i, s: (0, i))
    parts = call(
        functools.partial(main_kernel, ranks),
        [sds((m, hid), F32)] + [sds((m, hid))] * 3,
        got,
        gate_up_weight,
        w_other,
        upper_factor,
        u_other,
        scalars=s,
        grid=(pl.cdiv(hid, block),),
        in_specs=[
            whole(got),
            own_spec(gate_up_weight, block),
            pl.BlockSpec((w_other.shape[0], block), lambda i, s: (0, i)),
            own_spec(upper_factor, block),
            pl.BlockSpec((u_other.shape[0], block), lambda i, s: (0, i)),
        ],
        out_specs=[tile] * 4,
        scratch_shapes=[pltpu.VMEM((NQ * 2 * rows, width_sum), BF16)],
    )
    got = [permute(parts[d], TO_X[d]) for d in (2, 1, 3)]
    m = 2 * rows
    parts = simple(
        x_sum_kernel, [sds((m, hid), F32)] + [sds((m, hid))] * 3, parts[0], *got, scalars=s
    )
    got = [permute(parts[d], TO_Z[d]) for d in (2, 1, 3)]
    keep, send = simple(z_sum_kernel, [sds((rows, hid), F32)] * 2, parts[0], *got, scalars=s)
    hidden = simple(silu_kernel, sds((rows, hid)), keep, permute(send, CORE), scalars=s)

    got = {d: permute(hidden, TO_Z[d]) for d in (2, 1, 3)}
    hidden = jnp.concatenate([hidden, got[1], got[2], got[3]], axis=0)
    got = {d: permute(hidden, TO_X[d]) for d in (2, 1, 3)}
    first = c == 0
    cols = down_weight.shape[1]
    mixed = simple(
        down_kernel,
        sds((NQ, rows, 2 * cols)),
        hidden,
        got[1],
        got[2],
        got[3],
        down_weight,
        down_other,
        scalars=s,
    )
    got = lax.all_to_all(
        mixed.reshape(tensor, NQ // tensor, rows, 2 * cols), "tensor", 0, 0
    )
    keep, send = simple(
        out_sum_kernel, [sds((NQ // tensor, rows, cols), F32)] * 2, got, scalars=s
    )
    got = permute(send, CORE)
    out = jnp.stack([jnp.where(first, keep, got), jnp.where(first, got, keep)], axis=1)
    return out.reshape(NQ // tensor * NC * rows, cols)


def solution(mesh):
    in_specs = (
        P("task", "tensor"),
        P("task", None),
        P(None, "task", "tensor"),
        P("tensor", "task"),
        P(None, "tensor", "task"),
        P(None, "task", "tensor"),
    )
    out_specs = P("tensor", "task")
    return jax.shard_map(
        on_device, mesh=mesh, in_specs=in_specs, out_specs=out_specs, check_vma=False
    )
```

time: 416 us -> 160 us (0.38)
  waiting for transfers between devices: 284 us -> 65.9 us
  blocking collectives: 97.8 us -> 10.2 us
  starting transfers between devices: 0.17 us -> 47.5 us
  local copies, waits for them, and re-layouts: 0.01 us -> 17.6 us
  Pallas kernels: 0 us -> 16.1 us
  matrix products: 13.3 us -> 0 us
  between operations: 13.2 us -> 0.18 us
    reduce_scatter x2 -> x0, waiting for transfers between devices: 154 us -> none  [the longest x1 122 us: on_device(): lax.psum_scatter(jnp.einsum('td,gdf->tgf', part, gate_up_weight, preferre...]
    all_gather x2 -> x0, waiting for transfers between devices: 102 us -> none  [the longest x1 53.3 us: on_device(): lax.all_gather(hidden, 'task', axis=0, tiled=True)]
    all_gather x2 -> x0, blocking collectives: 97.8 us -> none  [the longest x1 53 us: on_device(): lax.all_gather(tokens, 'task', axis=0, tiled=True)]
    ppermute x0 -> x19, waiting for transfers between devices: none -> 50.8 us  [permute(): return lax.ppermute(a, 'task', perm)]
    psum x1 -> x0, waiting for transfers between devices: 27.7 us -> none  [on_device(): rank_sum = lax.psum(latent_part, 'tensor')]
    ppermute x0 -> x19, starting transfers between devices: none -> 26.6 us  [permute(): return lax.ppermute(a, 'task', perm)]
    all_to_all x0 -> x3, starting transfers between devices: none -> 20.9 us  [the longest x1 11.6 us: on_device(): lax.all_to_all(jnp.broadcast_to(mine[None], (NQ,) + mine.shape), 'task',...]
    pallas_call x0 -> x8, Pallas kernels: none -> 16.1 us  [call(): pl.pallas_call(kernel, out_shape=out_shape, grid_spec=pltpu.PrefetchScala...]
  transfers between devices with their start and end apart: 5 -> 22, of which waited for: 5 -> 15; matrix products, arithmetic and copies ran while one was open for 0% -> 10% of each run, Pallas kernels for 0% -> 8%
where the time goes in v1:
time: 160 us; the launch traced here: 159 us
  waiting for transfers between devices  65.9 us (41%)
  starting transfers between devices  47.5 us (30%)
  local copies, waits for them, and re-layouts  17.6 us (11%)
  Pallas kernels  16.1 us (10%)
  blocking collectives  10.2 us (6%)
  other arithmetic  1.6 us (1%)
    ppermute x19, waiting for transfers between devices, permute(): return lax.ppermute(a, 'task', perm)  50.8 us
    ppermute x19, starting transfers between devices, permute(): return lax.ppermute(a, 'task', perm)  26.6 us
    pallas_call x8, Pallas kernels, call(): pl.pallas_call(kernel, out_shape=out_shape, grid_spec=pltpu.PrefetchScala...  16.1 us
    all_to_all x1, starting transfers between devices, on_device(): lax.all_to_all(jnp.broadcast_to(mine[None], (NQ,) + mine.shape), 'task',...  11.6 us
    all_to_all x1, blocking collectives, on_device(): lax.all_to_all(mixed.reshape(tensor, NQ // tensor, rows, 2 * cols), 'tens...  10.2 us
    all_to_all x1, waiting for transfers between devices, on_device(): lax.all_to_all(jnp.broadcast_to(mine[None], (NQ,) + mine.shape), 'task',...  8.89 us
    unnamed x6, local copies, waits for them, and re-layouts  8.83 us
    all_to_all x1, waiting for transfers between devices, on_device(): lax.all_to_all(payload.reshape(tensor, group, width_sum), 'tensor', 0, 0)  6.17 us
  transfers between devices with their start and end apart: 22, of which 15 were waited for; matrix products, arithmetic and copies ran while one was open for 10% of the time, Pallas kernels for 8%

profile of v1, /device:TPU:1, one launch (start us, length us, event | category | flops | bytes accessed | tf_op | source)
XLA Modules:
  0.0 159.1 jit_solution(9455488652050161494)
XLA Ops:
  0.0 0.7 reduce-precision_convert_fusion
  0.7 0.1 fusion.3
  0.8 0.7 pad_maximum_fusion.2
  1.5 0.7 broadcast_in_dim.2
  2.2 11.6 %all-to-all-start = ((bf16[16,8,1152]{2,1,0:T(8,128)(2,1)}), bf16[16,8,1152]{2,1,0:T(8,128)(2,1)S(1)}, u32[]{:S(2)}, u32[]{:S(2)}) async-start(bf16[16,8,1152]{2,1,0:T(8,128)(2,1)} %broadcast_in_dim.2), calls=%async_computation | async-start | bytes 589824 | tf_op jit(solution)/shard_map/all_to_all | solution.py:199
  13.8 0.0 copy-start
  13.8 3.0 %dynamic-slice_bitcast_fusion = bf16[256,3696]{0,1:T(8,128)(2,1)} fusion(bf16[2,256,3696]{1,2,0:T(8,128)(2,1)} %param.8, s32[]{:T(128)S(6)} %select_n.31), kind=kLoop, calls=%fused_computation | loop fusion | bytes 3784708 | tf_op jit(solution)/shard_map/jit(dynamic_index_in_dim)/squeeze | solution.py:179
  16.8 1.0 collective-permute-start.2
  17.8 8.9 %all-to-all-done.own = bf16[16,8,1152]{2,1,0:T(8,128)(2,1)S(1)} async-done(((bf16[16,8,1152]{2,1,0:T(8,128)(2,1)}), bf16[16,8,1152]{2,1,0:T(8,128)(2,1)S(1)}, u32[]{:S(2)}, u32[]{:S(2)}) %all-to-all-start) | async-done | bytes 294944 | tf_op jit(solution)/shard_map/all_to_all | solution.py:199
  26.6 2.1 %collective-permute-start = (bf16[16,8,1152]{2,1,0:T(8,128)(2,1)S(1)}, bf16[16,8,1152]{2,1,0:T(8,128)(2,1)S(1)}, u32[]{:S(2)}, u32[]{:S(2)}) collective-permute-start(bf16[16,8,1152]{2,1,0:T(8,128)(2,1)S(1)} %all-to-all-done.own), channel_id=1, source_target_pairs={{0,8},{8,0},{16,24},{24,16},{32,40},{40,32},{48,56},{56,48},{64,72... | collective-permute-start | bytes 884744 | tf_op jit(solution)/shard_map/ppermute | solution.py:173
  28.7 0.1 collective-permute-start.1
  28.9 0.1 pad_add_fusion.s
  29.0 1.4 collective-permute-done.1.low_other
  30.4 0.0 collective-permute-done.other
  30.4 1.6 %shard_map.64 = bf16[16,16,768]{2,1,0:T(8,128)(2,1)} custom-call(s32[4]{0:T(128)S(1)} %pad_add_fusion.s, bf16[16,8,1152]{2,1,0:T(8,128)(2,1)S(1)} %all-to-all-done.own, bf16[16,8,1152]{2,1,0:T(8,128)(2,1)S(1)} %collective-permute-done.other, bf16[2,1024,128]{2,1,0:T(8,128)(2,1)S(1)} %copy-done, bf16[1024,128]{1,0:T(8,128)(2,1)S(1)} %collective-permute-done.1.low_other), custom_call_target="tpu_custom_call" | custom-call | tf_op jit(solution)/shard_map/pallas_call | solution.py:38
  32.0 4.6 %all-to-all-start.1 = ((bf16[8,32,768]{2,1,0:T(8,128)(2,1)}), bf16[8,32,768]{2,1,0:T(8,128)(2,1)S(1)}, u32[]{:S(2)}, u32[]{:S(2)}) async-start(bf16[8,32,768]{2,1,0:T(8,128)(2,1)} %bitcast.5), calls=%async_computation.1 | async-start | bytes 786432 | tf_op jit(solution)/shard_map/all_to_all | solution.py:222
  36.6 0.1 dynamic-slice_bitcast_fusion.1
  36.7 0.7 collective-permute-start.3
  37.4 6.2 %all-to-all-done.1.got = bf16[8,32,768]{2,1,0:T(8,128)(2,1)S(1)} async-done(((bf16[8,32,768]{2,1,0:T(8,128)(2,1)}), bf16[8,32,768]{2,1,0:T(8,128)(2,1)S(1)}, u32[]{:S(2)}, u32[]{:S(2)}) %all-to-all-start.1) | async-done | bytes 393248 | tf_op jit(solution)/shard_map/all_to_all | solution.py:222
  43.5 1.3 shard_map.65
  44.9 4.7 %all-to-all-start.2 = ((bf16[8,32,768]{2,1,0:T(8,128)(2,1)}), bf16[8,32,768]{2,1,0:T(8,128)(2,1)S(1)}, u32[]{:S(2)}, u32[]{:S(2)}) async-start(bf16[8,32,768]{2,1,0:T(8,128)(2,1)} %shard_map.65), calls=%async_computation.2 | async-start | bytes 786432 | tf_op jit(solution)/shard_map/all_to_all | solution.py:226
  49.5 1.2 collective-permute-start.17
  50.7 6.2 %copy.16.w_own = bf16[2,256,3696]{2,1,0:T(8,128)(2,1)} copy(bf16[2,256,3696]{1,2,0:T(8,128)(2,1)} %param.8) | data formatting | bytes 7569408 | tf_op args[2]
  57.0 2.6 %copy.18.u_own = bf16[2,128,3696]{2,1,0:T(8,128)(2,1)} copy(bf16[2,128,3696]{1,2,0:T(8,128)(2,1)S(1)} %copy-done.1) | data formatting | bytes 3784704 | tf_op args[5]
  59.6 0.0 collective-permute-done.3
  59.6 1.6 copy.19.u_other
  61.2 2.8 %copy.17.w_other = bf16[256,3696]{1,0:T(8,128)(2,1)S(1)} copy(bf16[256,3696]{0,1:T(8,128)(2,1)} %collective-permute-done.2) | data formatting | bytes 3784704 | tf_op jit(solution)/shard_map/ppermute | solution.py:173
  64.0 7.3 %shard_map.66 = (f32[64,3696]{1,0:T(8,128)S(1)}, bf16[64,3696]{1,0:T(8,128)(2,1)S(1)}, bf16[64,3696]{1,0:T(8,128)(2,1)S(1)}, bf16[64,3696]{1,0:T(8,128)(2,1)S(1)}) custom-call(s32[4]{0:T(128)S(1)} %pad_add_fusion.s, bf16[16,16,768]{2,1,0:T(8,128)(2,1)S(1)} %bitcast.18, bf16[2,256,3696]{2,1,0:T(8,128)(2,1)} %copy.16.w_own, ...), custom_call_target="tpu_custom_call" | custom-call | tf_op jit(solution)/shard_map/pallas_call | solution.py:38
  71.4 0.7 collective-permute-start.4
  72.0 0.6 collective-permute-start.5
  72.6 2.1 %collective-permute-start.6 = (bf16[64,3696]{1,0:T(8,128)(2,1)S(1)}, bf16[64,3696]{1,0:T(8,128)(2,1)S(1)}, u32[]{:S(2)}, u32[]{:S(2)}) collective-permute-start(bf16[64,3696]{1,0:T(8,128)(2,1)S(1)} %get-tuple-element.20), channel_id=1, source_target_pairs={{0,192},{8,200},{16,208},{24,216},{32,224},{40,232},{48,240},{56,2... | collective-permute-start | bytes 1419272 | tf_op jit(solution)/shard_map/ppermute | solution.py:173
  74.7 10.8 %collective-permute-done.4.a1 = bf16[64,3696]{1,0:T(8,128)(2,1)S(1)} collective-permute-done((bf16[64,3696]{1,0:T(8,128)(2,1)S(1)}, bf16[64,3696]{1,0:T(8,128)(2,1)S(1)}, u32[]{:S(2)}, u32[]{:S(2)}) %collective-permute-start.4) | collective-permute-done | bytes 473120 | tf_op jit(solution)/shard_map/ppermute | solution.py:173
  85.5 10.5 %collective-permute-done.5.a2 = bf16[64,3696]{1,0:T(8,128)(2,1)S(1)} collective-permute-done((bf16[64,3696]{1,0:T(8,128)(2,1)S(1)}, bf16[64,3696]{1,0:T(8,128)(2,1)S(1)}, u32[]{:S(2)}, u32[]{:S(2)}) %collective-permute-start.5) | collective-permute-done | bytes 473120 | tf_op jit(solution)/shard_map/ppermute | solution.py:173
  95.9 0.0 collective-permute-done.6.a3
  95.9 0.8 shard_map.67
  96.7 0.2 collective-permute-start.7
  97.0 2.1 %collective-permute-start.8 = (bf16[16,3696]{1,0:T(8,128)(2,1)S(1)}, bf16[16,3696]{1,0:T(8,128)(2,1)S(1)}, u32[]{:S(2)}, u32[]{:S(2)}) collective-permute-start(bf16[16,3696]{1,0:T(8,128)(2,1)S(1)} %get-tuple-element.23), channel_id=1, source_target_pairs={{0,16},{8,24},{16,32},{24,40},{32,48},{40,56},{48,0},{56,8},{64,80... | collective-permute-start | bytes 354824 | tf_op jit(solution)/shard_map/ppermute | solution.py:173
  99.0 1.6 %collective-permute-start.9 = (bf16[16,3696]{1,0:T(8,128)(2,1)S(1)}, bf16[16,3696]{1,0:T(8,128)(2,1)S(1)}, u32[]{:S(2)}, u32[]{:S(2)}) collective-permute-start(bf16[16,3696]{1,0:T(8,128)(2,1)S(1)} %get-tuple-element.24), channel_id=1, source_target_pairs={{0,48},{8,56},{16,0},{24,8},{32,16},{40,24},{48,32},{56,40},{64,11... | collective-permute-start | bytes 354824 | tf_op jit(solution)/shard_map/ppermute | solution.py:173
  100.6 4.6 %collective-permute-done.7.a1 = bf16[16,3696]{1,0:T(8,128)(2,1)S(1)} collective-permute-done((bf16[16,3696]{1,0:T(8,128)(2,1)S(1)}, bf16[16,3696]{1,0:T(8,128)(2,1)S(1)}, u32[]{:S(2)}, u32[]{:S(2)}) %collective-permute-start.7) | collective-permute-done | bytes 118304 | tf_op jit(solution)/shard_map/ppermute | solution.py:173
  105.2 3.1 %collective-permute-done.8.a2 = bf16[16,3696]{1,0:T(8,128)(2,1)S(1)} collective-permute-done((bf16[16,3696]{1,0:T(8,128)(2,1)S(1)}, bf16[16,3696]{1,0:T(8,128)(2,1)S(1)}, u32[]{:S(2)}, u32[]{:S(2)}) %collective-permute-start.8) | collective-permute-done | bytes 118304 | tf_op jit(solution)/shard_map/ppermute | solution.py:173
  108.3 2.8 %collective-permute-done.9.a3 = bf16[16,3696]{1,0:T(8,128)(2,1)S(1)} collective-permute-done((bf16[16,3696]{1,0:T(8,128)(2,1)S(1)}, bf16[16,3696]{1,0:T(8,128)(2,1)S(1)}, u32[]{:S(2)}, u32[]{:S(2)}) %collective-permute-start.9) | collective-permute-done | bytes 118304 | tf_op jit(solution)/shard_map/ppermute | solution.py:173
  111.1 0.6 shard_map.68
  111.7 1.2 collective-permute-start.10
  112.9 1.0 collective-permute-done.10.got
  113.9 0.6 shard_map.69
  114.5 3.5 %collective-permute-start.11 = (bf16[8,3696]{1,0:T(8,128)(2,1)S(1)}, bf16[8,3696]{1,0:T(8,128)(2,1)S(1)}, u32[]{:S(2)}, u32[]{:S(2)}) collective-permute-start(bf16[8,3696]{1,0:T(8,128)(2,1)S(1)} %shard_map.69), channel_id=1, source_target_pairs={{0,16},{8,24},{16,32},{24,40},{32,48},{40,56},{48,0},{56,8},{64,80... | collective-permute-start | bytes 177416 | tf_op jit(solution)/shard_map/ppermute | solution.py:173
  118.0 0.7 collective-permute-start.12
  118.7 2.9 %collective-permute-start.13 = (bf16[8,3696]{1,0:T(8,128)(2,1)S(1)}, bf16[8,3696]{1,0:T(8,128)(2,1)S(1)}, u32[]{:S(2)}, u32[]{:S(2)}) collective-permute-start(bf16[8,3696]{1,0:T(8,128)(2,1)S(1)} %shard_map.69), channel_id=1, source_target_pairs={{0,48},{8,56},{16,0},{24,8},{32,16},{40,24},{48,32},{56,40},{64,11... | collective-permute-start | bytes 177416 | tf_op jit(solution)/shard_map/ppermute | solution.py:173
  121.6 0.0 collective-permute-done.11
  121.6 4.9 %collective-permute-done.12 = bf16[8,3696]{1,0:T(8,128)(2,1)S(1)} collective-permute-done((bf16[8,3696]{1,0:T(8,128)(2,1)S(1)}, bf16[8,3696]{1,0:T(8,128)(2,1)S(1)}, u32[]{:S(2)}, u32[]{:S(2)}) %collective-permute-start.12) | collective-permute-done | bytes 59168 | tf_op jit(solution)/shard_map/ppermute | solution.py:173
  126.5 0.5 collective-permute-done.13
  127.0 0.1 collective-permute-start.14
  127.1 1.4 collective-permute-start.15
  128.5 1.2 collective-permute-start.16
  129.8 0.0 collective-permute-done.17.w_other
  129.8 6.3 %collective-permute-done.14.h1 = bf16[32,3696]{1,0:T(8,128)(2,1)S(1)} collective-permute-done((bf16[32,3696]{1,0:T(8,128)(2,1)S(1)}, bf16[32,3696]{1,0:T(8,128)(2,1)S(1)}, u32[]{:S(2)}, u32[]{:S(2)}) %collective-permute-start.14) | collective-permute-done | bytes 236576 | tf_op jit(solution)/shard_map/ppermute | solution.py:173
  136.1 2.5 %collective-permute-done.15.h2 = bf16[32,3696]{1,0:T(8,128)(2,1)S(1)} collective-permute-done((bf16[32,3696]{1,0:T(8,128)(2,1)S(1)}, bf16[32,3696]{1,0:T(8,128)(2,1)S(1)}, u32[]{:S(2)}, u32[]{:S(2)}) %collective-permute-start.15) | collective-permute-done | bytes 236576 | tf_op jit(solution)/shard_map/ppermute | solution.py:173
  138.6 1.6 %collective-permute-done.16.h3 = bf16[32,3696]{1,0:T(8,128)(2,1)S(1)} collective-permute-done((bf16[32,3696]{1,0:T(8,128)(2,1)S(1)}, bf16[32,3696]{1,0:T(8,128)(2,1)S(1)}, u32[]{:S(2)}, u32[]{:S(2)}) %collective-permute-start.16) | collective-permute-done | bytes 236576 | tf_op jit(solution)/shard_map/ppermute | solution.py:173
  140.2 3.3 %shard_map.70 = bf16[16,8,512]{2,1,0:T(8,128)(2,1)S(1)} custom-call(s32[4]{0:T(128)S(1)} %pad_add_fusion.s, bf16[32,3696]{1,0:T(8,128)(2,1)S(1)} %pad_maximum_fusion.h0, bf16[32,3696]{1,0:T(8,128)(2,1)S(1)} %collective-permute-done.14.h1, bf16[32,3696]{1,0:T(8,128)(2,1)S(1)} %collective-permute-done.15.h2, bf16[32,3696]{1,0:T(8,128)(2,1)S(1)} %collective-permute-done.16.h3, ...), custom_call_target="tpu_custom_call" | custom-call | tf_op jit(solution)/shard_map/pallas_call | solution.py:38
  143.5 10.2 %all_to_all.20.got = bf16[8,2,8,512]{3,2,1,0:T(8,128)(2,1)S(1)} all-to-all(bf16[8,2,8,512]{3,2,1,0:T(8,128)(2,1)S(1)} %bitcast.19), channel_id=1, replica_groups=mesh['task'=32,'tensor'=8] {'tensor'}, dimensions={0} | all-to-all | bytes 262144 | tf_op jit(solution)/shard_map/all_to_all | solution.py:276
  153.7 0.6 shard_map.71
  154.3 3.3 %collective-permute-start.18 = (f32[2,8,256]{2,1,0:T(8,128)S(1)}, f32[2,8,256]{2,1,0:T(8,128)S(1)}, u32[]{:S(2)}, u32[]{:S(2)}) collective-permute-start(f32[2,8,256]{2,1,0:T(8,128)S(1)} %get-tuple-element.28), channel_id=1, source_target_pairs={{0,8},{8,0},{16,24},{24,16},{32,40},{40,32},{48,56},{56,48},{64,72... | collective-permute-start | bytes 49160 | tf_op jit(solution)/shard_map/ppermute | solution.py:173
  157.6 0.8 collective-permute-done.18
  158.4 0.6 copy.20
  (9 shorter events, 0.1 us)
Async XLA Ops:
  2.2 24.4 %all-to-all-start = ((bf16[16,8,1152]{2,1,0:T(8,128)(2,1)}), bf16[16,8,1152]{2,1,0:T(8,128)(2,1)S(1)}, u32[]{:S(2)}, u32[]{:S(2)}) async-start(bf16[16,8,1152]{2,1,0:T(8,128)(2,1)} %broadcast_in_dim.2), calls=%async_computation | async-start | bytes 589824 | tf_op jit(solution)/shard_map/all_to_all | solution.py:199
  13.8 14.9 %copy-start = (bf16[2,1024,128]{2,1,0:T(8,128)(2,1)S(1)}, bf16[2,1024,128]{2,1,0:T(8,128)(2,1)}, u32[]{:S(2)}) copy-start(bf16[2,1024,128]{2,1,0:T(8,128)(2,1)} %low_own.1) | copy-start | bytes 1572868
  16.8 19.8 %copy-start.1 = (bf16[2,128,3696]{1,2,0:T(8,128)(2,1)S(1)}, bf16[2,128,3696]{1,2,0:T(8,128)(2,1)}, u32[]{:S(2)}) copy-start(bf16[2,128,3696]{1,2,0:T(8,128)(2,1)} %param.11) | copy-start | bytes 5677060
  16.8 44.4 %collective-permute-start.2 = (bf16[256,3696]{0,1:T(8,128)(2,1)}, bf16[256,3696]{0,1:T(8,128)(2,1)}, u32[]{:S(2)}, u32[]{:S(2)}) collective-permute-start(bf16[256,3696]{0,1:T(8,128)(2,1)} %dynamic-slice_bitcast_fusion), channel_id=1, source_target_pairs={{0,8},{8,0},{16,24},{24,16},{32,40},{40,32},{48,56},{56,48},{64,72... | collective-permute-start | bytes 5677064 | tf_op jit(solution)/shard_map/ppermute | solution.py:173
  26.6 3.7 %collective-permute-start = (bf16[16,8,1152]{2,1,0:T(8,128)(2,1)S(1)}, bf16[16,8,1152]{2,1,0:T(8,128)(2,1)S(1)}, u32[]{:S(2)}, u32[]{:S(2)}) collective-permute-start(bf16[16,8,1152]{2,1,0:T(8,128)(2,1)S(1)} %all-to-all-done.own), channel_id=1, source_target_pairs={{0,8},{8,0},{16,24},{24,16},{32,40},{40,32},{48,56},{56,48},{64,72... | collective-permute-start | bytes 884744 | tf_op jit(solution)/shard_map/ppermute | solution.py:173
  28.7 1.6 %collective-permute-start.1 = (bf16[1024,128]{1,0:T(8,128)(2,1)S(1)}, bf16[1024,128]{1,0:T(8,128)(2,1)S(1)}, u32[]{:S(2)}, u32[]{:S(2)}) collective-permute-start(bf16[1024,128]{1,0:T(8,128)(2,1)S(1)} %dynamic-slice_bitcast_fusion.2), channel_id=1, source_target_pairs={{0,8},{8,0},{16,24},{24,16},{32,40},{40,32},{48,56},{56,48},{64,72... | collective-permute-start | bytes 786440 | tf_op jit(solution)/shard_map/ppermute | solution.py:173
  32.0 11.6 %all-to-all-start.1 = ((bf16[8,32,768]{2,1,0:T(8,128)(2,1)}), bf16[8,32,768]{2,1,0:T(8,128)(2,1)S(1)}, u32[]{:S(2)}, u32[]{:S(2)}) async-start(bf16[8,32,768]{2,1,0:T(8,128)(2,1)} %bitcast.5), calls=%async_computation.1 | async-start | bytes 786432 | tf_op jit(solution)/shard_map/all_to_all | solution.py:222
  36.7 22.9 %collective-permute-start.3 = (bf16[128,3696]{0,1:T(8,128)(2,1)S(1)}, bf16[128,3696]{0,1:T(8,128)(2,1)}, u32[]{:S(2)}, u32[]{:S(2)}) collective-permute-start(bf16[128,3696]{0,1:T(8,128)(2,1)S(1)} %dynamic-slice_bitcast_fusion.1), channel_id=1, source_target_pairs={{0,8},{8,0},{16,24},{24,16},{32,40},{40,32},{48,56},{56,48},{64,72... | collective-permute-start | bytes 2838536 | tf_op jit(solution)/shard_map/ppermute | solution.py:173
  44.9 19.1 %all-to-all-start.2 = ((bf16[8,32,768]{2,1,0:T(8,128)(2,1)}), bf16[8,32,768]{2,1,0:T(8,128)(2,1)S(1)}, u32[]{:S(2)}, u32[]{:S(2)}) async-start(bf16[8,32,768]{2,1,0:T(8,128)(2,1)} %shard_map.65), calls=%async_computation.2 | async-start | bytes 786432 | tf_op jit(solution)/shard_map/all_to_all | solution.py:226
  49.5 80.2 %collective-permute-start.17 = (bf16[3696,256]{1,0:T(8,128)(2,1)}, bf16[3696,256]{1,0:T(8,128)(2,1)}, u32[]{:S(2)}, u32[]{:S(2)}) collective-permute-start(bf16[3696,256]{1,0:T(8,128)(2,1)} %w_own.2), channel_id=1, source_target_pairs={{0,8},{8,0},{16,24},{24,16},{32,40},{40,32},{48,56},{56,48},{64,72... | collective-permute-start | bytes 5677064 | tf_op jit(solution)/shard_map/ppermute | solution.py:173
  71.4 14.1 %collective-permute-start.4 = (bf16[64,3696]{1,0:T(8,128)(2,1)S(1)}, bf16[64,3696]{1,0:T(8,128)(2,1)S(1)}, u32[]{:S(2)}, u32[]{:S(2)}) collective-permute-start(bf16[64,3696]{1,0:T(8,128)(2,1)S(1)} %get-tuple-element.18), channel_id=1, source_target_pairs={{0,128},{8,136},{16,144},{24,152},{32,160},{40,168},{48,176},{56,1... | collective-permute-start | bytes 1419272 | tf_op jit(solution)/shard_map/ppermute | solution.py:173
  72.0 23.9 %collective-permute-start.5 = (bf16[64,3696]{1,0:T(8,128)(2,1)S(1)}, bf16[64,3696]{1,0:T(8,128)(2,1)S(1)}, u32[]{:S(2)}, u32[]{:S(2)}) collective-permute-start(bf16[64,3696]{1,0:T(8,128)(2,1)S(1)} %get-tuple-element.19), channel_id=1, source_target_pairs={{0,64},{8,72},{16,80},{24,88},{32,96},{40,104},{48,112},{56,120},{... | collective-permute-start | bytes 1419272 | tf_op jit(solution)/shard_map/ppermute | solution.py:173
  72.6 23.4 %collective-permute-start.6 = (bf16[64,3696]{1,0:T(8,128)(2,1)S(1)}, bf16[64,3696]{1,0:T(8,128)(2,1)S(1)}, u32[]{:S(2)}, u32[]{:S(2)}) collective-permute-start(bf16[64,3696]{1,0:T(8,128)(2,1)S(1)} %get-tuple-element.20), channel_id=1, source_target_pairs={{0,192},{8,200},{16,208},{24,216},{32,224},{40,232},{48,240},{56,2... | collective-permute-start | bytes 1419272 | tf_op jit(solution)/shard_map/ppermute | solution.py:173
  96.7 8.5 %collective-permute-start.7 = (bf16[16,3696]{1,0:T(8,128)(2,1)S(1)}, bf16[16,3696]{1,0:T(8,128)(2,1)S(1)}, u32[]{:S(2)}, u32[]{:S(2)}) collective-permute-start(bf16[16,3696]{1,0:T(8,128)(2,1)S(1)} %get-tuple-element.22), channel_id=1, source_target_pairs={{0,32},{8,40},{16,48},{24,56},{32,0},{40,8},{48,16},{56,24},{64,96... | collective-permute-start | bytes 354824 | tf_op jit(solution)/shard_map/ppermute | solution.py:173
  97.0 11.4 %collective-permute-start.8 = (bf16[16,3696]{1,0:T(8,128)(2,1)S(1)}, bf16[16,3696]{1,0:T(8,128)(2,1)S(1)}, u32[]{:S(2)}, u32[]{:S(2)}) collective-permute-start(bf16[16,3696]{1,0:T(8,128)(2,1)S(1)} %get-tuple-element.23), channel_id=1, source_target_pairs={{0,16},{8,24},{16,32},{24,40},{32,48},{40,56},{48,0},{56,8},{64,80... | collective-permute-start | bytes 354824 | tf_op jit(solution)/shard_map/ppermute | solution.py:173
  99.0 12.1 %collective-permute-start.9 = (bf16[16,3696]{1,0:T(8,128)(2,1)S(1)}, bf16[16,3696]{1,0:T(8,128)(2,1)S(1)}, u32[]{:S(2)}, u32[]{:S(2)}) collective-permute-start(bf16[16,3696]{1,0:T(8,128)(2,1)S(1)} %get-tuple-element.24), channel_id=1, source_target_pairs={{0,48},{8,56},{16,0},{24,8},{32,16},{40,24},{48,32},{56,40},{64,11... | collective-permute-start | bytes 354824 | tf_op jit(solution)/shard_map/ppermute | solution.py:173
  111.7 2.2 %collective-permute-start.10 = (f32[8,3696]{1,0:T(8,128)S(1)}, f32[8,3696]{1,0:T(8,128)S(1)}, u32[]{:S(2)}, u32[]{:S(2)}) collective-permute-start(f32[8,3696]{1,0:T(8,128)S(1)} %get-tuple-element.26), channel_id=1, source_target_pairs={{0,8},{8,0},{16,24},{24,16},{32,40},{40,32},{48,56},{56,48},{64,72... | collective-permute-start | bytes 354824 | tf_op jit(solution)/shard_map/ppermute | solution.py:173
  114.5 7.1 %collective-permute-start.11 = (bf16[8,3696]{1,0:T(8,128)(2,1)S(1)}, bf16[8,3696]{1,0:T(8,128)(2,1)S(1)}, u32[]{:S(2)}, u32[]{:S(2)}) collective-permute-start(bf16[8,3696]{1,0:T(8,128)(2,1)S(1)} %shard_map.69), channel_id=1, source_target_pairs={{0,16},{8,24},{16,32},{24,40},{32,48},{40,56},{48,0},{56,8},{64,80... | collective-permute-start | bytes 177416 | tf_op jit(solution)/shard_map/ppermute | solution.py:173
  118.0 8.5 %collective-permute-start.12 = (bf16[8,3696]{1,0:T(8,128)(2,1)S(1)}, bf16[8,3696]{1,0:T(8,128)(2,1)S(1)}, u32[]{:S(2)}, u32[]{:S(2)}) collective-permute-start(bf16[8,3696]{1,0:T(8,128)(2,1)S(1)} %shard_map.69), channel_id=1, source_target_pairs={{0,32},{8,40},{16,48},{24,56},{32,0},{40,8},{48,16},{56,24},{64,96... | collective-permute-start | bytes 177416 | tf_op jit(solution)/shard_map/ppermute | solution.py:173
  118.7 8.3 %collective-permute-start.13 = (bf16[8,3696]{1,0:T(8,128)(2,1)S(1)}, bf16[8,3696]{1,0:T(8,128)(2,1)S(1)}, u32[]{:S(2)}, u32[]{:S(2)}) collective-permute-start(bf16[8,3696]{1,0:T(8,128)(2,1)S(1)} %shard_map.69), channel_id=1, source_target_pairs={{0,48},{8,56},{16,0},{24,8},{32,16},{40,24},{48,32},{56,40},{64,11... | collective-permute-start | bytes 177416 | tf_op jit(solution)/shard_map/ppermute | solution.py:173
  127.0 9.1 %collective-permute-start.14 = (bf16[32,3696]{1,0:T(8,128)(2,1)S(1)}, bf16[32,3696]{1,0:T(8,128)(2,1)S(1)}, u32[]{:S(2)}, u32[]{:S(2)}) collective-permute-start(bf16[32,3696]{1,0:T(8,128)(2,1)S(1)} %pad_maximum_fusion.h0), channel_id=1, source_target_pairs={{0,64},{8,72},{16,80},{24,88},{32,96},{40,104},{48,112},{56,120},{... | collective-permute-start | bytes 709640 | tf_op jit(solution)/shard_map/ppermute | solution.py:173
  127.1 11.5 %collective-permute-start.15 = (bf16[32,3696]{1,0:T(8,128)(2,1)S(1)}, bf16[32,3696]{1,0:T(8,128)(2,1)S(1)}, u32[]{:S(2)}, u32[]{:S(2)}) collective-permute-start(bf16[32,3696]{1,0:T(8,128)(2,1)S(1)} %pad_maximum_fusion.h0), channel_id=1, source_target_pairs={{0,128},{8,136},{16,144},{24,152},{32,160},{40,168},{48,176},{56,1... | collective-permute-start | bytes 709640 | tf_op jit(solution)/shard_map/ppermute | solution.py:173
  128.5 11.7 %collective-permute-start.16 = (bf16[32,3696]{1,0:T(8,128)(2,1)S(1)}, bf16[32,3696]{1,0:T(8,128)(2,1)S(1)}, u32[]{:S(2)}, u32[]{:S(2)}) collective-permute-start(bf16[32,3696]{1,0:T(8,128)(2,1)S(1)} %pad_maximum_fusion.h0), channel_id=1, source_target_pairs={{0,192},{8,200},{16,208},{24,216},{32,224},{40,232},{48,240},{56,2... | collective-permute-start | bytes 709640 | tf_op jit(solution)/shard_map/ppermute | solution.py:173
  154.3 4.2 %collective-permute-start.18 = (f32[2,8,256]{2,1,0:T(8,128)S(1)}, f32[2,8,256]{2,1,0:T(8,128)S(1)}, u32[]{:S(2)}, u32[]{:S(2)}) collective-permute-start(f32[2,8,256]{2,1,0:T(8,128)S(1)} %get-tuple-element.28), channel_id=1, source_target_pairs={{0,8},{8,0},{16,24},{24,16},{32,40},{40,32},{48,56},{56,48},{64,72... | collective-permute-start | bytes 49160 | tf_op jit(solution)/shard_map/ppermute | solution.py:173

commit v2 on v0

v2 whole, which is shorter than its diff:
```python
import functools

import jax
import jax.numpy as jnp
from jax import lax
from jax.experimental import pallas as pl
from jax.experimental.pallas import tpu as pltpu
from jax.sharding import PartitionSpec as P

F32 = jnp.float32
BF16 = jnp.bfloat16
TASKS = 16
NX, NZ, NC = 4, 4, 2
NQ = NX * NZ
VMEM_BYTES = 48 * 1024 * 1024


def task_of(x, z, c):
    return (x * NZ + z) * NC + c


def task_perm(move):
    pairs = []
    for x in range(NX):
        for z in range(NZ):
            for c in range(NC):
                pairs.append((task_of(x, z, c), task_of(*move(x, z, c))))
    return pairs


CORE = task_perm(lambda x, z, c: (x, z, 1 - c))
TO_X = {d: task_perm(lambda x, z, c, d=d: ((x + d) % NX, z, c)) for d in (1, 2, 3)}
TO_Z = {d: task_perm(lambda x, z, c, d=d: (x, (z + d) % NZ, c)) for d in (1, 2, 3)}
CHIPS = [[task_of(x, z, c) for x in range(NX) for z in range(NZ)] for c in range(NC)]
FAR_FIRST = (2, 1, 3)


def sds(shape, dtype=BF16):
    return jax.ShapeDtypeStruct(shape, dtype)


def whole(a):
    return pl.BlockSpec(a.shape, lambda *_: (0,) * len(a.shape))


def call(kernel, out_shape, *args, scalars, grid=(1,), in_specs=None, out_specs=None, scratch=()):
    many = isinstance(out_shape, (list, tuple))
    if in_specs is None:
        in_specs = [whole(a) for a in args]
    if out_specs is None:
        out_specs = [whole(o) for o in out_shape] if many else whole(out_shape)
    return pl.pallas_call(
        kernel,
        out_shape=out_shape,
        grid_spec=pltpu.PrefetchScalarGridSpec(
            num_scalar_prefetch=1,
            grid=grid,
            in_specs=in_specs,
            out_specs=out_specs,
            scratch_shapes=list(scratch),
        ),
        compiler_params=pltpu.CompilerParams(vmem_limit_bytes=VMEM_BYTES),
    )(scalars, *args)


def rows_of(v):
    v = v.astype(F32)
    return v.reshape(v.shape[0] * v.shape[1], v.shape[2])


def pack_kernel(s, tokens, router, to_chips, to_tensor):
    high = router[...].astype(BF16)
    low = (router[...] - high.astype(F32)).astype(BF16)
    lane = lax.broadcasted_iota(jnp.int32, (TASKS, 128), 1)
    row = lax.broadcasted_iota(jnp.int32, (TASKS, 128), 0)
    tail = jnp.dot(high, (lane == row).astype(BF16), preferred_element_type=F32)
    tail += jnp.dot(low, (lane == row + TASKS).astype(BF16), preferred_element_type=F32)
    width = tokens.shape[1]
    for i in range(to_chips.shape[0]):
        to_chips[i, :, :width] = tokens[...]
        to_chips[i, :, width:] = tail.astype(BF16)
    for i in range(to_tensor.shape[0]):
        to_tensor[i] = tokens[...]


def latent_kernel(width, s, own, other, low_own, low_other, out):
    q = s[3]
    x = jnp.concatenate([rows_of(own[...]), rows_of(other[...])], axis=0)
    low = jnp.concatenate([low_own[0], low_other[...]], axis=1)
    lat = jnp.dot(x[:, :width].astype(BF16), low, preferred_element_type=F32)
    tail = x[:, width:]
    lane = lax.broadcasted_iota(jnp.int32, tail.shape, 1)
    weight = jnp.sum(
        jnp.where((lane == q) | (lane == TASKS + q), tail, 0.0), axis=1, keepdims=True
    )
    lat = (lat * weight).astype(BF16)
    for j in range(out.shape[0]):
        out[j] = lat


def gather_rows_kernel(s, lat, own, other, out):
    c = s[2]
    half = own.shape[2] // 2
    m = out.shape[0] // 2
    a = pl.multiple_of(c * half, half)
    b = pl.multiple_of((1 - c) * half, half)
    for k, ref in enumerate((own, other)):
        out[k * m : (k + 1) * m, :half] = rows_of(ref[:, :, pl.ds(a, half)]).astype(BF16)
        out[k * m : (k + 1) * m, half : 2 * half] = rows_of(ref[:, :, pl.ds(b, half)]).astype(
            BF16
        )
    total = lat[0].astype(F32)
    for j in range(1, lat.shape[0]):
        total += lat[j].astype(F32)
    out[:, 2 * half :] = total.astype(BF16)


def main_kernel(d, limit, s, rows, w_own, w_other, u_own, u_other, out):
    w = jnp.concatenate([w_own[0], w_other[...], u_own[0], u_other[...]], axis=1)
    p = lax.dot_general(w, rows[...], (((1,), (1,)), ((), ())), preferred_element_type=F32)
    start = (lax.rem(s[0] + d, NX) * 2 + pl.program_id(0)) * p.shape[0]
    at = start + lax.broadcasted_iota(jnp.int32, p.shape, 0)
    p = jnp.where(at < limit, p, 0.0)
    m = out.shape[1]
    out[0] = p[:m].astype(out.dtype)
    out[1] = p[m:].astype(out.dtype)


def x_sum_kernel(s, a0, a1, a2, a3, o0, o1, o2, o3):
    for i, o in enumerate((o0, o1, o2, o3)):
        k = lax.rem(s[1] + i, NZ)
        t = a0[k] + a1[k].astype(F32) + a2[k].astype(F32) + a3[k].astype(F32)
        o[...] = t.astype(o.dtype)


def z_sum_kernel(s, a0, a1, a2, a3, keep, send):
    t = a0[...] + a1[...].astype(F32) + a2[...].astype(F32) + a3[...].astype(F32)
    m = keep.shape[1]
    keep[...] = t[:, :m]
    send[...] = t[:, m:]


def silu_kernel(s, keep, got, out):
    first = s[2] == 0
    gate = jnp.where(first, keep[...], got[...])
    up = jnp.where(first, got[...], keep[...])
    out[...] = (gate / (1.0 + jnp.exp(-gate)) * up).astype(BF16)


def split_kernel(limit, s, w0, w1, w2, w3, *outs):
    for d, (w, o) in enumerate(zip((w0, w1, w2, w3), outs)):
        at = lax.rem(s[0] + d, NX) * w.shape[0] + lax.broadcasted_iota(jnp.int32, w.shape, 0)
        o[...] = jnp.where(at < limit, w[...].astype(F32), 0.0).astype(BF16)


def down_kernel(s, h0, h1, h2, h3, *rest):
    weights, (out, held) = rest[:-2], rest[-2:]
    m = h0.shape[0]
    for d, h in enumerate((h0, h1, h2, h3)):
        k = lax.rem(s[1] - d + NZ, NZ)
        held[pl.ds(pl.multiple_of(m * k, 8), m)] = h[...].astype(F32)
    h = held[...].T.astype(BF16)
    cols = weights[0].shape[1]
    for i, w in enumerate(weights):
        p = jnp.dot(h, w[...], preferred_element_type=F32).astype(BF16)
        out[:, :, i * cols : (i + 1) * cols] = p.reshape(out.shape[0], out.shape[1], cols)


def tensor_sum_kernel(s, got, o0, o1, o2, o3):
    t = got[0].astype(F32)
    for j in range(1, got.shape[0]):
        t += got[j].astype(F32)
    cols = o0.shape[1] // 2
    for d, o in enumerate((o0, o1, o2, o3)):
        o[:, :cols] = t[:, d * cols : (d + 1) * cols].astype(o.dtype)
        o[:, cols:] = t[:, (NX + d) * cols : (NX + d + 1) * cols].astype(o.dtype)


def out_sum_kernel(s, a0, a1, a2, a3, keep, send):
    t = a0[...] + a1[...].astype(F32) + a2[...].astype(F32) + a3[...].astype(F32)
    cols = keep.shape[1]
    keep[...] = t[:, :cols]
    send[...] = t[:, cols:]


def place_kernel(s, keep, got, out):
    first = s[2] == 0
    a = jnp.where(first, keep[...], got[...])
    b = jnp.where(first, got[...], keep[...])
    for i in range(out.shape[0] // 16):
        out[16 * i : 16 * i + 8] = a[8 * i : 8 * i + 8]
        out[16 * i + 8 : 16 * i + 16] = b[8 * i : 8 * i + 8]


def on_device(tokens, router, gate_up_weight, down_weight, lower_factor, upper_factor):
    t = lax.axis_index("task").astype(jnp.int32)
    c = lax.rem(t, NC)
    q = t // NC
    x, z = q // NZ, lax.rem(q, NZ)
    s = jnp.stack([x, z, c, q])
    tensor = lax.axis_size("tensor")
    run = functools.partial(call, scalars=s)

    def permute(a, perm):
        return lax.ppermute(a, "task", perm)

    def chips(a):
        return lax.all_to_all(a, "task", 0, 0, axis_index_groups=CHIPS)

    def across(a):
        return lax.all_to_all(a, "tensor", 0, 0)

    def other(a):
        return lax.dynamic_index_in_dim(a, 1 - c, 0, keepdims=False)

    rows, width = tokens.shape
    ranks = 2 * lower_factor.shape[2]
    feats = 2 * gate_up_weight.shape[1]
    hid = gate_up_weight.shape[2]
    count = NQ * NC * rows
    weight = jnp.swapaxes(gate_up_weight, 1, 2)
    upper = jnp.swapaxes(upper_factor, 1, 2)
    zb = -(-hid // (NX * NZ * 8)) * 8
    xb = NZ * zb

    low_other = permute(other(lower_factor), CORE)
    w_other = permute(other(weight), CORE)
    u_other = permute(other(upper), CORE)

    to_chips, to_tensor = run(
        pack_kernel,
        [sds((NQ, rows, width + 128)), sds((tensor, rows, width))],
        tokens,
        router,
    )
    own_rows = chips(to_chips)
    full = across(to_tensor)
    other_rows = permute(own_rows, CORE)
    full = full.reshape(tensor, rows, width // feats, feats).transpose(0, 2, 1, 3)
    own_cols = chips(full.reshape(NQ, rows, feats))
    other_cols = permute(own_cols, CORE)

    lat = run(
        functools.partial(latent_kernel, width),
        sds((tensor, count, ranks)),
        own_rows,
        other_rows,
        lower_factor,
        low_other,
        in_specs=[
            whole(own_rows),
            whole(other_rows),
            pl.BlockSpec((1,) + lower_factor.shape[1:], lambda i, s: (s[2], 0, 0)),
            whole(low_other),
        ],
    )
    lat = across(lat)

    pieces = run(
        functools.partial(split_kernel, hid),
        [sds((xb, down_weight.shape[1]))] * NX,
        *[down_weight] * NX,
        in_specs=[
            pl.BlockSpec(
                (xb, down_weight.shape[1]), lambda i, s, d=d: (lax.rem(s[0] + d, NX), 0)
            )
            for d in range(NX)
        ],
    )
    got = {d: permute(pieces[d], TO_X[d]) for d in FAR_FIRST}
    down_own = [pieces[0], got[1], got[2], got[3]]
    down_other = [permute(a, CORE) for a in down_own]

    cat = run(gather_rows_kernel, sds((count, feats + ranks)), lat, own_cols, other_cols)
    block = 2 * zb

    def main(d, dtype):
        def at(i, s):
            return lax.rem(s[0] + d, NX) * 2 + i

        def own_spec(a):
            return pl.BlockSpec((1, block, a.shape[2]), lambda i, s: (s[2], at(i, s), 0))

        def spec(a):
            return pl.BlockSpec((block, a.shape[1]), lambda i, s: (at(i, s), 0))

        return run(
            functools.partial(main_kernel, d, hid),
            sds((NZ, zb, count), dtype),
            cat,
            weight,
            w_other,
            upper,
            u_other,
            grid=(2,),
            in_specs=[whole(cat), own_spec(weight), spec(w_other), own_spec(upper), spec(u_other)],
            out_specs=pl.BlockSpec((2, zb, count), lambda i, s: (i, 0, 0)),
        )

    got = {d: permute(main(d, BF16), TO_X[d]) for d in FAR_FIRST}
    parts = run(
        x_sum_kernel,
        [sds((zb, count), F32)] + [sds((zb, count))] * 3,
        main(0, F32),
        got[1],
        got[2],
        got[3],
    )
    got = {d: permute(parts[d], TO_Z[d]) for d in FAR_FIRST}
    keep, send = run(
        z_sum_kernel, [sds((zb, count // 2), F32)] * 2, parts[0], got[1], got[2], got[3]
    )
    hidden = run(silu_kernel, sds((zb, count // 2)), keep, permute(send, CORE))

    got = {d: permute(hidden, TO_Z[d]) for d in FAR_FIRST}
    cols = down_weight.shape[1]
    out_rows = count // 2 // tensor
    mixed = run(
        down_kernel,
        sds((tensor, out_rows, 2 * NX * cols)),
        hidden,
        got[1],
        got[2],
        got[3],
        *down_own,
        *down_other,
        scratch=[pltpu.VMEM((xb, count // 2), F32)],
    )
    parts = run(
        tensor_sum_kernel,
        [sds((out_rows, 2 * cols), F32)] + [sds((out_rows, 2 * cols))] * 3,
        across(mixed),
    )
    got = {d: permute(parts[d], TO_X[NX - d]) for d in FAR_FIRST}
    keep, send = run(
        out_sum_kernel, [sds((out_rows, cols), F32)] * 2, parts[0], got[1], got[2], got[3]
    )
    return run(place_kernel, sds((2 * out_rows, cols), F32), keep, permute(send, CORE))


def solution(mesh):
    in_specs = (
        P("task", "tensor"),
        P("task", None),
        P(None, "task", "tensor"),
        P("tensor", "task"),
        P(None, "tensor", "task"),
        P(None, "task", "tensor"),
    )
    out_specs = P("tensor", "task")
    return jax.shard_map(
        on_device, mesh=mesh, in_specs=in_specs, out_specs=out_specs, check_vma=False
    )
```

time: 416 us -> 184 us (0.44); the launches traced: 411 us -> 183 us
  waiting for transfers between devices: 284 us -> 44.7 us
  starting transfers between devices: 0.17 us -> 87 us
  blocking collectives: 97.8 us -> 22.7 us
  Pallas kernels: 0 us -> 21.6 us
  matrix products: 13.3 us -> 0 us
  between operations: 13.2 us -> 0.22 us
  local copies, waits for them, and re-layouts: 0.01 us -> 6.36 us
    reduce_scatter x2 -> x0, waiting for transfers between devices: 154 us -> none  [the longest x1 122 us: on_device(): lax.psum_scatter(jnp.einsum('td,gdf->tgf', part, gate_up_weight, preferre...]
    all_gather x2 -> x0, waiting for transfers between devices: 102 us -> none  [the longest x1 53.3 us: on_device(): lax.all_gather(hidden, 'task', axis=0, tiled=True)]
    all_gather x2 -> x0, blocking collectives: 97.8 us -> none  [the longest x1 53 us: on_device(): lax.all_gather(tokens, 'task', axis=0, tiled=True)]
    ppermute x0 -> x26, starting transfers between devices: none -> 69.4 us  [permute(): return lax.ppermute(a, 'task', perm)]
    ppermute x0 -> x26, waiting for transfers between devices: none -> 33.4 us  [permute(): return lax.ppermute(a, 'task', perm)]
    psum x1 -> x0, waiting for transfers between devices: 27.7 us -> none  [on_device(): rank_sum = lax.psum(latent_part, 'tensor')]
    all_to_all x0 -> x2, blocking collectives: none -> 22.7 us  [across(): return lax.all_to_all(a, 'tensor', 0, 0)]
    pallas_call x0 -> x15, Pallas kernels: none -> 21.6 us  [call(): pl.pallas_call(kernel, out_shape=out_shape, grid_spec=pltpu.PrefetchScala...]
  transfers between devices with their start and end apart: 5 -> 29, of which waited for: 5 -> 13; matrix products, arithmetic and copies ran while one was open for 0% -> 3% of each run, Pallas kernels for 0% -> 8%
where the time goes in v2:
time: 184 us; the launch traced here: 183 us
  starting transfers between devices  87 us (47%)
  waiting for transfers between devices  44.7 us (24%)
  blocking collectives  22.7 us (12%)
  Pallas kernels  21.6 us (12%)
  local copies, waits for them, and re-layouts  6.36 us (3%)
    ppermute x26, starting transfers between devices, permute(): return lax.ppermute(a, 'task', perm)  69.4 us
    ppermute x26, waiting for transfers between devices, permute(): return lax.ppermute(a, 'task', perm)  33.4 us
    all_to_all x2, blocking collectives, across(): return lax.all_to_all(a, 'tensor', 0, 0)  22.7 us
    pallas_call x15, Pallas kernels, call(): pl.pallas_call(kernel, out_shape=out_shape, grid_spec=pltpu.PrefetchScala...  21.6 us
    all_to_all x2, starting transfers between devices, chips(): return lax.all_to_all(a, 'task', 0, 0, axis_index_groups=CHIPS)  13.4 us
    all_to_all x2, waiting for transfers between devices, chips(): return lax.all_to_all(a, 'task', 0, 0, axis_index_groups=CHIPS)  9.21 us
    squeeze x3, local copies, waits for them, and re-layouts, other(): return lax.dynamic_index_in_dim(a, 1 - c, 0, keepdims=False)  4.93 us
    all_to_all x1, starting transfers between devices, across(): return lax.all_to_all(a, 'tensor', 0, 0)  4.25 us
  transfers between devices with their start and end apart: 29, of which 13 were waited for; matrix products, arithmetic and copies ran while one was open for 3% of the time, Pallas kernels for 8%

profile of v2, /device:TPU:1, one launch (start us, length us, event | category | flops | bytes accessed | tf_op | source)
XLA Modules:
  0.0 183.4 jit_solution(14057717567018482126)
XLA Ops:
  0.0 0.1 pad_add_fusion.s
  0.1 0.7 copy-done.3
  0.8 0.7 copy-done.4
  1.5 1.4 shard_map.64
  2.9 11.6 %all_to_all.25 = bf16[8,8,1024]{2,1,0:T(8,128)(2,1)S(1)} all-to-all(bf16[8,8,1024]{2,1,0:T(8,128)(2,1)S(1)} %get-tuple-element.24), channel_id=1, replica_groups=mesh['task'=32,'tensor'=8] {'tensor'}, dimensions={0} | all-to-all | bytes 262144 | tf_op jit(solution)/shard_map/all_to_all | solution.py:211
  14.5 9.9 %all-to-all-start = ((bf16[16,8,1152]{2,1,0:T(8,128)(2,1)}), bf16[16,8,1152]{2,1,0:T(8,128)(2,1)S(1)}, u32[]{:S(2)}, u32[]{:S(2)}) async-start(bf16[16,8,1152]{2,1,0:T(8,128)(2,1)} %get-tuple-element.23), calls=%async_computation | async-start | bytes 589824 | tf_op jit(solution)/shard_map/all_to_all | solution.py:208
  24.3 1.0 dynamic-slice_bitcast_fusion.2
  25.3 2.5 %collective-permute-start.1 = (bf16[1024,128]{1,0:T(8,128)(2,1)S(1)}, bf16[1024,128]{1,0:T(8,128)(2,1)S(1)}, u32[]{:S(2)}, u32[]{:S(2)}) collective-permute-start(bf16[1024,128]{1,0:T(8,128)(2,1)S(1)} %dynamic-slice_bitcast_fusion.2), channel_id=1, source_target_pairs={{0,8},{8,0},{16,24},{24,16},{32,40},{40,32},{48,56},{56,48},{64,72... | collective-permute-start | bytes 786440 | tf_op jit(solution)/shard_map/ppermute | solution.py:205
  27.8 0.7 pad_maximum_fusion
  28.4 7.5 %all-to-all-done.own = bf16[16,8,1152]{2,1,0:T(8,128)(2,1)S(1)} async-done(((bf16[16,8,1152]{2,1,0:T(8,128)(2,1)}), bf16[16,8,1152]{2,1,0:T(8,128)(2,1)S(1)}, u32[]{:S(2)}, u32[]{:S(2)}) %all-to-all-start) | async-done | bytes 294944 | tf_op jit(solution)/shard_map/all_to_all | solution.py:208
  36.0 3.5 %all-to-all-start.3 = ((bf16[16,8,512]{2,1,0:T(8,128)(2,1)}), bf16[16,8,512]{2,1,0:T(8,128)(2,1)S(1)}, u32[]{:S(2)}, u32[]{:S(2)}) async-start(bf16[16,8,512]{2,1,0:T(8,128)(2,1)} %bitcast.5), calls=%async_computation.3 | async-start | bytes 262144 | tf_op jit(solution)/shard_map/all_to_all | solution.py:208
  39.5 3.0 %collective-permute-start = (bf16[16,8,1152]{2,1,0:T(8,128)(2,1)S(1)}, bf16[16,8,1152]{2,1,0:T(8,128)(2,1)S(1)}, u32[]{:S(2)}, u32[]{:S(2)}) collective-permute-start(bf16[16,8,1152]{2,1,0:T(8,128)(2,1)S(1)} %all-to-all-done.own), channel_id=1, source_target_pairs={{0,8},{8,0},{16,24},{24,16},{32,40},{40,32},{48,56},{56,48},{64,72... | collective-permute-start | bytes 884744 | tf_op jit(solution)/shard_map/ppermute | solution.py:205
  42.5 2.9 %dynamic-slice_bitcast_fusion = bf16[3696,256]{1,0:T(8,128)(2,1)} fusion(bf16[2,256,3696]{1,2,0:T(8,128)(2,1)} %param.8, s32[]{:T(128)S(6)} %select_n.18), kind=kLoop, calls=%fused_computation | loop fusion | bytes 3784708 | tf_op jit(solution)/shard_map/jit(dynamic_index_in_dim)/squeeze | solution.py:214
  45.5 0.1 collective-permute-start.3
  45.5 1.8 shard_map.65
  47.4 1.7 all-to-all-done.3.own
  49.1 4.2 %all-to-all-start.1 = ((bf16[8,256,256]{2,1,0:T(8,128)(2,1)}), bf16[8,256,256]{2,1,0:T(8,128)(2,1)}, u32[]{:S(2)}, u32[]{:S(2)}) async-start(bf16[8,256,256]{2,1,0:T(8,128)(2,1)} %shard_map.65), calls=%async_computation.1 | async-start | bytes 2097152 | tf_op jit(solution)/shard_map/all_to_all | solution.py:211
  53.3 1.0 dynamic-slice_bitcast_fusion.1
  54.3 4.2 %collective-permute-start.4 = (bf16[3696,128]{1,0:T(8,128)(2,1)}, bf16[3696,128]{1,0:T(8,128)(2,1)S(1)}, u32[]{:S(2)}, u32[]{:S(2)}) collective-permute-start(bf16[3696,128]{1,0:T(8,128)(2,1)} %dynamic-slice_bitcast_fusion.1), channel_id=1, source_target_pairs={{0,8},{8,0},{16,24},{24,16},{32,40},{40,32},{48,56},{56,48},{64,72... | collective-permute-start | bytes 2838536 | tf_op jit(solution)/shard_map/ppermute | solution.py:205
  58.6 2.2 %collective-permute-done.2.other = bf16[16,8,512]{2,1,0:T(8,128)(2,1)S(1)} collective-permute-done((bf16[16,8,512]{2,1,0:T(8,128)(2,1)S(1)}, bf16[16,8,512]{2,1,0:T(8,128)(2,1)S(1)}, u32[]{:S(2)}, u32[]{:S(2)}) %collective-permute-start.2) | collective-permute-done | bytes 131104 | tf_op jit(solution)/shard_map/ppermute | solution.py:205
  60.8 2.1 %all-to-all-done.1.lat = bf16[8,256,256]{2,1,0:T(8,128)(2,1)} async-done(((bf16[8,256,256]{2,1,0:T(8,128)(2,1)}), bf16[8,256,256]{2,1,0:T(8,128)(2,1)}, u32[]{:S(2)}, u32[]{:S(2)}) %all-to-all-start.1) | async-done | bytes 1048608 | tf_op jit(solution)/shard_map/all_to_all | solution.py:211
  62.9 1.9 %shard_map.66.rows = bf16[256,768]{1,0:T(8,128)(2,1)S(1)} custom-call(s32[4]{0:T(128)S(1)} %pad_add_fusion.s, bf16[8,256,256]{2,1,0:T(8,128)(2,1)} %all-to-all-done.1.lat, bf16[16,8,512]{2,1,0:T(8,128)(2,1)S(1)} %all-to-all-done.3.own, bf16[16,8,512]{2,1,0:T(8,128)(2,1)S(1)} %collective-permute-done.2.other), custom_call_target="tpu_custom_call" | custom-call | tf_op jit(solution)/shard_map/pallas_call | solution.py:52
  64.8 2.5 %shard_map.68 = bf16[4,232,256]{2,1,0:T(8,128)(2,1)S(1)} custom-call(s32[4]{0:T(128)S(1)} %pad_add_fusion.s, bf16[256,768]{1,0:T(8,128)(2,1)S(1)} %shard_map.66.rows, bf16[2,3696,256]{2,1,0:T(8,128)(2,1)} %bitcast.21, bf16[3696,256]{1,0:T(8,128)(2,1)} %collective-permute-done.3.w_other, bf16[2,3696,128]{2,1,0:T(8,128)(2,1)S(1)} %bitcast.17, ...), custom_call_target="tpu_custom_call" | custom-call | tf_op jit(solution)/shard_map/pallas_call | solution.py:52
  67.3 0.2 collective-permute-start.5
  67.5 2.5 %shard_map.69 = bf16[4,232,256]{2,1,0:T(8,128)(2,1)S(1)} custom-call(s32[4]{0:T(128)S(1)} %pad_add_fusion.s, bf16[256,768]{1,0:T(8,128)(2,1)S(1)} %shard_map.66.rows, bf16[2,3696,256]{2,1,0:T(8,128)(2,1)} %bitcast.22, bf16[3696,256]{1,0:T(8,128)(2,1)} %collective-permute-done.3.w_other, bf16[2,3696,128]{2,1,0:T(8,128)(2,1)S(1)} %bitcast.18, ...), custom_call_target="tpu_custom_call" | custom-call | tf_op jit(solution)/shard_map/pallas_call | solution.py:52
  70.0 2.8 %collective-permute-start.6 = (bf16[4,232,256]{2,1,0:T(8,128)(2,1)S(1)}, bf16[4,232,256]{2,1,0:T(8,128)(2,1)S(1)}, u32[]{:S(2)}, u32[]{:S(2)}) collective-permute-start(bf16[4,232,256]{2,1,0:T(8,128)(2,1)S(1)} %shard_map.69), channel_id=1, source_target_pairs={{0,128},{8,136},{16,144},{24,152},{32,160},{40,168},{48,176},{56,1... | collective-permute-start | bytes 1425416 | tf_op jit(solution)/shard_map/ppermute | solution.py:205
  72.8 2.5 %shard_map.70 = bf16[4,232,256]{2,1,0:T(8,128)(2,1)S(1)} custom-call(s32[4]{0:T(128)S(1)} %pad_add_fusion.s, bf16[256,768]{1,0:T(8,128)(2,1)S(1)} %shard_map.66.rows, bf16[2,3696,256]{2,1,0:T(8,128)(2,1)} %bitcast.23, bf16[3696,256]{1,0:T(8,128)(2,1)} %collective-permute-done.3.w_other, bf16[2,3696,128]{2,1,0:T(8,128)(2,1)S(1)} %bitcast.19, ...), custom_call_target="tpu_custom_call" | custom-call | tf_op jit(solution)/shard_map/pallas_call | solution.py:52
  75.3 1.5 collective-permute-start.7
  76.8 1.0 shard_map.74
  77.8 0.1 collective-permute-start.15
  77.9 1.2 collective-permute-start.16
  79.1 1.6 collective-permute-start.17
  80.7 2.4 %shard_map.67.a0 = f32[4,232,256]{2,1,0:T(8,128)S(1)} custom-call(s32[4]{0:T(128)S(1)} %pad_add_fusion.s, bf16[256,768]{1,0:T(8,128)(2,1)S(1)} %shard_map.66.rows, bf16[2,3696,256]{2,1,0:T(8,128)(2,1)} %bitcast.24, bf16[3696,256]{1,0:T(8,128)(2,1)} %collective-permute-done.3.w_other, bf16[2,3696,128]{2,1,0:T(8,128)(2,1)S(1)} %bitcast.20, ...), custom_call_target="tpu_custom_call" | custom-call | tf_op jit(solution)/shard_map/pallas_call | solution.py:52
  83.1 2.3 %collective-permute-done.6.a2 = bf16[4,232,256]{2,1,0:T(8,128)(2,1)S(1)} collective-permute-done((bf16[4,232,256]{2,1,0:T(8,128)(2,1)S(1)}, bf16[4,232,256]{2,1,0:T(8,128)(2,1)S(1)}, u32[]{:S(2)}, u32[]{:S(2)}) %collective-permute-start.6) | collective-permute-done | bytes 475168 | tf_op jit(solution)/shard_map/ppermute | solution.py:205
  85.5 7.6 %collective-permute-done.7.a3 = bf16[4,232,256]{2,1,0:T(8,128)(2,1)S(1)} collective-permute-done((bf16[4,232,256]{2,1,0:T(8,128)(2,1)S(1)}, bf16[4,232,256]{2,1,0:T(8,128)(2,1)S(1)}, u32[]{:S(2)}, u32[]{:S(2)}) %collective-permute-start.7) | collective-permute-done | bytes 475168 | tf_op jit(solution)/shard_map/ppermute | solution.py:205
  93.0 0.8 shard_map.71
  93.8 9.0 %collective-permute-start.10 = (bf16[232,256]{1,0:T(8,128)(2,1)S(1)}, bf16[232,256]{1,0:T(8,128)(2,1)S(1)}, u32[]{:S(2)}, u32[]{:S(2)}) collective-permute-start(bf16[232,256]{1,0:T(8,128)(2,1)S(1)} %get-tuple-element.28), channel_id=1, source_target_pairs={{0,48},{8,56},{16,0},{24,8},{32,16},{40,24},{48,32},{56,40},{64,11... | collective-permute-start | bytes 356360 | tf_op jit(solution)/shard_map/ppermute | solution.py:205
  102.8 2.5 %collective-permute-start.18 = (bf16[928,256]{1,0:T(8,128)(2,1)S(1)}, bf16[928,256]{1,0:T(8,128)(2,1)S(1)}, u32[]{:S(2)}, u32[]{:S(2)}) collective-permute-start(bf16[928,256]{1,0:T(8,128)(2,1)S(1)} %get-tuple-element.31.rest_0_), channel_id=1, source_target_pairs={{0,8},{8,0},{16,24},{24,16},{32,40},{40,32},{48,56},{56,48},{64,72... | collective-permute-start | bytes 1425416 | tf_op jit(solution)/shard_map/ppermute | solution.py:205
  105.3 7.5 %collective-permute-start.19 = (bf16[928,256]{1,0:T(8,128)(2,1)S(1)}, bf16[928,256]{1,0:T(8,128)(2,1)S(1)}, u32[]{:S(2)}, u32[]{:S(2)}) collective-permute-start(bf16[928,256]{1,0:T(8,128)(2,1)S(1)} %collective-permute-done.15.rest_1_), channel_id=1, source_target_pairs={{0,8},{8,0},{16,24},{24,16},{32,40},{40,32},{48,56},{56,48},{64,72... | collective-permute-start | bytes 1425416 | tf_op jit(solution)/shard_map/ppermute | solution.py:205
  112.8 0.0 collective-permute-start.20
  112.8 2.8 %collective-permute-start.21 = (bf16[928,256]{1,0:T(8,128)(2,1)S(1)}, bf16[928,256]{1,0:T(8,128)(2,1)S(1)}, u32[]{:S(2)}, u32[]{:S(2)}) collective-permute-start(bf16[928,256]{1,0:T(8,128)(2,1)S(1)} %collective-permute-done.17.rest_3_), channel_id=1, source_target_pairs={{0,8},{8,0},{16,24},{24,16},{32,40},{40,32},{48,56},{56,48},{64,72... | collective-permute-start | bytes 1425416 | tf_op jit(solution)/shard_map/ppermute | solution.py:205
  115.6 4.9 %collective-permute-start.8 = (bf16[232,256]{1,0:T(8,128)(2,1)S(1)}, bf16[232,256]{1,0:T(8,128)(2,1)S(1)}, u32[]{:S(2)}, u32[]{:S(2)}) collective-permute-start(bf16[232,256]{1,0:T(8,128)(2,1)S(1)} %get-tuple-element.26), channel_id=1, source_target_pairs={{0,16},{8,24},{16,32},{24,40},{32,48},{40,56},{48,0},{56,8},{64,80... | collective-permute-start | bytes 356360 | tf_op jit(solution)/shard_map/ppermute | solution.py:205
  120.5 5.7 %collective-permute-done.8.a1 = bf16[232,256]{1,0:T(8,128)(2,1)S(1)} collective-permute-done((bf16[232,256]{1,0:T(8,128)(2,1)S(1)}, bf16[232,256]{1,0:T(8,128)(2,1)S(1)}, u32[]{:S(2)}, u32[]{:S(2)}) %collective-permute-start.8) | collective-permute-done | bytes 118816 | tf_op jit(solution)/shard_map/ppermute | solution.py:205
  126.2 8.0 %collective-permute-start.9 = (bf16[232,256]{1,0:T(8,128)(2,1)S(1)}, bf16[232,256]{1,0:T(8,128)(2,1)S(1)}, u32[]{:S(2)}, u32[]{:S(2)}) collective-permute-start(bf16[232,256]{1,0:T(8,128)(2,1)S(1)} %get-tuple-element.27), channel_id=1, source_target_pairs={{0,32},{8,40},{16,48},{24,56},{32,0},{40,8},{48,16},{56,24},{64,96... | collective-permute-start | bytes 356360 | tf_op jit(solution)/shard_map/ppermute | solution.py:205
  134.2 5.6 %collective-permute-done.9.a2 = bf16[232,256]{1,0:T(8,128)(2,1)S(1)} collective-permute-done((bf16[232,256]{1,0:T(8,128)(2,1)S(1)}, bf16[232,256]{1,0:T(8,128)(2,1)S(1)}, u32[]{:S(2)}, u32[]{:S(2)}) %collective-permute-start.9) | collective-permute-done | bytes 118816 | tf_op jit(solution)/shard_map/ppermute | solution.py:205
  139.8 0.6 shard_map.72
  140.4 0.6 collective-permute-start.11
  141.0 1.0 collective-permute-done.11.got
  142.0 0.6 shard_map.73.h0
  142.6 0.1 collective-permute-start.12
  142.7 5.1 %collective-permute-start.13 = (bf16[232,128]{1,0:T(8,128)(2,1)S(1)}, bf16[232,128]{1,0:T(8,128)(2,1)S(1)}, u32[]{:S(2)}, u32[]{:S(2)}) collective-permute-start(bf16[232,128]{1,0:T(8,128)(2,1)S(1)} %shard_map.73.h0), channel_id=1, source_target_pairs={{0,32},{8,40},{16,48},{24,56},{32,0},{40,8},{48,16},{56,24},{64,96... | collective-permute-start | bytes 178184 | tf_op jit(solution)/shard_map/ppermute | solution.py:205
  147.8 3.5 %collective-permute-start.14 = (bf16[232,128]{1,0:T(8,128)(2,1)S(1)}, bf16[232,128]{1,0:T(8,128)(2,1)S(1)}, u32[]{:S(2)}, u32[]{:S(2)}) collective-permute-start(bf16[232,128]{1,0:T(8,128)(2,1)S(1)} %shard_map.73.h0), channel_id=1, source_target_pairs={{0,48},{8,56},{16,0},{24,8},{32,16},{40,24},{48,32},{56,40},{64,11... | collective-permute-start | bytes 178184 | tf_op jit(solution)/shard_map/ppermute | solution.py:205
  151.3 4.4 %collective-permute-done.14.h3 = bf16[232,128]{1,0:T(8,128)(2,1)S(1)} collective-permute-done((bf16[232,128]{1,0:T(8,128)(2,1)S(1)}, bf16[232,128]{1,0:T(8,128)(2,1)S(1)}, u32[]{:S(2)}, u32[]{:S(2)}) %collective-permute-start.14) | collective-permute-done | bytes 59424 | tf_op jit(solution)/shard_map/ppermute | solution.py:205
  155.7 1.3 shard_map.75
  157.0 11.1 %all_to_all.26.got = bf16[8,16,2048]{2,1,0:T(8,128)(2,1)S(1)} all-to-all(bf16[8,16,2048]{2,1,0:T(8,128)(2,1)S(1)} %shard_map.75), channel_id=1, replica_groups=mesh['task'=32,'tensor'=8] {'tensor'}, dimensions={0} | all-to-all | bytes 1048576 | tf_op jit(solution)/shard_map/all_to_all | solution.py:211
  168.1 0.6 shard_map.76
  168.8 2.4 %collective-permute-start.22 = (bf16[16,512]{1,0:T(8,128)(2,1)S(1)}, bf16[16,512]{1,0:T(8,128)(2,1)S(1)}, u32[]{:S(2)}, u32[]{:S(2)}) collective-permute-start(bf16[16,512]{1,0:T(8,128)(2,1)S(1)} %get-tuple-element.36), channel_id=1, source_target_pairs={{0,192},{8,200},{16,208},{24,216},{32,224},{40,232},{48,240},{56,2... | collective-permute-start | bytes 49160 | tf_op jit(solution)/shard_map/ppermute | solution.py:205
  171.1 1.9 %collective-permute-start.23 = (bf16[16,512]{1,0:T(8,128)(2,1)S(1)}, bf16[16,512]{1,0:T(8,128)(2,1)S(1)}, u32[]{:S(2)}, u32[]{:S(2)}) collective-permute-start(bf16[16,512]{1,0:T(8,128)(2,1)S(1)} %get-tuple-element.37), channel_id=1, source_target_pairs={{0,128},{8,136},{16,144},{24,152},{32,160},{40,168},{48,176},{56,1... | collective-permute-start | bytes 49160 | tf_op jit(solution)/shard_map/ppermute | solution.py:205
  173.0 2.2 %collective-permute-done.23.a2 = bf16[16,512]{1,0:T(8,128)(2,1)S(1)} collective-permute-done((bf16[16,512]{1,0:T(8,128)(2,1)S(1)}, bf16[16,512]{1,0:T(8,128)(2,1)S(1)}, u32[]{:S(2)}, u32[]{:S(2)}) %collective-permute-start.23) | collective-permute-done | bytes 16416 | tf_op jit(solution)/shard_map/ppermute | solution.py:205
  175.2 1.6 collective-permute-done.24.a3
  176.8 0.5 shard_map.77
  177.4 4.0 %collective-permute-start.25 = (f32[16,256]{1,0:T(8,128)S(1)}, f32[16,256]{1,0:T(8,128)S(1)}, u32[]{:S(2)}, u32[]{:S(2)}) collective-permute-start(f32[16,256]{1,0:T(8,128)S(1)} %get-tuple-element.40), channel_id=1, source_target_pairs={{0,8},{8,0},{16,24},{24,16},{32,40},{40,32},{48,56},{56,48},{64,72... | collective-permute-start | bytes 49160 | tf_op jit(solution)/shard_map/ppermute | solution.py:205
  181.4 0.8 collective-permute-done.25.got
  182.2 1.2 shard_map.78
  (27 shorter events, 0.1 us)
Async XLA Ops:
  0.1 0.7 copy-start.3
  0.8 0.7 copy-start.4
  14.5 21.5 %all-to-all-start = ((bf16[16,8,1152]{2,1,0:T(8,128)(2,1)}), bf16[16,8,1152]{2,1,0:T(8,128)(2,1)S(1)}, u32[]{:S(2)}, u32[]{:S(2)}) async-start(bf16[16,8,1152]{2,1,0:T(8,128)(2,1)} %get-tuple-element.23), calls=%async_computation | async-start | bytes 589824 | tf_op jit(solution)/shard_map/all_to_all | solution.py:208
  25.3 20.2 %collective-permute-start.1 = (bf16[1024,128]{1,0:T(8,128)(2,1)S(1)}, bf16[1024,128]{1,0:T(8,128)(2,1)S(1)}, u32[]{:S(2)}, u32[]{:S(2)}) collective-permute-start(bf16[1024,128]{1,0:T(8,128)(2,1)S(1)} %dynamic-slice_bitcast_fusion.2), channel_id=1, source_target_pairs={{0,8},{8,0},{16,24},{24,16},{32,40},{40,32},{48,56},{56,48},{64,72... | collective-permute-start | bytes 786440 | tf_op jit(solution)/shard_map/ppermute | solution.py:205
  36.0 13.1 %all-to-all-start.3 = ((bf16[16,8,512]{2,1,0:T(8,128)(2,1)}), bf16[16,8,512]{2,1,0:T(8,128)(2,1)S(1)}, u32[]{:S(2)}, u32[]{:S(2)}) async-start(bf16[16,8,512]{2,1,0:T(8,128)(2,1)} %bitcast.5), calls=%async_computation.3 | async-start | bytes 262144 | tf_op jit(solution)/shard_map/all_to_all | solution.py:208
  39.5 6.0 %copy-start.2 = (bf16[2,1024,128]{2,1,0:T(8,128)(2,1)S(1)}, bf16[2,1024,128]{2,1,0:T(8,128)(2,1)}, u32[]{:S(2)}) copy-start(bf16[2,1024,128]{2,1,0:T(8,128)(2,1)} %low_own.1) | copy-start | bytes 1572868
  39.5 6.0 %collective-permute-start = (bf16[16,8,1152]{2,1,0:T(8,128)(2,1)S(1)}, bf16[16,8,1152]{2,1,0:T(8,128)(2,1)S(1)}, u32[]{:S(2)}, u32[]{:S(2)}) collective-permute-start(bf16[16,8,1152]{2,1,0:T(8,128)(2,1)S(1)} %all-to-all-done.own), channel_id=1, source_target_pairs={{0,8},{8,0},{16,24},{24,16},{32,40},{40,32},{48,56},{56,48},{64,72... | collective-permute-start | bytes 884744 | tf_op jit(solution)/shard_map/ppermute | solution.py:205
  45.5 7.8 %copy-start = (bf16[2,128,3696]{1,2,0:T(8,128)(2,1)S(1)}, bf16[2,128,3696]{1,2,0:T(8,128)(2,1)}, u32[]{:S(2)}) copy-start(bf16[2,128,3696]{1,2,0:T(8,128)(2,1)} %param.11) | copy-start | bytes 5677060
  45.5 19.3 %collective-permute-start.3 = (bf16[3696,256]{1,0:T(8,128)(2,1)}, bf16[3696,256]{1,0:T(8,128)(2,1)}, u32[]{:S(2)}, u32[]{:S(2)}) collective-permute-start(bf16[3696,256]{1,0:T(8,128)(2,1)} %dynamic-slice_bitcast_fusion), channel_id=1, source_target_pairs={{0,8},{8,0},{16,24},{24,16},{32,40},{40,32},{48,56},{56,48},{64,72... | collective-permute-start | bytes 5677064 | tf_op jit(solution)/shard_map/ppermute | solution.py:205
  49.1 13.8 %all-to-all-start.1 = ((bf16[8,256,256]{2,1,0:T(8,128)(2,1)}), bf16[8,256,256]{2,1,0:T(8,128)(2,1)}, u32[]{:S(2)}, u32[]{:S(2)}) async-start(bf16[8,256,256]{2,1,0:T(8,128)(2,1)} %shard_map.65), calls=%async_computation.1 | async-start | bytes 2097152 | tf_op jit(solution)/shard_map/all_to_all | solution.py:211
  54.3 10.4 %collective-permute-start.4 = (bf16[3696,128]{1,0:T(8,128)(2,1)}, bf16[3696,128]{1,0:T(8,128)(2,1)S(1)}, u32[]{:S(2)}, u32[]{:S(2)}) collective-permute-start(bf16[3696,128]{1,0:T(8,128)(2,1)} %dynamic-slice_bitcast_fusion.1), channel_id=1, source_target_pairs={{0,8},{8,0},{16,24},{24,16},{32,40},{40,32},{48,56},{56,48},{64,72... | collective-permute-start | bytes 2838536 | tf_op jit(solution)/shard_map/ppermute | solution.py:205
  58.6 2.2 %collective-permute-start.2 = (bf16[16,8,512]{2,1,0:T(8,128)(2,1)S(1)}, bf16[16,8,512]{2,1,0:T(8,128)(2,1)S(1)}, u32[]{:S(2)}, u32[]{:S(2)}) collective-permute-start(bf16[16,8,512]{2,1,0:T(8,128)(2,1)S(1)} %all-to-all-done.3.own), channel_id=1, source_target_pairs={{0,8},{8,0},{16,24},{24,16},{32,40},{40,32},{48,56},{56,48},{64,72... | collective-permute-start | bytes 393224 | tf_op jit(solution)/shard_map/ppermute | solution.py:205
  67.3 11.8 %collective-permute-start.5 = (bf16[4,232,256]{2,1,0:T(8,128)(2,1)S(1)}, bf16[4,232,256]{2,1,0:T(8,128)(2,1)S(1)}, u32[]{:S(2)}, u32[]{:S(2)}) collective-permute-start(bf16[4,232,256]{2,1,0:T(8,128)(2,1)S(1)} %shard_map.68), channel_id=1, source_target_pairs={{0,64},{8,72},{16,80},{24,88},{32,96},{40,104},{48,112},{56,120},{... | collective-permute-start | bytes 1425416 | tf_op jit(solution)/shard_map/ppermute | solution.py:205
  70.0 6.8 %copy-start.1 = (bf16[3696,256]{1,0:T(8,128)(2,1)S(1)}, bf16[3696,256]{1,0:T(8,128)(2,1)}, u32[]{:S(2)}) copy-start(bf16[3696,256]{1,0:T(8,128)(2,1)} %w3.1) | copy-start | bytes 5677060
  70.0 15.5 %collective-permute-start.6 = (bf16[4,232,256]{2,1,0:T(8,128)(2,1)S(1)}, bf16[4,232,256]{2,1,0:T(8,128)(2,1)S(1)}, u32[]{:S(2)}, u32[]{:S(2)}) collective-permute-start(bf16[4,232,256]{2,1,0:T(8,128)(2,1)S(1)} %shard_map.69), channel_id=1, source_target_pairs={{0,128},{8,136},{16,144},{24,152},{32,160},{40,168},{48,176},{56,1... | collective-permute-start | bytes 1425416 | tf_op jit(solution)/shard_map/ppermute | solution.py:205
  75.3 17.7 %collective-permute-start.7 = (bf16[4,232,256]{2,1,0:T(8,128)(2,1)S(1)}, bf16[4,232,256]{2,1,0:T(8,128)(2,1)S(1)}, u32[]{:S(2)}, u32[]{:S(2)}) collective-permute-start(bf16[4,232,256]{2,1,0:T(8,128)(2,1)S(1)} %shard_map.70), channel_id=1, source_target_pairs={{0,192},{8,200},{16,208},{24,216},{32,224},{40,232},{48,240},{56,2... | collective-permute-start | bytes 1425416 | tf_op jit(solution)/shard_map/ppermute | solution.py:205
  77.8 27.5 %collective-permute-start.15 = (bf16[928,256]{1,0:T(8,128)(2,1)S(1)}, bf16[928,256]{1,0:T(8,128)(2,1)S(1)}, u32[]{:S(2)}, u32[]{:S(2)}) collective-permute-start(bf16[928,256]{1,0:T(8,128)(2,1)S(1)} %get-tuple-element.32), channel_id=1, source_target_pairs={{0,64},{8,72},{16,80},{24,88},{32,96},{40,104},{48,112},{56,120},{... | collective-permute-start | bytes 1425416 | tf_op jit(solution)/shard_map/ppermute | solution.py:205
  77.9 34.8 %collective-permute-start.16 = (bf16[928,256]{1,0:T(8,128)(2,1)S(1)}, bf16[928,256]{1,0:T(8,128)(2,1)S(1)}, u32[]{:S(2)}, u32[]{:S(2)}) collective-permute-start(bf16[928,256]{1,0:T(8,128)(2,1)S(1)} %get-tuple-element.33), channel_id=1, source_target_pairs={{0,128},{8,136},{16,144},{24,152},{32,160},{40,168},{48,176},{56,1... | collective-permute-start | bytes 1425416 | tf_op jit(solution)/shard_map/ppermute | solution.py:205
  79.1 33.7 %collective-permute-start.17 = (bf16[928,256]{1,0:T(8,128)(2,1)S(1)}, bf16[928,256]{1,0:T(8,128)(2,1)S(1)}, u32[]{:S(2)}, u32[]{:S(2)}) collective-permute-start(bf16[928,256]{1,0:T(8,128)(2,1)S(1)} %get-tuple-element.34), channel_id=1, source_target_pairs={{0,192},{8,200},{16,208},{24,216},{32,224},{40,232},{48,240},{56,2... | collective-permute-start | bytes 1425416 | tf_op jit(solution)/shard_map/ppermute | solution.py:205
  93.8 21.8 %collective-permute-start.10 = (bf16[232,256]{1,0:T(8,128)(2,1)S(1)}, bf16[232,256]{1,0:T(8,128)(2,1)S(1)}, u32[]{:S(2)}, u32[]{:S(2)}) collective-permute-start(bf16[232,256]{1,0:T(8,128)(2,1)S(1)} %get-tuple-element.28), channel_id=1, source_target_pairs={{0,48},{8,56},{16,0},{24,8},{32,16},{40,24},{48,32},{56,40},{64,11... | collective-permute-start | bytes 356360 | tf_op jit(solution)/shard_map/ppermute | solution.py:205
  102.8 39.8 %collective-permute-start.18 = (bf16[928,256]{1,0:T(8,128)(2,1)S(1)}, bf16[928,256]{1,0:T(8,128)(2,1)S(1)}, u32[]{:S(2)}, u32[]{:S(2)}) collective-permute-start(bf16[928,256]{1,0:T(8,128)(2,1)S(1)} %get-tuple-element.31.rest_0_), channel_id=1, source_target_pairs={{0,8},{8,0},{16,24},{24,16},{32,40},{40,32},{48,56},{56,48},{64,72... | collective-permute-start | bytes 1425416 | tf_op jit(solution)/shard_map/ppermute | solution.py:205
  105.3 42.5 %collective-permute-start.19 = (bf16[928,256]{1,0:T(8,128)(2,1)S(1)}, bf16[928,256]{1,0:T(8,128)(2,1)S(1)}, u32[]{:S(2)}, u32[]{:S(2)}) collective-permute-start(bf16[928,256]{1,0:T(8,128)(2,1)S(1)} %collective-permute-done.15.rest_1_), channel_id=1, source_target_pairs={{0,8},{8,0},{16,24},{24,16},{32,40},{40,32},{48,56},{56,48},{64,72... | collective-permute-start | bytes 1425416 | tf_op jit(solution)/shard_map/ppermute | solution.py:205
  112.8 38.5 %collective-permute-start.20 = (bf16[928,256]{1,0:T(8,128)(2,1)S(1)}, bf16[928,256]{1,0:T(8,128)(2,1)S(1)}, u32[]{:S(2)}, u32[]{:S(2)}) collective-permute-start(bf16[928,256]{1,0:T(8,128)(2,1)S(1)} %collective-permute-done.16.rest_2_), channel_id=1, source_target_pairs={{0,8},{8,0},{16,24},{24,16},{32,40},{40,32},{48,56},{56,48},{64,72... | collective-permute-start | bytes 1425416 | tf_op jit(solution)/shard_map/ppermute | solution.py:205
  112.8 38.5 %collective-permute-start.21 = (bf16[928,256]{1,0:T(8,128)(2,1)S(1)}, bf16[928,256]{1,0:T(8,128)(2,1)S(1)}, u32[]{:S(2)}, u32[]{:S(2)}) collective-permute-start(bf16[928,256]{1,0:T(8,128)(2,1)S(1)} %collective-permute-done.17.rest_3_), channel_id=1, source_target_pairs={{0,8},{8,0},{16,24},{24,16},{32,40},{40,32},{48,56},{56,48},{64,72... | collective-permute-start | bytes 1425416 | tf_op jit(solution)/shard_map/ppermute | solution.py:205
  115.6 10.6 %collective-permute-start.8 = (bf16[232,256]{1,0:T(8,128)(2,1)S(1)}, bf16[232,256]{1,0:T(8,128)(2,1)S(1)}, u32[]{:S(2)}, u32[]{:S(2)}) collective-permute-start(bf16[232,256]{1,0:T(8,128)(2,1)S(1)} %get-tuple-element.26), channel_id=1, source_target_pairs={{0,16},{8,24},{16,32},{24,40},{32,48},{40,56},{48,0},{56,8},{64,80... | collective-permute-start | bytes 356360 | tf_op jit(solution)/shard_map/ppermute | solution.py:205
  126.2 13.6 %collective-permute-start.9 = (bf16[232,256]{1,0:T(8,128)(2,1)S(1)}, bf16[232,256]{1,0:T(8,128)(2,1)S(1)}, u32[]{:S(2)}, u32[]{:S(2)}) collective-permute-start(bf16[232,256]{1,0:T(8,128)(2,1)S(1)} %get-tuple-element.27), channel_id=1, source_target_pairs={{0,32},{8,40},{16,48},{24,56},{32,0},{40,8},{48,16},{56,24},{64,96... | collective-permute-start | bytes 356360 | tf_op jit(solution)/shard_map/ppermute | solution.py:205
  140.4 1.5 collective-permute-start.11
  142.6 8.7 %collective-permute-start.12 = (bf16[232,128]{1,0:T(8,128)(2,1)S(1)}, bf16[232,128]{1,0:T(8,128)(2,1)S(1)}, u32[]{:S(2)}, u32[]{:S(2)}) collective-permute-start(bf16[232,128]{1,0:T(8,128)(2,1)S(1)} %shard_map.73.h0), channel_id=1, source_target_pairs={{0,16},{8,24},{16,32},{24,40},{32,48},{40,56},{48,0},{56,8},{64,80... | collective-permute-start | bytes 178184 | tf_op jit(solution)/shard_map/ppermute | solution.py:205
  142.7 8.6 %collective-permute-start.13 = (bf16[232,128]{1,0:T(8,128)(2,1)S(1)}, bf16[232,128]{1,0:T(8,128)(2,1)S(1)}, u32[]{:S(2)}, u32[]{:S(2)}) collective-permute-start(bf16[232,128]{1,0:T(8,128)(2,1)S(1)} %shard_map.73.h0), channel_id=1, source_target_pairs={{0,32},{8,40},{16,48},{24,56},{32,0},{40,8},{48,16},{56,24},{64,96... | collective-permute-start | bytes 178184 | tf_op jit(solution)/shard_map/ppermute | solution.py:205
  147.8 7.9 %collective-permute-start.14 = (bf16[232,128]{1,0:T(8,128)(2,1)S(1)}, bf16[232,128]{1,0:T(8,128)(2,1)S(1)}, u32[]{:S(2)}, u32[]{:S(2)}) collective-permute-start(bf16[232,128]{1,0:T(8,128)(2,1)S(1)} %shard_map.73.h0), channel_id=1, source_target_pairs={{0,48},{8,56},{16,0},{24,8},{32,16},{40,24},{48,32},{56,40},{64,11... | collective-permute-start | bytes 178184 | tf_op jit(solution)/shard_map/ppermute | solution.py:205
  168.8 4.3 %collective-permute-start.22 = (bf16[16,512]{1,0:T(8,128)(2,1)S(1)}, bf16[16,512]{1,0:T(8,128)(2,1)S(1)}, u32[]{:S(2)}, u32[]{:S(2)}) collective-permute-start(bf16[16,512]{1,0:T(8,128)(2,1)S(1)} %get-tuple-element.36), channel_id=1, source_target_pairs={{0,192},{8,200},{16,208},{24,216},{32,224},{40,232},{48,240},{56,2... | collective-permute-start | bytes 49160 | tf_op jit(solution)/shard_map/ppermute | solution.py:205
  171.1 4.1 %collective-permute-start.23 = (bf16[16,512]{1,0:T(8,128)(2,1)S(1)}, bf16[16,512]{1,0:T(8,128)(2,1)S(1)}, u32[]{:S(2)}, u32[]{:S(2)}) collective-permute-start(bf16[16,512]{1,0:T(8,128)(2,1)S(1)} %get-tuple-element.37), channel_id=1, source_target_pairs={{0,128},{8,136},{16,144},{24,152},{32,160},{40,168},{48,176},{56,1... | collective-permute-start | bytes 49160 | tf_op jit(solution)/shard_map/ppermute | solution.py:205
  173.0 3.8 %collective-permute-start.24 = (bf16[16,512]{1,0:T(8,128)(2,1)S(1)}, bf16[16,512]{1,0:T(8,128)(2,1)S(1)}, u32[]{:S(2)}, u32[]{:S(2)}) collective-permute-start(bf16[16,512]{1,0:T(8,128)(2,1)S(1)} %get-tuple-element.38), channel_id=1, source_target_pairs={{0,64},{8,72},{16,80},{24,88},{32,96},{40,104},{48,112},{56,120},{... | collective-permute-start | bytes 49160 | tf_op jit(solution)/shard_map/ppermute | solution.py:205
  177.4 4.9 %collective-permute-start.25 = (f32[16,256]{1,0:T(8,128)S(1)}, f32[16,256]{1,0:T(8,128)S(1)}, u32[]{:S(2)}, u32[]{:S(2)}) collective-permute-start(f32[16,256]{1,0:T(8,128)S(1)} %get-tuple-element.40), channel_id=1, source_target_pairs={{0,8},{8,0},{16,24},{24,16},{32,40},{40,32},{48,56},{56,48},{64,72... | collective-permute-start | bytes 49160 | tf_op jit(solution)/shard_map/ppermute | solution.py:205

commit v3 on v2

v3 whole, which is shorter than its diff:
```python
import functools

import jax
import jax.numpy as jnp
from jax import lax
from jax.experimental import pallas as pl
from jax.experimental.pallas import tpu as pltpu
from jax.sharding import PartitionSpec as P

F32 = jnp.float32
BF16 = jnp.bfloat16
TASKS = 16
NX, NZ, NC = 4, 4, 2
NQ = NX * NZ
VMEM_BYTES = 48 * 1024 * 1024


def task_of(x, z, c):
    return (x * NZ + z) * NC + c


def task_perm(move):
    pairs = []
    for x in range(NX):
        for z in range(NZ):
            for c in range(NC):
                pairs.append((task_of(x, z, c), task_of(*move(x, z, c))))
    return pairs


CORE = task_perm(lambda x, z, c: (x, z, 1 - c))
TO_X = {d: task_perm(lambda x, z, c, d=d: ((x + d) % NX, z, c)) for d in (1, 2, 3)}
TO_Z = {d: task_perm(lambda x, z, c, d=d: (x, (z + d) % NZ, c)) for d in (1, 2, 3)}
CHIPS = [[task_of(x, z, c) for x in range(NX) for z in range(NZ)] for c in range(NC)]
FAR_FIRST = (2, 1, 3)


def sds(shape, dtype=BF16):
    return jax.ShapeDtypeStruct(shape, dtype)


def whole(a):
    return pl.BlockSpec(a.shape, lambda *_: (0,) * len(a.shape))


def call(kernel, out_shape, *args, scalars, grid=(1,), in_specs=None, out_specs=None, scratch=()):
    many = isinstance(out_shape, (list, tuple))
    if in_specs is None:
        in_specs = [whole(a) for a in args]
    if out_specs is None:
        out_specs = [whole(o) for o in out_shape] if many else whole(out_shape)
    return pl.pallas_call(
        kernel,
        out_shape=out_shape,
        grid_spec=pltpu.PrefetchScalarGridSpec(
            num_scalar_prefetch=1,
            grid=grid,
            in_specs=in_specs,
            out_specs=out_specs,
            scratch_shapes=list(scratch),
        ),
        compiler_params=pltpu.CompilerParams(vmem_limit_bytes=VMEM_BYTES),
    )(scalars, *args)


def rows_of(v):
    v = v.astype(F32)
    return v.reshape(v.shape[0] * v.shape[1], v.shape[2])


def pack_kernel(s, tokens, router, out):
    high = router[...].astype(BF16)
    low = (router[...] - high.astype(F32)).astype(BF16)
    lane = lax.broadcasted_iota(jnp.int32, (TASKS, 128), 1)
    row = lax.broadcasted_iota(jnp.int32, (TASKS, 128), 0)
    tail = jnp.dot(high, (lane == row).astype(BF16), preferred_element_type=F32)
    tail += jnp.dot(low, (lane == row + TASKS).astype(BF16), preferred_element_type=F32)
    width = tokens.shape[1]
    for i in range(out.shape[0]):
        out[i, :, :width] = tokens[...]
        out[i, :, width:] = tail.astype(BF16)


def latent_kernel(width, s, own, other, low_own, low_other, out):
    q = s[3]
    x = jnp.concatenate([rows_of(own[...]), rows_of(other[...])], axis=0)
    low = jnp.concatenate([low_own[0], low_other[...]], axis=1)
    lat = jnp.dot(x[:, :width].astype(BF16), low, preferred_element_type=F32)
    tail = x[:, width:]
    lane = lax.broadcasted_iota(jnp.int32, tail.shape, 1)
    weight = jnp.sum(
        jnp.where((lane == q) | (lane == TASKS + q), tail, 0.0), axis=1, keepdims=True
    )
    ranks = lat.shape[1]
    out[:, :ranks] = (lat * weight).astype(BF16)
    feats = out.shape[1] - ranks
    start = pl.multiple_of(lax.rem(q, 2) * feats, feats)
    m = out.shape[0] // 2
    for k, ref in enumerate((own, other)):
        part = rows_of(ref[:, :, pl.ds(start, feats)])
        out[k * m : (k + 1) * m, ranks:] = part.astype(BF16)


def mid_kernel(ranks, s, got, out):
    c = s[2]
    total = got[0, :, :ranks].astype(F32)
    for j in range(1, got.shape[0]):
        total += got[j, :, :ranks].astype(F32)
    half = (got.shape[2] - ranks) // 2
    own = got[s[3] // 2, :, pl.ds(pl.multiple_of(ranks + c * half, half), half)]
    other = got[s[3] // 2, :, pl.ds(pl.multiple_of(ranks + (1 - c) * half, half), half)]
    for j in range(out.shape[0]):
        out[j, :, :half] = own
        out[j, :, half : 2 * half] = other
        out[j, :, 2 * half :] = total.astype(BF16)


def main_kernel(d, limit, s, rows, w_own, w_other, u_own, u_other, out_a, out_b):
    w = jnp.concatenate([w_own[0], w_other[...], u_own[0], u_other[...]], axis=1)
    p = lax.dot_general(w, rows[...], (((1,), (1,)), ((), ())), preferred_element_type=F32)
    i = pl.program_id(0)
    start = (lax.rem(s[0] + d, NX) * 2 + i) * p.shape[0]
    at = start + lax.broadcasted_iota(jnp.int32, p.shape, 0)
    p = jnp.where(at < limit, p, 0.0)
    m = out_a.shape[1]

    @pl.when(i == 0)
    def _():
        out_a[0] = p[:m].astype(out_a.dtype)
        out_a[1] = p[m:].astype(out_a.dtype)

    @pl.when(i == 1)
    def _():
        out_b[0] = p[:m].astype(out_b.dtype)
        out_b[1] = p[m:].astype(out_b.dtype)


def pass_kernel(s, a, got_a, b, got_b, out_a, out_b):
    out_a[...] = (a[...] + got_a[...].astype(F32)).astype(BF16)
    out_b[...] = (b[...] + got_b[...].astype(F32)).astype(BF16)


def x_sum_kernel(s, a0, a1, a2, b0, b1, b2, o0, o1, o2, o3, held):
    for k in range(2):
        held[k] = a0[k] + a1[k].astype(F32) + a2[k].astype(F32)
        held[2 + k] = b0[k] + b1[k].astype(F32) + b2[k].astype(F32)
    for i, o in enumerate((o0, o1, o2, o3)):
        o[...] = held[lax.rem(s[1] + i, NZ)].astype(o.dtype)


def z_sum_kernel(s, a0, a1, a2, a3, keep, send):
    t = a0[...] + a1[...].astype(F32) + a2[...].astype(F32) + a3[...].astype(F32)
    m = keep.shape[1]
    keep[...] = t[:, :m]
    send[...] = t[:, m:]


def silu_kernel(s, keep, got, out):
    first = s[2] == 0
    gate = jnp.where(first, keep[...], got[...])
    up = jnp.where(first, got[...], keep[...])
    out[...] = (gate / (1.0 + jnp.exp(-gate)) * up).astype(BF16)


def stack_kernel(s, h0, h1, h2, h3, out):
    for d, h in enumerate((h0, h1, h2, h3)):
        out[lax.rem(s[1] - d + NZ, NZ)] = h[...]


def down_kernel(s, h0, h1, h2, h3, w_own, w_other, out, held):
    n, m = h0.shape[:2]
    for d, h in enumerate((h0, h1, h2, h3)):
        start = lax.rem(s[0] - d + NX, NX) * (n * m)
        for k in range(n):
            held[pl.ds(pl.multiple_of(start + k * m, 8), m)] = h[k].astype(F32)
    h = held[...].T.astype(BF16)
    deep, cols = w_own.shape
    for i, w in enumerate((w_own, w_other)):
        p = jnp.dot(h[:, :deep], w[...], preferred_element_type=F32).astype(BF16)
        out[:, :, i * cols : (i + 1) * cols] = p.reshape(out.shape[0], out.shape[1], cols)


def tensor_sum_kernel(s, got, keep, send):
    t = got[0].astype(F32)
    for j in range(1, got.shape[0]):
        t += got[j].astype(F32)
    cols = keep.shape[1]
    keep[...] = t[:, :cols]
    send[...] = t[:, cols:]


def place_kernel(s, keep, got, out):
    first = s[2] == 0
    a = jnp.where(first, keep[...], got[...])
    b = jnp.where(first, got[...], keep[...])
    for i in range(out.shape[0] // 16):
        out[16 * i : 16 * i + 8] = a[8 * i : 8 * i + 8]
        out[16 * i + 8 : 16 * i + 16] = b[8 * i : 8 * i + 8]


def on_device(tokens, router, gate_up_weight, down_weight, lower_factor, upper_factor):
    t = lax.axis_index("task").astype(jnp.int32)
    c = lax.rem(t, NC)
    q = t // NC
    x, z = q // NZ, lax.rem(q, NZ)
    s = jnp.stack([x, z, c, q])
    tensor = lax.axis_size("tensor")
    run = functools.partial(call, scalars=s)

    def permute(a, perm):
        return lax.ppermute(a, "task", perm)

    def across(a):
        return lax.all_to_all(a, "tensor", 0, 0)

    def other(a):
        return lax.dynamic_index_in_dim(a, 1 - c, 0, keepdims=False)

    rows, width = tokens.shape
    ranks = 2 * lower_factor.shape[2]
    feats = 2 * gate_up_weight.shape[1]
    hid = gate_up_weight.shape[2]
    count = NQ * NC * rows
    weight = jnp.swapaxes(gate_up_weight, 1, 2)
    upper = jnp.swapaxes(upper_factor, 1, 2)
    zb = -(-hid // (NX * NZ * 8)) * 8
    xb = NZ * zb

    low_other = permute(other(lower_factor), CORE)
    w_other = permute(other(weight), CORE)
    u_other = permute(other(upper), CORE)
    down_other = permute(down_weight, CORE)

    packed = run(pack_kernel, sds((NQ, rows, width + 128)), tokens, router)
    own_rows = lax.all_to_all(packed, "task", 0, 0, axis_index_groups=CHIPS)
    other_rows = permute(own_rows, CORE)
    lat = run(
        functools.partial(latent_kernel, width),
        sds((count, ranks + feats)),
        own_rows,
        other_rows,
        lower_factor,
        low_other,
        in_specs=[
            whole(own_rows),
            whole(other_rows),
            pl.BlockSpec((1,) + lower_factor.shape[1:], lambda i, s: (s[2], 0, 0)),
            whole(low_other),
        ],
    )
    got = across(lat.reshape(tensor, count // tensor, ranks + feats))
    mid = run(functools.partial(mid_kernel, ranks), sds(got.shape), got)
    cat = across(mid).reshape(count, feats + ranks)

    block = 2 * zb

    def main(d, dtype_a, dtype_b):
        def at(i, s):
            return lax.rem(s[0] + d, NX) * 2 + i

        def own_spec(a):
            return pl.BlockSpec((1, block, a.shape[2]), lambda i, s: (s[2], at(i, s), 0))

        def spec(a):
            return pl.BlockSpec((block, a.shape[1]), lambda i, s: (at(i, s), 0))

        return run(
            functools.partial(main_kernel, d, hid),
            [sds((2, zb, count), dtype_a), sds((2, zb, count), dtype_b)],
            cat,
            weight,
            w_other,
            upper,
            u_other,
            grid=(2,),
            in_specs=[whole(cat), own_spec(weight), spec(w_other), own_spec(upper), spec(u_other)],
        )

    far_a, far_b = main(2, BF16, BF16)
    far_a = permute(far_a, TO_X[1])
    far_b = permute(far_b, TO_X[3])
    up_a, up_b = main(1, F32, BF16)
    down_a, down_b = main(3, BF16, F32)
    up_b = permute(up_b, TO_X[1])
    down_a = permute(down_a, TO_X[3])
    up_a, down_b = run(pass_kernel, [sds(far_a.shape)] * 2, up_a, far_a, down_b, far_b)
    up_a = permute(up_a, TO_X[1])
    down_b = permute(down_b, TO_X[3])
    own_a, own_b = main(0, F32, F32)
    parts = run(
        x_sum_kernel,
        [sds((zb, count), F32)] + [sds((zb, count))] * 3,
        own_a,
        down_a,
        up_a,
        own_b,
        up_b,
        down_b,
        scratch=[pltpu.VMEM((NZ, zb, count), F32)],
    )
    got = {d: permute(parts[d], TO_Z[d]) for d in FAR_FIRST}
    keep, send = run(
        z_sum_kernel, [sds((zb, count // 2), F32)] * 2, parts[0], got[1], got[2], got[3]
    )
    hidden = run(silu_kernel, sds((zb, count // 2)), keep, permute(send, CORE))

    got = {d: permute(hidden, TO_Z[d]) for d in FAR_FIRST}
    hidden = run(stack_kernel, sds((NZ, zb, count // 2)), hidden, got[1], got[2], got[3])
    got = {d: permute(hidden, TO_X[d]) for d in FAR_FIRST}
    cols = down_weight.shape[1]
    out_rows = count // 2 // tensor
    mixed = run(
        down_kernel,
        sds((tensor, out_rows, 2 * cols)),
        hidden,
        got[1],
        got[2],
        got[3],
        down_weight,
        down_other,
        scratch=[pltpu.VMEM((NX * xb, count // 2), F32)],
    )
    keep, send = run(tensor_sum_kernel, [sds((out_rows, cols), F32)] * 2, across(mixed))
    return run(place_kernel, sds((2 * out_rows, cols), F32), keep, permute(send, CORE))


def solution(mesh):
    in_specs = (
        P("task", "tensor"),
        P("task", None),
        P(None, "task", "tensor"),
        P("tensor", "task"),
        P(None, "tensor", "task"),
        P(None, "task", "tensor"),
    )
    out_specs = P("tensor", "task")
    return jax.shard_map(
        on_device, mesh=mesh, in_specs=in_specs, out_specs=out_specs, check_vma=False
    )
```

time: 184 us -> 144 us (0.78)
  starting transfers between devices: 87 us -> 56.7 us
  blocking collectives: 22.7 us -> 11 us
  waiting for transfers between devices: 44.7 us -> 47.5 us
    ppermute x26 -> x22, starting transfers between devices: 69.4 us -> 35.8 us  [permute(): return lax.ppermute(a, 'task', perm)]
    all_to_all x2 -> x1, blocking collectives: 22.7 us -> 11 us  [across(): return lax.all_to_all(a, 'tensor', 0, 0)]
    all_to_all x1 -> x2, waiting for transfers between devices: 2.1 us -> 12 us  [across(): return lax.all_to_all(a, 'tensor', 0, 0)]
    ppermute x26 -> x22, waiting for transfers between devices: 33.4 us -> 26.6 us  [permute(): return lax.ppermute(a, 'task', perm)]
    all_to_all x1 -> x2, starting transfers between devices: 4.25 us -> 9.3 us  [across(): return lax.all_to_all(a, 'tensor', 0, 0)]
    all_to_all x2 -> x1, starting transfers between devices: 13.4 us -> 11.6 us  [on_device(): own_rows = lax.all_to_all(packed, 'task', 0, 0, axis_index_groups=CHIPS)]
    all_to_all x2 -> x1, waiting for transfers between devices: 9.21 us -> 8.89 us  [on_device(): own_rows = lax.all_to_all(packed, 'task', 0, 0, axis_index_groups=CHIPS)]
  transfers between devices with their start and end apart: 29 -> 25, of which waited for: 13 -> 13; matrix products, arithmetic and copies ran while one was open for 3% -> 3% of each run, Pallas kernels for 8% -> 11%
where the time goes in v3:
time: 144 us
  starting transfers between devices  56.7 us (39%)
  waiting for transfers between devices  47.5 us (33%)
  Pallas kernels  21.9 us (15%)
  blocking collectives  11 us (8%)
  local copies, waits for them, and re-layouts  6.19 us (4%)
    ppermute x22, starting transfers between devices, permute(): return lax.ppermute(a, 'task', perm)  35.8 us
    ppermute x22, waiting for transfers between devices, permute(): return lax.ppermute(a, 'task', perm)  26.6 us
    pallas_call x15, Pallas kernels, call(): pl.pallas_call(kernel, out_shape=out_shape, grid_spec=pltpu.PrefetchScala...  21.9 us
    all_to_all x2, waiting for transfers between devices, across(): return lax.all_to_all(a, 'tensor', 0, 0)  12 us
    all_to_all x1, starting transfers between devices, on_device(): own_rows = lax.all_to_all(packed, 'task', 0, 0, axis_index_groups=CHIPS)  11.6 us
    all_to_all x1, blocking collectives, across(): return lax.all_to_all(a, 'tensor', 0, 0)  11 us
    all_to_all x2, starting transfers between devices, across(): return lax.all_to_all(a, 'tensor', 0, 0)  9.3 us
    all_to_all x1, waiting for transfers between devices, on_device(): own_rows = lax.all_to_all(packed, 'task', 0, 0, axis_index_groups=CHIPS)  8.89 us
  transfers between devices with their start and end apart: 25, of which 13 were waited for; matrix products, arithmetic and copies ran while one was open for 3% of the time, Pallas kernels for 11%

profile of v3, /device:TPU:1, one launch (start us, length us, event | category | flops | bytes accessed | tf_op | source)
XLA Modules:
  0.0 143.6 jit_solution(16577574157362007218)
XLA Ops:
  0.0 0.1 pad_add_fusion.s
  0.1 0.7 copy-done.3
  0.8 0.7 copy-done.4
  1.5 1.4 shard_map.64
  2.9 11.6 %all-to-all-start = ((bf16[16,8,1152]{2,1,0:T(8,128)(2,1)}), bf16[16,8,1152]{2,1,0:T(8,128)(2,1)S(1)}, u32[]{:S(2)}, u32[]{:S(2)}) async-start(bf16[16,8,1152]{2,1,0:T(8,128)(2,1)} %shard_map.64), calls=%async_computation | async-start | bytes 589824 | tf_op jit(solution)/shard_map/all_to_all | solution.py:235
  14.5 0.0 copy-start.2
  14.5 3.0 %dynamic-slice_bitcast_fusion = bf16[3696,256]{1,0:T(8,128)(2,1)} fusion(bf16[2,256,3696]{1,2,0:T(8,128)(2,1)} %param.8, s32[]{:T(128)S(6)} %select_n.18), kind=kLoop, calls=%fused_computation | loop fusion | bytes 3784708 | tf_op jit(solution)/shard_map/jit(dynamic_index_in_dim)/squeeze | solution.py:217
  17.4 1.0 collective-permute-start.2
  18.4 8.9 %all-to-all-done.own = bf16[16,8,1152]{2,1,0:T(8,128)(2,1)S(1)} async-done(((bf16[16,8,1152]{2,1,0:T(8,128)(2,1)}), bf16[16,8,1152]{2,1,0:T(8,128)(2,1)S(1)}, u32[]{:S(2)}, u32[]{:S(2)}) %all-to-all-start) | async-done | bytes 294944 | tf_op jit(solution)/shard_map/all_to_all | solution.py:235
  27.3 2.1 %collective-permute-start = (bf16[16,8,1152]{2,1,0:T(8,128)(2,1)S(1)}, bf16[16,8,1152]{2,1,0:T(8,128)(2,1)S(1)}, u32[]{:S(2)}, u32[]{:S(2)}) collective-permute-start(bf16[16,8,1152]{2,1,0:T(8,128)(2,1)S(1)} %all-to-all-done.own), channel_id=1, source_target_pairs={{0,8},{8,0},{16,24},{24,16},{32,40},{40,32},{48,56},{56,48},{64,72... | collective-permute-start | bytes 884744 | tf_op jit(solution)/shard_map/ppermute | solution.py:211
  29.4 0.1 collective-permute-start.1
  29.5 1.5 %collective-permute-done.1.low_other = bf16[1024,128]{1,0:T(8,128)(2,1)S(1)} collective-permute-done((bf16[1024,128]{1,0:T(8,128)(2,1)S(1)}, bf16[1024,128]{1,0:T(8,128)(2,1)S(1)}, u32[]{:S(2)}, u32[]{:S(2)}) %collective-permute-start.1) | collective-permute-done | bytes 262176 | tf_op jit(solution)/shard_map/ppermute | solution.py:211
  31.0 0.0 collective-permute-done.other
  31.0 1.6 %shard_map.65 = bf16[256,768]{1,0:T(8,128)(2,1)} custom-call(s32[4]{0:T(128)S(1)} %pad_add_fusion.s, bf16[16,8,1152]{2,1,0:T(8,128)(2,1)S(1)} %all-to-all-done.own, bf16[16,8,1152]{2,1,0:T(8,128)(2,1)S(1)} %collective-permute-done.other, bf16[2,1024,128]{2,1,0:T(8,128)(2,1)S(1)} %copy-done.2, bf16[1024,128]{1,0:T(8,128)(2,1)S(1)} %collective-permute-done.1.low_other), custom_call_target="tpu_custom_call" | custom-call | tf_op jit(solution)/shard_map/pallas_call | solution.py:52
  32.6 4.6 %all-to-all-start.1 = ((bf16[8,32,768]{2,1,0:T(8,128)(2,1)}), bf16[8,32,768]{2,1,0:T(8,128)(2,1)S(1)}, u32[]{:S(2)}, u32[]{:S(2)}) async-start(bf16[8,32,768]{2,1,0:T(8,128)(2,1)} %bitcast.5), calls=%async_computation.1 | async-start | bytes 786432 | tf_op jit(solution)/shard_map/all_to_all | solution.py:214
  37.3 1.0 dynamic-slice_bitcast_fusion.1
  38.3 0.6 collective-permute-start.3
  38.9 0.0 collective-permute-start.20
  38.9 5.3 %all-to-all-done.1.got = bf16[8,32,768]{2,1,0:T(8,128)(2,1)S(1)} async-done(((bf16[8,32,768]{2,1,0:T(8,128)(2,1)}), bf16[8,32,768]{2,1,0:T(8,128)(2,1)S(1)}, u32[]{:S(2)}, u32[]{:S(2)}) %all-to-all-start.1) | async-done | bytes 393248 | tf_op jit(solution)/shard_map/all_to_all | solution.py:214
  44.2 0.6 shard_map.66
  44.8 0.7 copy-done.1
  45.5 4.7 %all-to-all-start.2 = ((bf16[8,32,768]{2,1,0:T(8,128)(2,1)}), bf16[8,32,768]{2,1,0:T(8,128)(2,1)S(1)}, u32[]{:S(2)}, u32[]{:S(2)}) async-start(bf16[8,32,768]{2,1,0:T(8,128)(2,1)} %copy-done.1), calls=%async_computation.2 | async-start | bytes 786432 | tf_op jit(solution)/shard_map/all_to_all | solution.py:214
  50.2 0.0 collective-permute-done.2.w_other
  50.2 6.7 %all-to-all-done.2 = bf16[8,32,768]{2,1,0:T(8,128)(2,1)S(1)} async-done(((bf16[8,32,768]{2,1,0:T(8,128)(2,1)}), bf16[8,32,768]{2,1,0:T(8,128)(2,1)S(1)}, u32[]{:S(2)}, u32[]{:S(2)}) %all-to-all-start.2) | async-done | bytes 393248 | tf_op jit(solution)/shard_map/all_to_all | solution.py:214
  56.9 2.5 %shard_map.70 = (bf16[2,232,256]{2,1,0:T(8,128)(2,1)S(1)}, bf16[2,232,256]{2,1,0:T(8,128)(2,1)S(1)}) custom-call(s32[4]{0:T(128)S(1)} %pad_add_fusion.s, bf16[256,768]{1,0:T(8,128)(2,1)S(1)} %bitcast.22, bf16[2,3696,256]{2,1,0:T(8,128)(2,1)} %bitcast.26, bf16[3696,256]{1,0:T(8,128)(2,1)} %collective-permute-done.2.w_other, ...), custom_call_target="tpu_custom_call" | custom-call | tf_op jit(solution)/shard_map/pallas_call | solution.py:52
  59.4 0.1 collective-permute-start.5
  59.5 2.7 %collective-permute-start.6 = (bf16[2,232,256]{2,1,0:T(8,128)(2,1)S(1)}, bf16[2,232,256]{2,1,0:T(8,128)(2,1)S(1)}, u32[]{:S(2)}, u32[]{:S(2)}) collective-permute-start(bf16[2,232,256]{2,1,0:T(8,128)(2,1)S(1)} %get-tuple-element.28), channel_id=1, source_target_pairs={{0,192},{8,200},{16,208},{24,216},{32,224},{40,232},{48,240},{56,2... | collective-permute-start | bytes 712712 | tf_op jit(solution)/shard_map/ppermute | solution.py:211
  62.2 2.5 %shard_map.68 = (bf16[2,232,256]{2,1,0:T(8,128)(2,1)S(1)}, f32[2,232,256]{2,1,0:T(8,128)S(1)}) custom-call(s32[4]{0:T(128)S(1)} %pad_add_fusion.s, bf16[256,768]{1,0:T(8,128)(2,1)S(1)} %bitcast.23, bf16[2,3696,256]{2,1,0:T(8,128)(2,1)} %bitcast.27, bf16[3696,256]{1,0:T(8,128)(2,1)} %collective-permute-done.2.w_other, bf16[2,3696,128]{2,1,0:T(8,128)(2,1)S(1)} %bitcast.19, ...), custom_call_target="tpu_custom_call" | custom-call | tf_op jit(solution)/shard_map/pallas_call | solution.py:52
  64.7 0.1 collective-permute-start.4
  64.8 2.5 %shard_map.69 = (f32[2,232,256]{2,1,0:T(8,128)S(1)}, bf16[2,232,256]{2,1,0:T(8,128)(2,1)S(1)}) custom-call(s32[4]{0:T(128)S(1)} %pad_add_fusion.s, bf16[256,768]{1,0:T(8,128)(2,1)S(1)} %bitcast.24, bf16[2,3696,256]{2,1,0:T(8,128)(2,1)} %bitcast.28, bf16[3696,256]{1,0:T(8,128)(2,1)} %collective-permute-done.2.w_other, bf16[2,3696,128]{2,1,0:T(8,128)(2,1)S(1)} %bitcast.20, ...), custom_call_target="tpu_custom_call" | custom-call | tf_op jit(solution)/shard_map/pallas_call | solution.py:52
  67.3 1.5 %collective-permute-start.8 = (bf16[2,232,256]{2,1,0:T(8,128)(2,1)S(1)}, bf16[2,232,256]{2,1,0:T(8,128)(2,1)S(1)}, u32[]{:S(2)}, u32[]{:S(2)}) collective-permute-start(bf16[2,232,256]{2,1,0:T(8,128)(2,1)S(1)} %get-tuple-element.31), channel_id=1, source_target_pairs={{0,64},{8,72},{16,80},{24,88},{32,96},{40,104},{48,112},{56,120},{... | collective-permute-start | bytes 712712 | tf_op jit(solution)/shard_map/ppermute | solution.py:211
  68.8 0.6 shard_map.71
  69.4 0.1 collective-permute-start.7
  69.5 2.6 %collective-permute-start.9 = (bf16[2,232,256]{2,1,0:T(8,128)(2,1)S(1)}, bf16[2,232,256]{2,1,0:T(8,128)(2,1)S(1)}, u32[]{:S(2)}, u32[]{:S(2)}) collective-permute-start(bf16[2,232,256]{2,1,0:T(8,128)(2,1)S(1)} %get-tuple-element.32), channel_id=1, source_target_pairs={{0,192},{8,200},{16,208},{24,216},{32,224},{40,232},{48,240},{56,2... | collective-permute-start | bytes 712712 | tf_op jit(solution)/shard_map/ppermute | solution.py:211
  72.2 2.5 %shard_map.67 = (f32[2,232,256]{2,1,0:T(8,128)S(1)}, f32[2,232,256]{2,1,0:T(8,128)S(1)}) custom-call(s32[4]{0:T(128)S(1)} %pad_add_fusion.s, bf16[256,768]{1,0:T(8,128)(2,1)S(1)} %bitcast.25, bf16[2,3696,256]{2,1,0:T(8,128)(2,1)} %bitcast.29, bf16[3696,256]{1,0:T(8,128)(2,1)} %collective-permute-done.2.w_other, bf16[2,3696,128]{2,1,0:T(8,128)(2,1)S(1)} %bitcast.21, ...), custom_call_target="tpu_custom_call" | custom-call | tf_op jit(solution)/shard_map/pallas_call | solution.py:52
  74.7 3.0 %collective-permute-done.7.a2 = bf16[2,232,256]{2,1,0:T(8,128)(2,1)S(1)} collective-permute-done((bf16[2,232,256]{2,1,0:T(8,128)(2,1)S(1)}, bf16[2,232,256]{2,1,0:T(8,128)(2,1)S(1)}, u32[]{:S(2)}, u32[]{:S(2)}) %collective-permute-start.7) | collective-permute-done | bytes 237600 | tf_op jit(solution)/shard_map/ppermute | solution.py:211
  77.7 0.8 shard_map.72
  78.4 0.6 collective-permute-start.10
  79.0 1.7 %collective-permute-start.11 = (bf16[232,256]{1,0:T(8,128)(2,1)S(1)}, bf16[232,256]{1,0:T(8,128)(2,1)S(1)}, u32[]{:S(2)}, u32[]{:S(2)}) collective-permute-start(bf16[232,256]{1,0:T(8,128)(2,1)S(1)} %get-tuple-element.35), channel_id=1, source_target_pairs={{0,32},{8,40},{16,48},{24,56},{32,0},{40,8},{48,16},{56,24},{64,96... | collective-permute-start | bytes 356360 | tf_op jit(solution)/shard_map/ppermute | solution.py:211
  80.7 1.7 %collective-permute-start.12 = (bf16[232,256]{1,0:T(8,128)(2,1)S(1)}, bf16[232,256]{1,0:T(8,128)(2,1)S(1)}, u32[]{:S(2)}, u32[]{:S(2)}) collective-permute-start(bf16[232,256]{1,0:T(8,128)(2,1)S(1)} %get-tuple-element.36), channel_id=1, source_target_pairs={{0,48},{8,56},{16,0},{24,8},{32,16},{40,24},{48,32},{56,40},{64,11... | collective-permute-start | bytes 356360 | tf_op jit(solution)/shard_map/ppermute | solution.py:211
  82.4 3.2 %collective-permute-done.10.a1 = bf16[232,256]{1,0:T(8,128)(2,1)S(1)} collective-permute-done((bf16[232,256]{1,0:T(8,128)(2,1)S(1)}, bf16[232,256]{1,0:T(8,128)(2,1)S(1)}, u32[]{:S(2)}, u32[]{:S(2)}) %collective-permute-start.10) | collective-permute-done | bytes 118816 | tf_op jit(solution)/shard_map/ppermute | solution.py:211
  85.6 1.9 %collective-permute-done.11.a2 = bf16[232,256]{1,0:T(8,128)(2,1)S(1)} collective-permute-done((bf16[232,256]{1,0:T(8,128)(2,1)S(1)}, bf16[232,256]{1,0:T(8,128)(2,1)S(1)}, u32[]{:S(2)}, u32[]{:S(2)}) %collective-permute-start.11) | collective-permute-done | bytes 118816 | tf_op jit(solution)/shard_map/ppermute | solution.py:211
  87.5 2.3 %collective-permute-done.12.a3 = bf16[232,256]{1,0:T(8,128)(2,1)S(1)} collective-permute-done((bf16[232,256]{1,0:T(8,128)(2,1)S(1)}, bf16[232,256]{1,0:T(8,128)(2,1)S(1)}, u32[]{:S(2)}, u32[]{:S(2)}) %collective-permute-start.12) | collective-permute-done | bytes 118816 | tf_op jit(solution)/shard_map/ppermute | solution.py:211
  89.8 0.6 shard_map.73
  90.4 6.3 %collective-permute-start.13 = (f32[232,128]{1,0:T(8,128)S(1)}, f32[232,128]{1,0:T(8,128)S(1)}, u32[]{:S(2)}, u32[]{:S(2)}) collective-permute-start(f32[232,128]{1,0:T(8,128)S(1)} %get-tuple-element.38), channel_id=1, source_target_pairs={{0,8},{8,0},{16,24},{24,16},{32,40},{40,32},{48,56},{56,48},{64,72... | collective-permute-start | bytes 356360 | tf_op jit(solution)/shard_map/ppermute | solution.py:211
  96.6 1.0 collective-permute-done.13.got
  97.6 0.6 shard_map.74.h0
  98.2 1.8 %collective-permute-start.14 = (bf16[232,128]{1,0:T(8,128)(2,1)S(1)}, bf16[232,128]{1,0:T(8,128)(2,1)S(1)}, u32[]{:S(2)}, u32[]{:S(2)}) collective-permute-start(bf16[232,128]{1,0:T(8,128)(2,1)S(1)} %shard_map.74.h0), channel_id=1, source_target_pairs={{0,16},{8,24},{16,32},{24,40},{32,48},{40,56},{48,0},{56,8},{64,80... | collective-permute-start | bytes 178184 | tf_op jit(solution)/shard_map/ppermute | solution.py:211
  100.0 1.7 %collective-permute-start.15 = (bf16[232,128]{1,0:T(8,128)(2,1)S(1)}, bf16[232,128]{1,0:T(8,128)(2,1)S(1)}, u32[]{:S(2)}, u32[]{:S(2)}) collective-permute-start(bf16[232,128]{1,0:T(8,128)(2,1)S(1)} %shard_map.74.h0), channel_id=1, source_target_pairs={{0,32},{8,40},{16,48},{24,56},{32,0},{40,8},{48,16},{56,24},{64,96... | collective-permute-start | bytes 178184 | tf_op jit(solution)/shard_map/ppermute | solution.py:211
  101.7 1.9 %collective-permute-start.16 = (bf16[232,128]{1,0:T(8,128)(2,1)S(1)}, bf16[232,128]{1,0:T(8,128)(2,1)S(1)}, u32[]{:S(2)}, u32[]{:S(2)}) collective-permute-start(bf16[232,128]{1,0:T(8,128)(2,1)S(1)} %shard_map.74.h0), channel_id=1, source_target_pairs={{0,48},{8,56},{16,0},{24,8},{32,16},{40,24},{48,32},{56,40},{64,11... | collective-permute-start | bytes 178184 | tf_op jit(solution)/shard_map/ppermute | solution.py:211
  103.5 0.0 collective-permute-done.14.h1
  103.5 3.4 %collective-permute-done.15.h2 = bf16[232,128]{1,0:T(8,128)(2,1)S(1)} collective-permute-done((bf16[232,128]{1,0:T(8,128)(2,1)S(1)}, bf16[232,128]{1,0:T(8,128)(2,1)S(1)}, u32[]{:S(2)}, u32[]{:S(2)}) %collective-permute-start.15) | collective-permute-done | bytes 59424 | tf_op jit(solution)/shard_map/ppermute | solution.py:211
  106.9 0.6 shard_map.75.h0
  107.5 3.8 %collective-permute-start.17 = (bf16[4,232,128]{2,1,0:T(8,128)(2,1)S(1)}, bf16[4,232,128]{2,1,0:T(8,128)(2,1)S(1)}, u32[]{:S(2)}, u32[]{:S(2)}) collective-permute-start(bf16[4,232,128]{2,1,0:T(8,128)(2,1)S(1)} %shard_map.75.h0), channel_id=1, source_target_pairs={{0,64},{8,72},{16,80},{24,88},{32,96},{40,104},{48,112},{56,120},{... | collective-permute-start | bytes 712712 | tf_op jit(solution)/shard_map/ppermute | solution.py:211
  111.3 1.6 %collective-permute-start.18 = (bf16[4,232,128]{2,1,0:T(8,128)(2,1)S(1)}, bf16[4,232,128]{2,1,0:T(8,128)(2,1)S(1)}, u32[]{:S(2)}, u32[]{:S(2)}) collective-permute-start(bf16[4,232,128]{2,1,0:T(8,128)(2,1)S(1)} %shard_map.75.h0), channel_id=1, source_target_pairs={{0,128},{8,136},{16,144},{24,152},{32,160},{40,168},{48,176},{56,1... | collective-permute-start | bytes 712712 | tf_op jit(solution)/shard_map/ppermute | solution.py:211
  112.9 0.9 collective-permute-start.19
  113.8 2.2 %collective-permute-done.17.h1 = bf16[4,232,128]{2,1,0:T(8,128)(2,1)S(1)} collective-permute-done((bf16[4,232,128]{2,1,0:T(8,128)(2,1)S(1)}, bf16[4,232,128]{2,1,0:T(8,128)(2,1)S(1)}, u32[]{:S(2)}, u32[]{:S(2)}) %collective-permute-start.17) | collective-permute-done | bytes 237600 | tf_op jit(solution)/shard_map/ppermute | solution.py:211
  115.9 7.4 %collective-permute-done.18.h2 = bf16[4,232,128]{2,1,0:T(8,128)(2,1)S(1)} collective-permute-done((bf16[4,232,128]{2,1,0:T(8,128)(2,1)S(1)}, bf16[4,232,128]{2,1,0:T(8,128)(2,1)S(1)}, u32[]{:S(2)}, u32[]{:S(2)}) %collective-permute-start.18) | collective-permute-done | bytes 237600 | tf_op jit(solution)/shard_map/ppermute | solution.py:211
  123.3 3.5 %shard_map.76 = bf16[8,16,512]{2,1,0:T(8,128)(2,1)S(1)} custom-call(s32[4]{0:T(128)S(1)} %pad_add_fusion.s, bf16[4,232,128]{2,1,0:T(8,128)(2,1)S(1)} %shard_map.75.h0, bf16[4,232,128]{2,1,0:T(8,128)(2,1)S(1)} %collective-permute-done.17.h1, bf16[4,232,128]{2,1,0:T(8,128)(2,1)S(1)} %collective-permute-done.18.h2, ...), custom_call_target="tpu_custom_call" | custom-call | tf_op jit(solution)/shard_map/pallas_call | solution.py:52
  126.9 11.0 %all_to_all.20.got = bf16[8,16,512]{2,1,0:T(8,128)(2,1)S(1)} all-to-all(bf16[8,16,512]{2,1,0:T(8,128)(2,1)S(1)} %shard_map.76), channel_id=1, replica_groups=mesh['task'=32,'tensor'=8] {'tensor'}, dimensions={0} | all-to-all | bytes 262144 | tf_op jit(solution)/shard_map/all_to_all | solution.py:214
  137.9 0.6 shard_map.77
  138.5 3.1 %collective-permute-start.21 = (f32[16,256]{1,0:T(8,128)S(1)}, f32[16,256]{1,0:T(8,128)S(1)}, u32[]{:S(2)}, u32[]{:S(2)}) collective-permute-start(f32[16,256]{1,0:T(8,128)S(1)} %get-tuple-element.40), channel_id=1, source_target_pairs={{0,8},{8,0},{16,24},{24,16},{32,40},{40,32},{48,56},{56,48},{64,72... | collective-permute-start | bytes 49160 | tf_op jit(solution)/shard_map/ppermute | solution.py:211
  141.6 0.8 collective-permute-done.21.got
  142.5 1.2 shard_map.78
  (16 shorter events, 0.1 us)
Async XLA Ops:
  0.1 0.7 copy-start.3
  0.8 0.7 copy-start.4
  2.9 24.4 %all-to-all-start = ((bf16[16,8,1152]{2,1,0:T(8,128)(2,1)}), bf16[16,8,1152]{2,1,0:T(8,128)(2,1)S(1)}, u32[]{:S(2)}, u32[]{:S(2)}) async-start(bf16[16,8,1152]{2,1,0:T(8,128)(2,1)} %shard_map.64), calls=%async_computation | async-start | bytes 589824 | tf_op jit(solution)/shard_map/all_to_all | solution.py:235
  14.5 14.9 %copy-start.2 = (bf16[2,1024,128]{2,1,0:T(8,128)(2,1)S(1)}, bf16[2,1024,128]{2,1,0:T(8,128)(2,1)}, u32[]{:S(2)}) copy-start(bf16[2,1024,128]{2,1,0:T(8,128)(2,1)} %low_own.1) | copy-start | bytes 1572868
  17.4 19.8 %copy-start = (bf16[2,128,3696]{1,2,0:T(8,128)(2,1)S(1)}, bf16[2,128,3696]{1,2,0:T(8,128)(2,1)}, u32[]{:S(2)}) copy-start(bf16[2,128,3696]{1,2,0:T(8,128)(2,1)} %param.11) | copy-start | bytes 5677060
  17.4 32.8 %collective-permute-start.2 = (bf16[3696,256]{1,0:T(8,128)(2,1)}, bf16[3696,256]{1,0:T(8,128)(2,1)}, u32[]{:S(2)}, u32[]{:S(2)}) collective-permute-start(bf16[3696,256]{1,0:T(8,128)(2,1)} %dynamic-slice_bitcast_fusion), channel_id=1, source_target_pairs={{0,8},{8,0},{16,24},{24,16},{32,40},{40,32},{48,56},{56,48},{64,72... | collective-permute-start | bytes 5677064 | tf_op jit(solution)/shard_map/ppermute | solution.py:211
  27.3 3.7 %collective-permute-start = (bf16[16,8,1152]{2,1,0:T(8,128)(2,1)S(1)}, bf16[16,8,1152]{2,1,0:T(8,128)(2,1)S(1)}, u32[]{:S(2)}, u32[]{:S(2)}) collective-permute-start(bf16[16,8,1152]{2,1,0:T(8,128)(2,1)S(1)} %all-to-all-done.own), channel_id=1, source_target_pairs={{0,8},{8,0},{16,24},{24,16},{32,40},{40,32},{48,56},{56,48},{64,72... | collective-permute-start | bytes 884744 | tf_op jit(solution)/shard_map/ppermute | solution.py:211
  29.4 1.6 %collective-permute-start.1 = (bf16[1024,128]{1,0:T(8,128)(2,1)S(1)}, bf16[1024,128]{1,0:T(8,128)(2,1)S(1)}, u32[]{:S(2)}, u32[]{:S(2)}) collective-permute-start(bf16[1024,128]{1,0:T(8,128)(2,1)S(1)} %dynamic-slice_bitcast_fusion.2), channel_id=1, source_target_pairs={{0,8},{8,0},{16,24},{24,16},{32,40},{40,32},{48,56},{56,48},{64,72... | collective-permute-start | bytes 786440 | tf_op jit(solution)/shard_map/ppermute | solution.py:211
  32.6 11.6 %all-to-all-start.1 = ((bf16[8,32,768]{2,1,0:T(8,128)(2,1)}), bf16[8,32,768]{2,1,0:T(8,128)(2,1)S(1)}, u32[]{:S(2)}, u32[]{:S(2)}) async-start(bf16[8,32,768]{2,1,0:T(8,128)(2,1)} %bitcast.5), calls=%async_computation.1 | async-start | bytes 786432 | tf_op jit(solution)/shard_map/all_to_all | solution.py:214
  38.3 11.9 %collective-permute-start.3 = (bf16[3696,128]{1,0:T(8,128)(2,1)}, bf16[3696,128]{1,0:T(8,128)(2,1)S(1)}, u32[]{:S(2)}, u32[]{:S(2)}) collective-permute-start(bf16[3696,128]{1,0:T(8,128)(2,1)} %dynamic-slice_bitcast_fusion.1), channel_id=1, source_target_pairs={{0,8},{8,0},{16,24},{24,16},{32,40},{40,32},{48,56},{56,48},{64,72... | collective-permute-start | bytes 2838536 | tf_op jit(solution)/shard_map/ppermute | solution.py:211
  38.9 74.9 %collective-permute-start.20 = (bf16[3696,256]{1,0:T(8,128)(2,1)}, bf16[3696,256]{1,0:T(8,128)(2,1)}, u32[]{:S(2)}, u32[]{:S(2)}) collective-permute-start(bf16[3696,256]{1,0:T(8,128)(2,1)} %w_own.1), channel_id=1, source_target_pairs={{0,8},{8,0},{16,24},{24,16},{32,40},{40,32},{48,56},{56,48},{64,72... | collective-permute-start | bytes 5677064 | tf_op jit(solution)/shard_map/ppermute | solution.py:211
  44.8 0.8 copy-start.1
  45.5 11.4 %all-to-all-start.2 = ((bf16[8,32,768]{2,1,0:T(8,128)(2,1)}), bf16[8,32,768]{2,1,0:T(8,128)(2,1)S(1)}, u32[]{:S(2)}, u32[]{:S(2)}) async-start(bf16[8,32,768]{2,1,0:T(8,128)(2,1)} %copy-done.1), calls=%async_computation.2 | async-start | bytes 786432 | tf_op jit(solution)/shard_map/all_to_all | solution.py:214
  59.4 9.4 %collective-permute-start.5 = (bf16[2,232,256]{2,1,0:T(8,128)(2,1)S(1)}, bf16[2,232,256]{2,1,0:T(8,128)(2,1)S(1)}, u32[]{:S(2)}, u32[]{:S(2)}) collective-permute-start(bf16[2,232,256]{2,1,0:T(8,128)(2,1)S(1)} %get-tuple-element.26), channel_id=1, source_target_pairs={{0,64},{8,72},{16,80},{24,88},{32,96},{40,104},{48,112},{56,120},{... | collective-permute-start | bytes 712712 | tf_op jit(solution)/shard_map/ppermute | solution.py:211
  59.5 9.3 %collective-permute-start.6 = (bf16[2,232,256]{2,1,0:T(8,128)(2,1)S(1)}, bf16[2,232,256]{2,1,0:T(8,128)(2,1)S(1)}, u32[]{:S(2)}, u32[]{:S(2)}) collective-permute-start(bf16[2,232,256]{2,1,0:T(8,128)(2,1)S(1)} %get-tuple-element.28), channel_id=1, source_target_pairs={{0,192},{8,200},{16,208},{24,216},{32,224},{40,232},{48,240},{56,2... | collective-permute-start | bytes 712712 | tf_op jit(solution)/shard_map/ppermute | solution.py:211
  64.7 10.0 %collective-permute-start.4 = (bf16[2,232,256]{2,1,0:T(8,128)(2,1)S(1)}, bf16[2,232,256]{2,1,0:T(8,128)(2,1)S(1)}, u32[]{:S(2)}, u32[]{:S(2)}) collective-permute-start(bf16[2,232,256]{2,1,0:T(8,128)(2,1)S(1)} %get-tuple-element.24), channel_id=1, source_target_pairs={{0,192},{8,200},{16,208},{24,216},{32,224},{40,232},{48,240},{56,2... | collective-permute-start | bytes 712712 | tf_op jit(solution)/shard_map/ppermute | solution.py:211
  67.3 7.4 %collective-permute-start.8 = (bf16[2,232,256]{2,1,0:T(8,128)(2,1)S(1)}, bf16[2,232,256]{2,1,0:T(8,128)(2,1)S(1)}, u32[]{:S(2)}, u32[]{:S(2)}) collective-permute-start(bf16[2,232,256]{2,1,0:T(8,128)(2,1)S(1)} %get-tuple-element.31), channel_id=1, source_target_pairs={{0,64},{8,72},{16,80},{24,88},{32,96},{40,104},{48,112},{56,120},{... | collective-permute-start | bytes 712712 | tf_op jit(solution)/shard_map/ppermute | solution.py:211
  69.4 8.2 %collective-permute-start.7 = (bf16[2,232,256]{2,1,0:T(8,128)(2,1)S(1)}, bf16[2,232,256]{2,1,0:T(8,128)(2,1)S(1)}, u32[]{:S(2)}, u32[]{:S(2)}) collective-permute-start(bf16[2,232,256]{2,1,0:T(8,128)(2,1)S(1)} %get-tuple-element.29), channel_id=1, source_target_pairs={{0,64},{8,72},{16,80},{24,88},{32,96},{40,104},{48,112},{56,120},{... | collective-permute-start | bytes 712712 | tf_op jit(solution)/shard_map/ppermute | solution.py:211
  69.5 8.1 %collective-permute-start.9 = (bf16[2,232,256]{2,1,0:T(8,128)(2,1)S(1)}, bf16[2,232,256]{2,1,0:T(8,128)(2,1)S(1)}, u32[]{:S(2)}, u32[]{:S(2)}) collective-permute-start(bf16[2,232,256]{2,1,0:T(8,128)(2,1)S(1)} %get-tuple-element.32), channel_id=1, source_target_pairs={{0,192},{8,200},{16,208},{24,216},{32,224},{40,232},{48,240},{56,2... | collective-permute-start | bytes 712712 | tf_op jit(solution)/shard_map/ppermute | solution.py:211
  78.4 7.2 %collective-permute-start.10 = (bf16[232,256]{1,0:T(8,128)(2,1)S(1)}, bf16[232,256]{1,0:T(8,128)(2,1)S(1)}, u32[]{:S(2)}, u32[]{:S(2)}) collective-permute-start(bf16[232,256]{1,0:T(8,128)(2,1)S(1)} %get-tuple-element.34), channel_id=1, source_target_pairs={{0,16},{8,24},{16,32},{24,40},{32,48},{40,56},{48,0},{56,8},{64,80... | collective-permute-start | bytes 356360 | tf_op jit(solution)/shard_map/ppermute | solution.py:211
  79.0 8.4 %collective-permute-start.11 = (bf16[232,256]{1,0:T(8,128)(2,1)S(1)}, bf16[232,256]{1,0:T(8,128)(2,1)S(1)}, u32[]{:S(2)}, u32[]{:S(2)}) collective-permute-start(bf16[232,256]{1,0:T(8,128)(2,1)S(1)} %get-tuple-element.35), channel_id=1, source_target_pairs={{0,32},{8,40},{16,48},{24,56},{32,0},{40,8},{48,16},{56,24},{64,96... | collective-permute-start | bytes 356360 | tf_op jit(solution)/shard_map/ppermute | solution.py:211
  80.7 9.0 %collective-permute-start.12 = (bf16[232,256]{1,0:T(8,128)(2,1)S(1)}, bf16[232,256]{1,0:T(8,128)(2,1)S(1)}, u32[]{:S(2)}, u32[]{:S(2)}) collective-permute-start(bf16[232,256]{1,0:T(8,128)(2,1)S(1)} %get-tuple-element.36), channel_id=1, source_target_pairs={{0,48},{8,56},{16,0},{24,8},{32,16},{40,24},{48,32},{56,40},{64,11... | collective-permute-start | bytes 356360 | tf_op jit(solution)/shard_map/ppermute | solution.py:211
  90.4 7.2 %collective-permute-start.13 = (f32[232,128]{1,0:T(8,128)S(1)}, f32[232,128]{1,0:T(8,128)S(1)}, u32[]{:S(2)}, u32[]{:S(2)}) collective-permute-start(f32[232,128]{1,0:T(8,128)S(1)} %get-tuple-element.38), channel_id=1, source_target_pairs={{0,8},{8,0},{16,24},{24,16},{32,40},{40,32},{48,56},{56,48},{64,72... | collective-permute-start | bytes 356360 | tf_op jit(solution)/shard_map/ppermute | solution.py:211
  98.2 5.3 %collective-permute-start.14 = (bf16[232,128]{1,0:T(8,128)(2,1)S(1)}, bf16[232,128]{1,0:T(8,128)(2,1)S(1)}, u32[]{:S(2)}, u32[]{:S(2)}) collective-permute-start(bf16[232,128]{1,0:T(8,128)(2,1)S(1)} %shard_map.74.h0), channel_id=1, source_target_pairs={{0,16},{8,24},{16,32},{24,40},{32,48},{40,56},{48,0},{56,8},{64,80... | collective-permute-start | bytes 178184 | tf_op jit(solution)/shard_map/ppermute | solution.py:211
  100.0 7.0 %collective-permute-start.15 = (bf16[232,128]{1,0:T(8,128)(2,1)S(1)}, bf16[232,128]{1,0:T(8,128)(2,1)S(1)}, u32[]{:S(2)}, u32[]{:S(2)}) collective-permute-start(bf16[232,128]{1,0:T(8,128)(2,1)S(1)} %shard_map.74.h0), channel_id=1, source_target_pairs={{0,32},{8,40},{16,48},{24,56},{32,0},{40,8},{48,16},{56,24},{64,96... | collective-permute-start | bytes 178184 | tf_op jit(solution)/shard_map/ppermute | solution.py:211
  101.7 5.3 %collective-permute-start.16 = (bf16[232,128]{1,0:T(8,128)(2,1)S(1)}, bf16[232,128]{1,0:T(8,128)(2,1)S(1)}, u32[]{:S(2)}, u32[]{:S(2)}) collective-permute-start(bf16[232,128]{1,0:T(8,128)(2,1)S(1)} %shard_map.74.h0), channel_id=1, source_target_pairs={{0,48},{8,56},{16,0},{24,8},{32,16},{40,24},{48,32},{56,40},{64,11... | collective-permute-start | bytes 178184 | tf_op jit(solution)/shard_map/ppermute | solution.py:211
  107.5 8.4 %collective-permute-start.17 = (bf16[4,232,128]{2,1,0:T(8,128)(2,1)S(1)}, bf16[4,232,128]{2,1,0:T(8,128)(2,1)S(1)}, u32[]{:S(2)}, u32[]{:S(2)}) collective-permute-start(bf16[4,232,128]{2,1,0:T(8,128)(2,1)S(1)} %shard_map.75.h0), channel_id=1, source_target_pairs={{0,64},{8,72},{16,80},{24,88},{32,96},{40,104},{48,112},{56,120},{... | collective-permute-start | bytes 712712 | tf_op jit(solution)/shard_map/ppermute | solution.py:211
  111.3 12.1 %collective-permute-start.18 = (bf16[4,232,128]{2,1,0:T(8,128)(2,1)S(1)}, bf16[4,232,128]{2,1,0:T(8,128)(2,1)S(1)}, u32[]{:S(2)}, u32[]{:S(2)}) collective-permute-start(bf16[4,232,128]{2,1,0:T(8,128)(2,1)S(1)} %shard_map.75.h0), channel_id=1, source_target_pairs={{0,128},{8,136},{16,144},{24,152},{32,160},{40,168},{48,176},{56,1... | collective-permute-start | bytes 712712 | tf_op jit(solution)/shard_map/ppermute | solution.py:211
  112.9 10.5 %collective-permute-start.19 = (bf16[4,232,128]{2,1,0:T(8,128)(2,1)S(1)}, bf16[4,232,128]{2,1,0:T(8,128)(2,1)S(1)}, u32[]{:S(2)}, u32[]{:S(2)}) collective-permute-start(bf16[4,232,128]{2,1,0:T(8,128)(2,1)S(1)} %shard_map.75.h0), channel_id=1, source_target_pairs={{0,192},{8,200},{16,208},{24,216},{32,224},{40,232},{48,240},{56,2... | collective-permute-start | bytes 712712 | tf_op jit(solution)/shard_map/ppermute | solution.py:211
  138.5 4.0 %collective-permute-start.21 = (f32[16,256]{1,0:T(8,128)S(1)}, f32[16,256]{1,0:T(8,128)S(1)}, u32[]{:S(2)}, u32[]{:S(2)}) collective-permute-start(f32[16,256]{1,0:T(8,128)S(1)} %get-tuple-element.40), channel_id=1, source_target_pairs={{0,8},{8,0},{16,24},{24,16},{32,40},{40,32},{48,56},{56,48},{64,72... | collective-permute-start | bytes 49160 | tf_op jit(solution)/shard_map/ppermute | solution.py:211

commit v4 on v3

--- a/solution.py
+++ b/solution.py
@@ -13,6 +13,7 @@
 NX, NZ, NC = 4, 4, 2
 NQ = NX * NZ
 VMEM_BYTES = 48 * 1024 * 1024
+INSIDE_BYTES = 24 * 1024 * 1024
 
 
 def task_of(x, z, c):
@@ -63,22 +64,23 @@
     )(scalars, *args)
 
 
+def call_inside(kernel, out_shape, *args, scalars, hbm=0, scratch=()):
+    inside = pl.BlockSpec(memory_space=pltpu.VMEM)
+    specs = [pl.BlockSpec(memory_space=pltpu.HBM)] * hbm + [inside] * (len(args) - hbm)
+    many = isinstance(out_shape, (list, tuple))
+    return pl.pallas_call(
+        kernel,
+        out_shape=out_shape,
+        in_specs=[pl.BlockSpec(memory_space=pltpu.SMEM)] + specs,
+        out_specs=[inside] * len(out_shape) if many else inside,
+        scratch_shapes=list(scratch),
+        compiler_params=pltpu.CompilerParams(vmem_limit_bytes=INSIDE_BYTES),
+    )(scalars, *args)
+
+
 def rows_of(v):
     v = v.astype(F32)
     return v.reshape(v.shape[0] * v.shape[1], v.shape[2])
-
-
-def pack_kernel(s, tokens, router, out):
-    high = router[...].astype(BF16)
-    low = (router[...] - high.astype(F32)).astype(BF16)
-    lane = lax.broadcasted_iota(jnp.int32, (TASKS, 128), 1)
-    row = lax.broadcasted_iota(jnp.int32, (TASKS, 128), 0)
-    tail = jnp.dot(high, (lane == row).astype(BF16), preferred_element_type=F32)
-    tail += jnp.dot(low, (lane == row + TASKS).astype(BF16), preferred_element_type=F32)
-    width = tokens.shape[1]
-    for i in range(out.shape[0]):
-        out[i, :, :width] = tokens[...]
-        out[i, :, width:] = tail.astype(BF16)
 
 
 def latent_kernel(width, s, own, other, low_own, low_other, out):
@@ -115,24 +117,31 @@
         out[j, :, 2 * half :] = total.astype(BF16)
 
 
-def main_kernel(d, limit, s, rows, w_own, w_other, u_own, u_other, out_a, out_b):
+def pick(i, values):
+    v = values[0]
+    for k in range(1, len(values)):
+        v = jnp.where(i == k, values[k], v)
+    return v
+
+
+def main_kernel(limit, halves, s, rows, w_own, w_other, u_own, u_other, *outs):
+    i = pl.program_id(0)
     w = jnp.concatenate([w_own[0], w_other[...], u_own[0], u_other[...]], axis=1)
     p = lax.dot_general(w, rows[...], (((1,), (1,)), ((), ())), preferred_element_type=F32)
-    i = pl.program_id(0)
-    start = (lax.rem(s[0] + d, NX) * 2 + i) * p.shape[0]
-    at = start + lax.broadcasted_iota(jnp.int32, p.shape, 0)
+    n = p.shape[0]
+    at = half_block(halves, i, s) * n + lax.broadcasted_iota(jnp.int32, p.shape, 0)
     p = jnp.where(at < limit, p, 0.0)
-    m = out_a.shape[1]
-
-    @pl.when(i == 0)
-    def _():
-        out_a[0] = p[:m].astype(out_a.dtype)
-        out_a[1] = p[m:].astype(out_a.dtype)
-
-    @pl.when(i == 1)
-    def _():
-        out_b[0] = p[:m].astype(out_b.dtype)
-        out_b[1] = p[m:].astype(out_b.dtype)
+    for k, out in enumerate(outs):
+
+        @pl.when(i == k)
+        def _():
+            out[0] = p[: n // 2].astype(out.dtype)
+            out[1] = p[n // 2 :].astype(out.dtype)
+
+
+def half_block(halves, i, s):
+    d = pick(i, [d for d, _ in halves])
+    return lax.rem(s[0] + d, NX) * 2 + pick(i, [h for _, h in halves])
 
 
 def pass_kernel(s, a, got_a, b, got_b, out_a, out_b):
@@ -167,17 +176,38 @@
         out[lax.rem(s[1] - d + NZ, NZ)] = h[...]
 
 
-def down_kernel(s, h0, h1, h2, h3, w_own, w_other, out, held):
-    n, m = h0.shape[:2]
-    for d, h in enumerate((h0, h1, h2, h3)):
-        start = lax.rem(s[0] - d + NX, NX) * (n * m)
-        for k in range(n):
-            held[pl.ds(pl.multiple_of(start + k * m, 8), m)] = h[k].astype(F32)
-    h = held[...].T.astype(BF16)
-    deep, cols = w_own.shape
-    for i, w in enumerate((w_own, w_other)):
-        p = jnp.dot(h[:, :deep], w[...], preferred_element_type=F32).astype(BF16)
-        out[:, :, i * cols : (i + 1) * cols] = p.reshape(out.shape[0], out.shape[1], cols)
+def down_rows(d, s, h, held, deep_all):
+    n, m = h.shape[:2]
+    deep = n * m
+    held[:16] = jnp.zeros((16, held.shape[1]), F32)
+    for k in range(n):
+        held[16 + k * m : 16 + (k + 1) * m] = h[k].astype(F32)
+    at = lax.rem(s[0] - d + NX, NX)
+    shift = jnp.where(at == NX - 1, NX * deep - deep_all, 0)
+    t = held[pl.ds(pl.multiple_of(16 - shift, 8), deep)].T.astype(BF16)
+    return t, pl.ds(pl.multiple_of(at * deep - shift, 16), deep)
+
+
+def down_own_kernel(s, w_own, w_other, h, w, out, held, sems):
+    cols = w_own.shape[1]
+    copies = [
+        pltpu.make_async_copy(ref, w.at[:, pl.ds(i * cols, cols)], sems.at[i])
+        for i, ref in enumerate((w_own, w_other))
+    ]
+    for copy in copies:
+        copy.start()
+    t, at = down_rows(0, s, h, held, w.shape[0])
+    for copy in copies:
+        copy.wait()
+    out[...] = jnp.dot(t, w[at], preferred_element_type=F32)
+
+
+def down_kernel(s, acc, h1, h2, h3, w, out, held):
+    p = acc[...]
+    for d, h in enumerate((h1, h2, h3), 1):
+        t, at = down_rows(d, s, h, held.at[d - 1], w.shape[0])
+        p += jnp.dot(t, w[at], preferred_element_type=F32)
+    out[...] = p.astype(BF16).reshape(out.shape)
 
 
 def tensor_sum_kernel(s, got, keep, send):
@@ -231,7 +261,12 @@
     u_other = permute(other(upper), CORE)
     down_other = permute(down_weight, CORE)
 
-    packed = run(pack_kernel, sds((NQ, rows, width + 128)), tokens, router)
+    high = lax.reduce_precision(router, 8, 7)
+    fill = jnp.zeros((rows, 128 - 2 * TASKS), BF16)
+    packed = jnp.concatenate(
+        [tokens, high.astype(BF16), (router - high).astype(BF16), fill], axis=1
+    )
+    packed = jnp.broadcast_to(packed[None], (NQ,) + packed.shape)
     own_rows = lax.all_to_all(packed, "task", 0, 0, axis_index_groups=CHIPS)
     other_rows = permute(own_rows, CORE)
     lat = run(
@@ -252,41 +287,38 @@
     mid = run(functools.partial(mid_kernel, ranks), sds(got.shape), got)
     cat = across(mid).reshape(count, feats + ranks)
 
-    block = 2 * zb
-
-    def main(d, dtype_a, dtype_b):
-        def at(i, s):
-            return lax.rem(s[0] + d, NX) * 2 + i
-
+    inside = functools.partial(call_inside, scalars=s)
+    def main(halves, dtype):
         def own_spec(a):
-            return pl.BlockSpec((1, block, a.shape[2]), lambda i, s: (s[2], at(i, s), 0))
+            return pl.BlockSpec(
+                (1, xb // 2, a.shape[2]), lambda i, s: (s[2], half_block(halves, i, s), 0)
+            )
 
         def spec(a):
-            return pl.BlockSpec((block, a.shape[1]), lambda i, s: (at(i, s), 0))
+            return pl.BlockSpec((xb // 2, a.shape[1]), lambda i, s: (half_block(halves, i, s), 0))
 
         return run(
-            functools.partial(main_kernel, d, hid),
-            [sds((2, zb, count), dtype_a), sds((2, zb, count), dtype_b)],
+            functools.partial(main_kernel, hid, halves),
+            [sds((2, zb, count), dtype)] * len(halves),
             cat,
             weight,
             w_other,
             upper,
             u_other,
-            grid=(2,),
+            grid=(len(halves),),
             in_specs=[whole(cat), own_spec(weight), spec(w_other), own_spec(upper), spec(u_other)],
         )
 
-    far_a, far_b = main(2, BF16, BF16)
+    far_a, far_b = main(((2, 0), (2, 1)), BF16)
     far_a = permute(far_a, TO_X[1])
     far_b = permute(far_b, TO_X[3])
-    up_a, up_b = main(1, F32, BF16)
-    down_a, down_b = main(3, BF16, F32)
+    up_b, down_a = main(((1, 1), (3, 0)), BF16)
     up_b = permute(up_b, TO_X[1])
     down_a = permute(down_a, TO_X[3])
+    up_a, down_b, own_a, own_b = main(((1, 0), (3, 1), (0, 0), (0, 1)), F32)
     up_a, down_b = run(pass_kernel, [sds(far_a.shape)] * 2, up_a, far_a, down_b, far_b)
     up_a = permute(up_a, TO_X[1])
     down_b = permute(down_b, TO_X[3])
-    own_a, own_b = main(0, F32, F32)
     parts = run(
         x_sum_kernel,
         [sds((zb, count), F32)] + [sds((zb, count))] * 3,
@@ -309,16 +341,25 @@
     got = {d: permute(hidden, TO_X[d]) for d in FAR_FIRST}
     cols = down_weight.shape[1]
     out_rows = count // 2 // tensor
-    mixed = run(
+    half = count // 2
+    down, mixed = inside(
+        down_own_kernel,
+        [sds((hid, 2 * cols)), sds((half, 2 * cols), F32)],
+        down_weight,
+        down_other,
+        hidden,
+        hbm=2,
+        scratch=[pltpu.VMEM((xb + 16, half), F32), pltpu.SemaphoreType.DMA((2,))],
+    )
+    mixed = inside(
         down_kernel,
         sds((tensor, out_rows, 2 * cols)),
-        hidden,
+        mixed,
         got[1],
         got[2],
         got[3],
-        down_weight,
-        down_other,
-        scratch=[pltpu.VMEM((NX * xb, count // 2), F32)],
+        down,
+        scratch=[pltpu.VMEM((3, xb + 16, half), F32)],
     )
     keep, send = run(tensor_sum_kernel, [sds((out_rows, cols), F32)] * 2, across(mixed))
     return run(place_kernel, sds((2 * out_rows, cols), F32), keep, permute(send, CORE))

time: 144 us -> 140 us (0.972)
  starting transfers between devices: 56.7 us -> 51.9 us
  waiting for transfers between devices: 47.5 us -> 51.7 us
  blocking collectives: 11 us -> 7.82 us
    pallas_call x15 -> x12, Pallas kernels: 21.9 us -> 16.4 us  [call(): pl.pallas_call(kernel, out_shape=out_shape, grid_spec=pltpu.PrefetchScala...]
    ppermute x22, starting transfers between devices: 35.8 us -> 31 us  [permute(): return lax.ppermute(a, 'task', perm)]
    pallas_call x0 -> x2, Pallas kernels: none -> 4.29 us  [call_inside(): pl.pallas_call(kernel, out_shape=out_shape, in_specs=[pl.BlockSpec(memory...]
    ppermute x22, waiting for transfers between devices: 26.6 us -> 30.8 us  [permute(): return lax.ppermute(a, 'task', perm)]
    all_to_all x1, blocking collectives: 11 us -> 7.82 us  [across(): return lax.all_to_all(a, 'tensor', 0, 0)]
  transfers between devices with their start and end apart: 25 -> 25, of which waited for: 13 -> 16; matrix products, arithmetic and copies ran while one was open for 3% -> 3% of each run, Pallas kernels for 11% -> 13%
where the time goes in v4:
time: 140 us; the launch traced here: 139 us
  starting transfers between devices  51.9 us (37%)
  waiting for transfers between devices  51.7 us (37%)
  Pallas kernels  20.6 us (15%)
  blocking collectives  7.82 us (6%)
  local copies, waits for them, and re-layouts  6.32 us (5%)
    ppermute x22, starting transfers between devices, permute(): return lax.ppermute(a, 'task', perm)  31 us
    ppermute x22, waiting for transfers between devices, permute(): return lax.ppermute(a, 'task', perm)  30.8 us
    pallas_call x12, Pallas kernels, call(): pl.pallas_call(kernel, out_shape=out_shape, grid_spec=pltpu.PrefetchScala...  16.4 us
    all_to_all x2, waiting for transfers between devices, across(): return lax.all_to_all(a, 'tensor', 0, 0)  12 us
    all_to_all x1, starting transfers between devices, on_device(): own_rows = lax.all_to_all(packed, 'task', 0, 0, axis_index_groups=CHIPS)  11.6 us
    all_to_all x2, starting transfers between devices, across(): return lax.all_to_all(a, 'tensor', 0, 0)  9.3 us
    all_to_all x1, waiting for transfers between devices, on_device(): own_rows = lax.all_to_all(packed, 'task', 0, 0, axis_index_groups=CHIPS)  8.9 us
    all_to_all x1, blocking collectives, across(): return lax.all_to_all(a, 'tensor', 0, 0)  7.82 us
  transfers between devices with their start and end apart: 25, of which 16 were waited for; matrix products, arithmetic and copies ran while one was open for 3% of the time, Pallas kernels for 13%

profile of v4, /device:TPU:1, one launch (start us, length us, event | category | flops | bytes accessed | tf_op | source)
XLA Modules:
  0.0 139.3 jit_solution(9619689026899673845)
XLA Ops:
  0.0 0.7 fusion
  0.7 0.8 concatenate.3
  1.5 0.7 broadcast_in_dim.10
  2.2 11.6 %all-to-all-start = ((bf16[16,8,1152]{2,1,0:T(8,128)(2,1)}), bf16[16,8,1152]{2,1,0:T(8,128)(2,1)S(1)}, u32[]{:S(2)}, u32[]{:S(2)}) async-start(bf16[16,8,1152]{2,1,0:T(8,128)(2,1)} %broadcast_in_dim.10), calls=%async_computation | async-start | bytes 589824 | tf_op jit(solution)/shard_map/all_to_all | solution.py:270
  13.8 0.0 copy-start.2
  13.8 3.0 %dynamic-slice_bitcast_fusion = bf16[3696,256]{1,0:T(8,128)(2,1)} fusion(bf16[2,256,3696]{1,2,0:T(8,128)(2,1)} %param.8, s32[]{:T(128)S(6)} %select_n.18), kind=kLoop, calls=%fused_computation | loop fusion | bytes 3784708 | tf_op jit(solution)/shard_map/jit(dynamic_index_in_dim)/squeeze | solution.py:247
  16.8 1.0 collective-permute-start.3
  17.8 8.9 %all-to-all-done.own = bf16[16,8,1152]{2,1,0:T(8,128)(2,1)S(1)} async-done(((bf16[16,8,1152]{2,1,0:T(8,128)(2,1)}), bf16[16,8,1152]{2,1,0:T(8,128)(2,1)S(1)}, u32[]{:S(2)}, u32[]{:S(2)}) %all-to-all-start) | async-done | bytes 294944 | tf_op jit(solution)/shard_map/all_to_all | solution.py:270
  26.7 2.1 %collective-permute-start.1 = (bf16[16,8,1152]{2,1,0:T(8,128)(2,1)S(1)}, bf16[16,8,1152]{2,1,0:T(8,128)(2,1)S(1)}, u32[]{:S(2)}, u32[]{:S(2)}) collective-permute-start(bf16[16,8,1152]{2,1,0:T(8,128)(2,1)S(1)} %all-to-all-done.own), channel_id=1, source_target_pairs={{0,8},{8,0},{16,24},{24,16},{32,40},{40,32},{48,56},{56,48},{64,72... | collective-permute-start | bytes 884744 | tf_op jit(solution)/shard_map/ppermute | solution.py:241
  28.8 0.1 collective-permute-start.2
  28.9 0.1 pad_add_fusion.s
  29.0 1.4 %collective-permute-done.2.low_other = bf16[1024,128]{1,0:T(8,128)(2,1)S(1)} collective-permute-done((bf16[1024,128]{1,0:T(8,128)(2,1)S(1)}, bf16[1024,128]{1,0:T(8,128)(2,1)S(1)}, u32[]{:S(2)}, u32[]{:S(2)}) %collective-permute-start.2) | collective-permute-done | bytes 262176 | tf_op jit(solution)/shard_map/ppermute | solution.py:241
  30.4 0.0 collective-permute-done.1.other
  30.4 1.6 %shard_map.64 = bf16[256,768]{1,0:T(8,128)(2,1)} custom-call(s32[4]{0:T(128)S(1)} %pad_add_fusion.s, bf16[16,8,1152]{2,1,0:T(8,128)(2,1)S(1)} %all-to-all-done.own, bf16[16,8,1152]{2,1,0:T(8,128)(2,1)S(1)} %collective-permute-done.1.other, bf16[2,1024,128]{2,1,0:T(8,128)(2,1)S(1)} %copy-done.2, bf16[1024,128]{1,0:T(8,128)(2,1)S(1)} %collective-permute-done.2.low_other), custom_call_target="tpu_custom_call" | custom-call | tf_op jit(solution)/shard_map/pallas_call | solution.py:53
  32.0 4.6 %all-to-all-start.1 = ((bf16[8,32,768]{2,1,0:T(8,128)(2,1)}), bf16[8,32,768]{2,1,0:T(8,128)(2,1)S(1)}, u32[]{:S(2)}, u32[]{:S(2)}) async-start(bf16[8,32,768]{2,1,0:T(8,128)(2,1)} %bitcast.5), calls=%async_computation.1 | async-start | bytes 786432 | tf_op jit(solution)/shard_map/all_to_all | solution.py:244
  36.6 1.0 dynamic-slice_bitcast_fusion.1
  37.7 0.6 collective-permute-start.4
  38.3 5.3 %all-to-all-done.1.got = bf16[8,32,768]{2,1,0:T(8,128)(2,1)S(1)} async-done(((bf16[8,32,768]{2,1,0:T(8,128)(2,1)}), bf16[8,32,768]{2,1,0:T(8,128)(2,1)S(1)}, u32[]{:S(2)}, u32[]{:S(2)}) %all-to-all-start.1) | async-done | bytes 393248 | tf_op jit(solution)/shard_map/all_to_all | solution.py:244
  43.6 0.6 shard_map.65
  44.2 0.8 copy-done.1
  44.9 4.7 %all-to-all-start.2 = ((bf16[8,32,768]{2,1,0:T(8,128)(2,1)}), bf16[8,32,768]{2,1,0:T(8,128)(2,1)S(1)}, u32[]{:S(2)}, u32[]{:S(2)}) async-start(bf16[8,32,768]{2,1,0:T(8,128)(2,1)} %copy-done.1), calls=%async_computation.2 | async-start | bytes 786432 | tf_op jit(solution)/shard_map/all_to_all | solution.py:244
  49.6 6.7 %all-to-all-done.2 = bf16[8,32,768]{2,1,0:T(8,128)(2,1)S(1)} async-done(((bf16[8,32,768]{2,1,0:T(8,128)(2,1)}), bf16[8,32,768]{2,1,0:T(8,128)(2,1)S(1)}, u32[]{:S(2)}, u32[]{:S(2)}) %all-to-all-start.2) | async-done | bytes 393248 | tf_op jit(solution)/shard_map/all_to_all | solution.py:244
  56.3 2.5 %shard_map.68 = (bf16[2,232,256]{2,1,0:T(8,128)(2,1)S(1)}, bf16[2,232,256]{2,1,0:T(8,128)(2,1)S(1)}) custom-call(s32[4]{0:T(128)S(1)} %pad_add_fusion.s, bf16[256,768]{1,0:T(8,128)(2,1)S(1)} %bitcast.21, bf16[2,3696,256]{2,1,0:T(8,128)(2,1)} %bitcast.24, bf16[3696,256]{1,0:T(8,128)(2,1)} %collective-permute-done.3.w_other, ...), custom_call_target="tpu_custom_call" | custom-call | tf_op jit(solution)/shard_map/pallas_call | solution.py:53
  58.8 0.1 collective-permute-start.6
  58.9 2.7 %collective-permute-start.7 = (bf16[2,232,256]{2,1,0:T(8,128)(2,1)S(1)}, bf16[2,232,256]{2,1,0:T(8,128)(2,1)S(1)}, u32[]{:S(2)}, u32[]{:S(2)}) collective-permute-start(bf16[2,232,256]{2,1,0:T(8,128)(2,1)S(1)} %get-tuple-element.30), channel_id=1, source_target_pairs={{0,192},{8,200},{16,208},{24,216},{32,224},{40,232},{48,240},{56,2... | collective-permute-start | bytes 712712 | tf_op jit(solution)/shard_map/ppermute | solution.py:241
  61.5 2.5 %shard_map.67 = (bf16[2,232,256]{2,1,0:T(8,128)(2,1)S(1)}, bf16[2,232,256]{2,1,0:T(8,128)(2,1)S(1)}) custom-call(s32[4]{0:T(128)S(1)} %pad_add_fusion.s, bf16[256,768]{1,0:T(8,128)(2,1)S(1)} %bitcast.22, bf16[2,3696,256]{2,1,0:T(8,128)(2,1)} %bitcast.25, bf16[3696,256]{1,0:T(8,128)(2,1)} %collective-permute-done.3.w_other, ...), custom_call_target="tpu_custom_call" | custom-call | tf_op jit(solution)/shard_map/pallas_call | solution.py:53
  64.1 0.1 collective-permute-start.5
  64.2 1.5 %collective-permute-start.9 = (bf16[2,232,256]{2,1,0:T(8,128)(2,1)S(1)}, bf16[2,232,256]{2,1,0:T(8,128)(2,1)S(1)}, u32[]{:S(2)}, u32[]{:S(2)}) collective-permute-start(bf16[2,232,256]{2,1,0:T(8,128)(2,1)S(1)} %get-tuple-element.33), channel_id=1, source_target_pairs={{0,64},{8,72},{16,80},{24,88},{32,96},{40,104},{48,112},{56,120},{... | collective-permute-start | bytes 712712 | tf_op jit(solution)/shard_map/ppermute | solution.py:241
  65.6 4.3 %shard_map.66 = (f32[2,232,256]{2,1,0:T(8,128)S(1)}, f32[2,232,256]{2,1,0:T(8,128)S(1)}, f32[2,232,256]{2,1,0:T(8,128)S(1)}, f32[2,232,256]{2,1,0:T(8,128)S(1)}) custom-call(s32[4]{0:T(128)S(1)} %pad_add_fusion.s, bf16[256,768]{1,0:T(8,128)(2,1)S(1)} %bitcast.23, bf16[2,3696,256]{2,1,0:T(8,128)(2,1)} %bitcast.26, ...), custom_call_target="tpu_custom_call" | custom-call | tf_op jit(solution)/shard_map/pallas_call | solution.py:53
  70.0 0.6 shard_map.69
  70.6 1.4 collective-permute-start.10
  72.0 0.2 collective-permute-start.8
  72.1 3.5 %collective-permute-done.10.b2 = bf16[2,232,256]{2,1,0:T(8,128)(2,1)S(1)} collective-permute-done((bf16[2,232,256]{2,1,0:T(8,128)(2,1)S(1)}, bf16[2,232,256]{2,1,0:T(8,128)(2,1)S(1)}, u32[]{:S(2)}, u32[]{:S(2)}) %collective-permute-start.10) | collective-permute-done | bytes 237600 | tf_op jit(solution)/shard_map/ppermute | solution.py:241
  75.6 2.5 %collective-permute-done.8.a2 = bf16[2,232,256]{2,1,0:T(8,128)(2,1)S(1)} collective-permute-done((bf16[2,232,256]{2,1,0:T(8,128)(2,1)S(1)}, bf16[2,232,256]{2,1,0:T(8,128)(2,1)S(1)}, u32[]{:S(2)}, u32[]{:S(2)}) %collective-permute-start.8) | collective-permute-done | bytes 237600 | tf_op jit(solution)/shard_map/ppermute | solution.py:241
  78.1 0.8 shard_map.70
  78.9 0.6 collective-permute-start.11
  79.5 1.7 %collective-permute-start.12 = (bf16[232,256]{1,0:T(8,128)(2,1)S(1)}, bf16[232,256]{1,0:T(8,128)(2,1)S(1)}, u32[]{:S(2)}, u32[]{:S(2)}) collective-permute-start(bf16[232,256]{1,0:T(8,128)(2,1)S(1)} %get-tuple-element.37), channel_id=1, source_target_pairs={{0,32},{8,40},{16,48},{24,56},{32,0},{40,8},{48,16},{56,24},{64,96... | collective-permute-start | bytes 356360 | tf_op jit(solution)/shard_map/ppermute | solution.py:241
  81.2 1.7 %collective-permute-start.13 = (bf16[232,256]{1,0:T(8,128)(2,1)S(1)}, bf16[232,256]{1,0:T(8,128)(2,1)S(1)}, u32[]{:S(2)}, u32[]{:S(2)}) collective-permute-start(bf16[232,256]{1,0:T(8,128)(2,1)S(1)} %get-tuple-element.38), channel_id=1, source_target_pairs={{0,48},{8,56},{16,0},{24,8},{32,16},{40,24},{48,32},{56,40},{64,11... | collective-permute-start | bytes 356360 | tf_op jit(solution)/shard_map/ppermute | solution.py:241
  82.9 2.5 %collective-permute-done.11.a1 = bf16[232,256]{1,0:T(8,128)(2,1)S(1)} collective-permute-done((bf16[232,256]{1,0:T(8,128)(2,1)S(1)}, bf16[232,256]{1,0:T(8,128)(2,1)S(1)}, u32[]{:S(2)}, u32[]{:S(2)}) %collective-permute-start.11) | collective-permute-done | bytes 118816 | tf_op jit(solution)/shard_map/ppermute | solution.py:241
  85.4 1.8 %collective-permute-done.12.a2 = bf16[232,256]{1,0:T(8,128)(2,1)S(1)} collective-permute-done((bf16[232,256]{1,0:T(8,128)(2,1)S(1)}, bf16[232,256]{1,0:T(8,128)(2,1)S(1)}, u32[]{:S(2)}, u32[]{:S(2)}) %collective-permute-start.12) | collective-permute-done | bytes 118816 | tf_op jit(solution)/shard_map/ppermute | solution.py:241
  87.2 2.7 %collective-permute-done.13.a3 = bf16[232,256]{1,0:T(8,128)(2,1)S(1)} collective-permute-done((bf16[232,256]{1,0:T(8,128)(2,1)S(1)}, bf16[232,256]{1,0:T(8,128)(2,1)S(1)}, u32[]{:S(2)}, u32[]{:S(2)}) %collective-permute-start.13) | collective-permute-done | bytes 118816 | tf_op jit(solution)/shard_map/ppermute | solution.py:241
  89.9 0.6 shard_map.71
  90.5 7.3 %collective-permute-start.14 = (f32[232,128]{1,0:T(8,128)S(1)}, f32[232,128]{1,0:T(8,128)S(1)}, u32[]{:S(2)}, u32[]{:S(2)}) collective-permute-start(f32[232,128]{1,0:T(8,128)S(1)} %get-tuple-element.40), channel_id=1, source_target_pairs={{0,8},{8,0},{16,24},{24,16},{32,40},{40,32},{48,56},{56,48},{64,72... | collective-permute-start | bytes 356360 | tf_op jit(solution)/shard_map/ppermute | solution.py:241
  97.8 1.0 collective-permute-done.14.got
  98.8 0.6 shard_map.72.h0
  99.4 0.9 collective-permute-start.15
  100.3 2.1 %collective-permute-start.16 = (bf16[232,128]{1,0:T(8,128)(2,1)S(1)}, bf16[232,128]{1,0:T(8,128)(2,1)S(1)}, u32[]{:S(2)}, u32[]{:S(2)}) collective-permute-start(bf16[232,128]{1,0:T(8,128)(2,1)S(1)} %shard_map.72.h0), channel_id=1, source_target_pairs={{0,32},{8,40},{16,48},{24,56},{32,0},{40,8},{48,16},{56,24},{64,96... | collective-permute-start | bytes 178184 | tf_op jit(solution)/shard_map/ppermute | solution.py:241
  102.4 1.5 %collective-permute-start.17 = (bf16[232,128]{1,0:T(8,128)(2,1)S(1)}, bf16[232,128]{1,0:T(8,128)(2,1)S(1)}, u32[]{:S(2)}, u32[]{:S(2)}) collective-permute-start(bf16[232,128]{1,0:T(8,128)(2,1)S(1)} %shard_map.72.h0), channel_id=1, source_target_pairs={{0,48},{8,56},{16,0},{24,8},{32,16},{40,24},{48,32},{56,40},{64,11... | collective-permute-start | bytes 178184 | tf_op jit(solution)/shard_map/ppermute | solution.py:241
  104.0 0.6 collective-permute-done.15.h1
  104.6 2.7 %collective-permute-done.16.h2 = bf16[232,128]{1,0:T(8,128)(2,1)S(1)} collective-permute-done((bf16[232,128]{1,0:T(8,128)(2,1)S(1)}, bf16[232,128]{1,0:T(8,128)(2,1)S(1)}, u32[]{:S(2)}, u32[]{:S(2)}) %collective-permute-start.16) | collective-permute-done | bytes 59424 | tf_op jit(solution)/shard_map/ppermute | solution.py:241
  107.3 3.3 %collective-permute-done.17.h3 = bf16[232,128]{1,0:T(8,128)(2,1)S(1)} collective-permute-done((bf16[232,128]{1,0:T(8,128)(2,1)S(1)}, bf16[232,128]{1,0:T(8,128)(2,1)S(1)}, u32[]{:S(2)}, u32[]{:S(2)}) %collective-permute-start.17) | collective-permute-done | bytes 59424 | tf_op jit(solution)/shard_map/ppermute | solution.py:241
  110.6 0.6 shard_map.73.h
  111.2 0.1 collective-permute-start.18
  111.3 0.8 collective-permute-start.19
  112.1 1.8 %collective-permute-start.20 = (bf16[4,232,128]{2,1,0:T(8,128)(2,1)S(1)}, bf16[4,232,128]{2,1,0:T(8,128)(2,1)S(1)}, u32[]{:S(2)}, u32[]{:S(2)}) collective-permute-start(bf16[4,232,128]{2,1,0:T(8,128)(2,1)S(1)} %shard_map.73.h), channel_id=1, source_target_pairs={{0,192},{8,200},{16,208},{24,216},{32,224},{40,232},{48,240},{56,2... | collective-permute-start | bytes 712712 | tf_op jit(solution)/shard_map/ppermute | solution.py:241
  113.9 3.0 %shard_map.74 = (bf16[3696,512]{1,0:T(8,128)(2,1)S(1)}, f32[128,512]{1,0:T(8,128)S(1)}) custom-call(s32[4]{0:T(128)S(1)} %pad_add_fusion.s, bf16[3696,256]{1,0:T(8,128)(2,1)} %w_own.1, bf16[3696,256]{1,0:T(8,128)(2,1)} %collective-permute-done.w_other, bf16[4,232,128]{2,1,0:T(8,128)(2,1)S(1)} %shard_map.73.h), custom_call_target="tpu_custom_call" | custom-call | tf_op jit(solution)/shard_map/pallas_call | solution.py:71
  116.9 7.5 %collective-permute-done.18.h1 = bf16[4,232,128]{2,1,0:T(8,128)(2,1)S(1)} collective-permute-done((bf16[4,232,128]{2,1,0:T(8,128)(2,1)S(1)}, bf16[4,232,128]{2,1,0:T(8,128)(2,1)S(1)}, u32[]{:S(2)}, u32[]{:S(2)}) %collective-permute-start.18) | collective-permute-done | bytes 237600 | tf_op jit(solution)/shard_map/ppermute | solution.py:241
  124.4 0.3 collective-permute-done.20.h3
  124.8 1.3 shard_map.75
  126.1 7.8 %all_to_all.20.got = bf16[8,16,512]{2,1,0:T(8,128)(2,1)S(1)} all-to-all(bf16[8,16,512]{2,1,0:T(8,128)(2,1)S(1)} %shard_map.75), channel_id=1, replica_groups=mesh['task'=32,'tensor'=8] {'tensor'}, dimensions={0} | all-to-all | bytes 262144 | tf_op jit(solution)/shard_map/all_to_all | solution.py:244
  133.9 0.6 shard_map.76
  134.5 2.9 %collective-permute-start.21 = (f32[16,256]{1,0:T(8,128)S(1)}, f32[16,256]{1,0:T(8,128)S(1)}, u32[]{:S(2)}, u32[]{:S(2)}) collective-permute-start(f32[16,256]{1,0:T(8,128)S(1)} %get-tuple-element.44), channel_id=1, source_target_pairs={{0,8},{8,0},{16,24},{24,16},{32,40},{40,32},{48,56},{56,48},{64,72... | collective-permute-start | bytes 49160 | tf_op jit(solution)/shard_map/ppermute | solution.py:241
  137.3 0.8 collective-permute-done.21.got
  138.2 1.2 shard_map.77
  (15 shorter events, 0.1 us)
Async XLA Ops:
  2.2 24.4 %all-to-all-start = ((bf16[16,8,1152]{2,1,0:T(8,128)(2,1)}), bf16[16,8,1152]{2,1,0:T(8,128)(2,1)S(1)}, u32[]{:S(2)}, u32[]{:S(2)}) async-start(bf16[16,8,1152]{2,1,0:T(8,128)(2,1)} %broadcast_in_dim.10), calls=%async_computation | async-start | bytes 589824 | tf_op jit(solution)/shard_map/all_to_all | solution.py:270
  13.8 14.9 %copy-start.2 = (bf16[2,1024,128]{2,1,0:T(8,128)(2,1)S(1)}, bf16[2,1024,128]{2,1,0:T(8,128)(2,1)}, u32[]{:S(2)}) copy-start(bf16[2,1024,128]{2,1,0:T(8,128)(2,1)} %low_own.1) | copy-start | bytes 1572868
  16.8 19.8 %copy-start = (bf16[2,128,3696]{1,2,0:T(8,128)(2,1)S(1)}, bf16[2,128,3696]{1,2,0:T(8,128)(2,1)}, u32[]{:S(2)}) copy-start(bf16[2,128,3696]{1,2,0:T(8,128)(2,1)} %param.11) | copy-start | bytes 5677060
  16.8 32.8 %collective-permute-start.3 = (bf16[3696,256]{1,0:T(8,128)(2,1)}, bf16[3696,256]{1,0:T(8,128)(2,1)}, u32[]{:S(2)}, u32[]{:S(2)}) collective-permute-start(bf16[3696,256]{1,0:T(8,128)(2,1)} %dynamic-slice_bitcast_fusion), channel_id=1, source_target_pairs={{0,8},{8,0},{16,24},{24,16},{32,40},{40,32},{48,56},{56,48},{64,72... | collective-permute-start | bytes 5677064 | tf_op jit(solution)/shard_map/ppermute | solution.py:241
  26.7 3.7 %collective-permute-start.1 = (bf16[16,8,1152]{2,1,0:T(8,128)(2,1)S(1)}, bf16[16,8,1152]{2,1,0:T(8,128)(2,1)S(1)}, u32[]{:S(2)}, u32[]{:S(2)}) collective-permute-start(bf16[16,8,1152]{2,1,0:T(8,128)(2,1)S(1)} %all-to-all-done.own), channel_id=1, source_target_pairs={{0,8},{8,0},{16,24},{24,16},{32,40},{40,32},{48,56},{56,48},{64,72... | collective-permute-start | bytes 884744 | tf_op jit(solution)/shard_map/ppermute | solution.py:241
  28.8 1.6 %collective-permute-start.2 = (bf16[1024,128]{1,0:T(8,128)(2,1)S(1)}, bf16[1024,128]{1,0:T(8,128)(2,1)S(1)}, u32[]{:S(2)}, u32[]{:S(2)}) collective-permute-start(bf16[1024,128]{1,0:T(8,128)(2,1)S(1)} %dynamic-slice_bitcast_fusion.2), channel_id=1, source_target_pairs={{0,8},{8,0},{16,24},{24,16},{32,40},{40,32},{48,56},{56,48},{64,72... | collective-permute-start | bytes 786440 | tf_op jit(solution)/shard_map/ppermute | solution.py:241
  32.0 11.6 %all-to-all-start.1 = ((bf16[8,32,768]{2,1,0:T(8,128)(2,1)}), bf16[8,32,768]{2,1,0:T(8,128)(2,1)S(1)}, u32[]{:S(2)}, u32[]{:S(2)}) async-start(bf16[8,32,768]{2,1,0:T(8,128)(2,1)} %bitcast.5), calls=%async_computation.1 | async-start | bytes 786432 | tf_op jit(solution)/shard_map/all_to_all | solution.py:244
  37.7 11.9 %collective-permute-start.4 = (bf16[3696,128]{1,0:T(8,128)(2,1)}, bf16[3696,128]{1,0:T(8,128)(2,1)S(1)}, u32[]{:S(2)}, u32[]{:S(2)}) collective-permute-start(bf16[3696,128]{1,0:T(8,128)(2,1)} %dynamic-slice_bitcast_fusion.1), channel_id=1, source_target_pairs={{0,8},{8,0},{16,24},{24,16},{32,40},{40,32},{48,56},{56,48},{64,72... | collective-permute-start | bytes 2838536 | tf_op jit(solution)/shard_map/ppermute | solution.py:241
  38.3 75.7 %collective-permute-start = (bf16[3696,256]{1,0:T(8,128)(2,1)}, bf16[3696,256]{1,0:T(8,128)(2,1)}, u32[]{:S(2)}, u32[]{:S(2)}) collective-permute-start(bf16[3696,256]{1,0:T(8,128)(2,1)} %w_own.1), channel_id=1, source_target_pairs={{0,8},{8,0},{16,24},{24,16},{32,40},{40,32},{48,56},{56,48},{64,72... | collective-permute-start | bytes 5677064 | tf_op jit(solution)/shard_map/ppermute | solution.py:241
  44.2 0.8 copy-start.1
  44.9 11.4 %all-to-all-start.2 = ((bf16[8,32,768]{2,1,0:T(8,128)(2,1)}), bf16[8,32,768]{2,1,0:T(8,128)(2,1)S(1)}, u32[]{:S(2)}, u32[]{:S(2)}) async-start(bf16[8,32,768]{2,1,0:T(8,128)(2,1)} %copy-done.1), calls=%async_computation.2 | async-start | bytes 786432 | tf_op jit(solution)/shard_map/all_to_all | solution.py:244
  58.8 11.1 %collective-permute-start.6 = (bf16[2,232,256]{2,1,0:T(8,128)(2,1)S(1)}, bf16[2,232,256]{2,1,0:T(8,128)(2,1)S(1)}, u32[]{:S(2)}, u32[]{:S(2)}) collective-permute-start(bf16[2,232,256]{2,1,0:T(8,128)(2,1)S(1)} %get-tuple-element.28), channel_id=1, source_target_pairs={{0,64},{8,72},{16,80},{24,88},{32,96},{40,104},{48,112},{56,120},{... | collective-permute-start | bytes 712712 | tf_op jit(solution)/shard_map/ppermute | solution.py:241
  58.9 11.1 %collective-permute-start.7 = (bf16[2,232,256]{2,1,0:T(8,128)(2,1)S(1)}, bf16[2,232,256]{2,1,0:T(8,128)(2,1)S(1)}, u32[]{:S(2)}, u32[]{:S(2)}) collective-permute-start(bf16[2,232,256]{2,1,0:T(8,128)(2,1)S(1)} %get-tuple-element.30), channel_id=1, source_target_pairs={{0,192},{8,200},{16,208},{24,216},{32,224},{40,232},{48,240},{56,2... | collective-permute-start | bytes 712712 | tf_op jit(solution)/shard_map/ppermute | solution.py:241
  64.1 8.1 %collective-permute-start.5 = (bf16[2,232,256]{2,1,0:T(8,128)(2,1)S(1)}, bf16[2,232,256]{2,1,0:T(8,128)(2,1)S(1)}, u32[]{:S(2)}, u32[]{:S(2)}) collective-permute-start(bf16[2,232,256]{2,1,0:T(8,128)(2,1)S(1)} %get-tuple-element.26), channel_id=1, source_target_pairs={{0,192},{8,200},{16,208},{24,216},{32,224},{40,232},{48,240},{56,2... | collective-permute-start | bytes 712712 | tf_op jit(solution)/shard_map/ppermute | solution.py:241
  64.2 8.0 %collective-permute-start.9 = (bf16[2,232,256]{2,1,0:T(8,128)(2,1)S(1)}, bf16[2,232,256]{2,1,0:T(8,128)(2,1)S(1)}, u32[]{:S(2)}, u32[]{:S(2)}) collective-permute-start(bf16[2,232,256]{2,1,0:T(8,128)(2,1)S(1)} %get-tuple-element.33), channel_id=1, source_target_pairs={{0,64},{8,72},{16,80},{24,88},{32,96},{40,104},{48,112},{56,120},{... | collective-permute-start | bytes 712712 | tf_op jit(solution)/shard_map/ppermute | solution.py:241
  70.6 5.0 %collective-permute-start.10 = (bf16[2,232,256]{2,1,0:T(8,128)(2,1)S(1)}, bf16[2,232,256]{2,1,0:T(8,128)(2,1)S(1)}, u32[]{:S(2)}, u32[]{:S(2)}) collective-permute-start(bf16[2,232,256]{2,1,0:T(8,128)(2,1)S(1)} %get-tuple-element.34), channel_id=1, source_target_pairs={{0,192},{8,200},{16,208},{24,216},{32,224},{40,232},{48,240},{56,2... | collective-permute-start | bytes 712712 | tf_op jit(solution)/shard_map/ppermute | solution.py:241
  72.0 6.2 %collective-permute-start.8 = (bf16[2,232,256]{2,1,0:T(8,128)(2,1)S(1)}, bf16[2,232,256]{2,1,0:T(8,128)(2,1)S(1)}, u32[]{:S(2)}, u32[]{:S(2)}) collective-permute-start(bf16[2,232,256]{2,1,0:T(8,128)(2,1)S(1)} %get-tuple-element.31), channel_id=1, source_target_pairs={{0,64},{8,72},{16,80},{24,88},{32,96},{40,104},{48,112},{56,120},{... | collective-permute-start | bytes 712712 | tf_op jit(solution)/shard_map/ppermute | solution.py:241
  78.9 6.5 %collective-permute-start.11 = (bf16[232,256]{1,0:T(8,128)(2,1)S(1)}, bf16[232,256]{1,0:T(8,128)(2,1)S(1)}, u32[]{:S(2)}, u32[]{:S(2)}) collective-permute-start(bf16[232,256]{1,0:T(8,128)(2,1)S(1)} %get-tuple-element.36), channel_id=1, source_target_pairs={{0,16},{8,24},{16,32},{24,40},{32,48},{40,56},{48,0},{56,8},{64,80... | collective-permute-start | bytes 356360 | tf_op jit(solution)/shard_map/ppermute | solution.py:241
  79.5 7.7 %collective-permute-start.12 = (bf16[232,256]{1,0:T(8,128)(2,1)S(1)}, bf16[232,256]{1,0:T(8,128)(2,1)S(1)}, u32[]{:S(2)}, u32[]{:S(2)}) collective-permute-start(bf16[232,256]{1,0:T(8,128)(2,1)S(1)} %get-tuple-element.37), channel_id=1, source_target_pairs={{0,32},{8,40},{16,48},{24,56},{32,0},{40,8},{48,16},{56,24},{64,96... | collective-permute-start | bytes 356360 | tf_op jit(solution)/shard_map/ppermute | solution.py:241
  81.2 8.7 %collective-permute-start.13 = (bf16[232,256]{1,0:T(8,128)(2,1)S(1)}, bf16[232,256]{1,0:T(8,128)(2,1)S(1)}, u32[]{:S(2)}, u32[]{:S(2)}) collective-permute-start(bf16[232,256]{1,0:T(8,128)(2,1)S(1)} %get-tuple-element.38), channel_id=1, source_target_pairs={{0,48},{8,56},{16,0},{24,8},{32,16},{40,24},{48,32},{56,40},{64,11... | collective-permute-start | bytes 356360 | tf_op jit(solution)/shard_map/ppermute | solution.py:241
  90.5 8.2 %collective-permute-start.14 = (f32[232,128]{1,0:T(8,128)S(1)}, f32[232,128]{1,0:T(8,128)S(1)}, u32[]{:S(2)}, u32[]{:S(2)}) collective-permute-start(f32[232,128]{1,0:T(8,128)S(1)} %get-tuple-element.40), channel_id=1, source_target_pairs={{0,8},{8,0},{16,24},{24,16},{32,40},{40,32},{48,56},{56,48},{64,72... | collective-permute-start | bytes 356360 | tf_op jit(solution)/shard_map/ppermute | solution.py:241
  99.4 5.2 %collective-permute-start.15 = (bf16[232,128]{1,0:T(8,128)(2,1)S(1)}, bf16[232,128]{1,0:T(8,128)(2,1)S(1)}, u32[]{:S(2)}, u32[]{:S(2)}) collective-permute-start(bf16[232,128]{1,0:T(8,128)(2,1)S(1)} %shard_map.72.h0), channel_id=1, source_target_pairs={{0,16},{8,24},{16,32},{24,40},{32,48},{40,56},{48,0},{56,8},{64,80... | collective-permute-start | bytes 178184 | tf_op jit(solution)/shard_map/ppermute | solution.py:241
  100.3 7.0 %collective-permute-start.16 = (bf16[232,128]{1,0:T(8,128)(2,1)S(1)}, bf16[232,128]{1,0:T(8,128)(2,1)S(1)}, u32[]{:S(2)}, u32[]{:S(2)}) collective-permute-start(bf16[232,128]{1,0:T(8,128)(2,1)S(1)} %shard_map.72.h0), channel_id=1, source_target_pairs={{0,32},{8,40},{16,48},{24,56},{32,0},{40,8},{48,16},{56,24},{64,96... | collective-permute-start | bytes 178184 | tf_op jit(solution)/shard_map/ppermute | solution.py:241
  102.4 8.2 %collective-permute-start.17 = (bf16[232,128]{1,0:T(8,128)(2,1)S(1)}, bf16[232,128]{1,0:T(8,128)(2,1)S(1)}, u32[]{:S(2)}, u32[]{:S(2)}) collective-permute-start(bf16[232,128]{1,0:T(8,128)(2,1)S(1)} %shard_map.72.h0), channel_id=1, source_target_pairs={{0,48},{8,56},{16,0},{24,8},{32,16},{40,24},{48,32},{56,40},{64,11... | collective-permute-start | bytes 178184 | tf_op jit(solution)/shard_map/ppermute | solution.py:241
  111.2 13.2 %collective-permute-start.18 = (bf16[4,232,128]{2,1,0:T(8,128)(2,1)S(1)}, bf16[4,232,128]{2,1,0:T(8,128)(2,1)S(1)}, u32[]{:S(2)}, u32[]{:S(2)}) collective-permute-start(bf16[4,232,128]{2,1,0:T(8,128)(2,1)S(1)} %shard_map.73.h), channel_id=1, source_target_pairs={{0,64},{8,72},{16,80},{24,88},{32,96},{40,104},{48,112},{56,120},{... | collective-permute-start | bytes 712712 | tf_op jit(solution)/shard_map/ppermute | solution.py:241
  111.3 13.1 %collective-permute-start.19 = (bf16[4,232,128]{2,1,0:T(8,128)(2,1)S(1)}, bf16[4,232,128]{2,1,0:T(8,128)(2,1)S(1)}, u32[]{:S(2)}, u32[]{:S(2)}) collective-permute-start(bf16[4,232,128]{2,1,0:T(8,128)(2,1)S(1)} %shard_map.73.h), channel_id=1, source_target_pairs={{0,128},{8,136},{16,144},{24,152},{32,160},{40,168},{48,176},{56,1... | collective-permute-start | bytes 712712 | tf_op jit(solution)/shard_map/ppermute | solution.py:241
  112.1 12.6 %collective-permute-start.20 = (bf16[4,232,128]{2,1,0:T(8,128)(2,1)S(1)}, bf16[4,232,128]{2,1,0:T(8,128)(2,1)S(1)}, u32[]{:S(2)}, u32[]{:S(2)}) collective-permute-start(bf16[4,232,128]{2,1,0:T(8,128)(2,1)S(1)} %shard_map.73.h), channel_id=1, source_target_pairs={{0,192},{8,200},{16,208},{24,216},{32,224},{40,232},{48,240},{56,2... | collective-permute-start | bytes 712712 | tf_op jit(solution)/shard_map/ppermute | solution.py:241
  134.5 3.7 %collective-permute-start.21 = (f32[16,256]{1,0:T(8,128)S(1)}, f32[16,256]{1,0:T(8,128)S(1)}, u32[]{:S(2)}, u32[]{:S(2)}) collective-permute-start(f32[16,256]{1,0:T(8,128)S(1)} %get-tuple-element.44), channel_id=1, source_target_pairs={{0,8},{8,0},{16,24},{24,16},{32,40},{40,32},{48,56},{56,48},{64,72... | collective-permute-start | bytes 49160 | tf_op jit(solution)/shard_map/ppermute | solution.py:241

commit v5 on v4

--- a/solution.py
+++ b/solution.py
@@ -83,10 +83,10 @@
     return v.reshape(v.shape[0] * v.shape[1], v.shape[2])
 
 
-def latent_kernel(width, s, own, other, low_own, low_other, out):
-    q = s[3]
-    x = jnp.concatenate([rows_of(own[...]), rows_of(other[...])], axis=0)
-    low = jnp.concatenate([low_own[0], low_other[...]], axis=1)
+def latent_kernel(width, s, tokens, low_own, low_other, out):
+    c, q = s[2], s[3]
+    x = rows_of(tokens[...])
+    low = jnp.concatenate([low_own[c], low_other[c], low_other[1 - c], low_own[1 - c]], axis=1)
     lat = jnp.dot(x[:, :width].astype(BF16), low, preferred_element_type=F32)
     tail = x[:, width:]
     lane = lax.broadcasted_iota(jnp.int32, tail.shape, 1)
@@ -97,10 +97,7 @@
     out[:, :ranks] = (lat * weight).astype(BF16)
     feats = out.shape[1] - ranks
     start = pl.multiple_of(lax.rem(q, 2) * feats, feats)
-    m = out.shape[0] // 2
-    for k, ref in enumerate((own, other)):
-        part = rows_of(ref[:, :, pl.ds(start, feats)])
-        out[k * m : (k + 1) * m, ranks:] = part.astype(BF16)
+    out[:, ranks:] = rows_of(tokens[:, :, pl.ds(start, feats)]).astype(BF16)
 
 
 def mid_kernel(ranks, s, got, out):
@@ -117,17 +114,30 @@
         out[j, :, 2 * half :] = total.astype(BF16)
 
 
-def pick(i, values):
-    v = values[0]
-    for k in range(1, len(values)):
-        v = jnp.where(i == k, values[k], v)
-    return v
-
-
-def main_kernel(limit, halves, s, rows, w_own, w_other, u_own, u_other, *outs):
+def token_rows(own, other):
+    n = own.shape[1] // 4
+    a = own[:, : 3 * n]
+    b = jnp.concatenate([other[:, n : 2 * n], other[:, :n], other[:, 3 * n :]], axis=1)
+    return jnp.concatenate([a, b], axis=0)
+
+
+def main_kernel(limit, d, s, rows_own, rows_other, w_own, w_other, u_own, u_other, out_a, out_b):
+    w = jnp.concatenate([w_own[0], w_other[...], u_own[0], u_other[...]], axis=1)
+    rows = token_rows(rows_own, rows_other)
+    p = lax.dot_general(w, rows, (((1,), (1,)), ((), ())), preferred_element_type=F32)
+    n = p.shape[0]
+    at = lax.rem(s[0] + d, NX) * n + lax.broadcasted_iota(jnp.int32, p.shape, 0)
+    p = jnp.where(at < limit, p, 0.0)
+    m = out_a.shape[1]
+    for k, out in enumerate((out_a, out_a, out_b, out_b)):
+        out[k % 2] = p[k * m : (k + 1) * m].astype(out.dtype)
+
+
+def near_kernel(limit, halves, s, rows_own, rows_other, w_own, w_other, u_own, u_other, *outs):
     i = pl.program_id(0)
     w = jnp.concatenate([w_own[0], w_other[...], u_own[0], u_other[...]], axis=1)
-    p = lax.dot_general(w, rows[...], (((1,), (1,)), ((), ())), preferred_element_type=F32)
+    rows = token_rows(rows_own, rows_other)
+    p = lax.dot_general(w, rows, (((1,), (1,)), ((), ())), preferred_element_type=F32)
     n = p.shape[0]
     at = half_block(halves, i, s) * n + lax.broadcasted_iota(jnp.int32, p.shape, 0)
     p = jnp.where(at < limit, p, 0.0)
@@ -140,8 +150,8 @@
 
 
 def half_block(halves, i, s):
-    d = pick(i, [d for d, _ in halves])
-    return lax.rem(s[0] + d, NX) * 2 + pick(i, [h for _, h in halves])
+    (d, h), (e, g) = halves
+    return lax.rem(s[0] + jnp.where(i == 0, d, e), NX) * 2 + jnp.where(i == 0, h, g)
 
 
 def pass_kernel(s, a, got_a, b, got_b, out_a, out_b):
@@ -171,7 +181,7 @@
     out[...] = (gate / (1.0 + jnp.exp(-gate)) * up).astype(BF16)
 
 
-def stack_kernel(s, h0, h1, h2, h3, out):
+def stack_kernel(s, h0, h2, h1, h3, out):
     for d, h in enumerate((h0, h1, h2, h3)):
         out[lax.rem(s[1] - d + NZ, NZ)] = h[...]
 
@@ -202,7 +212,7 @@
     out[...] = jnp.dot(t, w[at], preferred_element_type=F32)
 
 
-def down_kernel(s, acc, h1, h2, h3, w, out, held):
+def down_kernel(s, acc, h2, h1, h3, w, out, held):
     p = acc[...]
     for d, h in enumerate((h1, h2, h3), 1):
         t, at = down_rows(d, s, h, held.at[d - 1], w.shape[0])
@@ -256,7 +266,7 @@
     zb = -(-hid // (NX * NZ * 8)) * 8
     xb = NZ * zb
 
-    low_other = permute(other(lower_factor), CORE)
+    low_other = permute(lower_factor, CORE)
     w_other = permute(other(weight), CORE)
     u_other = permute(other(upper), CORE)
     down_other = permute(down_weight, CORE)
@@ -268,57 +278,67 @@
     )
     packed = jnp.broadcast_to(packed[None], (NQ,) + packed.shape)
     own_rows = lax.all_to_all(packed, "task", 0, 0, axis_index_groups=CHIPS)
-    other_rows = permute(own_rows, CORE)
+    half = count // 2
+    columns = 2 * ranks + feats
     lat = run(
         functools.partial(latent_kernel, width),
-        sds((count, ranks + feats)),
+        sds((half, columns)),
         own_rows,
-        other_rows,
         lower_factor,
         low_other,
-        in_specs=[
-            whole(own_rows),
-            whole(other_rows),
-            pl.BlockSpec((1,) + lower_factor.shape[1:], lambda i, s: (s[2], 0, 0)),
-            whole(low_other),
-        ],
-    )
-    got = across(lat.reshape(tensor, count // tensor, ranks + feats))
-    mid = run(functools.partial(mid_kernel, ranks), sds(got.shape), got)
-    cat = across(mid).reshape(count, feats + ranks)
-
+    )
+    got = across(lat.reshape(tensor, half // tensor, columns))
+    mid = run(functools.partial(mid_kernel, 2 * ranks), sds(got.shape), got)
+    cat = across(mid).reshape(half, columns)
+    cat_other = permute(cat, CORE)
     inside = functools.partial(call_inside, scalars=s)
-    def main(halves, dtype):
+
+    def product(kernel, block, at, dtype, steps=1):
         def own_spec(a):
-            return pl.BlockSpec(
-                (1, xb // 2, a.shape[2]), lambda i, s: (s[2], half_block(halves, i, s), 0)
-            )
+            return pl.BlockSpec((1, block, a.shape[2]), lambda i, s: (s[2], at(i, s), 0))
 
         def spec(a):
-            return pl.BlockSpec((xb // 2, a.shape[1]), lambda i, s: (half_block(halves, i, s), 0))
+            return pl.BlockSpec((block, a.shape[1]), lambda i, s: (at(i, s), 0))
 
         return run(
-            functools.partial(main_kernel, hid, halves),
-            [sds((2, zb, count), dtype)] * len(halves),
+            kernel,
+            [sds((2, zb, count), dtype)] * 2,
             cat,
+            cat_other,
             weight,
             w_other,
             upper,
             u_other,
-            grid=(len(halves),),
-            in_specs=[whole(cat), own_spec(weight), spec(w_other), own_spec(upper), spec(u_other)],
+            grid=(steps,),
+            in_specs=[
+                whole(cat),
+                whole(cat_other),
+                own_spec(weight),
+                spec(w_other),
+                own_spec(upper),
+                spec(u_other),
+            ],
         )
 
-    far_a, far_b = main(((2, 0), (2, 1)), BF16)
+    def main(d, dtype):
+        kernel = functools.partial(main_kernel, hid, d)
+        return product(kernel, xb, lambda i, s: lax.rem(s[0] + d, NX), dtype)
+
+    def near(halves, dtype):
+        kernel = functools.partial(near_kernel, hid, halves)
+        return product(kernel, xb // 2, functools.partial(half_block, halves), dtype, 2)
+
+    far_a, far_b = main(2, BF16)
     far_a = permute(far_a, TO_X[1])
     far_b = permute(far_b, TO_X[3])
-    up_b, down_a = main(((1, 1), (3, 0)), BF16)
+    up_b, down_a = near(((1, 1), (3, 0)), BF16)
     up_b = permute(up_b, TO_X[1])
     down_a = permute(down_a, TO_X[3])
-    up_a, down_b, own_a, own_b = main(((1, 0), (3, 1), (0, 0), (0, 1)), F32)
+    up_a, down_b = near(((1, 0), (3, 1)), F32)
     up_a, down_b = run(pass_kernel, [sds(far_a.shape)] * 2, up_a, far_a, down_b, far_b)
     up_a = permute(up_a, TO_X[1])
     down_b = permute(down_b, TO_X[3])
+    own_a, own_b = main(0, F32)
     parts = run(
         x_sum_kernel,
         [sds((zb, count), F32)] + [sds((zb, count))] * 3,
@@ -332,16 +352,15 @@
     )
     got = {d: permute(parts[d], TO_Z[d]) for d in FAR_FIRST}
     keep, send = run(
-        z_sum_kernel, [sds((zb, count // 2), F32)] * 2, parts[0], got[1], got[2], got[3]
+        z_sum_kernel, [sds((zb, count // 2), F32)] * 2, parts[0], got[2], got[1], got[3]
     )
     hidden = run(silu_kernel, sds((zb, count // 2)), keep, permute(send, CORE))
 
     got = {d: permute(hidden, TO_Z[d]) for d in FAR_FIRST}
-    hidden = run(stack_kernel, sds((NZ, zb, count // 2)), hidden, got[1], got[2], got[3])
+    hidden = run(stack_kernel, sds((NZ, zb, count // 2)), hidden, got[2], got[1], got[3])
     got = {d: permute(hidden, TO_X[d]) for d in FAR_FIRST}
     cols = down_weight.shape[1]
     out_rows = count // 2 // tensor
-    half = count // 2
     down, mixed = inside(
         down_own_kernel,
         [sds((hid, 2 * cols)), sds((half, 2 * cols), F32)],
@@ -355,8 +374,8 @@
         down_kernel,
         sds((tensor, out_rows, 2 * cols)),
         mixed,
+        got[2],
         got[1],
-        got[2],
         got[3],
         down,
         scratch=[pltpu.VMEM((3, xb + 16, half), F32)],

time: 140 us -> 134 us (0.957)
  waiting for transfers between devices: 51.7 us -> 39.5 us
  blocking collectives: 7.82 us -> 17.9 us
  starting transfers between devices: 51.9 us -> 48.9 us
    all_to_all x1 -> x2, blocking collectives: 7.82 us -> 17.9 us  [across(): return lax.all_to_all(a, 'tensor', 0, 0)]
    all_to_all x2 -> x1, waiting for transfers between devices: 12 us -> 2.86 us  [across(): return lax.all_to_all(a, 'tensor', 0, 0)]
    all_to_all x2 -> x1, starting transfers between devices: 9.3 us -> 4.81 us  [across(): return lax.all_to_all(a, 'tensor', 0, 0)]
    ppermute x22, waiting for transfers between devices: 30.8 us -> 27.9 us  [permute(): return lax.ppermute(a, 'task', perm)]
    ppermute x22, starting transfers between devices: 31 us -> 32.5 us  [permute(): return lax.ppermute(a, 'task', perm)]
    pallas_call x12 -> x13, Pallas kernels: 16.4 us -> 16.6 us  [call(): pl.pallas_call(kernel, out_shape=out_shape, grid_spec=pltpu.PrefetchScala...]
    squeeze x3 -> x2, local copies, waits for them, and re-layouts: 4.01 us -> 4 us  [other(): return lax.dynamic_index_in_dim(a, 1 - c, 0, keepdims=False)]
  transfers between devices with their start and end apart: 25 -> 24, of which waited for: 16 -> 14; matrix products, arithmetic and copies ran while one was open for 3% -> 3% of each run, Pallas kernels for 13% -> 13%
where the time goes in v5:
time: 134 us
  starting transfers between devices  48.9 us (36%)
  waiting for transfers between devices  39.5 us (29%)
  Pallas kernels  20.9 us (16%)
  blocking collectives  17.9 us (13%)
  local copies, waits for them, and re-layouts  5.56 us (4%)
    ppermute x22, starting transfers between devices, permute(): return lax.ppermute(a, 'task', perm)  32.5 us
    ppermute x22, waiting for transfers between devices, permute(): return lax.ppermute(a, 'task', perm)  27.9 us
    all_to_all x2, blocking collectives, across(): return lax.all_to_all(a, 'tensor', 0, 0)  17.9 us
    pallas_call x13, Pallas kernels, call(): pl.pallas_call(kernel, out_shape=out_shape, grid_spec=pltpu.PrefetchScala...  16.6 us
    all_to_all x1, starting transfers between devices, on_device(): own_rows = lax.all_to_all(packed, 'task', 0, 0, axis_index_groups=CHIPS)  11.6 us
    all_to_all x1, waiting for transfers between devices, on_device(): own_rows = lax.all_to_all(packed, 'task', 0, 0, axis_index_groups=CHIPS)  8.7 us
    all_to_all x1, starting transfers between devices, across(): return lax.all_to_all(a, 'tensor', 0, 0)  4.81 us
    pallas_call x2, Pallas kernels, call_inside(): pl.pallas_call(kernel, out_shape=out_shape, in_specs=[pl.BlockSpec(memory...  4.29 us
  transfers between devices with their start and end apart: 24, of which 14 were waited for; matrix products, arithmetic and copies ran while one was open for 3% of the time, Pallas kernels for 13%

profile of v5, /device:TPU:1, one launch (start us, length us, event | category | flops | bytes accessed | tf_op | source)
XLA Modules:
  0.0 133.6 jit_solution(542966048371866382)
XLA Ops:
  0.0 0.7 fusion
  0.7 0.8 concatenate.3
  1.5 0.7 broadcast_in_dim.10
  2.2 11.6 %all-to-all-start = ((bf16[16,8,1152]{2,1,0:T(8,128)(2,1)}), bf16[16,8,1152]{2,1,0:T(8,128)(2,1)S(1)}, u32[]{:S(2)}, u32[]{:S(2)}) async-start(bf16[16,8,1152]{2,1,0:T(8,128)(2,1)} %broadcast_in_dim.10), calls=%async_computation | async-start | bytes 589824 | tf_op jit(solution)/shard_map/all_to_all | solution.py:280
  13.8 1.0 collective-permute-start.1
  14.9 3.0 %dynamic-slice_bitcast_fusion = bf16[3696,256]{1,0:T(8,128)(2,1)} fusion(bf16[2,256,3696]{1,2,0:T(8,128)(2,1)} %param.8, s32[]{:T(128)S(6)} %select_n.16), kind=kLoop, calls=%fused_computation | loop fusion | bytes 3784708 | tf_op jit(solution)/shard_map/jit(dynamic_index_in_dim)/squeeze | solution.py:257
  17.9 0.0 collective-permute-start.3
  17.9 0.1 pad_add_fusion.s
  18.0 8.7 %all-to-all-done.tokens = bf16[16,8,1152]{2,1,0:T(8,128)(2,1)S(1)} async-done(((bf16[16,8,1152]{2,1,0:T(8,128)(2,1)}), bf16[16,8,1152]{2,1,0:T(8,128)(2,1)S(1)}, u32[]{:S(2)}, u32[]{:S(2)}) %all-to-all-start) | async-done | bytes 294944 | tf_op jit(solution)/shard_map/all_to_all | solution.py:280
  26.7 1.6 %shard_map.64 = bf16[128,1024]{1,0:T(8,128)(2,1)} custom-call(s32[4]{0:T(128)S(1)} %pad_add_fusion.s, bf16[16,8,1152]{2,1,0:T(8,128)(2,1)S(1)} %all-to-all-done.tokens, bf16[2,1024,128]{2,1,0:T(8,128)(2,1)S(1)} %copy-done.1, bf16[2,1024,128]{2,1,0:T(8,128)(2,1)S(1)} %collective-permute-done.1.low_other), custom_call_target="tpu_custom_call" | custom-call | tf_op jit(solution)/shard_map/pallas_call | solution.py:53
  28.2 4.8 %all-to-all-start.1 = ((bf16[8,16,1024]{2,1,0:T(8,128)(2,1)}), bf16[8,16,1024]{2,1,0:T(8,128)(2,1)S(1)}, u32[]{:S(2)}, u32[]{:S(2)}) async-start(bf16[8,16,1024]{2,1,0:T(8,128)(2,1)} %bitcast.4), calls=%async_computation.1 | async-start | bytes 524288 | tf_op jit(solution)/shard_map/all_to_all | solution.py:254
  33.1 1.0 dynamic-slice_bitcast_fusion.1
  34.1 2.2 %collective-permute-start.4 = (bf16[3696,128]{1,0:T(8,128)(2,1)}, bf16[3696,128]{1,0:T(8,128)(2,1)S(1)}, u32[]{:S(2)}, u32[]{:S(2)}) collective-permute-start(bf16[3696,128]{1,0:T(8,128)(2,1)} %dynamic-slice_bitcast_fusion.1), channel_id=1, source_target_pairs={{0,8},{8,0},{16,24},{24,16},{32,40},{40,32},{48,56},{56,48},{64,72... | collective-permute-start | bytes 2838536 | tf_op jit(solution)/shard_map/ppermute | solution.py:251
  36.3 2.9 %all-to-all-done.1.got = bf16[8,16,1024]{2,1,0:T(8,128)(2,1)S(1)} async-done(((bf16[8,16,1024]{2,1,0:T(8,128)(2,1)}), bf16[8,16,1024]{2,1,0:T(8,128)(2,1)S(1)}, u32[]{:S(2)}, u32[]{:S(2)}) %all-to-all-start.1) | async-done | bytes 262176 | tf_op jit(solution)/shard_map/all_to_all | solution.py:254
  39.1 0.6 shard_map.65
  39.7 8.7 %all_to_all.20 = bf16[8,16,1024]{2,1,0:T(8,128)(2,1)S(1)} all-to-all(bf16[8,16,1024]{2,1,0:T(8,128)(2,1)S(1)} %shard_map.65), channel_id=1, replica_groups=mesh['task'=32,'tensor'=8] {'tensor'}, dimensions={0} | all-to-all | bytes 524288 | tf_op jit(solution)/shard_map/all_to_all | solution.py:254
  48.4 4.5 %collective-permute-start.2 = (bf16[128,1024]{1,0:T(8,128)(2,1)S(1)}, bf16[128,1024]{1,0:T(8,128)(2,1)S(1)}, u32[]{:S(2)}, u32[]{:S(2)}) collective-permute-start(bf16[128,1024]{1,0:T(8,128)(2,1)S(1)} %bitcast.20), channel_id=1, source_target_pairs={{0,8},{8,0},{16,24},{24,16},{32,40},{40,32},{48,56},{56,48},{64,72... | collective-permute-start | bytes 786440 | tf_op jit(solution)/shard_map/ppermute | solution.py:251
  52.8 0.0 collective-permute-done.4.u_other
  52.9 1.2 collective-permute-done.2.rows_other
  54.0 2.3 %shard_map.69 = (bf16[2,232,256]{2,1,0:T(8,128)(2,1)S(1)}, bf16[2,232,256]{2,1,0:T(8,128)(2,1)S(1)}) custom-call(s32[4]{0:T(128)S(1)} %pad_add_fusion.s, bf16[128,1024]{1,0:T(8,128)(2,1)S(1)} %bitcast.21, bf16[128,1024]{1,0:T(8,128)(2,1)S(1)} %collective-permute-done.2.rows_other, bf16[2,3696,256]{2,1,0:T(8,128)(2,1)} %bitcast.25, ...), custom_call_target="tpu_custom_call" | custom-call | tf_op jit(solution)/shard_map/pallas_call | solution.py:53
  56.3 0.1 collective-permute-start.6
  56.4 2.7 %collective-permute-start.7 = (bf16[2,232,256]{2,1,0:T(8,128)(2,1)S(1)}, bf16[2,232,256]{2,1,0:T(8,128)(2,1)S(1)}, u32[]{:S(2)}, u32[]{:S(2)}) collective-permute-start(bf16[2,232,256]{2,1,0:T(8,128)(2,1)S(1)} %get-tuple-element.30), channel_id=1, source_target_pairs={{0,192},{8,200},{16,208},{24,216},{32,224},{40,232},{48,240},{56,2... | collective-permute-start | bytes 712712 | tf_op jit(solution)/shard_map/ppermute | solution.py:251
  59.1 2.5 %shard_map.67 = (bf16[2,232,256]{2,1,0:T(8,128)(2,1)S(1)}, bf16[2,232,256]{2,1,0:T(8,128)(2,1)S(1)}) custom-call(s32[4]{0:T(128)S(1)} %pad_add_fusion.s, bf16[128,1024]{1,0:T(8,128)(2,1)S(1)} %bitcast.22, bf16[128,1024]{1,0:T(8,128)(2,1)S(1)} %collective-permute-done.2.rows_other, bf16[2,3696,256]{2,1,0:T(8,128)(2,1)} %bitcast.26, ...), custom_call_target="tpu_custom_call" | custom-call | tf_op jit(solution)/shard_map/pallas_call | solution.py:53
  61.6 0.1 collective-permute-start.5
  61.7 1.5 %collective-permute-start.9 = (bf16[2,232,256]{2,1,0:T(8,128)(2,1)S(1)}, bf16[2,232,256]{2,1,0:T(8,128)(2,1)S(1)}, u32[]{:S(2)}, u32[]{:S(2)}) collective-permute-start(bf16[2,232,256]{2,1,0:T(8,128)(2,1)S(1)} %get-tuple-element.33), channel_id=1, source_target_pairs={{0,64},{8,72},{16,80},{24,88},{32,96},{40,104},{48,112},{56,120},{... | collective-permute-start | bytes 712712 | tf_op jit(solution)/shard_map/ppermute | solution.py:251
  63.1 2.5 %shard_map.68 = (f32[2,232,256]{2,1,0:T(8,128)S(1)}, f32[2,232,256]{2,1,0:T(8,128)S(1)}) custom-call(s32[4]{0:T(128)S(1)} %pad_add_fusion.s, bf16[128,1024]{1,0:T(8,128)(2,1)S(1)} %bitcast.23, bf16[128,1024]{1,0:T(8,128)(2,1)S(1)} %collective-permute-done.2.rows_other, bf16[2,3696,256]{2,1,0:T(8,128)(2,1)} %bitcast.27, ...), custom_call_target="tpu_custom_call" | custom-call | tf_op jit(solution)/shard_map/pallas_call | solution.py:53
  65.7 0.0 collective-permute-done.7.got_b
  65.7 0.6 shard_map.70
  66.3 1.4 %collective-permute-start.10 = (bf16[2,232,256]{2,1,0:T(8,128)(2,1)S(1)}, bf16[2,232,256]{2,1,0:T(8,128)(2,1)S(1)}, u32[]{:S(2)}, u32[]{:S(2)}) collective-permute-start(bf16[2,232,256]{2,1,0:T(8,128)(2,1)S(1)} %get-tuple-element.34), channel_id=1, source_target_pairs={{0,192},{8,200},{16,208},{24,216},{32,224},{40,232},{48,240},{56,2... | collective-permute-start | bytes 712712 | tf_op jit(solution)/shard_map/ppermute | solution.py:251
  67.7 0.2 collective-permute-start.8
  67.9 2.3 %shard_map.66 = (f32[2,232,256]{2,1,0:T(8,128)S(1)}, f32[2,232,256]{2,1,0:T(8,128)S(1)}) custom-call(s32[4]{0:T(128)S(1)} %pad_add_fusion.s, bf16[128,1024]{1,0:T(8,128)(2,1)S(1)} %bitcast.24, bf16[128,1024]{1,0:T(8,128)(2,1)S(1)} %collective-permute-done.2.rows_other, bf16[2,3696,256]{2,1,0:T(8,128)(2,1)} %bitcast.28, ...), custom_call_target="tpu_custom_call" | custom-call | tf_op jit(solution)/shard_map/pallas_call | solution.py:53
  70.2 0.0 collective-permute-done.5.a1
  70.2 0.0 collective-permute-done.9.b1
  70.2 3.1 %collective-permute-done.10.b2 = bf16[2,232,256]{2,1,0:T(8,128)(2,1)S(1)} collective-permute-done((bf16[2,232,256]{2,1,0:T(8,128)(2,1)S(1)}, bf16[2,232,256]{2,1,0:T(8,128)(2,1)S(1)}, u32[]{:S(2)}, u32[]{:S(2)}) %collective-permute-start.10) | collective-permute-done | bytes 237600 | tf_op jit(solution)/shard_map/ppermute | solution.py:251
  73.3 0.6 collective-permute-done.8.a2
  73.9 0.8 shard_map.71
  74.7 0.2 collective-permute-start.11
  74.9 2.1 %collective-permute-start.12 = (bf16[232,256]{1,0:T(8,128)(2,1)S(1)}, bf16[232,256]{1,0:T(8,128)(2,1)S(1)}, u32[]{:S(2)}, u32[]{:S(2)}) collective-permute-start(bf16[232,256]{1,0:T(8,128)(2,1)S(1)} %get-tuple-element.37), channel_id=1, source_target_pairs={{0,16},{8,24},{16,32},{24,40},{32,48},{40,56},{48,0},{56,8},{64,80... | collective-permute-start | bytes 356360 | tf_op jit(solution)/shard_map/ppermute | solution.py:251
  76.9 1.6 %collective-permute-start.13 = (bf16[232,256]{1,0:T(8,128)(2,1)S(1)}, bf16[232,256]{1,0:T(8,128)(2,1)S(1)}, u32[]{:S(2)}, u32[]{:S(2)}) collective-permute-start(bf16[232,256]{1,0:T(8,128)(2,1)S(1)} %get-tuple-element.38), channel_id=1, source_target_pairs={{0,48},{8,56},{16,0},{24,8},{32,16},{40,24},{48,32},{56,40},{64,11... | collective-permute-start | bytes 356360 | tf_op jit(solution)/shard_map/ppermute | solution.py:251
  78.5 3.9 %collective-permute-done.11.a1 = bf16[232,256]{1,0:T(8,128)(2,1)S(1)} collective-permute-done((bf16[232,256]{1,0:T(8,128)(2,1)S(1)}, bf16[232,256]{1,0:T(8,128)(2,1)S(1)}, u32[]{:S(2)}, u32[]{:S(2)}) %collective-permute-start.11) | collective-permute-done | bytes 118816 | tf_op jit(solution)/shard_map/ppermute | solution.py:251
  82.4 1.3 collective-permute-done.12.a2
  83.7 4.6 %collective-permute-done.13.a3 = bf16[232,256]{1,0:T(8,128)(2,1)S(1)} collective-permute-done((bf16[232,256]{1,0:T(8,128)(2,1)S(1)}, bf16[232,256]{1,0:T(8,128)(2,1)S(1)}, u32[]{:S(2)}, u32[]{:S(2)}) %collective-permute-start.13) | collective-permute-done | bytes 118816 | tf_op jit(solution)/shard_map/ppermute | solution.py:251
  88.2 0.6 shard_map.72
  88.8 2.1 %collective-permute-start.14 = (f32[232,128]{1,0:T(8,128)S(1)}, f32[232,128]{1,0:T(8,128)S(1)}, u32[]{:S(2)}, u32[]{:S(2)}) collective-permute-start(f32[232,128]{1,0:T(8,128)S(1)} %get-tuple-element.40), channel_id=1, source_target_pairs={{0,8},{8,0},{16,24},{24,16},{32,40},{40,32},{48,56},{56,48},{64,72... | collective-permute-start | bytes 356360 | tf_op jit(solution)/shard_map/ppermute | solution.py:251
  91.0 1.0 collective-permute-done.14.got
  92.0 0.6 shard_map.73.h0
  92.6 2.4 %collective-permute-start.15 = (bf16[232,128]{1,0:T(8,128)(2,1)S(1)}, bf16[232,128]{1,0:T(8,128)(2,1)S(1)}, u32[]{:S(2)}, u32[]{:S(2)}) collective-permute-start(bf16[232,128]{1,0:T(8,128)(2,1)S(1)} %shard_map.73.h0), channel_id=1, source_target_pairs={{0,32},{8,40},{16,48},{24,56},{32,0},{40,8},{48,16},{56,24},{64,96... | collective-permute-start | bytes 178184 | tf_op jit(solution)/shard_map/ppermute | solution.py:251
  94.9 1.1 collective-permute-start.16
  96.0 3.2 %collective-permute-start.17 = (bf16[232,128]{1,0:T(8,128)(2,1)S(1)}, bf16[232,128]{1,0:T(8,128)(2,1)S(1)}, u32[]{:S(2)}, u32[]{:S(2)}) collective-permute-start(bf16[232,128]{1,0:T(8,128)(2,1)S(1)} %shard_map.73.h0), channel_id=1, source_target_pairs={{0,48},{8,56},{16,0},{24,8},{32,16},{40,24},{48,32},{56,40},{64,11... | collective-permute-start | bytes 178184 | tf_op jit(solution)/shard_map/ppermute | solution.py:251
  99.2 0.4 collective-permute-done.15.h2
  99.6 3.8 %collective-permute-done.16.h1 = bf16[232,128]{1,0:T(8,128)(2,1)S(1)} collective-permute-done((bf16[232,128]{1,0:T(8,128)(2,1)S(1)}, bf16[232,128]{1,0:T(8,128)(2,1)S(1)}, u32[]{:S(2)}, u32[]{:S(2)}) %collective-permute-start.16) | collective-permute-done | bytes 59424 | tf_op jit(solution)/shard_map/ppermute | solution.py:251
  103.4 0.6 shard_map.74.h
  104.0 1.4 %collective-permute-start.18 = (bf16[4,232,128]{2,1,0:T(8,128)(2,1)S(1)}, bf16[4,232,128]{2,1,0:T(8,128)(2,1)S(1)}, u32[]{:S(2)}, u32[]{:S(2)}) collective-permute-start(bf16[4,232,128]{2,1,0:T(8,128)(2,1)S(1)} %shard_map.74.h), channel_id=1, source_target_pairs={{0,128},{8,136},{16,144},{24,152},{32,160},{40,168},{48,176},{56,1... | collective-permute-start | bytes 712712 | tf_op jit(solution)/shard_map/ppermute | solution.py:251
  105.4 1.8 %collective-permute-start.19 = (bf16[4,232,128]{2,1,0:T(8,128)(2,1)S(1)}, bf16[4,232,128]{2,1,0:T(8,128)(2,1)S(1)}, u32[]{:S(2)}, u32[]{:S(2)}) collective-permute-start(bf16[4,232,128]{2,1,0:T(8,128)(2,1)S(1)} %shard_map.74.h), channel_id=1, source_target_pairs={{0,64},{8,72},{16,80},{24,88},{32,96},{40,104},{48,112},{56,120},{... | collective-permute-start | bytes 712712 | tf_op jit(solution)/shard_map/ppermute | solution.py:251
  107.2 0.9 collective-permute-start.20
  108.1 3.0 %shard_map.75 = (bf16[3696,512]{1,0:T(8,128)(2,1)S(1)}, f32[128,512]{1,0:T(8,128)S(1)}) custom-call(s32[4]{0:T(128)S(1)} %pad_add_fusion.s, bf16[3696,256]{1,0:T(8,128)(2,1)} %w_own.1, bf16[3696,256]{1,0:T(8,128)(2,1)} %collective-permute-done.w_other, bf16[4,232,128]{2,1,0:T(8,128)(2,1)S(1)} %shard_map.74.h), custom_call_target="tpu_custom_call" | custom-call | tf_op jit(solution)/shard_map/pallas_call | solution.py:71
  111.0 0.2 collective-permute-done.18.h2
  111.2 7.2 %collective-permute-done.19.h1 = bf16[4,232,128]{2,1,0:T(8,128)(2,1)S(1)} collective-permute-done((bf16[4,232,128]{2,1,0:T(8,128)(2,1)S(1)}, bf16[4,232,128]{2,1,0:T(8,128)(2,1)S(1)}, u32[]{:S(2)}, u32[]{:S(2)}) %collective-permute-start.19) | collective-permute-done | bytes 237600 | tf_op jit(solution)/shard_map/ppermute | solution.py:251
  118.4 1.3 shard_map.76
  119.7 9.2 %all_to_all.21.got = bf16[8,16,512]{2,1,0:T(8,128)(2,1)S(1)} all-to-all(bf16[8,16,512]{2,1,0:T(8,128)(2,1)S(1)} %shard_map.76), channel_id=1, replica_groups=mesh['task'=32,'tensor'=8] {'tensor'}, dimensions={0} | all-to-all | bytes 262144 | tf_op jit(solution)/shard_map/all_to_all | solution.py:254
  128.9 0.6 shard_map.77
  129.5 2.2 %collective-permute-start.21 = (f32[16,256]{1,0:T(8,128)S(1)}, f32[16,256]{1,0:T(8,128)S(1)}, u32[]{:S(2)}, u32[]{:S(2)}) collective-permute-start(f32[16,256]{1,0:T(8,128)S(1)} %get-tuple-element.44), channel_id=1, source_target_pairs={{0,8},{8,0},{16,24},{24,16},{32,40},{40,32},{48,56},{56,48},{64,72... | collective-permute-start | bytes 49160 | tf_op jit(solution)/shard_map/ppermute | solution.py:251
  131.6 0.8 collective-permute-done.21.got
  132.5 1.2 shard_map.78
  (12 shorter events, 0.0 us)
Async XLA Ops:
  2.2 24.4 %all-to-all-start = ((bf16[16,8,1152]{2,1,0:T(8,128)(2,1)}), bf16[16,8,1152]{2,1,0:T(8,128)(2,1)S(1)}, u32[]{:S(2)}, u32[]{:S(2)}) async-start(bf16[16,8,1152]{2,1,0:T(8,128)(2,1)} %broadcast_in_dim.10), calls=%async_computation | async-start | bytes 589824 | tf_op jit(solution)/shard_map/all_to_all | solution.py:280
  13.8 4.1 %collective-permute-start.1 = (bf16[2,1024,128]{2,1,0:T(8,128)(2,1)}, bf16[2,1024,128]{2,1,0:T(8,128)(2,1)S(1)}, u32[]{:S(2)}, u32[]{:S(2)}) collective-permute-start(bf16[2,1024,128]{2,1,0:T(8,128)(2,1)} %low_own.1), channel_id=1, source_target_pairs={{0,8},{8,0},{16,24},{24,16},{32,40},{40,32},{48,56},{56,48},{64,72... | collective-permute-start | bytes 1572872 | tf_op jit(solution)/shard_map/ppermute | solution.py:251
  14.9 11.8 %copy-start.1 = (bf16[2,1024,128]{2,1,0:T(8,128)(2,1)S(1)}, bf16[2,1024,128]{2,1,0:T(8,128)(2,1)}, u32[]{:S(2)}) copy-start(bf16[2,1024,128]{2,1,0:T(8,128)(2,1)} %low_own.1) | copy-start | bytes 1572868
  17.8 15.2 %copy-start = (bf16[2,128,3696]{1,2,0:T(8,128)(2,1)S(1)}, bf16[2,128,3696]{1,2,0:T(8,128)(2,1)}, u32[]{:S(2)}) copy-start(bf16[2,128,3696]{1,2,0:T(8,128)(2,1)} %param.11) | copy-start | bytes 5677060
  17.9 36.2 %collective-permute-start.3 = (bf16[3696,256]{1,0:T(8,128)(2,1)}, bf16[3696,256]{1,0:T(8,128)(2,1)}, u32[]{:S(2)}, u32[]{:S(2)}) collective-permute-start(bf16[3696,256]{1,0:T(8,128)(2,1)} %dynamic-slice_bitcast_fusion), channel_id=1, source_target_pairs={{0,8},{8,0},{16,24},{24,16},{32,40},{40,32},{48,56},{56,48},{64,72... | collective-permute-start | bytes 5677064 | tf_op jit(solution)/shard_map/ppermute | solution.py:251
  28.2 10.9 %all-to-all-start.1 = ((bf16[8,16,1024]{2,1,0:T(8,128)(2,1)}), bf16[8,16,1024]{2,1,0:T(8,128)(2,1)S(1)}, u32[]{:S(2)}, u32[]{:S(2)}) async-start(bf16[8,16,1024]{2,1,0:T(8,128)(2,1)} %bitcast.4), calls=%async_computation.1 | async-start | bytes 524288 | tf_op jit(solution)/shard_map/all_to_all | solution.py:254
  34.1 18.8 %collective-permute-start.4 = (bf16[3696,128]{1,0:T(8,128)(2,1)}, bf16[3696,128]{1,0:T(8,128)(2,1)S(1)}, u32[]{:S(2)}, u32[]{:S(2)}) collective-permute-start(bf16[3696,128]{1,0:T(8,128)(2,1)} %dynamic-slice_bitcast_fusion.1), channel_id=1, source_target_pairs={{0,8},{8,0},{16,24},{24,16},{32,40},{40,32},{48,56},{56,48},{64,72... | collective-permute-start | bytes 2838536 | tf_op jit(solution)/shard_map/ppermute | solution.py:251
  36.3 71.8 %collective-permute-start = (bf16[3696,256]{1,0:T(8,128)(2,1)}, bf16[3696,256]{1,0:T(8,128)(2,1)}, u32[]{:S(2)}, u32[]{:S(2)}) collective-permute-start(bf16[3696,256]{1,0:T(8,128)(2,1)} %w_own.1), channel_id=1, source_target_pairs={{0,8},{8,0},{16,24},{24,16},{32,40},{40,32},{48,56},{56,48},{64,72... | collective-permute-start | bytes 5677064 | tf_op jit(solution)/shard_map/ppermute | solution.py:251
  48.4 5.6 %collective-permute-start.2 = (bf16[128,1024]{1,0:T(8,128)(2,1)S(1)}, bf16[128,1024]{1,0:T(8,128)(2,1)S(1)}, u32[]{:S(2)}, u32[]{:S(2)}) collective-permute-start(bf16[128,1024]{1,0:T(8,128)(2,1)S(1)} %bitcast.20), channel_id=1, source_target_pairs={{0,8},{8,0},{16,24},{24,16},{32,40},{40,32},{48,56},{56,48},{64,72... | collective-permute-start | bytes 786440 | tf_op jit(solution)/shard_map/ppermute | solution.py:251
  56.3 9.4 %collective-permute-start.6 = (bf16[2,232,256]{2,1,0:T(8,128)(2,1)S(1)}, bf16[2,232,256]{2,1,0:T(8,128)(2,1)S(1)}, u32[]{:S(2)}, u32[]{:S(2)}) collective-permute-start(bf16[2,232,256]{2,1,0:T(8,128)(2,1)S(1)} %get-tuple-element.28), channel_id=1, source_target_pairs={{0,64},{8,72},{16,80},{24,88},{32,96},{40,104},{48,112},{56,120},{... | collective-permute-start | bytes 712712 | tf_op jit(solution)/shard_map/ppermute | solution.py:251
  56.4 9.3 %collective-permute-start.7 = (bf16[2,232,256]{2,1,0:T(8,128)(2,1)S(1)}, bf16[2,232,256]{2,1,0:T(8,128)(2,1)S(1)}, u32[]{:S(2)}, u32[]{:S(2)}) collective-permute-start(bf16[2,232,256]{2,1,0:T(8,128)(2,1)S(1)} %get-tuple-element.30), channel_id=1, source_target_pairs={{0,192},{8,200},{16,208},{24,216},{32,224},{40,232},{48,240},{56,2... | collective-permute-start | bytes 712712 | tf_op jit(solution)/shard_map/ppermute | solution.py:251
  61.6 8.6 %collective-permute-start.5 = (bf16[2,232,256]{2,1,0:T(8,128)(2,1)S(1)}, bf16[2,232,256]{2,1,0:T(8,128)(2,1)S(1)}, u32[]{:S(2)}, u32[]{:S(2)}) collective-permute-start(bf16[2,232,256]{2,1,0:T(8,128)(2,1)S(1)} %get-tuple-element.26), channel_id=1, source_target_pairs={{0,192},{8,200},{16,208},{24,216},{32,224},{40,232},{48,240},{56,2... | collective-permute-start | bytes 712712 | tf_op jit(solution)/shard_map/ppermute | solution.py:251
  61.7 8.5 %collective-permute-start.9 = (bf16[2,232,256]{2,1,0:T(8,128)(2,1)S(1)}, bf16[2,232,256]{2,1,0:T(8,128)(2,1)S(1)}, u32[]{:S(2)}, u32[]{:S(2)}) collective-permute-start(bf16[2,232,256]{2,1,0:T(8,128)(2,1)S(1)} %get-tuple-element.33), channel_id=1, source_target_pairs={{0,64},{8,72},{16,80},{24,88},{32,96},{40,104},{48,112},{56,120},{... | collective-permute-start | bytes 712712 | tf_op jit(solution)/shard_map/ppermute | solution.py:251
  66.3 6.9 %collective-permute-start.10 = (bf16[2,232,256]{2,1,0:T(8,128)(2,1)S(1)}, bf16[2,232,256]{2,1,0:T(8,128)(2,1)S(1)}, u32[]{:S(2)}, u32[]{:S(2)}) collective-permute-start(bf16[2,232,256]{2,1,0:T(8,128)(2,1)S(1)} %get-tuple-element.34), channel_id=1, source_target_pairs={{0,192},{8,200},{16,208},{24,216},{32,224},{40,232},{48,240},{56,2... | collective-permute-start | bytes 712712 | tf_op jit(solution)/shard_map/ppermute | solution.py:251
  67.7 6.2 %collective-permute-start.8 = (bf16[2,232,256]{2,1,0:T(8,128)(2,1)S(1)}, bf16[2,232,256]{2,1,0:T(8,128)(2,1)S(1)}, u32[]{:S(2)}, u32[]{:S(2)}) collective-permute-start(bf16[2,232,256]{2,1,0:T(8,128)(2,1)S(1)} %get-tuple-element.31), channel_id=1, source_target_pairs={{0,64},{8,72},{16,80},{24,88},{32,96},{40,104},{48,112},{56,120},{... | collective-permute-start | bytes 712712 | tf_op jit(solution)/shard_map/ppermute | solution.py:251
  74.7 7.7 %collective-permute-start.11 = (bf16[232,256]{1,0:T(8,128)(2,1)S(1)}, bf16[232,256]{1,0:T(8,128)(2,1)S(1)}, u32[]{:S(2)}, u32[]{:S(2)}) collective-permute-start(bf16[232,256]{1,0:T(8,128)(2,1)S(1)} %get-tuple-element.36), channel_id=1, source_target_pairs={{0,32},{8,40},{16,48},{24,56},{32,0},{40,8},{48,16},{56,24},{64,96... | collective-permute-start | bytes 356360 | tf_op jit(solution)/shard_map/ppermute | solution.py:251
  74.9 8.8 %collective-permute-start.12 = (bf16[232,256]{1,0:T(8,128)(2,1)S(1)}, bf16[232,256]{1,0:T(8,128)(2,1)S(1)}, u32[]{:S(2)}, u32[]{:S(2)}) collective-permute-start(bf16[232,256]{1,0:T(8,128)(2,1)S(1)} %get-tuple-element.37), channel_id=1, source_target_pairs={{0,16},{8,24},{16,32},{24,40},{32,48},{40,56},{48,0},{56,8},{64,80... | collective-permute-start | bytes 356360 | tf_op jit(solution)/shard_map/ppermute | solution.py:251
  76.9 11.3 %collective-permute-start.13 = (bf16[232,256]{1,0:T(8,128)(2,1)S(1)}, bf16[232,256]{1,0:T(8,128)(2,1)S(1)}, u32[]{:S(2)}, u32[]{:S(2)}) collective-permute-start(bf16[232,256]{1,0:T(8,128)(2,1)S(1)} %get-tuple-element.38), channel_id=1, source_target_pairs={{0,48},{8,56},{16,0},{24,8},{32,16},{40,24},{48,32},{56,40},{64,11... | collective-permute-start | bytes 356360 | tf_op jit(solution)/shard_map/ppermute | solution.py:251
  88.8 3.1 %collective-permute-start.14 = (f32[232,128]{1,0:T(8,128)S(1)}, f32[232,128]{1,0:T(8,128)S(1)}, u32[]{:S(2)}, u32[]{:S(2)}) collective-permute-start(f32[232,128]{1,0:T(8,128)S(1)} %get-tuple-element.40), channel_id=1, source_target_pairs={{0,8},{8,0},{16,24},{24,16},{32,40},{40,32},{48,56},{56,48},{64,72... | collective-permute-start | bytes 356360 | tf_op jit(solution)/shard_map/ppermute | solution.py:251
  92.6 7.0 %collective-permute-start.15 = (bf16[232,128]{1,0:T(8,128)(2,1)S(1)}, bf16[232,128]{1,0:T(8,128)(2,1)S(1)}, u32[]{:S(2)}, u32[]{:S(2)}) collective-permute-start(bf16[232,128]{1,0:T(8,128)(2,1)S(1)} %shard_map.73.h0), channel_id=1, source_target_pairs={{0,32},{8,40},{16,48},{24,56},{32,0},{40,8},{48,16},{56,24},{64,96... | collective-permute-start | bytes 178184 | tf_op jit(solution)/shard_map/ppermute | solution.py:251
  94.9 8.5 %collective-permute-start.16 = (bf16[232,128]{1,0:T(8,128)(2,1)S(1)}, bf16[232,128]{1,0:T(8,128)(2,1)S(1)}, u32[]{:S(2)}, u32[]{:S(2)}) collective-permute-start(bf16[232,128]{1,0:T(8,128)(2,1)S(1)} %shard_map.73.h0), channel_id=1, source_target_pairs={{0,16},{8,24},{16,32},{24,40},{32,48},{40,56},{48,0},{56,8},{64,80... | collective-permute-start | bytes 178184 | tf_op jit(solution)/shard_map/ppermute | solution.py:251
  96.0 7.4 %collective-permute-start.17 = (bf16[232,128]{1,0:T(8,128)(2,1)S(1)}, bf16[232,128]{1,0:T(8,128)(2,1)S(1)}, u32[]{:S(2)}, u32[]{:S(2)}) collective-permute-start(bf16[232,128]{1,0:T(8,128)(2,1)S(1)} %shard_map.73.h0), channel_id=1, source_target_pairs={{0,48},{8,56},{16,0},{24,8},{32,16},{40,24},{48,32},{56,40},{64,11... | collective-permute-start | bytes 178184 | tf_op jit(solution)/shard_map/ppermute | solution.py:251
  104.0 7.2 %collective-permute-start.18 = (bf16[4,232,128]{2,1,0:T(8,128)(2,1)S(1)}, bf16[4,232,128]{2,1,0:T(8,128)(2,1)S(1)}, u32[]{:S(2)}, u32[]{:S(2)}) collective-permute-start(bf16[4,232,128]{2,1,0:T(8,128)(2,1)S(1)} %shard_map.74.h), channel_id=1, source_target_pairs={{0,128},{8,136},{16,144},{24,152},{32,160},{40,168},{48,176},{56,1... | collective-permute-start | bytes 712712 | tf_op jit(solution)/shard_map/ppermute | solution.py:251
  105.4 13.0 %collective-permute-start.19 = (bf16[4,232,128]{2,1,0:T(8,128)(2,1)S(1)}, bf16[4,232,128]{2,1,0:T(8,128)(2,1)S(1)}, u32[]{:S(2)}, u32[]{:S(2)}) collective-permute-start(bf16[4,232,128]{2,1,0:T(8,128)(2,1)S(1)} %shard_map.74.h), channel_id=1, source_target_pairs={{0,64},{8,72},{16,80},{24,88},{32,96},{40,104},{48,112},{56,120},{... | collective-permute-start | bytes 712712 | tf_op jit(solution)/shard_map/ppermute | solution.py:251
  107.2 11.2 %collective-permute-start.20 = (bf16[4,232,128]{2,1,0:T(8,128)(2,1)S(1)}, bf16[4,232,128]{2,1,0:T(8,128)(2,1)S(1)}, u32[]{:S(2)}, u32[]{:S(2)}) collective-permute-start(bf16[4,232,128]{2,1,0:T(8,128)(2,1)S(1)} %shard_map.74.h), channel_id=1, source_target_pairs={{0,192},{8,200},{16,208},{24,216},{32,224},{40,232},{48,240},{56,2... | collective-permute-start | bytes 712712 | tf_op jit(solution)/shard_map/ppermute | solution.py:251
  129.5 3.0 %collective-permute-start.21 = (f32[16,256]{1,0:T(8,128)S(1)}, f32[16,256]{1,0:T(8,128)S(1)}, u32[]{:S(2)}, u32[]{:S(2)}) collective-permute-start(f32[16,256]{1,0:T(8,128)S(1)} %get-tuple-element.44), channel_id=1, source_target_pairs={{0,8},{8,0},{16,24},{24,16},{32,40},{40,32},{48,56},{56,48},{64,72... | collective-permute-start | bytes 49160 | tf_op jit(solution)/shard_map/ppermute | solution.py:251

commit v6 on v5

--- a/solution.py
+++ b/solution.py
@@ -13,6 +13,7 @@
 NX, NZ, NC = 4, 4, 2
 NQ = NX * NZ
 VMEM_BYTES = 48 * 1024 * 1024
+JOIN_BYTES = 46 * 1024 * 1024
 INSIDE_BYTES = 24 * 1024 * 1024
 
 
@@ -122,7 +123,7 @@
 
 
 def main_kernel(limit, d, s, rows_own, rows_other, w_own, w_other, u_own, u_other, out_a, out_b):
-    w = jnp.concatenate([w_own[0], w_other[...], u_own[0], u_other[...]], axis=1)
+    w = jnp.concatenate([w_own[0], w_other[0], u_own[0], u_other[0]], axis=1)
     rows = token_rows(rows_own, rows_other)
     p = lax.dot_general(w, rows, (((1,), (1,)), ((), ())), preferred_element_type=F32)
     n = p.shape[0]
@@ -133,25 +134,54 @@
         out[k % 2] = p[k * m : (k + 1) * m].astype(out.dtype)
 
 
-def near_kernel(limit, halves, s, rows_own, rows_other, w_own, w_other, u_own, u_other, *outs):
-    i = pl.program_id(0)
-    w = jnp.concatenate([w_own[0], w_other[...], u_own[0], u_other[...]], axis=1)
+def weights_kernel(d, s, w_own, w_other, u_own, u_other, out, sems):
+    deep, limit = out.shape[0], w_other.shape[0]
+    spare = NX * deep - limit
+    copies = []
+    start = lax.rem(s[0] + d, NX) * deep
+    col = 0
+    for n, ref in enumerate((w_own.at[s[2]], w_other, u_own.at[s[2]], u_other)):
+        cols = pl.ds(col, ref.shape[1])
+        col += ref.shape[1]
+        for h, (a, b) in enumerate(((0, deep - spare), (deep - spare, deep))):
+            first = jnp.minimum(start + a, limit - (b - a))
+            copies.append(
+                pltpu.make_async_copy(
+                    ref.at[pl.ds(pl.multiple_of(first, 16), b - a)],
+                    out.at[pl.ds(a, b - a), cols],
+                    sems.at[n, h],
+                )
+            )
+    for copy in copies:
+        copy.start()
+    for copy in copies:
+        copy.wait()
+
+
+def far_kernel(s, rows_own, rows_other, w, *outs):
     rows = token_rows(rows_own, rows_other)
-    p = lax.dot_general(w, rows, (((1,), (1,)), ((), ())), preferred_element_type=F32)
-    n = p.shape[0]
-    at = half_block(halves, i, s) * n + lax.broadcasted_iota(jnp.int32, p.shape, 0)
-    p = jnp.where(at < limit, p, 0.0)
+    p = lax.dot_general(w[...], rows, (((1,), (1,)), ((), ())), preferred_element_type=F32)
+    n = outs[0].shape[1]
+    for k in range(4):
+        outs[k // 2][k % 2] = p[k * n : (k + 1) * n].astype(outs[0].dtype)
+
+
+def near_kernel(limit, halves, s, rows_own, rows_other, *rest):
+    weights, outs = rest[:-2], rest[-2:]
+    rows = token_rows(rows_own, rows_other)
     for k, out in enumerate(outs):
-
-        @pl.when(i == k)
-        def _():
-            out[0] = p[: n // 2].astype(out.dtype)
-            out[1] = p[n // 2 :].astype(out.dtype)
-
-
-def half_block(halves, i, s):
-    (d, h), (e, g) = halves
-    return lax.rem(s[0] + jnp.where(i == 0, d, e), NX) * 2 + jnp.where(i == 0, h, g)
+        w = jnp.concatenate([weights[2 * i + k][0] for i in range(4)], axis=1)
+        p = lax.dot_general(w, rows, (((1,), (1,)), ((), ())), preferred_element_type=F32)
+        n = p.shape[0]
+        at = half_block(halves[k], s) * n + lax.broadcasted_iota(jnp.int32, p.shape, 0)
+        p = jnp.where(at < limit, p, 0.0)
+        out[0] = p[: n // 2].astype(out.dtype)
+        out[1] = p[n // 2 :].astype(out.dtype)
+
+
+def half_block(half, s):
+    d, h = half
+    return lax.rem(s[0] + d, NX) * 2 + h
 
 
 def pass_kernel(s, a, got_a, b, got_b, out_a, out_b):
@@ -293,42 +323,46 @@
     cat_other = permute(cat, CORE)
     inside = functools.partial(call_inside, scalars=s)
 
-    def product(kernel, block, at, dtype, steps=1):
-        def own_spec(a):
-            return pl.BlockSpec((1, block, a.shape[2]), lambda i, s: (s[2], at(i, s), 0))
-
-        def spec(a):
-            return pl.BlockSpec((block, a.shape[1]), lambda i, s: (at(i, s), 0))
-
+    joined = (weight, w_other[None], upper, u_other[None])
+
+    def spec(a, block, at):
+        def index(i, s):
+            return (s[2] if a.shape[0] > 1 else 0, at(s), 0)
+
+        return pl.BlockSpec((1, block, a.shape[2]), index)
+
+    def product(kernel, specs, args, dtype):
         return run(
             kernel,
             [sds((2, zb, count), dtype)] * 2,
             cat,
             cat_other,
-            weight,
-            w_other,
-            upper,
-            u_other,
-            grid=(steps,),
-            in_specs=[
-                whole(cat),
-                whole(cat_other),
-                own_spec(weight),
-                spec(w_other),
-                own_spec(upper),
-                spec(u_other),
-            ],
+            *args,
+            in_specs=[whole(cat), whole(cat_other)] + specs,
         )
 
     def main(d, dtype):
-        kernel = functools.partial(main_kernel, hid, d)
-        return product(kernel, xb, lambda i, s: lax.rem(s[0] + d, NX), dtype)
+        specs = [spec(a, xb, lambda s: lax.rem(s[0] + d, NX)) for a in joined]
+        return product(functools.partial(main_kernel, hid, d), specs, joined, dtype)
 
     def near(halves, dtype):
-        kernel = functools.partial(near_kernel, hid, halves)
-        return product(kernel, xb // 2, functools.partial(half_block, halves), dtype, 2)
-
-    far_a, far_b = main(2, BF16)
+        specs, args = [], []
+        for a in joined:
+            for half_at in halves:
+                specs.append(spec(a, xb // 2, functools.partial(half_block, half_at)))
+                args.append(a)
+        return product(functools.partial(near_kernel, hid, halves), specs, args, dtype)
+
+    far = pl.pallas_call(
+        functools.partial(weights_kernel, 2),
+        out_shape=sds((xb, feats + ranks)),
+        in_specs=[pl.BlockSpec(memory_space=pltpu.SMEM)]
+        + [pl.BlockSpec(memory_space=pl.ANY)] * 4,
+        out_specs=pl.BlockSpec(memory_space=pl.ANY),
+        scratch_shapes=[pltpu.SemaphoreType.DMA((4, 2))],
+        compiler_params=pltpu.CompilerParams(vmem_limit_bytes=JOIN_BYTES),
+    )(s, weight, w_other, upper, u_other)
+    far_a, far_b = run(far_kernel, [sds((2, zb, count))] * 2, cat, cat_other, far)
     far_a = permute(far_a, TO_X[1])
     far_b = permute(far_b, TO_X[3])
     up_b, down_a = near(((1, 1), (3, 0)), BF16)

time: 134 us -> 134 us (level)
  starting transfers between devices: 48.9 us -> 46.5 us
  waiting for transfers between devices: 39.5 us -> 41.3 us
    ppermute x22, starting transfers between devices: 32.5 us -> 30.1 us  [permute(): return lax.ppermute(a, 'task', perm)]
    pallas_call x0 -> x1, Pallas kernels: none -> 1.81 us  [on_device(): pl.pallas_call(functools.partial(weights_kernel, 2), out_shape=sds((xb, f...]
    ppermute x22, waiting for transfers between devices: 27.9 us -> 29.7 us  [permute(): return lax.ppermute(a, 'task', perm)]
    pallas_call x13, Pallas kernels: 16.6 us -> 15.2 us  [call(): pl.pallas_call(kernel, out_shape=out_shape, grid_spec=pltpu.PrefetchScala...]
  transfers between devices with their start and end apart: 24 -> 24, of which waited for: 14 -> 14; matrix products, arithmetic and copies ran while one was open for 3% -> 3% of each run, Pallas kernels for 13% -> 14%
where the time goes in v6:
time: 134 us; the launch traced here: 133 us
  starting transfers between devices  46.5 us (35%)
  waiting for transfers between devices  41.3 us (31%)
  Pallas kernels  21.3 us (16%)
  blocking collectives  17.8 us (13%)
  local copies, waits for them, and re-layouts  5.56 us (4%)
    ppermute x22, starting transfers between devices, permute(): return lax.ppermute(a, 'task', perm)  30.1 us
    ppermute x22, waiting for transfers between devices, permute(): return lax.ppermute(a, 'task', perm)  29.7 us
    all_to_all x2, blocking collectives, across(): return lax.all_to_all(a, 'tensor', 0, 0)  17.8 us
    pallas_call x13, Pallas kernels, call(): pl.pallas_call(kernel, out_shape=out_shape, grid_spec=pltpu.PrefetchScala...  15.2 us
    all_to_all x1, starting transfers between devices, on_device(): own_rows = lax.all_to_all(packed, 'task', 0, 0, axis_index_groups=CHIPS)  11.6 us
    all_to_all x1, waiting for transfers between devices, on_device(): own_rows = lax.all_to_all(packed, 'task', 0, 0, axis_index_groups=CHIPS)  8.7 us
    all_to_all x1, starting transfers between devices, across(): return lax.all_to_all(a, 'tensor', 0, 0)  4.81 us
    pallas_call x2, Pallas kernels, call_inside(): pl.pallas_call(kernel, out_shape=out_shape, in_specs=[pl.BlockSpec(memory...  4.29 us
  transfers between devices with their start and end apart: 24, of which 14 were waited for; matrix products, arithmetic and copies ran while one was open for 3% of the time, Pallas kernels for 14%

profile of v6, /device:TPU:1, one launch (start us, length us, event | category | flops | bytes accessed | tf_op | source)
XLA Modules:
  0.0 133.4 jit_solution(555678912114664719)
XLA Ops:
  0.0 0.7 fusion
  0.7 0.8 concatenate.3
  1.5 0.7 broadcast_in_dim.16
  2.2 11.6 %all-to-all-start = ((bf16[16,8,1152]{2,1,0:T(8,128)(2,1)}), bf16[16,8,1152]{2,1,0:T(8,128)(2,1)S(1)}, u32[]{:S(2)}, u32[]{:S(2)}) async-start(bf16[16,8,1152]{2,1,0:T(8,128)(2,1)} %broadcast_in_dim.16), calls=%async_computation | async-start | bytes 589824 | tf_op jit(solution)/shard_map/all_to_all | solution.py:310
  13.8 1.0 collective-permute-start.1
  14.9 3.0 %dynamic-slice_bitcast_fusion = bf16[3696,256]{1,0:T(8,128)(2,1)} fusion(bf16[2,256,3696]{1,2,0:T(8,128)(2,1)} %param.8, s32[]{:T(128)S(6)} %select_n.16), kind=kLoop, calls=%fused_computation | loop fusion | bytes 3784708 | tf_op jit(solution)/shard_map/jit(dynamic_index_in_dim)/squeeze | solution.py:287
  17.9 0.0 collective-permute-start.3
  17.9 0.1 pad_add_fusion.s
  18.0 0.0 collective-permute-done.1.low_other
  18.0 8.7 %all-to-all-done.tokens = bf16[16,8,1152]{2,1,0:T(8,128)(2,1)S(1)} async-done(((bf16[16,8,1152]{2,1,0:T(8,128)(2,1)}), bf16[16,8,1152]{2,1,0:T(8,128)(2,1)S(1)}, u32[]{:S(2)}, u32[]{:S(2)}) %all-to-all-start) | async-done | bytes 294944 | tf_op jit(solution)/shard_map/all_to_all | solution.py:310
  26.7 1.6 %shard_map.64 = bf16[128,1024]{1,0:T(8,128)(2,1)} custom-call(s32[4]{0:T(128)S(1)} %pad_add_fusion.s, bf16[16,8,1152]{2,1,0:T(8,128)(2,1)S(1)} %all-to-all-done.tokens, bf16[2,1024,128]{2,1,0:T(8,128)(2,1)S(1)} %copy-done.1, bf16[2,1024,128]{2,1,0:T(8,128)(2,1)S(1)} %collective-permute-done.1.low_other), custom_call_target="tpu_custom_call" | custom-call | tf_op jit(solution)/shard_map/pallas_call | solution.py:54
  28.2 4.8 %all-to-all-start.1 = ((bf16[8,16,1024]{2,1,0:T(8,128)(2,1)}), bf16[8,16,1024]{2,1,0:T(8,128)(2,1)S(1)}, u32[]{:S(2)}, u32[]{:S(2)}) async-start(bf16[8,16,1024]{2,1,0:T(8,128)(2,1)} %bitcast.4), calls=%async_computation.1 | async-start | bytes 524288 | tf_op jit(solution)/shard_map/all_to_all | solution.py:284
  33.1 1.0 dynamic-slice_bitcast_fusion.1
  34.1 2.2 %collective-permute-start.4 = (bf16[3696,128]{1,0:T(8,128)(2,1)}, bf16[3696,128]{1,0:T(8,128)(2,1)S(1)}, u32[]{:S(2)}, u32[]{:S(2)}) collective-permute-start(bf16[3696,128]{1,0:T(8,128)(2,1)} %dynamic-slice_bitcast_fusion.1), channel_id=1, source_target_pairs={{0,8},{8,0},{16,24},{24,16},{32,40},{40,32},{48,56},{56,48},{64,72... | collective-permute-start | bytes 2838536 | tf_op jit(solution)/shard_map/ppermute | solution.py:281
  36.3 0.0 collective-permute-start
  36.3 2.9 %all-to-all-done.1.got = bf16[8,16,1024]{2,1,0:T(8,128)(2,1)S(1)} async-done(((bf16[8,16,1024]{2,1,0:T(8,128)(2,1)}), bf16[8,16,1024]{2,1,0:T(8,128)(2,1)S(1)}, u32[]{:S(2)}, u32[]{:S(2)}) %all-to-all-start.1) | async-done | bytes 262176 | tf_op jit(solution)/shard_map/all_to_all | solution.py:284
  39.1 0.6 shard_map.65
  39.7 8.7 %all_to_all.20 = bf16[8,16,1024]{2,1,0:T(8,128)(2,1)S(1)} all-to-all(bf16[8,16,1024]{2,1,0:T(8,128)(2,1)S(1)} %shard_map.65), channel_id=1, replica_groups=mesh['task'=32,'tensor'=8] {'tensor'}, dimensions={0} | all-to-all | bytes 524288 | tf_op jit(solution)/shard_map/all_to_all | solution.py:284
  48.4 4.5 %collective-permute-start.2 = (bf16[128,1024]{1,0:T(8,128)(2,1)S(1)}, bf16[128,1024]{1,0:T(8,128)(2,1)S(1)}, u32[]{:S(2)}, u32[]{:S(2)}) collective-permute-start(bf16[128,1024]{1,0:T(8,128)(2,1)S(1)} %bitcast.29), channel_id=1, source_target_pairs={{0,8},{8,0},{16,24},{24,16},{32,40},{40,32},{48,56},{56,48},{64,72... | collective-permute-start | bytes 786440 | tf_op jit(solution)/shard_map/ppermute | solution.py:281
  52.9 1.8 %shard_map.69.w = bf16[928,768]{1,0:T(8,128)(2,1)S(1)} custom-call(s32[4]{0:T(128)S(1)} %pad_add_fusion.s, bf16[2,3696,256]{2,1,0:T(8,128)(2,1)} %bitcast.34, bf16[3696,256]{1,0:T(8,128)(2,1)} %collective-permute-done.3.w_other, bf16[2,3696,128]{2,1,0:T(8,128)(2,1)S(1)} %bitcast.18, bf16[3696,128]{1,0:T(8,128)(2,1)S(1)} %collective-permute-done.4.u_other), custom_call_target="tpu_custom_call" | custom-call | tf_op jit(solution)/shard_map/pallas_call | solution.py:356
  54.7 0.0 collective-permute-done.2.rows_other
  54.7 1.1 shard_map.70
  55.8 0.1 collective-permute-start.6
  55.9 2.7 %collective-permute-start.7 = (bf16[2,232,256]{2,1,0:T(8,128)(2,1)S(1)}, bf16[2,232,256]{2,1,0:T(8,128)(2,1)S(1)}, u32[]{:S(2)}, u32[]{:S(2)}) collective-permute-start(bf16[2,232,256]{2,1,0:T(8,128)(2,1)S(1)} %get-tuple-element.30), channel_id=1, source_target_pairs={{0,192},{8,200},{16,208},{24,216},{32,224},{40,232},{48,240},{56,2... | collective-permute-start | bytes 712712 | tf_op jit(solution)/shard_map/ppermute | solution.py:281
  58.6 2.4 %shard_map.67 = (bf16[2,232,256]{2,1,0:T(8,128)(2,1)S(1)}, bf16[2,232,256]{2,1,0:T(8,128)(2,1)S(1)}) custom-call(s32[4]{0:T(128)S(1)} %pad_add_fusion.s, bf16[128,1024]{1,0:T(8,128)(2,1)S(1)} %bitcast.31, bf16[128,1024]{1,0:T(8,128)(2,1)S(1)} %collective-permute-done.2.rows_other, bf16[2,3696,256]{2,1,0:T(8,128)(2,1)} %bitcast.35, ...), custom_call_target="tpu_custom_call" | custom-call | tf_op jit(solution)/shard_map/pallas_call | solution.py:54
  61.0 0.1 collective-permute-start.5
  61.1 1.5 %collective-permute-start.9 = (bf16[2,232,256]{2,1,0:T(8,128)(2,1)S(1)}, bf16[2,232,256]{2,1,0:T(8,128)(2,1)S(1)}, u32[]{:S(2)}, u32[]{:S(2)}) collective-permute-start(bf16[2,232,256]{2,1,0:T(8,128)(2,1)S(1)} %get-tuple-element.33), channel_id=1, source_target_pairs={{0,64},{8,72},{16,80},{24,88},{32,96},{40,104},{48,112},{56,120},{... | collective-permute-start | bytes 712712 | tf_op jit(solution)/shard_map/ppermute | solution.py:281
  62.5 2.4 %shard_map.68 = (f32[2,232,256]{2,1,0:T(8,128)S(1)}, f32[2,232,256]{2,1,0:T(8,128)S(1)}) custom-call(s32[4]{0:T(128)S(1)} %pad_add_fusion.s, bf16[128,1024]{1,0:T(8,128)(2,1)S(1)} %bitcast.32, bf16[128,1024]{1,0:T(8,128)(2,1)S(1)} %collective-permute-done.2.rows_other, bf16[2,3696,256]{2,1,0:T(8,128)(2,1)} %bitcast.37, bf16[2,3696,256]{2,1,0:T(8,128)(2,1)} %bitcast.38, ...), custom_call_target="tpu_custom_call" | custom-call | tf_op jit(solution)/shard_map/pallas_call | solution.py:54
  64.9 0.0 collective-permute-done.6.got_a
  65.0 0.6 shard_map.71
  65.6 2.0 %collective-permute-start.10 = (bf16[2,232,256]{2,1,0:T(8,128)(2,1)S(1)}, bf16[2,232,256]{2,1,0:T(8,128)(2,1)S(1)}, u32[]{:S(2)}, u32[]{:S(2)}) collective-permute-start(bf16[2,232,256]{2,1,0:T(8,128)(2,1)S(1)} %get-tuple-element.34), channel_id=1, source_target_pairs={{0,192},{8,200},{16,208},{24,216},{32,224},{40,232},{48,240},{56,2... | collective-permute-start | bytes 712712 | tf_op jit(solution)/shard_map/ppermute | solution.py:281
  67.6 2.3 %shard_map.66 = (f32[2,232,256]{2,1,0:T(8,128)S(1)}, f32[2,232,256]{2,1,0:T(8,128)S(1)}) custom-call(s32[4]{0:T(128)S(1)} %pad_add_fusion.s, bf16[128,1024]{1,0:T(8,128)(2,1)S(1)} %bitcast.33, bf16[128,1024]{1,0:T(8,128)(2,1)S(1)} %collective-permute-done.2.rows_other, bf16[2,3696,256]{2,1,0:T(8,128)(2,1)} %bitcast.39, ...), custom_call_target="tpu_custom_call" | custom-call | tf_op jit(solution)/shard_map/pallas_call | solution.py:54
  69.9 3.3 %collective-permute-done.10.b2 = bf16[2,232,256]{2,1,0:T(8,128)(2,1)S(1)} collective-permute-done((bf16[2,232,256]{2,1,0:T(8,128)(2,1)S(1)}, bf16[2,232,256]{2,1,0:T(8,128)(2,1)S(1)}, u32[]{:S(2)}, u32[]{:S(2)}) %collective-permute-start.10) | collective-permute-done | bytes 237600 | tf_op jit(solution)/shard_map/ppermute | solution.py:281
  73.2 0.6 collective-permute-done.8.a2
  73.7 0.8 shard_map.72
  74.5 0.2 collective-permute-start.11
  74.7 2.1 %collective-permute-start.12 = (bf16[232,256]{1,0:T(8,128)(2,1)S(1)}, bf16[232,256]{1,0:T(8,128)(2,1)S(1)}, u32[]{:S(2)}, u32[]{:S(2)}) collective-permute-start(bf16[232,256]{1,0:T(8,128)(2,1)S(1)} %get-tuple-element.37), channel_id=1, source_target_pairs={{0,16},{8,24},{16,32},{24,40},{32,48},{40,56},{48,0},{56,8},{64,80... | collective-permute-start | bytes 356360 | tf_op jit(solution)/shard_map/ppermute | solution.py:281
  76.8 1.6 %collective-permute-start.13 = (bf16[232,256]{1,0:T(8,128)(2,1)S(1)}, bf16[232,256]{1,0:T(8,128)(2,1)S(1)}, u32[]{:S(2)}, u32[]{:S(2)}) collective-permute-start(bf16[232,256]{1,0:T(8,128)(2,1)S(1)} %get-tuple-element.38), channel_id=1, source_target_pairs={{0,48},{8,56},{16,0},{24,8},{32,16},{40,24},{48,32},{56,40},{64,11... | collective-permute-start | bytes 356360 | tf_op jit(solution)/shard_map/ppermute | solution.py:281
  78.4 3.9 %collective-permute-done.11.a1 = bf16[232,256]{1,0:T(8,128)(2,1)S(1)} collective-permute-done((bf16[232,256]{1,0:T(8,128)(2,1)S(1)}, bf16[232,256]{1,0:T(8,128)(2,1)S(1)}, u32[]{:S(2)}, u32[]{:S(2)}) %collective-permute-start.11) | collective-permute-done | bytes 118816 | tf_op jit(solution)/shard_map/ppermute | solution.py:281
  82.2 1.6 %collective-permute-done.12.a2 = bf16[232,256]{1,0:T(8,128)(2,1)S(1)} collective-permute-done((bf16[232,256]{1,0:T(8,128)(2,1)S(1)}, bf16[232,256]{1,0:T(8,128)(2,1)S(1)}, u32[]{:S(2)}, u32[]{:S(2)}) %collective-permute-start.12) | collective-permute-done | bytes 118816 | tf_op jit(solution)/shard_map/ppermute | solution.py:281
  83.8 6.1 %collective-permute-done.13.a3 = bf16[232,256]{1,0:T(8,128)(2,1)S(1)} collective-permute-done((bf16[232,256]{1,0:T(8,128)(2,1)S(1)}, bf16[232,256]{1,0:T(8,128)(2,1)S(1)}, u32[]{:S(2)}, u32[]{:S(2)}) %collective-permute-start.13) | collective-permute-done | bytes 118816 | tf_op jit(solution)/shard_map/ppermute | solution.py:281
  90.0 0.6 shard_map.73
  90.6 0.7 collective-permute-start.14
  91.3 1.0 collective-permute-done.14.got
  92.2 0.6 shard_map.74.h0
  92.8 1.6 %collective-permute-start.15 = (bf16[232,128]{1,0:T(8,128)(2,1)S(1)}, bf16[232,128]{1,0:T(8,128)(2,1)S(1)}, u32[]{:S(2)}, u32[]{:S(2)}) collective-permute-start(bf16[232,128]{1,0:T(8,128)(2,1)S(1)} %shard_map.74.h0), channel_id=1, source_target_pairs={{0,32},{8,40},{16,48},{24,56},{32,0},{40,8},{48,16},{56,24},{64,96... | collective-permute-start | bytes 178184 | tf_op jit(solution)/shard_map/ppermute | solution.py:281
  94.5 1.2 collective-permute-start.16
  95.7 2.4 %collective-permute-start.17 = (bf16[232,128]{1,0:T(8,128)(2,1)S(1)}, bf16[232,128]{1,0:T(8,128)(2,1)S(1)}, u32[]{:S(2)}, u32[]{:S(2)}) collective-permute-start(bf16[232,128]{1,0:T(8,128)(2,1)S(1)} %shard_map.74.h0), channel_id=1, source_target_pairs={{0,48},{8,56},{16,0},{24,8},{32,16},{40,24},{48,32},{56,40},{64,11... | collective-permute-start | bytes 178184 | tf_op jit(solution)/shard_map/ppermute | solution.py:281
  98.0 3.1 %collective-permute-done.15.h2 = bf16[232,128]{1,0:T(8,128)(2,1)S(1)} collective-permute-done((bf16[232,128]{1,0:T(8,128)(2,1)S(1)}, bf16[232,128]{1,0:T(8,128)(2,1)S(1)}, u32[]{:S(2)}, u32[]{:S(2)}) %collective-permute-start.15) | collective-permute-done | bytes 59424 | tf_op jit(solution)/shard_map/ppermute | solution.py:281
  101.1 1.4 %collective-permute-done.16.h1 = bf16[232,128]{1,0:T(8,128)(2,1)S(1)} collective-permute-done((bf16[232,128]{1,0:T(8,128)(2,1)S(1)}, bf16[232,128]{1,0:T(8,128)(2,1)S(1)}, u32[]{:S(2)}, u32[]{:S(2)}) %collective-permute-start.16) | collective-permute-done | bytes 59424 | tf_op jit(solution)/shard_map/ppermute | solution.py:281
  102.5 1.0 collective-permute-done.17.h3
  103.5 0.6 shard_map.75.h
  104.0 1.7 %collective-permute-start.18 = (bf16[4,232,128]{2,1,0:T(8,128)(2,1)S(1)}, bf16[4,232,128]{2,1,0:T(8,128)(2,1)S(1)}, u32[]{:S(2)}, u32[]{:S(2)}) collective-permute-start(bf16[4,232,128]{2,1,0:T(8,128)(2,1)S(1)} %shard_map.75.h), channel_id=1, source_target_pairs={{0,128},{8,136},{16,144},{24,152},{32,160},{40,168},{48,176},{56,1... | collective-permute-start | bytes 712712 | tf_op jit(solution)/shard_map/ppermute | solution.py:281
  105.8 1.3 %collective-permute-start.19 = (bf16[4,232,128]{2,1,0:T(8,128)(2,1)S(1)}, bf16[4,232,128]{2,1,0:T(8,128)(2,1)S(1)}, u32[]{:S(2)}, u32[]{:S(2)}) collective-permute-start(bf16[4,232,128]{2,1,0:T(8,128)(2,1)S(1)} %shard_map.75.h), channel_id=1, source_target_pairs={{0,64},{8,72},{16,80},{24,88},{32,96},{40,104},{48,112},{56,120},{... | collective-permute-start | bytes 712712 | tf_op jit(solution)/shard_map/ppermute | solution.py:281
  107.1 1.3 %collective-permute-start.20 = (bf16[4,232,128]{2,1,0:T(8,128)(2,1)S(1)}, bf16[4,232,128]{2,1,0:T(8,128)(2,1)S(1)}, u32[]{:S(2)}, u32[]{:S(2)}) collective-permute-start(bf16[4,232,128]{2,1,0:T(8,128)(2,1)S(1)} %shard_map.75.h), channel_id=1, source_target_pairs={{0,192},{8,200},{16,208},{24,216},{32,224},{40,232},{48,240},{56,2... | collective-permute-start | bytes 712712 | tf_op jit(solution)/shard_map/ppermute | solution.py:281
  108.5 3.0 %shard_map.76 = (bf16[3696,512]{1,0:T(8,128)(2,1)S(1)}, f32[128,512]{1,0:T(8,128)S(1)}) custom-call(s32[4]{0:T(128)S(1)} %pad_add_fusion.s, bf16[3696,256]{1,0:T(8,128)(2,1)} %w_own.1, bf16[3696,256]{1,0:T(8,128)(2,1)} %collective-permute-done.w_other, bf16[4,232,128]{2,1,0:T(8,128)(2,1)S(1)} %shard_map.75.h), custom_call_target="tpu_custom_call" | custom-call | tf_op jit(solution)/shard_map/pallas_call | solution.py:72
  111.4 1.0 collective-permute-done.18.h2
  112.4 6.0 %collective-permute-done.19.h1 = bf16[4,232,128]{2,1,0:T(8,128)(2,1)S(1)} collective-permute-done((bf16[4,232,128]{2,1,0:T(8,128)(2,1)S(1)}, bf16[4,232,128]{2,1,0:T(8,128)(2,1)S(1)}, u32[]{:S(2)}, u32[]{:S(2)}) %collective-permute-start.19) | collective-permute-done | bytes 237600 | tf_op jit(solution)/shard_map/ppermute | solution.py:281
  118.4 1.3 shard_map.77
  119.8 9.1 %all_to_all.21.got = bf16[8,16,512]{2,1,0:T(8,128)(2,1)S(1)} all-to-all(bf16[8,16,512]{2,1,0:T(8,128)(2,1)S(1)} %shard_map.77), channel_id=1, replica_groups=mesh['task'=32,'tensor'=8] {'tensor'}, dimensions={0} | all-to-all | bytes 262144 | tf_op jit(solution)/shard_map/all_to_all | solution.py:284
  128.9 0.6 shard_map.78
  129.5 1.9 %collective-permute-start.21 = (f32[16,256]{1,0:T(8,128)S(1)}, f32[16,256]{1,0:T(8,128)S(1)}, u32[]{:S(2)}, u32[]{:S(2)}) collective-permute-start(f32[16,256]{1,0:T(8,128)S(1)} %get-tuple-element.44), channel_id=1, source_target_pairs={{0,8},{8,0},{16,24},{24,16},{32,40},{40,32},{48,56},{56,48},{64,72... | collective-permute-start | bytes 49160 | tf_op jit(solution)/shard_map/ppermute | solution.py:281
  131.4 0.8 collective-permute-done.21.got
  132.2 1.2 shard_map.79
  (13 shorter events, 0.0 us)
Async XLA Ops:
  2.2 24.4 %all-to-all-start = ((bf16[16,8,1152]{2,1,0:T(8,128)(2,1)}), bf16[16,8,1152]{2,1,0:T(8,128)(2,1)S(1)}, u32[]{:S(2)}, u32[]{:S(2)}) async-start(bf16[16,8,1152]{2,1,0:T(8,128)(2,1)} %broadcast_in_dim.16), calls=%async_computation | async-start | bytes 589824 | tf_op jit(solution)/shard_map/all_to_all | solution.py:310
  13.8 4.1 %collective-permute-start.1 = (bf16[2,1024,128]{2,1,0:T(8,128)(2,1)}, bf16[2,1024,128]{2,1,0:T(8,128)(2,1)S(1)}, u32[]{:S(2)}, u32[]{:S(2)}) collective-permute-start(bf16[2,1024,128]{2,1,0:T(8,128)(2,1)} %low_own.1), channel_id=1, source_target_pairs={{0,8},{8,0},{16,24},{24,16},{32,40},{40,32},{48,56},{56,48},{64,72... | collective-permute-start | bytes 1572872 | tf_op jit(solution)/shard_map/ppermute | solution.py:281
  14.9 11.8 %copy-start.1 = (bf16[2,1024,128]{2,1,0:T(8,128)(2,1)S(1)}, bf16[2,1024,128]{2,1,0:T(8,128)(2,1)}, u32[]{:S(2)}) copy-start(bf16[2,1024,128]{2,1,0:T(8,128)(2,1)} %low_own.1) | copy-start | bytes 1572868
  17.8 15.2 %copy-start = (bf16[2,128,3696]{1,2,0:T(8,128)(2,1)S(1)}, bf16[2,128,3696]{1,2,0:T(8,128)(2,1)}, u32[]{:S(2)}) copy-start(bf16[2,128,3696]{1,2,0:T(8,128)(2,1)} %param.11) | copy-start | bytes 5677060
  17.9 35.0 %collective-permute-start.3 = (bf16[3696,256]{1,0:T(8,128)(2,1)}, bf16[3696,256]{1,0:T(8,128)(2,1)}, u32[]{:S(2)}, u32[]{:S(2)}) collective-permute-start(bf16[3696,256]{1,0:T(8,128)(2,1)} %dynamic-slice_bitcast_fusion), channel_id=1, source_target_pairs={{0,8},{8,0},{16,24},{24,16},{32,40},{40,32},{48,56},{56,48},{64,72... | collective-permute-start | bytes 5677064 | tf_op jit(solution)/shard_map/ppermute | solution.py:281
  28.2 10.9 %all-to-all-start.1 = ((bf16[8,16,1024]{2,1,0:T(8,128)(2,1)}), bf16[8,16,1024]{2,1,0:T(8,128)(2,1)S(1)}, u32[]{:S(2)}, u32[]{:S(2)}) async-start(bf16[8,16,1024]{2,1,0:T(8,128)(2,1)} %bitcast.4), calls=%async_computation.1 | async-start | bytes 524288 | tf_op jit(solution)/shard_map/all_to_all | solution.py:284
  34.1 18.8 %collective-permute-start.4 = (bf16[3696,128]{1,0:T(8,128)(2,1)}, bf16[3696,128]{1,0:T(8,128)(2,1)S(1)}, u32[]{:S(2)}, u32[]{:S(2)}) collective-permute-start(bf16[3696,128]{1,0:T(8,128)(2,1)} %dynamic-slice_bitcast_fusion.1), channel_id=1, source_target_pairs={{0,8},{8,0},{16,24},{24,16},{32,40},{40,32},{48,56},{56,48},{64,72... | collective-permute-start | bytes 2838536 | tf_op jit(solution)/shard_map/ppermute | solution.py:281
  36.3 72.2 %collective-permute-start = (bf16[3696,256]{1,0:T(8,128)(2,1)}, bf16[3696,256]{1,0:T(8,128)(2,1)}, u32[]{:S(2)}, u32[]{:S(2)}) collective-permute-start(bf16[3696,256]{1,0:T(8,128)(2,1)} %w_own.1), channel_id=1, source_target_pairs={{0,8},{8,0},{16,24},{24,16},{32,40},{40,32},{48,56},{56,48},{64,72... | collective-permute-start | bytes 5677064 | tf_op jit(solution)/shard_map/ppermute | solution.py:281
  48.4 6.3 %collective-permute-start.2 = (bf16[128,1024]{1,0:T(8,128)(2,1)S(1)}, bf16[128,1024]{1,0:T(8,128)(2,1)S(1)}, u32[]{:S(2)}, u32[]{:S(2)}) collective-permute-start(bf16[128,1024]{1,0:T(8,128)(2,1)S(1)} %bitcast.29), channel_id=1, source_target_pairs={{0,8},{8,0},{16,24},{24,16},{32,40},{40,32},{48,56},{56,48},{64,72... | collective-permute-start | bytes 786440 | tf_op jit(solution)/shard_map/ppermute | solution.py:281
  55.8 9.1 %collective-permute-start.6 = (bf16[2,232,256]{2,1,0:T(8,128)(2,1)S(1)}, bf16[2,232,256]{2,1,0:T(8,128)(2,1)S(1)}, u32[]{:S(2)}, u32[]{:S(2)}) collective-permute-start(bf16[2,232,256]{2,1,0:T(8,128)(2,1)S(1)} %get-tuple-element.28), channel_id=1, source_target_pairs={{0,64},{8,72},{16,80},{24,88},{32,96},{40,104},{48,112},{56,120},{... | collective-permute-start | bytes 712712 | tf_op jit(solution)/shard_map/ppermute | solution.py:281
  55.9 9.1 %collective-permute-start.7 = (bf16[2,232,256]{2,1,0:T(8,128)(2,1)S(1)}, bf16[2,232,256]{2,1,0:T(8,128)(2,1)S(1)}, u32[]{:S(2)}, u32[]{:S(2)}) collective-permute-start(bf16[2,232,256]{2,1,0:T(8,128)(2,1)S(1)} %get-tuple-element.30), channel_id=1, source_target_pairs={{0,192},{8,200},{16,208},{24,216},{32,224},{40,232},{48,240},{56,2... | collective-permute-start | bytes 712712 | tf_op jit(solution)/shard_map/ppermute | solution.py:281
  61.0 8.9 %collective-permute-start.5 = (bf16[2,232,256]{2,1,0:T(8,128)(2,1)S(1)}, bf16[2,232,256]{2,1,0:T(8,128)(2,1)S(1)}, u32[]{:S(2)}, u32[]{:S(2)}) collective-permute-start(bf16[2,232,256]{2,1,0:T(8,128)(2,1)S(1)} %get-tuple-element.26), channel_id=1, source_target_pairs={{0,192},{8,200},{16,208},{24,216},{32,224},{40,232},{48,240},{56,2... | collective-permute-start | bytes 712712 | tf_op jit(solution)/shard_map/ppermute | solution.py:281
  61.1 8.8 %collective-permute-start.9 = (bf16[2,232,256]{2,1,0:T(8,128)(2,1)S(1)}, bf16[2,232,256]{2,1,0:T(8,128)(2,1)S(1)}, u32[]{:S(2)}, u32[]{:S(2)}) collective-permute-start(bf16[2,232,256]{2,1,0:T(8,128)(2,1)S(1)} %get-tuple-element.33), channel_id=1, source_target_pairs={{0,64},{8,72},{16,80},{24,88},{32,96},{40,104},{48,112},{56,120},{... | collective-permute-start | bytes 712712 | tf_op jit(solution)/shard_map/ppermute | solution.py:281
  65.6 7.6 %collective-permute-start.10 = (bf16[2,232,256]{2,1,0:T(8,128)(2,1)S(1)}, bf16[2,232,256]{2,1,0:T(8,128)(2,1)S(1)}, u32[]{:S(2)}, u32[]{:S(2)}) collective-permute-start(bf16[2,232,256]{2,1,0:T(8,128)(2,1)S(1)} %get-tuple-element.34), channel_id=1, source_target_pairs={{0,192},{8,200},{16,208},{24,216},{32,224},{40,232},{48,240},{56,2... | collective-permute-start | bytes 712712 | tf_op jit(solution)/shard_map/ppermute | solution.py:281
  67.6 6.2 %collective-permute-start.8 = (bf16[2,232,256]{2,1,0:T(8,128)(2,1)S(1)}, bf16[2,232,256]{2,1,0:T(8,128)(2,1)S(1)}, u32[]{:S(2)}, u32[]{:S(2)}) collective-permute-start(bf16[2,232,256]{2,1,0:T(8,128)(2,1)S(1)} %get-tuple-element.31), channel_id=1, source_target_pairs={{0,64},{8,72},{16,80},{24,88},{32,96},{40,104},{48,112},{56,120},{... | collective-permute-start | bytes 712712 | tf_op jit(solution)/shard_map/ppermute | solution.py:281
  74.5 7.8 %collective-permute-start.11 = (bf16[232,256]{1,0:T(8,128)(2,1)S(1)}, bf16[232,256]{1,0:T(8,128)(2,1)S(1)}, u32[]{:S(2)}, u32[]{:S(2)}) collective-permute-start(bf16[232,256]{1,0:T(8,128)(2,1)S(1)} %get-tuple-element.36), channel_id=1, source_target_pairs={{0,32},{8,40},{16,48},{24,56},{32,0},{40,8},{48,16},{56,24},{64,96... | collective-permute-start | bytes 356360 | tf_op jit(solution)/shard_map/ppermute | solution.py:281
  74.7 9.1 %collective-permute-start.12 = (bf16[232,256]{1,0:T(8,128)(2,1)S(1)}, bf16[232,256]{1,0:T(8,128)(2,1)S(1)}, u32[]{:S(2)}, u32[]{:S(2)}) collective-permute-start(bf16[232,256]{1,0:T(8,128)(2,1)S(1)} %get-tuple-element.37), channel_id=1, source_target_pairs={{0,16},{8,24},{16,32},{24,40},{32,48},{40,56},{48,0},{56,8},{64,80... | collective-permute-start | bytes 356360 | tf_op jit(solution)/shard_map/ppermute | solution.py:281
  76.8 13.2 %collective-permute-start.13 = (bf16[232,256]{1,0:T(8,128)(2,1)S(1)}, bf16[232,256]{1,0:T(8,128)(2,1)S(1)}, u32[]{:S(2)}, u32[]{:S(2)}) collective-permute-start(bf16[232,256]{1,0:T(8,128)(2,1)S(1)} %get-tuple-element.38), channel_id=1, source_target_pairs={{0,48},{8,56},{16,0},{24,8},{32,16},{40,24},{48,32},{56,40},{64,11... | collective-permute-start | bytes 356360 | tf_op jit(solution)/shard_map/ppermute | solution.py:281
  90.6 1.7 %collective-permute-start.14 = (f32[232,128]{1,0:T(8,128)S(1)}, f32[232,128]{1,0:T(8,128)S(1)}, u32[]{:S(2)}, u32[]{:S(2)}) collective-permute-start(f32[232,128]{1,0:T(8,128)S(1)} %get-tuple-element.40), channel_id=1, source_target_pairs={{0,8},{8,0},{16,24},{24,16},{32,40},{40,32},{48,56},{56,48},{64,72... | collective-permute-start | bytes 356360 | tf_op jit(solution)/shard_map/ppermute | solution.py:281
  92.8 8.3 %collective-permute-start.15 = (bf16[232,128]{1,0:T(8,128)(2,1)S(1)}, bf16[232,128]{1,0:T(8,128)(2,1)S(1)}, u32[]{:S(2)}, u32[]{:S(2)}) collective-permute-start(bf16[232,128]{1,0:T(8,128)(2,1)S(1)} %shard_map.74.h0), channel_id=1, source_target_pairs={{0,32},{8,40},{16,48},{24,56},{32,0},{40,8},{48,16},{56,24},{64,96... | collective-permute-start | bytes 178184 | tf_op jit(solution)/shard_map/ppermute | solution.py:281
  94.5 8.0 %collective-permute-start.16 = (bf16[232,128]{1,0:T(8,128)(2,1)S(1)}, bf16[232,128]{1,0:T(8,128)(2,1)S(1)}, u32[]{:S(2)}, u32[]{:S(2)}) collective-permute-start(bf16[232,128]{1,0:T(8,128)(2,1)S(1)} %shard_map.74.h0), channel_id=1, source_target_pairs={{0,16},{8,24},{16,32},{24,40},{32,48},{40,56},{48,0},{56,8},{64,80... | collective-permute-start | bytes 178184 | tf_op jit(solution)/shard_map/ppermute | solution.py:281
  95.7 7.8 %collective-permute-start.17 = (bf16[232,128]{1,0:T(8,128)(2,1)S(1)}, bf16[232,128]{1,0:T(8,128)(2,1)S(1)}, u32[]{:S(2)}, u32[]{:S(2)}) collective-permute-start(bf16[232,128]{1,0:T(8,128)(2,1)S(1)} %shard_map.74.h0), channel_id=1, source_target_pairs={{0,48},{8,56},{16,0},{24,8},{32,16},{40,24},{48,32},{56,40},{64,11... | collective-permute-start | bytes 178184 | tf_op jit(solution)/shard_map/ppermute | solution.py:281
  104.0 8.4 %collective-permute-start.18 = (bf16[4,232,128]{2,1,0:T(8,128)(2,1)S(1)}, bf16[4,232,128]{2,1,0:T(8,128)(2,1)S(1)}, u32[]{:S(2)}, u32[]{:S(2)}) collective-permute-start(bf16[4,232,128]{2,1,0:T(8,128)(2,1)S(1)} %shard_map.75.h), channel_id=1, source_target_pairs={{0,128},{8,136},{16,144},{24,152},{32,160},{40,168},{48,176},{56,1... | collective-permute-start | bytes 712712 | tf_op jit(solution)/shard_map/ppermute | solution.py:281
  105.8 12.7 %collective-permute-start.19 = (bf16[4,232,128]{2,1,0:T(8,128)(2,1)S(1)}, bf16[4,232,128]{2,1,0:T(8,128)(2,1)S(1)}, u32[]{:S(2)}, u32[]{:S(2)}) collective-permute-start(bf16[4,232,128]{2,1,0:T(8,128)(2,1)S(1)} %shard_map.75.h), channel_id=1, source_target_pairs={{0,64},{8,72},{16,80},{24,88},{32,96},{40,104},{48,112},{56,120},{... | collective-permute-start | bytes 712712 | tf_op jit(solution)/shard_map/ppermute | solution.py:281
  107.1 11.3 %collective-permute-start.20 = (bf16[4,232,128]{2,1,0:T(8,128)(2,1)S(1)}, bf16[4,232,128]{2,1,0:T(8,128)(2,1)S(1)}, u32[]{:S(2)}, u32[]{:S(2)}) collective-permute-start(bf16[4,232,128]{2,1,0:T(8,128)(2,1)S(1)} %shard_map.75.h), channel_id=1, source_target_pairs={{0,192},{8,200},{16,208},{24,216},{32,224},{40,232},{48,240},{56,2... | collective-permute-start | bytes 712712 | tf_op jit(solution)/shard_map/ppermute | solution.py:281
  129.5 2.8 %collective-permute-start.21 = (f32[16,256]{1,0:T(8,128)S(1)}, f32[16,256]{1,0:T(8,128)S(1)}, u32[]{:S(2)}, u32[]{:S(2)}) collective-permute-start(f32[16,256]{1,0:T(8,128)S(1)} %get-tuple-element.44), channel_id=1, source_target_pairs={{0,8},{8,0},{16,24},{24,16},{32,40},{40,32},{48,56},{56,48},{64,72... | collective-permute-start | bytes 49160 | tf_op jit(solution)/shard_map/ppermute | solution.py:281

commit v7 on v6

--- a/solution.py
+++ b/solution.py
@@ -84,21 +84,27 @@
     return v.reshape(v.shape[0] * v.shape[1], v.shape[2])
 
 
-def latent_kernel(width, s, tokens, low_own, low_other, out):
-    c, q = s[2], s[3]
-    x = rows_of(tokens[...])
+def latent_kernel(width, s, own, far, up, down, low_own, low_other, out):
+    x, z, c, q = s[0], s[1], s[2], s[3]
+    blocks = [ref[...] for ref in (own, far, up, down)]
+    tokens = jnp.concatenate([rows_of(b) for b in blocks], axis=0)
     low = jnp.concatenate([low_own[c], low_other[c], low_other[1 - c], low_own[1 - c]], axis=1)
-    lat = jnp.dot(x[:, :width].astype(BF16), low, preferred_element_type=F32)
-    tail = x[:, width:]
+    lat = jnp.dot(tokens[:, :width].astype(BF16), low, preferred_element_type=F32)
+    tail = tokens[:, width:]
     lane = lax.broadcasted_iota(jnp.int32, tail.shape, 1)
     weight = jnp.sum(
         jnp.where((lane == q) | (lane == TASKS + q), tail, 0.0), axis=1, keepdims=True
     )
-    ranks = lat.shape[1]
-    out[:, :ranks] = (lat * weight).astype(BF16)
-    feats = out.shape[1] - ranks
+    lat = lat * weight
+    n, ranks = own.shape[1], lat.shape[1]
+    feats = out.shape[2] - ranks
     start = pl.multiple_of(lax.rem(q, 2) * feats, feats)
-    out[:, ranks:] = rows_of(tokens[:, :, pl.ds(start, feats)]).astype(BF16)
+    for i, (d, ref) in enumerate(zip((0, 2, 1, 3), (own, far, up, down))):
+        for k, e in enumerate((0, 2, 1, 3)):
+            at = lax.rem(x - d + NX, NX) * NZ + lax.rem(z - e + NZ, NZ)
+            r = (i * NZ + k) * n
+            out[at, :, :ranks] = lat[r : r + n].astype(BF16)
+            out[at, :, ranks:] = ref[k, :, pl.ds(start, feats)]
 
 
 def mid_kernel(ranks, s, got, out):
@@ -297,8 +303,7 @@
     xb = NZ * zb
 
     low_other = permute(lower_factor, CORE)
-    w_other = permute(other(weight), CORE)
-    u_other = permute(other(upper), CORE)
+    u_branch = other(upper)
     down_other = permute(down_weight, CORE)
 
     high = lax.reduce_precision(router, 8, 7)
@@ -306,17 +311,24 @@
     packed = jnp.concatenate(
         [tokens, high.astype(BF16), (router - high).astype(BF16), fill], axis=1
     )
-    packed = jnp.broadcast_to(packed[None], (NQ,) + packed.shape)
-    own_rows = lax.all_to_all(packed, "task", 0, 0, axis_index_groups=CHIPS)
+    got = [permute(packed, TO_Z[d]) for d in FAR_FIRST]
+    packed = jnp.stack([packed] + got)
+    packed, w_late = lax.optimization_barrier((packed, weight))
+    w_branch = other(w_late)
+    got = [permute(packed, TO_X[d]) for d in FAR_FIRST]
     half = count // 2
     columns = 2 * ranks + feats
     lat = run(
         functools.partial(latent_kernel, width),
-        sds((half, columns)),
-        own_rows,
+        sds((NQ, rows, columns)),
+        packed,
+        *got,
         lower_factor,
         low_other,
     )
+    lat, w_branch, u_branch = lax.optimization_barrier((lat, w_branch, u_branch))
+    w_other = permute(w_branch, CORE)
+    u_other = permute(u_branch, CORE)
     got = across(lat.reshape(tensor, half // tensor, columns))
     mid = run(functools.partial(mid_kernel, 2 * ranks), sds(got.shape), got)
     cat = across(mid).reshape(half, columns)

time: 134 us -> 134 us (level)
  waiting for transfers between devices: 41.3 us -> 33.4 us
  starting transfers between devices: 46.5 us -> 50.2 us
  blocking collectives: 17.8 us -> 21.5 us
    ppermute x22 -> x28, starting transfers between devices: 30.1 us -> 45.6 us  [permute(): return lax.ppermute(a, 'task', perm)]
    all_to_all x1 -> x0, starting transfers between devices: 11.6 us -> none  [on_device(): own_rows = lax.all_to_all(packed, 'task', 0, 0, axis_index_groups=CHIPS)]
    all_to_all x1 -> x0, waiting for transfers between devices: 8.7 us -> none  [on_device(): own_rows = lax.all_to_all(packed, 'task', 0, 0, axis_index_groups=CHIPS)]
    all_to_all x2, blocking collectives: 17.8 us -> 21.5 us  [across(): return lax.all_to_all(a, 'tensor', 0, 0)]
    all_to_all x1, waiting for transfers between devices: 2.86 us -> 5.62 us  [across(): return lax.all_to_all(a, 'tensor', 0, 0)]
    ppermute x22 -> x28, waiting for transfers between devices: 29.7 us -> 27.8 us  [permute(): return lax.ppermute(a, 'task', perm)]
  transfers between devices with their start and end apart: 24 -> 29, of which waited for: 14 -> 10; matrix products, arithmetic and copies ran while one was open for 3% -> 4% of each run, Pallas kernels for 14% -> 12%
where the time goes in v7:
time: 134 us; the launch traced here: 133 us
  starting transfers between devices  50.2 us (37%)
  waiting for transfers between devices  33.4 us (25%)
  blocking collectives  21.5 us (16%)
  Pallas kernels  20.9 us (16%)
  local copies, waits for them, and re-layouts  5.97 us (4%)
    ppermute x28, starting transfers between devices, permute(): return lax.ppermute(a, 'task', perm)  45.6 us
    ppermute x28, waiting for transfers between devices, permute(): return lax.ppermute(a, 'task', perm)  27.8 us
    all_to_all x2, blocking collectives, across(): return lax.all_to_all(a, 'tensor', 0, 0)  21.5 us
    pallas_call x13, Pallas kernels, call(): pl.pallas_call(kernel, out_shape=out_shape, grid_spec=pltpu.PrefetchScala...  15.2 us
    all_to_all x1, waiting for transfers between devices, across(): return lax.all_to_all(a, 'tensor', 0, 0)  5.62 us
    squeeze x2, local copies, waits for them, and re-layouts, other(): return lax.dynamic_index_in_dim(a, 1 - c, 0, keepdims=False)  5.15 us
    all_to_all x1, starting transfers between devices, across(): return lax.all_to_all(a, 'tensor', 0, 0)  4.64 us
    pallas_call x2, Pallas kernels, call_inside(): pl.pallas_call(kernel, out_shape=out_shape, in_specs=[pl.BlockSpec(memory...  3.88 us
  transfers between devices with their start and end apart: 29, of which 10 were waited for; matrix products, arithmetic and copies ran while one was open for 4% of the time, Pallas kernels for 12%

profile of v7, /device:TPU:1, one launch (start us, length us, event | category | flops | bytes accessed | tf_op | source)
XLA Modules:
  0.0 133.1 jit_solution(619906481202840179)
XLA Ops:
  0.0 0.7 fusion
  0.7 0.8 concatenate.3
  1.5 7.8 %collective-permute-start.1 = (bf16[8,1152]{1,0:T(8,128)(2,1)S(1)}, bf16[8,1152]{1,0:T(8,128)(2,1)S(1)}, u32[]{:S(2)}, u32[]{:S(2)}) collective-permute-start(bf16[8,1152]{1,0:T(8,128)(2,1)S(1)} %concatenate.3), channel_id=1, source_target_pairs={{0,32},{8,40},{16,48},{24,56},{32,0},{40,8},{48,16},{56,24},{64,96... | collective-permute-start | bytes 55304 | tf_op jit(solution)/shard_map/ppermute | solution.py:287
  9.3 1.2 collective-permute-start.2
  10.4 2.4 %collective-permute-start.3 = (bf16[8,1152]{1,0:T(8,128)(2,1)S(1)}, bf16[8,1152]{1,0:T(8,128)(2,1)S(1)}, u32[]{:S(2)}, u32[]{:S(2)}) collective-permute-start(bf16[8,1152]{1,0:T(8,128)(2,1)S(1)} %concatenate.3), channel_id=1, source_target_pairs={{0,48},{8,56},{16,0},{24,8},{32,16},{40,24},{48,32},{56,40},{64,11... | collective-permute-start | bytes 55304 | tf_op jit(solution)/shard_map/ppermute | solution.py:287
  12.8 1.5 %collective-permute-start.7 = (bf16[2,1024,128]{2,1,0:T(8,128)(2,1)}, bf16[2,1024,128]{2,1,0:T(8,128)(2,1)S(1)}, u32[]{:S(2)}, u32[]{:S(2)}) collective-permute-start(bf16[2,1024,128]{2,1,0:T(8,128)(2,1)} %low_own.1), channel_id=1, source_target_pairs={{0,8},{8,0},{16,24},{24,16},{32,40},{40,32},{48,56},{56,48},{64,72... | collective-permute-start | bytes 1572872 | tf_op jit(solution)/shard_map/ppermute | solution.py:287
  14.3 2.2 %dynamic-slice_bitcast_fusion.1 = bf16[3696,128]{1,0:T(8,128)(2,1)} fusion(bf16[2,128,3696]{1,2,0:T(8,128)(2,1)} %param.11, s32[]{:T(128)S(6)} %select_n.16), kind=kLoop, calls=%fused_computation.1 | loop fusion | bytes 1892356 | tf_op jit(solution)/shard_map/jit(dynamic_index_in_dim)/squeeze | solution.py:293
  16.6 0.1 pad_add_fusion.s
  16.6 0.0 collective-permute-done.2
  16.7 0.0 copy-start.2
  16.7 2.8 %collective-permute-start.4 = (bf16[4,8,1152]{2,1,0:T(8,128)(2,1)S(1)}, bf16[4,8,1152]{2,1,0:T(8,128)(2,1)S(1)}, u32[]{:S(2)}, u32[]{:S(2)}) collective-permute-start(bf16[4,8,1152]{2,1,0:T(8,128)(2,1)S(1)} %pad_maximum_fusion.own), channel_id=1, source_target_pairs={{0,128},{8,136},{16,144},{24,152},{32,160},{40,168},{48,176},{56,1... | collective-permute-start | bytes 221192 | tf_op jit(solution)/shard_map/ppermute | solution.py:287
  19.5 0.3 collective-permute-start.5
  19.8 2.4 %collective-permute-start.6 = (bf16[4,8,1152]{2,1,0:T(8,128)(2,1)S(1)}, bf16[4,8,1152]{2,1,0:T(8,128)(2,1)S(1)}, u32[]{:S(2)}, u32[]{:S(2)}) collective-permute-start(bf16[4,8,1152]{2,1,0:T(8,128)(2,1)S(1)} %pad_maximum_fusion.own), channel_id=1, source_target_pairs={{0,192},{8,200},{16,208},{24,216},{32,224},{40,232},{48,240},{56,2... | collective-permute-start | bytes 221192 | tf_op jit(solution)/shard_map/ppermute | solution.py:287
  22.2 2.9 %dynamic-slice_bitcast_fusion = bf16[3696,256]{1,0:T(8,128)(2,1)} fusion(bf16[2,3696,256]{2,1,0:T(8,128)(2,1)} %bitcast.36, s32[]{:T(128)S(6)} %select_n.16), kind=kLoop, calls=%fused_computation | loop fusion | bytes 3784708 | tf_op jit(solution)/shard_map/jit(dynamic_index_in_dim)/squeeze | solution.py:293
  25.2 1.6 %shard_map.64 = bf16[16,8,1024]{2,1,0:T(8,128)(2,1)} custom-call(s32[4]{0:T(128)S(1)} %pad_add_fusion.s, bf16[4,8,1152]{2,1,0:T(8,128)(2,1)S(1)} %pad_maximum_fusion.own, bf16[4,8,1152]{2,1,0:T(8,128)(2,1)S(1)} %collective-permute-done.4.far, bf16[4,8,1152]{2,1,0:T(8,128)(2,1)S(1)} %collective-permute-done.5.up, ...), custom_call_target="tpu_custom_call" | custom-call | tf_op jit(solution)/shard_map/pallas_call | solution.py:54
  26.7 0.8 collective-permute-start.9
  27.6 4.6 %all-to-all-start = ((bf16[8,16,1024]{2,1,0:T(8,128)(2,1)}), bf16[8,16,1024]{2,1,0:T(8,128)(2,1)S(1)}, u32[]{:S(2)}, u32[]{:S(2)}) async-start(bf16[8,16,1024]{2,1,0:T(8,128)(2,1)} %bitcast.12), calls=%async_computation | async-start | bytes 524288 | tf_op jit(solution)/shard_map/all_to_all | solution.py:290
  32.2 0.3 collective-permute-start.10
  32.5 0.2 collective-permute-start
  32.7 5.6 %all-to-all-done.got = bf16[8,16,1024]{2,1,0:T(8,128)(2,1)S(1)} async-done(((bf16[8,16,1024]{2,1,0:T(8,128)(2,1)}), bf16[8,16,1024]{2,1,0:T(8,128)(2,1)S(1)}, u32[]{:S(2)}, u32[]{:S(2)}) %all-to-all-start) | async-done | bytes 262176 | tf_op jit(solution)/shard_map/all_to_all | solution.py:290
  38.4 0.6 shard_map.65
  38.9 10.1 %all_to_all.15 = bf16[8,16,1024]{2,1,0:T(8,128)(2,1)S(1)} all-to-all(bf16[8,16,1024]{2,1,0:T(8,128)(2,1)S(1)} %shard_map.65), channel_id=1, replica_groups=mesh['task'=32,'tensor'=8] {'tensor'}, dimensions={0} | all-to-all | bytes 524288 | tf_op jit(solution)/shard_map/all_to_all | solution.py:290
  49.0 2.0 %collective-permute-start.8 = (bf16[128,1024]{1,0:T(8,128)(2,1)S(1)}, bf16[128,1024]{1,0:T(8,128)(2,1)S(1)}, u32[]{:S(2)}, u32[]{:S(2)}) collective-permute-start(bf16[128,1024]{1,0:T(8,128)(2,1)S(1)} %bitcast.31), channel_id=1, source_target_pairs={{0,8},{8,0},{16,24},{24,16},{32,40},{40,32},{48,56},{56,48},{64,72... | collective-permute-start | bytes 786440 | tf_op jit(solution)/shard_map/ppermute | solution.py:287
  51.0 1.8 %shard_map.69.w = bf16[928,768]{1,0:T(8,128)(2,1)S(1)} custom-call(s32[4]{0:T(128)S(1)} %pad_add_fusion.s, bf16[2,3696,256]{2,1,0:T(8,128)(2,1)} %bitcast.37, bf16[3696,256]{1,0:T(8,128)(2,1)} %collective-permute-done.9.w_other, bf16[2,3696,128]{2,1,0:T(8,128)(2,1)S(1)} %bitcast.20, bf16[3696,128]{1,0:T(8,128)(2,1)S(1)} %collective-permute-done.10.u_other), custom_call_target="tpu_custom_call" | custom-call | tf_op jit(solution)/shard_map/pallas_call | solution.py:368
  52.8 1.1 shard_map.70
  53.9 0.1 collective-permute-start.12
  54.0 2.7 %collective-permute-start.13 = (bf16[2,232,256]{2,1,0:T(8,128)(2,1)S(1)}, bf16[2,232,256]{2,1,0:T(8,128)(2,1)S(1)}, u32[]{:S(2)}, u32[]{:S(2)}) collective-permute-start(bf16[2,232,256]{2,1,0:T(8,128)(2,1)S(1)} %get-tuple-element.40), channel_id=1, source_target_pairs={{0,192},{8,200},{16,208},{24,216},{32,224},{40,232},{48,240},{56,2... | collective-permute-start | bytes 712712 | tf_op jit(solution)/shard_map/ppermute | solution.py:287
  56.7 2.4 %shard_map.67 = (bf16[2,232,256]{2,1,0:T(8,128)(2,1)S(1)}, bf16[2,232,256]{2,1,0:T(8,128)(2,1)S(1)}) custom-call(s32[4]{0:T(128)S(1)} %pad_add_fusion.s, bf16[128,1024]{1,0:T(8,128)(2,1)S(1)} %bitcast.33, bf16[128,1024]{1,0:T(8,128)(2,1)S(1)} %collective-permute-done.8.rows_other, bf16[2,3696,256]{2,1,0:T(8,128)(2,1)} %bitcast.38, ...), custom_call_target="tpu_custom_call" | custom-call | tf_op jit(solution)/shard_map/pallas_call | solution.py:54
  59.1 1.2 collective-permute-start.11
  60.3 0.4 collective-permute-start.15
  60.7 2.4 %shard_map.68 = (f32[2,232,256]{2,1,0:T(8,128)S(1)}, f32[2,232,256]{2,1,0:T(8,128)S(1)}) custom-call(s32[4]{0:T(128)S(1)} %pad_add_fusion.s, bf16[128,1024]{1,0:T(8,128)(2,1)S(1)} %bitcast.34, bf16[128,1024]{1,0:T(8,128)(2,1)S(1)} %collective-permute-done.8.rows_other, bf16[2,3696,256]{2,1,0:T(8,128)(2,1)} %bitcast.40, bf16[2,3696,256]{2,1,0:T(8,128)(2,1)} %bitcast.41, ...), custom_call_target="tpu_custom_call" | custom-call | tf_op jit(solution)/shard_map/pallas_call | solution.py:54
  63.1 0.6 shard_map.71
  63.7 0.1 collective-permute-start.14
  63.8 2.6 %collective-permute-start.16 = (bf16[2,232,256]{2,1,0:T(8,128)(2,1)S(1)}, bf16[2,232,256]{2,1,0:T(8,128)(2,1)S(1)}, u32[]{:S(2)}, u32[]{:S(2)}) collective-permute-start(bf16[2,232,256]{2,1,0:T(8,128)(2,1)S(1)} %get-tuple-element.44), channel_id=1, source_target_pairs={{0,192},{8,200},{16,208},{24,216},{32,224},{40,232},{48,240},{56,2... | collective-permute-start | bytes 712712 | tf_op jit(solution)/shard_map/ppermute | solution.py:287
  66.5 2.3 %shard_map.66 = (f32[2,232,256]{2,1,0:T(8,128)S(1)}, f32[2,232,256]{2,1,0:T(8,128)S(1)}) custom-call(s32[4]{0:T(128)S(1)} %pad_add_fusion.s, bf16[128,1024]{1,0:T(8,128)(2,1)S(1)} %bitcast.35, bf16[128,1024]{1,0:T(8,128)(2,1)S(1)} %collective-permute-done.8.rows_other, bf16[2,3696,256]{2,1,0:T(8,128)(2,1)} %bitcast.42, ...), custom_call_target="tpu_custom_call" | custom-call | tf_op jit(solution)/shard_map/pallas_call | solution.py:54
  68.8 0.0 copy-start.1
  68.8 4.2 %collective-permute-done.14.a2 = bf16[2,232,256]{2,1,0:T(8,128)(2,1)S(1)} collective-permute-done((bf16[2,232,256]{2,1,0:T(8,128)(2,1)S(1)}, bf16[2,232,256]{2,1,0:T(8,128)(2,1)S(1)}, u32[]{:S(2)}, u32[]{:S(2)}) %collective-permute-start.14) | collective-permute-done | bytes 237600 | tf_op jit(solution)/shard_map/ppermute | solution.py:287
  73.1 0.8 shard_map.72
  73.8 1.6 %collective-permute-start.17 = (bf16[232,256]{1,0:T(8,128)(2,1)S(1)}, bf16[232,256]{1,0:T(8,128)(2,1)S(1)}, u32[]{:S(2)}, u32[]{:S(2)}) collective-permute-start(bf16[232,256]{1,0:T(8,128)(2,1)S(1)} %get-tuple-element.46), channel_id=1, source_target_pairs={{0,32},{8,40},{16,48},{24,56},{32,0},{40,8},{48,16},{56,24},{64,96... | collective-permute-start | bytes 356360 | tf_op jit(solution)/shard_map/ppermute | solution.py:287
  75.4 3.9 %collective-permute-start.18 = (bf16[232,256]{1,0:T(8,128)(2,1)S(1)}, bf16[232,256]{1,0:T(8,128)(2,1)S(1)}, u32[]{:S(2)}, u32[]{:S(2)}) collective-permute-start(bf16[232,256]{1,0:T(8,128)(2,1)S(1)} %get-tuple-element.47), channel_id=1, source_target_pairs={{0,16},{8,24},{16,32},{24,40},{32,48},{40,56},{48,0},{56,8},{64,80... | collective-permute-start | bytes 356360 | tf_op jit(solution)/shard_map/ppermute | solution.py:287
  79.3 2.4 %collective-permute-done.17.a1 = bf16[232,256]{1,0:T(8,128)(2,1)S(1)} collective-permute-done((bf16[232,256]{1,0:T(8,128)(2,1)S(1)}, bf16[232,256]{1,0:T(8,128)(2,1)S(1)}, u32[]{:S(2)}, u32[]{:S(2)}) %collective-permute-start.17) | collective-permute-done | bytes 118816 | tf_op jit(solution)/shard_map/ppermute | solution.py:287
  81.7 3.3 %collective-permute-done.18.a2 = bf16[232,256]{1,0:T(8,128)(2,1)S(1)} collective-permute-done((bf16[232,256]{1,0:T(8,128)(2,1)S(1)}, bf16[232,256]{1,0:T(8,128)(2,1)S(1)}, u32[]{:S(2)}, u32[]{:S(2)}) %collective-permute-start.18) | collective-permute-done | bytes 118816 | tf_op jit(solution)/shard_map/ppermute | solution.py:287
  84.9 5.7 %collective-permute-done.19.a3 = bf16[232,256]{1,0:T(8,128)(2,1)S(1)} collective-permute-done((bf16[232,256]{1,0:T(8,128)(2,1)S(1)}, bf16[232,256]{1,0:T(8,128)(2,1)S(1)}, u32[]{:S(2)}, u32[]{:S(2)}) %collective-permute-start.19) | collective-permute-done | bytes 118816 | tf_op jit(solution)/shard_map/ppermute | solution.py:287
  90.7 0.6 shard_map.73
  91.3 0.6 collective-permute-start.20
  91.9 1.0 collective-permute-done.20.got
  92.8 0.6 shard_map.74.h0
  93.4 0.7 collective-permute-start.21
  94.2 2.4 %collective-permute-start.22 = (bf16[232,128]{1,0:T(8,128)(2,1)S(1)}, bf16[232,128]{1,0:T(8,128)(2,1)S(1)}, u32[]{:S(2)}, u32[]{:S(2)}) collective-permute-start(bf16[232,128]{1,0:T(8,128)(2,1)S(1)} %shard_map.74.h0), channel_id=1, source_target_pairs={{0,16},{8,24},{16,32},{24,40},{32,48},{40,56},{48,0},{56,8},{64,80... | collective-permute-start | bytes 178184 | tf_op jit(solution)/shard_map/ppermute | solution.py:287
  96.5 1.2 collective-permute-start.23
  97.7 2.9 %collective-permute-done.21.h2 = bf16[232,128]{1,0:T(8,128)(2,1)S(1)} collective-permute-done((bf16[232,128]{1,0:T(8,128)(2,1)S(1)}, bf16[232,128]{1,0:T(8,128)(2,1)S(1)}, u32[]{:S(2)}, u32[]{:S(2)}) %collective-permute-start.21) | collective-permute-done | bytes 59424 | tf_op jit(solution)/shard_map/ppermute | solution.py:287
  100.6 1.2 collective-permute-done.22.h1
  101.8 0.6 shard_map.75.h
  102.4 2.0 %collective-permute-start.24 = (bf16[4,232,128]{2,1,0:T(8,128)(2,1)S(1)}, bf16[4,232,128]{2,1,0:T(8,128)(2,1)S(1)}, u32[]{:S(2)}, u32[]{:S(2)}) collective-permute-start(bf16[4,232,128]{2,1,0:T(8,128)(2,1)S(1)} %shard_map.75.h), channel_id=1, source_target_pairs={{0,128},{8,136},{16,144},{24,152},{32,160},{40,168},{48,176},{56,1... | collective-permute-start | bytes 712712 | tf_op jit(solution)/shard_map/ppermute | solution.py:287
  104.4 0.3 collective-permute-start.25
  104.7 2.4 %collective-permute-start.26 = (bf16[4,232,128]{2,1,0:T(8,128)(2,1)S(1)}, bf16[4,232,128]{2,1,0:T(8,128)(2,1)S(1)}, u32[]{:S(2)}, u32[]{:S(2)}) collective-permute-start(bf16[4,232,128]{2,1,0:T(8,128)(2,1)S(1)} %shard_map.75.h), channel_id=1, source_target_pairs={{0,192},{8,200},{16,208},{24,216},{32,224},{40,232},{48,240},{56,2... | collective-permute-start | bytes 712712 | tf_op jit(solution)/shard_map/ppermute | solution.py:287
  107.0 2.6 %shard_map.76 = (bf16[3696,512]{1,0:T(8,128)(2,1)S(1)}, f32[128,512]{1,0:T(8,128)S(1)}) custom-call(s32[4]{0:T(128)S(1)} %pad_add_fusion.s, bf16[3696,256]{1,0:T(8,128)(2,1)S(1)} %copy-done.1, bf16[3696,256]{1,0:T(8,128)(2,1)} %collective-permute-done.w_other, bf16[4,232,128]{2,1,0:T(8,128)(2,1)S(1)} %shard_map.75.h), custom_call_target="tpu_custom_call" | custom-call | tf_op jit(solution)/shard_map/pallas_call | solution.py:72
  109.6 6.3 %collective-permute-done.25.h1 = bf16[4,232,128]{2,1,0:T(8,128)(2,1)S(1)} collective-permute-done((bf16[4,232,128]{2,1,0:T(8,128)(2,1)S(1)}, bf16[4,232,128]{2,1,0:T(8,128)(2,1)S(1)}, u32[]{:S(2)}, u32[]{:S(2)}) %collective-permute-start.25) | collective-permute-done | bytes 237600 | tf_op jit(solution)/shard_map/ppermute | solution.py:287
  115.9 1.3 shard_map.77
  117.2 11.4 %all_to_all.16.got = bf16[8,16,512]{2,1,0:T(8,128)(2,1)S(1)} all-to-all(bf16[8,16,512]{2,1,0:T(8,128)(2,1)S(1)} %shard_map.77), channel_id=1, replica_groups=mesh['task'=32,'tensor'=8] {'tensor'}, dimensions={0} | all-to-all | bytes 262144 | tf_op jit(solution)/shard_map/all_to_all | solution.py:290
  128.6 0.6 shard_map.78
  129.1 1.9 %collective-permute-start.27 = (f32[16,256]{1,0:T(8,128)S(1)}, f32[16,256]{1,0:T(8,128)S(1)}, u32[]{:S(2)}, u32[]{:S(2)}) collective-permute-start(f32[16,256]{1,0:T(8,128)S(1)} %get-tuple-element.54), channel_id=1, source_target_pairs={{0,8},{8,0},{16,24},{24,16},{32,40},{40,32},{48,56},{56,48},{64,72... | collective-permute-start | bytes 49160 | tf_op jit(solution)/shard_map/ppermute | solution.py:287
  131.1 0.8 collective-permute-done.27.got
  131.9 1.2 shard_map.79
  (25 shorter events, 0.1 us)
Async XLA Ops:
  1.5 15.1 %collective-permute-start.1 = (bf16[8,1152]{1,0:T(8,128)(2,1)S(1)}, bf16[8,1152]{1,0:T(8,128)(2,1)S(1)}, u32[]{:S(2)}, u32[]{:S(2)}) collective-permute-start(bf16[8,1152]{1,0:T(8,128)(2,1)S(1)} %concatenate.3), channel_id=1, source_target_pairs={{0,32},{8,40},{16,48},{24,56},{32,0},{40,8},{48,16},{56,24},{64,96... | collective-permute-start | bytes 55304 | tf_op jit(solution)/shard_map/ppermute | solution.py:287
  9.3 7.4 %collective-permute-start.2 = (bf16[8,1152]{1,0:T(8,128)(2,1)S(1)}, bf16[8,1152]{1,0:T(8,128)(2,1)S(1)}, u32[]{:S(2)}, u32[]{:S(2)}) collective-permute-start(bf16[8,1152]{1,0:T(8,128)(2,1)S(1)} %concatenate.3), channel_id=1, source_target_pairs={{0,16},{8,24},{16,32},{24,40},{32,48},{40,56},{48,0},{56,8},{64,80... | collective-permute-start | bytes 55304 | tf_op jit(solution)/shard_map/ppermute | solution.py:287
  10.4 6.2 %collective-permute-start.3 = (bf16[8,1152]{1,0:T(8,128)(2,1)S(1)}, bf16[8,1152]{1,0:T(8,128)(2,1)S(1)}, u32[]{:S(2)}, u32[]{:S(2)}) collective-permute-start(bf16[8,1152]{1,0:T(8,128)(2,1)S(1)} %concatenate.3), channel_id=1, source_target_pairs={{0,48},{8,56},{16,0},{24,8},{32,16},{40,24},{48,32},{56,40},{64,11... | collective-permute-start | bytes 55304 | tf_op jit(solution)/shard_map/ppermute | solution.py:287
  12.8 12.3 %collective-permute-start.7 = (bf16[2,1024,128]{2,1,0:T(8,128)(2,1)}, bf16[2,1024,128]{2,1,0:T(8,128)(2,1)S(1)}, u32[]{:S(2)}, u32[]{:S(2)}) collective-permute-start(bf16[2,1024,128]{2,1,0:T(8,128)(2,1)} %low_own.1), channel_id=1, source_target_pairs={{0,8},{8,0},{16,24},{24,16},{32,40},{40,32},{48,56},{56,48},{64,72... | collective-permute-start | bytes 1572872 | tf_op jit(solution)/shard_map/ppermute | solution.py:287
  16.7 8.5 %copy-start.2 = (bf16[2,1024,128]{2,1,0:T(8,128)(2,1)S(1)}, bf16[2,1024,128]{2,1,0:T(8,128)(2,1)}, u32[]{:S(2)}) copy-start(bf16[2,1024,128]{2,1,0:T(8,128)(2,1)} %low_own.1) | copy-start | bytes 1572868
  16.7 8.4 %collective-permute-start.4 = (bf16[4,8,1152]{2,1,0:T(8,128)(2,1)S(1)}, bf16[4,8,1152]{2,1,0:T(8,128)(2,1)S(1)}, u32[]{:S(2)}, u32[]{:S(2)}) collective-permute-start(bf16[4,8,1152]{2,1,0:T(8,128)(2,1)S(1)} %pad_maximum_fusion.own), channel_id=1, source_target_pairs={{0,128},{8,136},{16,144},{24,152},{32,160},{40,168},{48,176},{56,1... | collective-permute-start | bytes 221192 | tf_op jit(solution)/shard_map/ppermute | solution.py:287
  19.5 5.6 %collective-permute-start.5 = (bf16[4,8,1152]{2,1,0:T(8,128)(2,1)S(1)}, bf16[4,8,1152]{2,1,0:T(8,128)(2,1)S(1)}, u32[]{:S(2)}, u32[]{:S(2)}) collective-permute-start(bf16[4,8,1152]{2,1,0:T(8,128)(2,1)S(1)} %pad_maximum_fusion.own), channel_id=1, source_target_pairs={{0,64},{8,72},{16,80},{24,88},{32,96},{40,104},{48,112},{56,120},{... | collective-permute-start | bytes 221192 | tf_op jit(solution)/shard_map/ppermute | solution.py:287
  19.8 5.3 %collective-permute-start.6 = (bf16[4,8,1152]{2,1,0:T(8,128)(2,1)S(1)}, bf16[4,8,1152]{2,1,0:T(8,128)(2,1)S(1)}, u32[]{:S(2)}, u32[]{:S(2)}) collective-permute-start(bf16[4,8,1152]{2,1,0:T(8,128)(2,1)S(1)} %pad_maximum_fusion.own), channel_id=1, source_target_pairs={{0,192},{8,200},{16,208},{24,216},{32,224},{40,232},{48,240},{56,2... | collective-permute-start | bytes 221192 | tf_op jit(solution)/shard_map/ppermute | solution.py:287
  25.1 25.9 %copy-start = (bf16[2,128,3696]{1,2,0:T(8,128)(2,1)S(1)}, bf16[2,128,3696]{1,2,0:T(8,128)(2,1)}, u32[]{:S(2)}) copy-start(bf16[2,128,3696]{1,2,0:T(8,128)(2,1)} %param.11) | copy-start | bytes 5677060
  26.7 24.3 %collective-permute-start.9 = (bf16[3696,256]{1,0:T(8,128)(2,1)}, bf16[3696,256]{1,0:T(8,128)(2,1)}, u32[]{:S(2)}, u32[]{:S(2)}) collective-permute-start(bf16[3696,256]{1,0:T(8,128)(2,1)} %dynamic-slice_bitcast_fusion), channel_id=1, source_target_pairs={{0,8},{8,0},{16,24},{24,16},{32,40},{40,32},{48,56},{56,48},{64,72... | collective-permute-start | bytes 5677064 | tf_op jit(solution)/shard_map/ppermute | solution.py:287
  27.6 10.8 %all-to-all-start = ((bf16[8,16,1024]{2,1,0:T(8,128)(2,1)}), bf16[8,16,1024]{2,1,0:T(8,128)(2,1)S(1)}, u32[]{:S(2)}, u32[]{:S(2)}) async-start(bf16[8,16,1024]{2,1,0:T(8,128)(2,1)} %bitcast.12), calls=%async_computation | async-start | bytes 524288 | tf_op jit(solution)/shard_map/all_to_all | solution.py:290
  32.2 18.8 %collective-permute-start.10 = (bf16[3696,128]{1,0:T(8,128)(2,1)}, bf16[3696,128]{1,0:T(8,128)(2,1)S(1)}, u32[]{:S(2)}, u32[]{:S(2)}) collective-permute-start(bf16[3696,128]{1,0:T(8,128)(2,1)} %dynamic-slice_bitcast_fusion.1), channel_id=1, source_target_pairs={{0,8},{8,0},{16,24},{24,16},{32,40},{40,32},{48,56},{56,48},{64,72... | collective-permute-start | bytes 2838536 | tf_op jit(solution)/shard_map/ppermute | solution.py:287
  32.5 74.5 %collective-permute-start = (bf16[3696,256]{1,0:T(8,128)(2,1)}, bf16[3696,256]{1,0:T(8,128)(2,1)}, u32[]{:S(2)}, u32[]{:S(2)}) collective-permute-start(bf16[3696,256]{1,0:T(8,128)(2,1)} %w_own.1), channel_id=1, source_target_pairs={{0,8},{8,0},{16,24},{24,16},{32,40},{40,32},{48,56},{56,48},{64,72... | collective-permute-start | bytes 5677064 | tf_op jit(solution)/shard_map/ppermute | solution.py:287
  49.0 3.8 %collective-permute-start.8 = (bf16[128,1024]{1,0:T(8,128)(2,1)S(1)}, bf16[128,1024]{1,0:T(8,128)(2,1)S(1)}, u32[]{:S(2)}, u32[]{:S(2)}) collective-permute-start(bf16[128,1024]{1,0:T(8,128)(2,1)S(1)} %bitcast.31), channel_id=1, source_target_pairs={{0,8},{8,0},{16,24},{24,16},{32,40},{40,32},{48,56},{56,48},{64,72... | collective-permute-start | bytes 786440 | tf_op jit(solution)/shard_map/ppermute | solution.py:287
  53.9 9.1 %collective-permute-start.12 = (bf16[2,232,256]{2,1,0:T(8,128)(2,1)S(1)}, bf16[2,232,256]{2,1,0:T(8,128)(2,1)S(1)}, u32[]{:S(2)}, u32[]{:S(2)}) collective-permute-start(bf16[2,232,256]{2,1,0:T(8,128)(2,1)S(1)} %get-tuple-element.38), channel_id=1, source_target_pairs={{0,64},{8,72},{16,80},{24,88},{32,96},{40,104},{48,112},{56,120},{... | collective-permute-start | bytes 712712 | tf_op jit(solution)/shard_map/ppermute | solution.py:287
  54.0 9.1 %collective-permute-start.13 = (bf16[2,232,256]{2,1,0:T(8,128)(2,1)S(1)}, bf16[2,232,256]{2,1,0:T(8,128)(2,1)S(1)}, u32[]{:S(2)}, u32[]{:S(2)}) collective-permute-start(bf16[2,232,256]{2,1,0:T(8,128)(2,1)S(1)} %get-tuple-element.40), channel_id=1, source_target_pairs={{0,192},{8,200},{16,208},{24,216},{32,224},{40,232},{48,240},{56,2... | collective-permute-start | bytes 712712 | tf_op jit(solution)/shard_map/ppermute | solution.py:287
  59.1 9.7 %collective-permute-start.11 = (bf16[2,232,256]{2,1,0:T(8,128)(2,1)S(1)}, bf16[2,232,256]{2,1,0:T(8,128)(2,1)S(1)}, u32[]{:S(2)}, u32[]{:S(2)}) collective-permute-start(bf16[2,232,256]{2,1,0:T(8,128)(2,1)S(1)} %get-tuple-element.36), channel_id=1, source_target_pairs={{0,192},{8,200},{16,208},{24,216},{32,224},{40,232},{48,240},{56,2... | collective-permute-start | bytes 712712 | tf_op jit(solution)/shard_map/ppermute | solution.py:287
  60.3 8.5 %collective-permute-start.15 = (bf16[2,232,256]{2,1,0:T(8,128)(2,1)S(1)}, bf16[2,232,256]{2,1,0:T(8,128)(2,1)S(1)}, u32[]{:S(2)}, u32[]{:S(2)}) collective-permute-start(bf16[2,232,256]{2,1,0:T(8,128)(2,1)S(1)} %get-tuple-element.43), channel_id=1, source_target_pairs={{0,64},{8,72},{16,80},{24,88},{32,96},{40,104},{48,112},{56,120},{... | collective-permute-start | bytes 712712 | tf_op jit(solution)/shard_map/ppermute | solution.py:287
  63.7 9.3 %collective-permute-start.14 = (bf16[2,232,256]{2,1,0:T(8,128)(2,1)S(1)}, bf16[2,232,256]{2,1,0:T(8,128)(2,1)S(1)}, u32[]{:S(2)}, u32[]{:S(2)}) collective-permute-start(bf16[2,232,256]{2,1,0:T(8,128)(2,1)S(1)} %get-tuple-element.41), channel_id=1, source_target_pairs={{0,64},{8,72},{16,80},{24,88},{32,96},{40,104},{48,112},{56,120},{... | collective-permute-start | bytes 712712 | tf_op jit(solution)/shard_map/ppermute | solution.py:287
  63.8 9.2 %collective-permute-start.16 = (bf16[2,232,256]{2,1,0:T(8,128)(2,1)S(1)}, bf16[2,232,256]{2,1,0:T(8,128)(2,1)S(1)}, u32[]{:S(2)}, u32[]{:S(2)}) collective-permute-start(bf16[2,232,256]{2,1,0:T(8,128)(2,1)S(1)} %get-tuple-element.44), channel_id=1, source_target_pairs={{0,192},{8,200},{16,208},{24,216},{32,224},{40,232},{48,240},{56,2... | collective-permute-start | bytes 712712 | tf_op jit(solution)/shard_map/ppermute | solution.py:287
  68.8 38.2 %copy-start.1 = (bf16[3696,256]{1,0:T(8,128)(2,1)S(1)}, bf16[3696,256]{1,0:T(8,128)(2,1)}, u32[]{:S(2)}) copy-start(bf16[3696,256]{1,0:T(8,128)(2,1)} %w_own.1) | copy-start | bytes 5677060
  73.8 7.9 %collective-permute-start.17 = (bf16[232,256]{1,0:T(8,128)(2,1)S(1)}, bf16[232,256]{1,0:T(8,128)(2,1)S(1)}, u32[]{:S(2)}, u32[]{:S(2)}) collective-permute-start(bf16[232,256]{1,0:T(8,128)(2,1)S(1)} %get-tuple-element.46), channel_id=1, source_target_pairs={{0,32},{8,40},{16,48},{24,56},{32,0},{40,8},{48,16},{56,24},{64,96... | collective-permute-start | bytes 356360 | tf_op jit(solution)/shard_map/ppermute | solution.py:287
  75.4 9.5 %collective-permute-start.18 = (bf16[232,256]{1,0:T(8,128)(2,1)S(1)}, bf16[232,256]{1,0:T(8,128)(2,1)S(1)}, u32[]{:S(2)}, u32[]{:S(2)}) collective-permute-start(bf16[232,256]{1,0:T(8,128)(2,1)S(1)} %get-tuple-element.47), channel_id=1, source_target_pairs={{0,16},{8,24},{16,32},{24,40},{32,48},{40,56},{48,0},{56,8},{64,80... | collective-permute-start | bytes 356360 | tf_op jit(solution)/shard_map/ppermute | solution.py:287
  79.2 11.4 %collective-permute-start.19 = (bf16[232,256]{1,0:T(8,128)(2,1)S(1)}, bf16[232,256]{1,0:T(8,128)(2,1)S(1)}, u32[]{:S(2)}, u32[]{:S(2)}) collective-permute-start(bf16[232,256]{1,0:T(8,128)(2,1)S(1)} %get-tuple-element.48), channel_id=1, source_target_pairs={{0,48},{8,56},{16,0},{24,8},{32,16},{40,24},{48,32},{56,40},{64,11... | collective-permute-start | bytes 356360 | tf_op jit(solution)/shard_map/ppermute | solution.py:287
  91.3 1.6 %collective-permute-start.20 = (f32[232,128]{1,0:T(8,128)S(1)}, f32[232,128]{1,0:T(8,128)S(1)}, u32[]{:S(2)}, u32[]{:S(2)}) collective-permute-start(f32[232,128]{1,0:T(8,128)S(1)} %get-tuple-element.50), channel_id=1, source_target_pairs={{0,8},{8,0},{16,24},{24,16},{32,40},{40,32},{48,56},{56,48},{64,72... | collective-permute-start | bytes 356360 | tf_op jit(solution)/shard_map/ppermute | solution.py:287
  93.4 7.2 %collective-permute-start.21 = (bf16[232,128]{1,0:T(8,128)(2,1)S(1)}, bf16[232,128]{1,0:T(8,128)(2,1)S(1)}, u32[]{:S(2)}, u32[]{:S(2)}) collective-permute-start(bf16[232,128]{1,0:T(8,128)(2,1)S(1)} %shard_map.74.h0), channel_id=1, source_target_pairs={{0,32},{8,40},{16,48},{24,56},{32,0},{40,8},{48,16},{56,24},{64,96... | collective-permute-start | bytes 178184 | tf_op jit(solution)/shard_map/ppermute | solution.py:287
  94.2 7.7 %collective-permute-start.22 = (bf16[232,128]{1,0:T(8,128)(2,1)S(1)}, bf16[232,128]{1,0:T(8,128)(2,1)S(1)}, u32[]{:S(2)}, u32[]{:S(2)}) collective-permute-start(bf16[232,128]{1,0:T(8,128)(2,1)S(1)} %shard_map.74.h0), channel_id=1, source_target_pairs={{0,16},{8,24},{16,32},{24,40},{32,48},{40,56},{48,0},{56,8},{64,80... | collective-permute-start | bytes 178184 | tf_op jit(solution)/shard_map/ppermute | solution.py:287
  96.5 5.3 %collective-permute-start.23 = (bf16[232,128]{1,0:T(8,128)(2,1)S(1)}, bf16[232,128]{1,0:T(8,128)(2,1)S(1)}, u32[]{:S(2)}, u32[]{:S(2)}) collective-permute-start(bf16[232,128]{1,0:T(8,128)(2,1)S(1)} %shard_map.74.h0), channel_id=1, source_target_pairs={{0,48},{8,56},{16,0},{24,8},{32,16},{40,24},{48,32},{56,40},{64,11... | collective-permute-start | bytes 178184 | tf_op jit(solution)/shard_map/ppermute | solution.py:287
  102.4 7.2 %collective-permute-start.24 = (bf16[4,232,128]{2,1,0:T(8,128)(2,1)S(1)}, bf16[4,232,128]{2,1,0:T(8,128)(2,1)S(1)}, u32[]{:S(2)}, u32[]{:S(2)}) collective-permute-start(bf16[4,232,128]{2,1,0:T(8,128)(2,1)S(1)} %shard_map.75.h), channel_id=1, source_target_pairs={{0,128},{8,136},{16,144},{24,152},{32,160},{40,168},{48,176},{56,1... | collective-permute-start | bytes 712712 | tf_op jit(solution)/shard_map/ppermute | solution.py:287
  104.4 11.5 %collective-permute-start.25 = (bf16[4,232,128]{2,1,0:T(8,128)(2,1)S(1)}, bf16[4,232,128]{2,1,0:T(8,128)(2,1)S(1)}, u32[]{:S(2)}, u32[]{:S(2)}) collective-permute-start(bf16[4,232,128]{2,1,0:T(8,128)(2,1)S(1)} %shard_map.75.h), channel_id=1, source_target_pairs={{0,64},{8,72},{16,80},{24,88},{32,96},{40,104},{48,112},{56,120},{... | collective-permute-start | bytes 712712 | tf_op jit(solution)/shard_map/ppermute | solution.py:287
  104.7 11.2 %collective-permute-start.26 = (bf16[4,232,128]{2,1,0:T(8,128)(2,1)S(1)}, bf16[4,232,128]{2,1,0:T(8,128)(2,1)S(1)}, u32[]{:S(2)}, u32[]{:S(2)}) collective-permute-start(bf16[4,232,128]{2,1,0:T(8,128)(2,1)S(1)} %shard_map.75.h), channel_id=1, source_target_pairs={{0,192},{8,200},{16,208},{24,216},{32,224},{40,232},{48,240},{56,2... | collective-permute-start | bytes 712712 | tf_op jit(solution)/shard_map/ppermute | solution.py:287
  129.1 2.8 %collective-permute-start.27 = (f32[16,256]{1,0:T(8,128)S(1)}, f32[16,256]{1,0:T(8,128)S(1)}, u32[]{:S(2)}, u32[]{:S(2)}) collective-permute-start(f32[16,256]{1,0:T(8,128)S(1)} %get-tuple-element.54), channel_id=1, source_target_pairs={{0,8},{8,0},{16,24},{24,16},{32,40},{40,32},{48,56},{56,48},{64,72... | collective-permute-start | bytes 49160 | tf_op jit(solution)/shard_map/ppermute | solution.py:287

commit v8 on v7

--- a/solution.py
+++ b/solution.py
@@ -303,7 +303,6 @@
     xb = NZ * zb
 
     low_other = permute(lower_factor, CORE)
-    u_branch = other(upper)
     down_other = permute(down_weight, CORE)
 
     high = lax.reduce_precision(router, 8, 7)
@@ -326,9 +325,9 @@
         lower_factor,
         low_other,
     )
-    lat, w_branch, u_branch = lax.optimization_barrier((lat, w_branch, u_branch))
+    lat, w_branch, u_late = lax.optimization_barrier((lat, w_branch, upper))
     w_other = permute(w_branch, CORE)
-    u_other = permute(u_branch, CORE)
+    u_other = permute(other(u_late), CORE)
     got = across(lat.reshape(tensor, half // tensor, columns))
     mid = run(functools.partial(mid_kernel, 2 * ranks), sds(got.shape), got)
     cat = across(mid).reshape(half, columns)

time: 134 us -> 134 us (level)
  waiting for transfers between devices: 33.4 us -> 34.9 us
  blocking collectives: 21.5 us -> 20.1 us
    ppermute x28, waiting for transfers between devices: 27.8 us -> 30.3 us  [permute(): return lax.ppermute(a, 'task', perm)]
    all_to_all x2, blocking collectives: 21.5 us -> 20.1 us  [across(): return lax.all_to_all(a, 'tensor', 0, 0)]
  transfers between devices with their start and end apart: 29 -> 29, of which waited for: 10 -> 12; matrix products, arithmetic and copies ran while one was open for 4% -> 3% of each run, Pallas kernels for 12% -> 13%
where the time goes in v8:
time: 134 us; the launch traced here: 133 us
  starting transfers between devices  51 us (38%)
  waiting for transfers between devices  34.9 us (26%)
  Pallas kernels  21.3 us (16%)
  blocking collectives  20.1 us (15%)
  local copies, waits for them, and re-layouts  4.77 us (4%)
    ppermute x28, starting transfers between devices, permute(): return lax.ppermute(a, 'task', perm)  46.3 us
    ppermute x28, waiting for transfers between devices, permute(): return lax.ppermute(a, 'task', perm)  30.3 us
    all_to_all x2, blocking collectives, across(): return lax.all_to_all(a, 'tensor', 0, 0)  20.1 us
    pallas_call x13, Pallas kernels, call(): pl.pallas_call(kernel, out_shape=out_shape, grid_spec=pltpu.PrefetchScala...  15.2 us
    all_to_all x1, starting transfers between devices, across(): return lax.all_to_all(a, 'tensor', 0, 0)  4.65 us
    all_to_all x1, waiting for transfers between devices, across(): return lax.all_to_all(a, 'tensor', 0, 0)  4.58 us
    pallas_call x2, Pallas kernels, call_inside(): pl.pallas_call(kernel, out_shape=out_shape, in_specs=[pl.BlockSpec(memory...  4.28 us
    squeeze x2, local copies, waits for them, and re-layouts, other(): return lax.dynamic_index_in_dim(a, 1 - c, 0, keepdims=False)  3.95 us
  transfers between devices with their start and end apart: 29, of which 12 were waited for; matrix products, arithmetic and copies ran while one was open for 3% of the time, Pallas kernels for 13%

profile of v8, /device:TPU:1, one launch (start us, length us, event | category | flops | bytes accessed | tf_op | source)
XLA Modules:
  0.0 133.0 jit_solution(17963185016566250393)
XLA Ops:
  0.0 0.7 fusion
  0.7 0.8 concatenate.3
  1.5 7.8 %collective-permute-start.1 = (bf16[8,1152]{1,0:T(8,128)(2,1)S(1)}, bf16[8,1152]{1,0:T(8,128)(2,1)S(1)}, u32[]{:S(2)}, u32[]{:S(2)}) collective-permute-start(bf16[8,1152]{1,0:T(8,128)(2,1)S(1)} %concatenate.3), channel_id=1, source_target_pairs={{0,32},{8,40},{16,48},{24,56},{32,0},{40,8},{48,16},{56,24},{64,96... | collective-permute-start | bytes 55304 | tf_op jit(solution)/shard_map/ppermute | solution.py:287
  9.3 1.2 collective-permute-start.2
  10.4 2.4 %collective-permute-start.3 = (bf16[8,1152]{1,0:T(8,128)(2,1)S(1)}, bf16[8,1152]{1,0:T(8,128)(2,1)S(1)}, u32[]{:S(2)}, u32[]{:S(2)}) collective-permute-start(bf16[8,1152]{1,0:T(8,128)(2,1)S(1)} %concatenate.3), channel_id=1, source_target_pairs={{0,48},{8,56},{16,0},{24,8},{32,16},{40,24},{48,32},{56,40},{64,11... | collective-permute-start | bytes 55304 | tf_op jit(solution)/shard_map/ppermute | solution.py:287
  12.8 1.5 %collective-permute-start.7 = (bf16[2,1024,128]{2,1,0:T(8,128)(2,1)}, bf16[2,1024,128]{2,1,0:T(8,128)(2,1)S(1)}, u32[]{:S(2)}, u32[]{:S(2)}) collective-permute-start(bf16[2,1024,128]{2,1,0:T(8,128)(2,1)} %low_own.1), channel_id=1, source_target_pairs={{0,8},{8,0},{16,24},{24,16},{32,40},{40,32},{48,56},{56,48},{64,72... | collective-permute-start | bytes 1572872 | tf_op jit(solution)/shard_map/ppermute | solution.py:287
  14.3 0.1 pad_add_fusion.s
  14.5 0.0 copy-start.1
  14.5 2.8 %collective-permute-start.4 = (bf16[4,8,1152]{2,1,0:T(8,128)(2,1)S(1)}, bf16[4,8,1152]{2,1,0:T(8,128)(2,1)S(1)}, u32[]{:S(2)}, u32[]{:S(2)}) collective-permute-start(bf16[4,8,1152]{2,1,0:T(8,128)(2,1)S(1)} %pad_maximum_fusion.own), channel_id=1, source_target_pairs={{0,128},{8,136},{16,144},{24,152},{32,160},{40,168},{48,176},{56,1... | collective-permute-start | bytes 221192 | tf_op jit(solution)/shard_map/ppermute | solution.py:287
  17.3 0.3 collective-permute-start.5
  17.6 2.4 %collective-permute-start.6 = (bf16[4,8,1152]{2,1,0:T(8,128)(2,1)S(1)}, bf16[4,8,1152]{2,1,0:T(8,128)(2,1)S(1)}, u32[]{:S(2)}, u32[]{:S(2)}) collective-permute-start(bf16[4,8,1152]{2,1,0:T(8,128)(2,1)S(1)} %pad_maximum_fusion.own), channel_id=1, source_target_pairs={{0,192},{8,200},{16,208},{24,216},{32,224},{40,232},{48,240},{56,2... | collective-permute-start | bytes 221192 | tf_op jit(solution)/shard_map/ppermute | solution.py:287
  20.0 2.9 %dynamic-slice_bitcast_fusion = bf16[3696,256]{1,0:T(8,128)(2,1)} fusion(bf16[2,3696,256]{2,1,0:T(8,128)(2,1)} %bitcast.35, s32[]{:T(128)S(6)} %select_n.16), kind=kLoop, calls=%fused_computation | loop fusion | bytes 3784708 | tf_op jit(solution)/shard_map/jit(dynamic_index_in_dim)/squeeze | solution.py:293
  22.9 1.6 %shard_map.64 = bf16[16,8,1024]{2,1,0:T(8,128)(2,1)} custom-call(s32[4]{0:T(128)S(1)} %pad_add_fusion.s, bf16[4,8,1152]{2,1,0:T(8,128)(2,1)S(1)} %pad_maximum_fusion.own, bf16[4,8,1152]{2,1,0:T(8,128)(2,1)S(1)} %collective-permute-done.4.far, bf16[4,8,1152]{2,1,0:T(8,128)(2,1)S(1)} %collective-permute-done.5.up, ...), custom_call_target="tpu_custom_call" | custom-call | tf_op jit(solution)/shard_map/pallas_call | solution.py:54
  24.5 2.7 %collective-permute-start.9 = (bf16[3696,256]{1,0:T(8,128)(2,1)}, bf16[3696,256]{1,0:T(8,128)(2,1)}, u32[]{:S(2)}, u32[]{:S(2)}) collective-permute-start(bf16[3696,256]{1,0:T(8,128)(2,1)} %dynamic-slice_bitcast_fusion), channel_id=1, source_target_pairs={{0,8},{8,0},{16,24},{24,16},{32,40},{40,32},{48,56},{56,48},{64,72... | collective-permute-start | bytes 5677064 | tf_op jit(solution)/shard_map/ppermute | solution.py:287
  27.2 4.6 %all-to-all-start = ((bf16[8,16,1024]{2,1,0:T(8,128)(2,1)}), bf16[8,16,1024]{2,1,0:T(8,128)(2,1)S(1)}, u32[]{:S(2)}, u32[]{:S(2)}) async-start(bf16[8,16,1024]{2,1,0:T(8,128)(2,1)} %bitcast.11), calls=%async_computation | async-start | bytes 524288 | tf_op jit(solution)/shard_map/all_to_all | solution.py:290
  31.9 1.0 dynamic-slice_bitcast_fusion.1
  32.9 0.3 collective-permute-start.10
  33.2 0.2 collective-permute-start
  33.4 4.6 %all-to-all-done.got = bf16[8,16,1024]{2,1,0:T(8,128)(2,1)S(1)} async-done(((bf16[8,16,1024]{2,1,0:T(8,128)(2,1)}), bf16[8,16,1024]{2,1,0:T(8,128)(2,1)S(1)}, u32[]{:S(2)}, u32[]{:S(2)}) %all-to-all-start) | async-done | bytes 262176 | tf_op jit(solution)/shard_map/all_to_all | solution.py:290
  38.0 0.6 shard_map.65
  38.6 10.1 %all_to_all.15 = bf16[8,16,1024]{2,1,0:T(8,128)(2,1)S(1)} all-to-all(bf16[8,16,1024]{2,1,0:T(8,128)(2,1)S(1)} %shard_map.65), channel_id=1, replica_groups=mesh['task'=32,'tensor'=8] {'tensor'}, dimensions={0} | all-to-all | bytes 524288 | tf_op jit(solution)/shard_map/all_to_all | solution.py:290
  48.7 2.0 %collective-permute-start.8 = (bf16[128,1024]{1,0:T(8,128)(2,1)S(1)}, bf16[128,1024]{1,0:T(8,128)(2,1)S(1)}, u32[]{:S(2)}, u32[]{:S(2)}) collective-permute-start(bf16[128,1024]{1,0:T(8,128)(2,1)S(1)} %bitcast.30), channel_id=1, source_target_pairs={{0,8},{8,0},{16,24},{24,16},{32,40},{40,32},{48,56},{56,48},{64,72... | collective-permute-start | bytes 786440 | tf_op jit(solution)/shard_map/ppermute | solution.py:287
  50.7 1.8 %shard_map.69.w = bf16[928,768]{1,0:T(8,128)(2,1)S(1)} custom-call(s32[4]{0:T(128)S(1)} %pad_add_fusion.s, bf16[2,3696,256]{2,1,0:T(8,128)(2,1)} %bitcast.36, bf16[3696,256]{1,0:T(8,128)(2,1)} %collective-permute-done.9.w_other, bf16[2,3696,128]{2,1,0:T(8,128)(2,1)S(1)} %bitcast.19, bf16[3696,128]{1,0:T(8,128)(2,1)S(1)} %collective-permute-done.10.u_other), custom_call_target="tpu_custom_call" | custom-call | tf_op jit(solution)/shard_map/pallas_call | solution.py:367
  52.5 1.1 shard_map.70
  53.6 0.1 collective-permute-start.12
  53.7 2.7 %collective-permute-start.13 = (bf16[2,232,256]{2,1,0:T(8,128)(2,1)S(1)}, bf16[2,232,256]{2,1,0:T(8,128)(2,1)S(1)}, u32[]{:S(2)}, u32[]{:S(2)}) collective-permute-start(bf16[2,232,256]{2,1,0:T(8,128)(2,1)S(1)} %get-tuple-element.40), channel_id=1, source_target_pairs={{0,192},{8,200},{16,208},{24,216},{32,224},{40,232},{48,240},{56,2... | collective-permute-start | bytes 712712 | tf_op jit(solution)/shard_map/ppermute | solution.py:287
  56.4 2.4 %shard_map.67 = (bf16[2,232,256]{2,1,0:T(8,128)(2,1)S(1)}, bf16[2,232,256]{2,1,0:T(8,128)(2,1)S(1)}) custom-call(s32[4]{0:T(128)S(1)} %pad_add_fusion.s, bf16[128,1024]{1,0:T(8,128)(2,1)S(1)} %bitcast.32, bf16[128,1024]{1,0:T(8,128)(2,1)S(1)} %collective-permute-done.8.rows_other, bf16[2,3696,256]{2,1,0:T(8,128)(2,1)} %bitcast.37, ...), custom_call_target="tpu_custom_call" | custom-call | tf_op jit(solution)/shard_map/pallas_call | solution.py:54
  58.8 1.2 collective-permute-start.11
  60.0 0.4 collective-permute-start.15
  60.3 2.4 %shard_map.68 = (f32[2,232,256]{2,1,0:T(8,128)S(1)}, f32[2,232,256]{2,1,0:T(8,128)S(1)}) custom-call(s32[4]{0:T(128)S(1)} %pad_add_fusion.s, bf16[128,1024]{1,0:T(8,128)(2,1)S(1)} %bitcast.33, bf16[128,1024]{1,0:T(8,128)(2,1)S(1)} %collective-permute-done.8.rows_other, bf16[2,3696,256]{2,1,0:T(8,128)(2,1)} %bitcast.39, bf16[2,3696,256]{2,1,0:T(8,128)(2,1)} %bitcast.40, ...), custom_call_target="tpu_custom_call" | custom-call | tf_op jit(solution)/shard_map/pallas_call | solution.py:54
  62.8 0.6 shard_map.71
  63.4 0.1 collective-permute-start.14
  63.5 2.6 %collective-permute-start.16 = (bf16[2,232,256]{2,1,0:T(8,128)(2,1)S(1)}, bf16[2,232,256]{2,1,0:T(8,128)(2,1)S(1)}, u32[]{:S(2)}, u32[]{:S(2)}) collective-permute-start(bf16[2,232,256]{2,1,0:T(8,128)(2,1)S(1)} %get-tuple-element.44), channel_id=1, source_target_pairs={{0,192},{8,200},{16,208},{24,216},{32,224},{40,232},{48,240},{56,2... | collective-permute-start | bytes 712712 | tf_op jit(solution)/shard_map/ppermute | solution.py:287
  66.1 2.3 %shard_map.66 = (f32[2,232,256]{2,1,0:T(8,128)S(1)}, f32[2,232,256]{2,1,0:T(8,128)S(1)}) custom-call(s32[4]{0:T(128)S(1)} %pad_add_fusion.s, bf16[128,1024]{1,0:T(8,128)(2,1)S(1)} %bitcast.34, bf16[128,1024]{1,0:T(8,128)(2,1)S(1)} %collective-permute-done.8.rows_other, bf16[2,3696,256]{2,1,0:T(8,128)(2,1)} %bitcast.41, ...), custom_call_target="tpu_custom_call" | custom-call | tf_op jit(solution)/shard_map/pallas_call | solution.py:54
  68.5 4.3 %collective-permute-done.14.a2 = bf16[2,232,256]{2,1,0:T(8,128)(2,1)S(1)} collective-permute-done((bf16[2,232,256]{2,1,0:T(8,128)(2,1)S(1)}, bf16[2,232,256]{2,1,0:T(8,128)(2,1)S(1)}, u32[]{:S(2)}, u32[]{:S(2)}) %collective-permute-start.14) | collective-permute-done | bytes 237600 | tf_op jit(solution)/shard_map/ppermute | solution.py:287
  72.7 0.8 shard_map.72
  73.5 1.9 %collective-permute-start.17 = (bf16[232,256]{1,0:T(8,128)(2,1)S(1)}, bf16[232,256]{1,0:T(8,128)(2,1)S(1)}, u32[]{:S(2)}, u32[]{:S(2)}) collective-permute-start(bf16[232,256]{1,0:T(8,128)(2,1)S(1)} %get-tuple-element.46), channel_id=1, source_target_pairs={{0,32},{8,40},{16,48},{24,56},{32,0},{40,8},{48,16},{56,24},{64,96... | collective-permute-start | bytes 356360 | tf_op jit(solution)/shard_map/ppermute | solution.py:287
  75.4 3.9 %collective-permute-start.18 = (bf16[232,256]{1,0:T(8,128)(2,1)S(1)}, bf16[232,256]{1,0:T(8,128)(2,1)S(1)}, u32[]{:S(2)}, u32[]{:S(2)}) collective-permute-start(bf16[232,256]{1,0:T(8,128)(2,1)S(1)} %get-tuple-element.47), channel_id=1, source_target_pairs={{0,16},{8,24},{16,32},{24,40},{32,48},{40,56},{48,0},{56,8},{64,80... | collective-permute-start | bytes 356360 | tf_op jit(solution)/shard_map/ppermute | solution.py:287
  79.3 2.1 %collective-permute-done.17.a1 = bf16[232,256]{1,0:T(8,128)(2,1)S(1)} collective-permute-done((bf16[232,256]{1,0:T(8,128)(2,1)S(1)}, bf16[232,256]{1,0:T(8,128)(2,1)S(1)}, u32[]{:S(2)}, u32[]{:S(2)}) %collective-permute-start.17) | collective-permute-done | bytes 118816 | tf_op jit(solution)/shard_map/ppermute | solution.py:287
  81.4 3.8 %collective-permute-done.18.a2 = bf16[232,256]{1,0:T(8,128)(2,1)S(1)} collective-permute-done((bf16[232,256]{1,0:T(8,128)(2,1)S(1)}, bf16[232,256]{1,0:T(8,128)(2,1)S(1)}, u32[]{:S(2)}, u32[]{:S(2)}) %collective-permute-start.18) | collective-permute-done | bytes 118816 | tf_op jit(solution)/shard_map/ppermute | solution.py:287
  85.1 5.2 %collective-permute-done.19.a3 = bf16[232,256]{1,0:T(8,128)(2,1)S(1)} collective-permute-done((bf16[232,256]{1,0:T(8,128)(2,1)S(1)}, bf16[232,256]{1,0:T(8,128)(2,1)S(1)}, u32[]{:S(2)}, u32[]{:S(2)}) %collective-permute-start.19) | collective-permute-done | bytes 118816 | tf_op jit(solution)/shard_map/ppermute | solution.py:287
  90.3 0.6 shard_map.73
  90.9 0.6 collective-permute-start.20
  91.5 1.0 collective-permute-done.20.got
  92.5 0.6 shard_map.74.h0
  93.1 1.0 collective-permute-start.21
  94.1 2.4 %collective-permute-start.22 = (bf16[232,128]{1,0:T(8,128)(2,1)S(1)}, bf16[232,128]{1,0:T(8,128)(2,1)S(1)}, u32[]{:S(2)}, u32[]{:S(2)}) collective-permute-start(bf16[232,128]{1,0:T(8,128)(2,1)S(1)} %shard_map.74.h0), channel_id=1, source_target_pairs={{0,16},{8,24},{16,32},{24,40},{32,48},{40,56},{48,0},{56,8},{64,80... | collective-permute-start | bytes 178184 | tf_op jit(solution)/shard_map/ppermute | solution.py:287
  96.5 1.2 collective-permute-start.23
  97.7 2.6 %collective-permute-done.21.h2 = bf16[232,128]{1,0:T(8,128)(2,1)S(1)} collective-permute-done((bf16[232,128]{1,0:T(8,128)(2,1)S(1)}, bf16[232,128]{1,0:T(8,128)(2,1)S(1)}, u32[]{:S(2)}, u32[]{:S(2)}) %collective-permute-start.21) | collective-permute-done | bytes 59424 | tf_op jit(solution)/shard_map/ppermute | solution.py:287
  100.3 1.4 %collective-permute-done.22.h1 = bf16[232,128]{1,0:T(8,128)(2,1)S(1)} collective-permute-done((bf16[232,128]{1,0:T(8,128)(2,1)S(1)}, bf16[232,128]{1,0:T(8,128)(2,1)S(1)}, u32[]{:S(2)}, u32[]{:S(2)}) %collective-permute-start.22) | collective-permute-done | bytes 59424 | tf_op jit(solution)/shard_map/ppermute | solution.py:287
  101.7 0.9 collective-permute-done.23.h3
  102.7 0.6 shard_map.75.h
  103.2 0.1 collective-permute-start.24
  103.3 0.9 collective-permute-start.25
  104.2 1.9 %collective-permute-start.26 = (bf16[4,232,128]{2,1,0:T(8,128)(2,1)S(1)}, bf16[4,232,128]{2,1,0:T(8,128)(2,1)S(1)}, u32[]{:S(2)}, u32[]{:S(2)}) collective-permute-start(bf16[4,232,128]{2,1,0:T(8,128)(2,1)S(1)} %shard_map.75.h), channel_id=1, source_target_pairs={{0,192},{8,200},{16,208},{24,216},{32,224},{40,232},{48,240},{56,2... | collective-permute-start | bytes 712712 | tf_op jit(solution)/shard_map/ppermute | solution.py:287
  106.1 3.0 %shard_map.76 = (bf16[3696,512]{1,0:T(8,128)(2,1)S(1)}, f32[128,512]{1,0:T(8,128)S(1)}) custom-call(s32[4]{0:T(128)S(1)} %pad_add_fusion.s, bf16[3696,256]{1,0:T(8,128)(2,1)} %w_own.1, bf16[3696,256]{1,0:T(8,128)(2,1)} %collective-permute-done.w_other, bf16[4,232,128]{2,1,0:T(8,128)(2,1)S(1)} %shard_map.75.h), custom_call_target="tpu_custom_call" | custom-call | tf_op jit(solution)/shard_map/pallas_call | solution.py:72
  109.1 2.0 %collective-permute-done.24.h2 = bf16[4,232,128]{2,1,0:T(8,128)(2,1)S(1)} collective-permute-done((bf16[4,232,128]{2,1,0:T(8,128)(2,1)S(1)}, bf16[4,232,128]{2,1,0:T(8,128)(2,1)S(1)}, u32[]{:S(2)}, u32[]{:S(2)}) %collective-permute-start.24) | collective-permute-done | bytes 237600 | tf_op jit(solution)/shard_map/ppermute | solution.py:287
  111.1 6.2 %collective-permute-done.25.h1 = bf16[4,232,128]{2,1,0:T(8,128)(2,1)S(1)} collective-permute-done((bf16[4,232,128]{2,1,0:T(8,128)(2,1)S(1)}, bf16[4,232,128]{2,1,0:T(8,128)(2,1)S(1)}, u32[]{:S(2)}, u32[]{:S(2)}) %collective-permute-start.25) | collective-permute-done | bytes 237600 | tf_op jit(solution)/shard_map/ppermute | solution.py:287
  117.2 1.3 shard_map.77
  118.5 10.0 %all_to_all.16.got = bf16[8,16,512]{2,1,0:T(8,128)(2,1)S(1)} all-to-all(bf16[8,16,512]{2,1,0:T(8,128)(2,1)S(1)} %shard_map.77), channel_id=1, replica_groups=mesh['task'=32,'tensor'=8] {'tensor'}, dimensions={0} | all-to-all | bytes 262144 | tf_op jit(solution)/shard_map/all_to_all | solution.py:290
  128.6 0.6 shard_map.78
  129.1 1.9 %collective-permute-start.27 = (f32[16,256]{1,0:T(8,128)S(1)}, f32[16,256]{1,0:T(8,128)S(1)}, u32[]{:S(2)}, u32[]{:S(2)}) collective-permute-start(f32[16,256]{1,0:T(8,128)S(1)} %get-tuple-element.54), channel_id=1, source_target_pairs={{0,8},{8,0},{16,24},{24,16},{32,40},{40,32},{48,56},{56,48},{64,72... | collective-permute-start | bytes 49160 | tf_op jit(solution)/shard_map/ppermute | solution.py:287
  131.0 0.8 collective-permute-done.27.got
  131.9 1.2 shard_map.79
  (23 shorter events, 0.1 us)
Async XLA Ops:
  1.5 12.9 %collective-permute-start.1 = (bf16[8,1152]{1,0:T(8,128)(2,1)S(1)}, bf16[8,1152]{1,0:T(8,128)(2,1)S(1)}, u32[]{:S(2)}, u32[]{:S(2)}) collective-permute-start(bf16[8,1152]{1,0:T(8,128)(2,1)S(1)} %concatenate.3), channel_id=1, source_target_pairs={{0,32},{8,40},{16,48},{24,56},{32,0},{40,8},{48,16},{56,24},{64,96... | collective-permute-start | bytes 55304 | tf_op jit(solution)/shard_map/ppermute | solution.py:287
  9.3 5.2 %collective-permute-start.2 = (bf16[8,1152]{1,0:T(8,128)(2,1)S(1)}, bf16[8,1152]{1,0:T(8,128)(2,1)S(1)}, u32[]{:S(2)}, u32[]{:S(2)}) collective-permute-start(bf16[8,1152]{1,0:T(8,128)(2,1)S(1)} %concatenate.3), channel_id=1, source_target_pairs={{0,16},{8,24},{16,32},{24,40},{32,48},{40,56},{48,0},{56,8},{64,80... | collective-permute-start | bytes 55304 | tf_op jit(solution)/shard_map/ppermute | solution.py:287
  10.4 4.0 %collective-permute-start.3 = (bf16[8,1152]{1,0:T(8,128)(2,1)S(1)}, bf16[8,1152]{1,0:T(8,128)(2,1)S(1)}, u32[]{:S(2)}, u32[]{:S(2)}) collective-permute-start(bf16[8,1152]{1,0:T(8,128)(2,1)S(1)} %concatenate.3), channel_id=1, source_target_pairs={{0,48},{8,56},{16,0},{24,8},{32,16},{40,24},{48,32},{56,40},{64,11... | collective-permute-start | bytes 55304 | tf_op jit(solution)/shard_map/ppermute | solution.py:287
  12.8 10.1 %collective-permute-start.7 = (bf16[2,1024,128]{2,1,0:T(8,128)(2,1)}, bf16[2,1024,128]{2,1,0:T(8,128)(2,1)S(1)}, u32[]{:S(2)}, u32[]{:S(2)}) collective-permute-start(bf16[2,1024,128]{2,1,0:T(8,128)(2,1)} %low_own.1), channel_id=1, source_target_pairs={{0,8},{8,0},{16,24},{24,16},{32,40},{40,32},{48,56},{56,48},{64,72... | collective-permute-start | bytes 1572872 | tf_op jit(solution)/shard_map/ppermute | solution.py:287
  14.5 8.5 %copy-start.1 = (bf16[2,1024,128]{2,1,0:T(8,128)(2,1)S(1)}, bf16[2,1024,128]{2,1,0:T(8,128)(2,1)}, u32[]{:S(2)}) copy-start(bf16[2,1024,128]{2,1,0:T(8,128)(2,1)} %low_own.1) | copy-start | bytes 1572868
  14.5 8.4 %collective-permute-start.4 = (bf16[4,8,1152]{2,1,0:T(8,128)(2,1)S(1)}, bf16[4,8,1152]{2,1,0:T(8,128)(2,1)S(1)}, u32[]{:S(2)}, u32[]{:S(2)}) collective-permute-start(bf16[4,8,1152]{2,1,0:T(8,128)(2,1)S(1)} %pad_maximum_fusion.own), channel_id=1, source_target_pairs={{0,128},{8,136},{16,144},{24,152},{32,160},{40,168},{48,176},{56,1... | collective-permute-start | bytes 221192 | tf_op jit(solution)/shard_map/ppermute | solution.py:287
  17.3 5.6 %collective-permute-start.5 = (bf16[4,8,1152]{2,1,0:T(8,128)(2,1)S(1)}, bf16[4,8,1152]{2,1,0:T(8,128)(2,1)S(1)}, u32[]{:S(2)}, u32[]{:S(2)}) collective-permute-start(bf16[4,8,1152]{2,1,0:T(8,128)(2,1)S(1)} %pad_maximum_fusion.own), channel_id=1, source_target_pairs={{0,64},{8,72},{16,80},{24,88},{32,96},{40,104},{48,112},{56,120},{... | collective-permute-start | bytes 221192 | tf_op jit(solution)/shard_map/ppermute | solution.py:287
  17.6 5.3 %collective-permute-start.6 = (bf16[4,8,1152]{2,1,0:T(8,128)(2,1)S(1)}, bf16[4,8,1152]{2,1,0:T(8,128)(2,1)S(1)}, u32[]{:S(2)}, u32[]{:S(2)}) collective-permute-start(bf16[4,8,1152]{2,1,0:T(8,128)(2,1)S(1)} %pad_maximum_fusion.own), channel_id=1, source_target_pairs={{0,192},{8,200},{16,208},{24,216},{32,224},{40,232},{48,240},{56,2... | collective-permute-start | bytes 221192 | tf_op jit(solution)/shard_map/ppermute | solution.py:287
  22.9 9.0 %copy-start = (bf16[2,128,3696]{1,2,0:T(8,128)(2,1)S(1)}, bf16[2,128,3696]{1,2,0:T(8,128)(2,1)}, u32[]{:S(2)}) copy-start(bf16[2,128,3696]{1,2,0:T(8,128)(2,1)} %param.11) | copy-start | bytes 5677060
  24.5 26.2 %collective-permute-start.9 = (bf16[3696,256]{1,0:T(8,128)(2,1)}, bf16[3696,256]{1,0:T(8,128)(2,1)}, u32[]{:S(2)}, u32[]{:S(2)}) collective-permute-start(bf16[3696,256]{1,0:T(8,128)(2,1)} %dynamic-slice_bitcast_fusion), channel_id=1, source_target_pairs={{0,8},{8,0},{16,24},{24,16},{32,40},{40,32},{48,56},{56,48},{64,72... | collective-permute-start | bytes 5677064 | tf_op jit(solution)/shard_map/ppermute | solution.py:287
  27.2 10.8 %all-to-all-start = ((bf16[8,16,1024]{2,1,0:T(8,128)(2,1)}), bf16[8,16,1024]{2,1,0:T(8,128)(2,1)S(1)}, u32[]{:S(2)}, u32[]{:S(2)}) async-start(bf16[8,16,1024]{2,1,0:T(8,128)(2,1)} %bitcast.11), calls=%async_computation | async-start | bytes 524288 | tf_op jit(solution)/shard_map/all_to_all | solution.py:290
  32.9 17.7 %collective-permute-start.10 = (bf16[3696,128]{1,0:T(8,128)(2,1)}, bf16[3696,128]{1,0:T(8,128)(2,1)S(1)}, u32[]{:S(2)}, u32[]{:S(2)}) collective-permute-start(bf16[3696,128]{1,0:T(8,128)(2,1)} %dynamic-slice_bitcast_fusion.1), channel_id=1, source_target_pairs={{0,8},{8,0},{16,24},{24,16},{32,40},{40,32},{48,56},{56,48},{64,72... | collective-permute-start | bytes 2838536 | tf_op jit(solution)/shard_map/ppermute | solution.py:287
  33.2 72.9 %collective-permute-start = (bf16[3696,256]{1,0:T(8,128)(2,1)}, bf16[3696,256]{1,0:T(8,128)(2,1)}, u32[]{:S(2)}, u32[]{:S(2)}) collective-permute-start(bf16[3696,256]{1,0:T(8,128)(2,1)} %w_own.1), channel_id=1, source_target_pairs={{0,8},{8,0},{16,24},{24,16},{32,40},{40,32},{48,56},{56,48},{64,72... | collective-permute-start | bytes 5677064 | tf_op jit(solution)/shard_map/ppermute | solution.py:287
  48.7 3.8 %collective-permute-start.8 = (bf16[128,1024]{1,0:T(8,128)(2,1)S(1)}, bf16[128,1024]{1,0:T(8,128)(2,1)S(1)}, u32[]{:S(2)}, u32[]{:S(2)}) collective-permute-start(bf16[128,1024]{1,0:T(8,128)(2,1)S(1)} %bitcast.30), channel_id=1, source_target_pairs={{0,8},{8,0},{16,24},{24,16},{32,40},{40,32},{48,56},{56,48},{64,72... | collective-permute-start | bytes 786440 | tf_op jit(solution)/shard_map/ppermute | solution.py:287
  53.6 9.1 %collective-permute-start.12 = (bf16[2,232,256]{2,1,0:T(8,128)(2,1)S(1)}, bf16[2,232,256]{2,1,0:T(8,128)(2,1)S(1)}, u32[]{:S(2)}, u32[]{:S(2)}) collective-permute-start(bf16[2,232,256]{2,1,0:T(8,128)(2,1)S(1)} %get-tuple-element.38), channel_id=1, source_target_pairs={{0,64},{8,72},{16,80},{24,88},{32,96},{40,104},{48,112},{56,120},{... | collective-permute-start | bytes 712712 | tf_op jit(solution)/shard_map/ppermute | solution.py:287
  53.7 9.1 %collective-permute-start.13 = (bf16[2,232,256]{2,1,0:T(8,128)(2,1)S(1)}, bf16[2,232,256]{2,1,0:T(8,128)(2,1)S(1)}, u32[]{:S(2)}, u32[]{:S(2)}) collective-permute-start(bf16[2,232,256]{2,1,0:T(8,128)(2,1)S(1)} %get-tuple-element.40), channel_id=1, source_target_pairs={{0,192},{8,200},{16,208},{24,216},{32,224},{40,232},{48,240},{56,2... | collective-permute-start | bytes 712712 | tf_op jit(solution)/shard_map/ppermute | solution.py:287
  58.8 9.7 %collective-permute-start.11 = (bf16[2,232,256]{2,1,0:T(8,128)(2,1)S(1)}, bf16[2,232,256]{2,1,0:T(8,128)(2,1)S(1)}, u32[]{:S(2)}, u32[]{:S(2)}) collective-permute-start(bf16[2,232,256]{2,1,0:T(8,128)(2,1)S(1)} %get-tuple-element.36), channel_id=1, source_target_pairs={{0,192},{8,200},{16,208},{24,216},{32,224},{40,232},{48,240},{56,2... | collective-permute-start | bytes 712712 | tf_op jit(solution)/shard_map/ppermute | solution.py:287
  60.0 8.5 %collective-permute-start.15 = (bf16[2,232,256]{2,1,0:T(8,128)(2,1)S(1)}, bf16[2,232,256]{2,1,0:T(8,128)(2,1)S(1)}, u32[]{:S(2)}, u32[]{:S(2)}) collective-permute-start(bf16[2,232,256]{2,1,0:T(8,128)(2,1)S(1)} %get-tuple-element.43), channel_id=1, source_target_pairs={{0,64},{8,72},{16,80},{24,88},{32,96},{40,104},{48,112},{56,120},{... | collective-permute-start | bytes 712712 | tf_op jit(solution)/shard_map/ppermute | solution.py:287
  63.4 9.3 %collective-permute-start.14 = (bf16[2,232,256]{2,1,0:T(8,128)(2,1)S(1)}, bf16[2,232,256]{2,1,0:T(8,128)(2,1)S(1)}, u32[]{:S(2)}, u32[]{:S(2)}) collective-permute-start(bf16[2,232,256]{2,1,0:T(8,128)(2,1)S(1)} %get-tuple-element.41), channel_id=1, source_target_pairs={{0,64},{8,72},{16,80},{24,88},{32,96},{40,104},{48,112},{56,120},{... | collective-permute-start | bytes 712712 | tf_op jit(solution)/shard_map/ppermute | solution.py:287
  63.5 9.2 %collective-permute-start.16 = (bf16[2,232,256]{2,1,0:T(8,128)(2,1)S(1)}, bf16[2,232,256]{2,1,0:T(8,128)(2,1)S(1)}, u32[]{:S(2)}, u32[]{:S(2)}) collective-permute-start(bf16[2,232,256]{2,1,0:T(8,128)(2,1)S(1)} %get-tuple-element.44), channel_id=1, source_target_pairs={{0,192},{8,200},{16,208},{24,216},{32,224},{40,232},{48,240},{56,2... | collective-permute-start | bytes 712712 | tf_op jit(solution)/shard_map/ppermute | solution.py:287
  73.5 7.9 %collective-permute-start.17 = (bf16[232,256]{1,0:T(8,128)(2,1)S(1)}, bf16[232,256]{1,0:T(8,128)(2,1)S(1)}, u32[]{:S(2)}, u32[]{:S(2)}) collective-permute-start(bf16[232,256]{1,0:T(8,128)(2,1)S(1)} %get-tuple-element.46), channel_id=1, source_target_pairs={{0,32},{8,40},{16,48},{24,56},{32,0},{40,8},{48,16},{56,24},{64,96... | collective-permute-start | bytes 356360 | tf_op jit(solution)/shard_map/ppermute | solution.py:287
  75.4 9.7 %collective-permute-start.18 = (bf16[232,256]{1,0:T(8,128)(2,1)S(1)}, bf16[232,256]{1,0:T(8,128)(2,1)S(1)}, u32[]{:S(2)}, u32[]{:S(2)}) collective-permute-start(bf16[232,256]{1,0:T(8,128)(2,1)S(1)} %get-tuple-element.47), channel_id=1, source_target_pairs={{0,16},{8,24},{16,32},{24,40},{32,48},{40,56},{48,0},{56,8},{64,80... | collective-permute-start | bytes 356360 | tf_op jit(solution)/shard_map/ppermute | solution.py:287
  79.3 11.1 %collective-permute-start.19 = (bf16[232,256]{1,0:T(8,128)(2,1)S(1)}, bf16[232,256]{1,0:T(8,128)(2,1)S(1)}, u32[]{:S(2)}, u32[]{:S(2)}) collective-permute-start(bf16[232,256]{1,0:T(8,128)(2,1)S(1)} %get-tuple-element.48), channel_id=1, source_target_pairs={{0,48},{8,56},{16,0},{24,8},{32,16},{40,24},{48,32},{56,40},{64,11... | collective-permute-start | bytes 356360 | tf_op jit(solution)/shard_map/ppermute | solution.py:287
  90.9 1.6 %collective-permute-start.20 = (f32[232,128]{1,0:T(8,128)S(1)}, f32[232,128]{1,0:T(8,128)S(1)}, u32[]{:S(2)}, u32[]{:S(2)}) collective-permute-start(f32[232,128]{1,0:T(8,128)S(1)} %get-tuple-element.50), channel_id=1, source_target_pairs={{0,8},{8,0},{16,24},{24,16},{32,40},{40,32},{48,56},{56,48},{64,72... | collective-permute-start | bytes 356360 | tf_op jit(solution)/shard_map/ppermute | solution.py:287
  93.1 7.3 %collective-permute-start.21 = (bf16[232,128]{1,0:T(8,128)(2,1)S(1)}, bf16[232,128]{1,0:T(8,128)(2,1)S(1)}, u32[]{:S(2)}, u32[]{:S(2)}) collective-permute-start(bf16[232,128]{1,0:T(8,128)(2,1)S(1)} %shard_map.74.h0), channel_id=1, source_target_pairs={{0,32},{8,40},{16,48},{24,56},{32,0},{40,8},{48,16},{56,24},{64,96... | collective-permute-start | bytes 178184 | tf_op jit(solution)/shard_map/ppermute | solution.py:287
  94.1 7.6 %collective-permute-start.22 = (bf16[232,128]{1,0:T(8,128)(2,1)S(1)}, bf16[232,128]{1,0:T(8,128)(2,1)S(1)}, u32[]{:S(2)}, u32[]{:S(2)}) collective-permute-start(bf16[232,128]{1,0:T(8,128)(2,1)S(1)} %shard_map.74.h0), channel_id=1, source_target_pairs={{0,16},{8,24},{16,32},{24,40},{32,48},{40,56},{48,0},{56,8},{64,80... | collective-permute-start | bytes 178184 | tf_op jit(solution)/shard_map/ppermute | solution.py:287
  96.5 6.2 %collective-permute-start.23 = (bf16[232,128]{1,0:T(8,128)(2,1)S(1)}, bf16[232,128]{1,0:T(8,128)(2,1)S(1)}, u32[]{:S(2)}, u32[]{:S(2)}) collective-permute-start(bf16[232,128]{1,0:T(8,128)(2,1)S(1)} %shard_map.74.h0), channel_id=1, source_target_pairs={{0,48},{8,56},{16,0},{24,8},{32,16},{40,24},{48,32},{56,40},{64,11... | collective-permute-start | bytes 178184 | tf_op jit(solution)/shard_map/ppermute | solution.py:287
  103.2 7.8 %collective-permute-start.24 = (bf16[4,232,128]{2,1,0:T(8,128)(2,1)S(1)}, bf16[4,232,128]{2,1,0:T(8,128)(2,1)S(1)}, u32[]{:S(2)}, u32[]{:S(2)}) collective-permute-start(bf16[4,232,128]{2,1,0:T(8,128)(2,1)S(1)} %shard_map.75.h), channel_id=1, source_target_pairs={{0,128},{8,136},{16,144},{24,152},{32,160},{40,168},{48,176},{56,1... | collective-permute-start | bytes 712712 | tf_op jit(solution)/shard_map/ppermute | solution.py:287
  103.3 13.9 %collective-permute-start.25 = (bf16[4,232,128]{2,1,0:T(8,128)(2,1)S(1)}, bf16[4,232,128]{2,1,0:T(8,128)(2,1)S(1)}, u32[]{:S(2)}, u32[]{:S(2)}) collective-permute-start(bf16[4,232,128]{2,1,0:T(8,128)(2,1)S(1)} %shard_map.75.h), channel_id=1, source_target_pairs={{0,64},{8,72},{16,80},{24,88},{32,96},{40,104},{48,112},{56,120},{... | collective-permute-start | bytes 712712 | tf_op jit(solution)/shard_map/ppermute | solution.py:287
  104.2 13.0 %collective-permute-start.26 = (bf16[4,232,128]{2,1,0:T(8,128)(2,1)S(1)}, bf16[4,232,128]{2,1,0:T(8,128)(2,1)S(1)}, u32[]{:S(2)}, u32[]{:S(2)}) collective-permute-start(bf16[4,232,128]{2,1,0:T(8,128)(2,1)S(1)} %shard_map.75.h), channel_id=1, source_target_pairs={{0,192},{8,200},{16,208},{24,216},{32,224},{40,232},{48,240},{56,2... | collective-permute-start | bytes 712712 | tf_op jit(solution)/shard_map/ppermute | solution.py:287
  129.1 2.7 %collective-permute-start.27 = (f32[16,256]{1,0:T(8,128)S(1)}, f32[16,256]{1,0:T(8,128)S(1)}, u32[]{:S(2)}, u32[]{:S(2)}) collective-permute-start(f32[16,256]{1,0:T(8,128)S(1)} %get-tuple-element.54), channel_id=1, source_target_pairs={{0,8},{8,0},{16,24},{24,16},{32,40},{40,32},{48,56},{56,48},{64,72... | collective-permute-start | bytes 49160 | tf_op jit(solution)/shard_map/ppermute | solution.py:287
